TPU v7x, 128 devices: a whole 4x4x4 slice. The times are simulated.
128 devices in a mesh: patch: 32 (over y, x, z_hi), tp: 4 (over z_lo, core).
Axes of the slice: x: 4, y: 4, z: 4 (z_hi: 2, z_lo: 2; z = z_hi * 2 + z_lo), core: 2. Of those that a mesh axis runs over, the one named last changes fastest.
Arguments:
- hidden: bfloat16 [2, 4608, 5120], P(None, 'patch', 'tp'), may hold values from -6 to 6
- mod_shift: float32 [2, 5120], replicated, may hold values from -3 to 3
- mod_scale: float32 [2, 5120], replicated, may hold values from -3 to 3
- w_query: bfloat16 [5120, 2560], P(None, 'tp'), may hold values from -4 to 4
- w_key: bfloat16 [5120, 2560], P(None, 'tp'), may hold values from -4 to 4
- w_value: bfloat16 [5120, 2560], P(None, 'tp'), may hold values from -0.078125 to 0.078125
- q_gain: float32 [2560], P('tp'), may hold values from 1 to 4
- k_gain: float32 [2560], P('tp'), may hold values from 0.5 to 1.5
- token_place: int32 [4608], P('patch'), may hold values from 0 to 4607, each once
- stale_keys: bfloat16 [2, 4608, 2560], P(None, 'patch', 'tp'), may hold values from -160 to 160
- stale_values: bfloat16 [2, 4608, 2560], P(None, 'patch', 'tp'), may hold values from -6 to 6
Outputs:
- attended: bfloat16 [2, 4608, 2560], P(None, 'patch', 'tp')
- fresh_keys: bfloat16 [2, 4608, 2560], P(None, 'patch', 'tp')
- fresh_values: bfloat16 [2, 4608, 2560], P(None, 'patch', 'tp')
Inputs may be any that keep to these rules, and one draw needn't show every extreme that they name: `token_place`: each slot holds a different grid token.
All inputs are finite; a program needn't handle non-finite values.
Results may differ from a plain program's by a relative error of at most 0.015.
The roundings to bfloat16 on the way count: a program that leaves them out, or rounds other values in their place, can miss the bound.
Values may be sent and summed in bfloat16 or wider, within the bound.
No kernel may reach another device: no remote copies, remote signals or barrier semaphores. Data moves between devices by JAX's collectives and lax.ppermute only.
A program may use at most 192 MiB of HBM per device.

v0:
```python
import math

import jax
import jax.numpy as jnp
from jax import lax
from jax.sharding import PartitionSpec as P

D = 5120
HEADS = 20
HD = 128
FRAMES = 3
GRID_W = 48


masked_score = -1e30
epsilon = 1e-06


def pair_angles(place, frame_tok, head_dim):
    half_dim = head_dim // 2
    third_dim = half_dim // 3
    frame_pairs = half_dim - 2 * third_dim
    frame_id = (place // frame_tok).astype(jnp.float32)
    within = place % frame_tok
    grid_row = (within // GRID_W).astype(jnp.float32)
    grid_col = (within % GRID_W).astype(jnp.float32)
    pair_idx = jnp.arange(half_dim)
    in_frame = pair_idx < frame_pairs
    in_row = (pair_idx >= frame_pairs) & (pair_idx < frame_pairs + third_dim)
    offset_pair = jnp.where(
        in_frame,
        pair_idx,
        jnp.where(in_row, pair_idx - frame_pairs, pair_idx - frame_pairs - third_dim),
    ).astype(jnp.float32)
    part_width = jnp.where(in_frame, 2 * frame_pairs, 2 * third_dim).astype(jnp.float32)
    frequency = jnp.exp(-math.log(10000.0) * 2.0 * offset_pair / part_width)
    position = jnp.where(
        in_frame[None, :],
        frame_id[:, None],
        jnp.where(in_row[None, :], grid_row[:, None], grid_col[:, None]),
    )
    return position * frequency[None, :]


def rope_tables(place, frame_tok, heads_count):
    angles = pair_angles(place, frame_tok, HD)
    cos_full = jnp.tile(jnp.repeat(jnp.cos(angles), 2, axis=1), (1, heads_count))
    sin_full = jnp.tile(jnp.repeat(jnp.sin(angles), 2, axis=1), (1, heads_count))
    return (cos_full, sin_full)


def rope_rotate(values, cos_full, sin_full):
    cols = values.shape[-1]
    even_slot = jnp.arange(cols) % 2 == 0
    next_entry = jnp.roll(values, -1, axis=-1)
    prev_entry = jnp.roll(values, 1, axis=-1)
    swapped = jnp.where(even_slot, -next_entry, prev_entry)
    return values * cos_full + swapped * sin_full


def shards(
    hidden,
    mod_shift,
    mod_scale,
    w_query,
    w_key,
    w_value,
    q_gain,
    k_gain,
    token_place,
    stale_keys,
    stale_values,
):
    batch, tok_dev, d_part = hidden.shape
    n_patch = lax.axis_size("patch")
    tokens_all = tok_dev * n_patch
    frame_tok = tokens_all // FRAMES
    frame_id = token_place // frame_tok
    clean_rows = (frame_id == 0) | (frame_id == FRAMES - 1)
    whole = lax.all_gather(hidden, "tp", axis=2, tiled=True).astype(jnp.float32)
    row_mean = jnp.mean(whole, axis=-1, keepdims=True)
    centered = whole - row_mean
    variance = jnp.mean(centered * centered, axis=-1, keepdims=True)
    normed = centered * lax.rsqrt(variance + epsilon)
    bias_rows = jnp.where(clean_rows[:, None], mod_shift[1][None, :], mod_shift[0][None, :])
    gain_rows = jnp.where(clean_rows[:, None], mod_scale[1][None, :], mod_scale[0][None, :])
    modded = (normed * (1.0 + gain_rows) + bias_rows).astype(jnp.bfloat16)
    flat_rows = modded.reshape(batch * tok_dev, D)
    queries = jnp.dot(flat_rows, w_query, preferred_element_type=jnp.float32)
    keys_new = jnp.dot(flat_rows, w_key, preferred_element_type=jnp.float32)
    values_new = jnp.dot(flat_rows, w_value, preferred_element_type=jnp.float32).astype(
        jnp.bfloat16
    )
    query_sq, key_sq = lax.psum(
        (jnp.sum(queries * queries, axis=-1), jnp.sum(keys_new * keys_new, axis=-1)), "tp"
    )
    queries = queries * lax.rsqrt(query_sq[:, None] / (HEADS * HD) + epsilon) * q_gain[None, :]
    keys_new = keys_new * lax.rsqrt(key_sq[:, None] / (HEADS * HD) + epsilon) * k_gain[None, :]
    width_dev = w_query.shape[1]
    heads_dev = width_dev // HD
    cos_full, sin_full = rope_tables(token_place, frame_tok, heads_dev)
    queries = rope_rotate(queries.reshape(batch, tok_dev, width_dev), cos_full, sin_full).astype(
        jnp.bfloat16
    )
    keys_new = rope_rotate(keys_new.reshape(batch, tok_dev, width_dev), cos_full, sin_full).astype(
        jnp.bfloat16
    )
    values_new = values_new.reshape(batch, tok_dev, width_dev)
    inverse_sqrt_scale = 1.0 / math.sqrt(HD)
    query_heads = queries.reshape(batch, tok_dev, heads_dev, HD)
    key_heads = keys_new.reshape(batch, tok_dev, heads_dev, HD)
    value_heads = values_new.reshape(batch, tok_dev, heads_dev, HD)
    scores = (
        jnp.einsum("bqhd,bkhd->bhqk", query_heads, key_heads, preferred_element_type=jnp.float32)
        * inverse_sqrt_scale
    )
    row_top = jnp.max(scores, axis=-1)
    probs = jnp.exp(scores - row_top[..., None])
    row_sum = jnp.sum(probs, axis=-1)
    output_total = jnp.einsum(
        "bhqk,bkhd->bhqd",
        probs.astype(jnp.bfloat16),
        value_heads,
        preferred_element_type=jnp.float32,
    )
    my_index = lax.axis_index("patch")
    own_first = my_index * tok_dev
    part_keys = lax.all_gather(stale_keys, "patch", axis=1, tiled=True)
    part_values = lax.all_gather(stale_values, "patch", axis=1, tiled=True)
    key_count = part_keys.shape[1]
    key_block = part_keys.reshape(batch, key_count, heads_dev, HD)
    value_block = part_values.reshape(batch, key_count, heads_dev, HD)
    block_scores = (
        jnp.einsum("bqhd,bkhd->bhqk", query_heads, key_block, preferred_element_type=jnp.float32)
        * inverse_sqrt_scale
    )
    key_index = jnp.arange(key_count)
    own_keys = (key_index >= own_first) & (key_index < own_first + tok_dev)
    block_scores = jnp.where(own_keys[None, None, None, :], masked_score, block_scores)
    new_top = jnp.maximum(row_top, jnp.max(block_scores, axis=-1))
    rescale = jnp.exp(row_top - new_top)
    block_probs = jnp.exp(block_scores - new_top[..., None])
    new_sum = row_sum * rescale + jnp.sum(block_probs, axis=-1)
    new_accum = output_total * rescale[..., None] + jnp.einsum(
        "bhqk,bkhd->bhqd",
        block_probs.astype(jnp.bfloat16),
        value_block,
        preferred_element_type=jnp.float32,
    )
    attended = (
        (new_accum / new_sum[..., None])
        .transpose(0, 2, 1, 3)
        .reshape(batch, tok_dev, width_dev)
        .astype(jnp.bfloat16)
    )
    return (attended, keys_new, values_new)


def solution(mesh):
    in_specs = (
        P(None, "patch", "tp"),
        P(),
        P(),
        P(None, "tp"),
        P(None, "tp"),
        P(None, "tp"),
        P("tp"),
        P("tp"),
        P("patch"),
        P(None, "patch", "tp"),
        P(None, "patch", "tp"),
    )
    out_specs = (P(None, "patch", "tp"), P(None, "patch", "tp"), P(None, "patch", "tp"))
    return jax.shard_map(shards, mesh=mesh, in_specs=in_specs, out_specs=out_specs, check_vma=False)
```

profile of v0, /device:TPU:0, one launch (start us, length us, event | category | flops | bytes accessed | tf_op | source)
XLA Modules:
  0.0 361.4 jit_solution(8606806057825949370)
XLA Ops:
  7.2 0.7 all-gather.4.cloned.1.call-update
  8.0 2.0 copy.40
  10.1 2.0 copy.44
  12.1 0.7 fusion.45
  12.9 0.3 fusion.33
  13.3 0.1 copy.34
  13.6 0.1 copy.35
  13.7 0.8 copy.73
  14.6 0.8 copy.74
  15.4 0.6 fusion.37
  16.0 0.6 fusion.36
  16.7 2.3 select_add_fusion
  19.0 29.1 %all-gather.4.cloned.1.call-done = bf16[2,144,5120]{2,1,0:T(8,128)(2,1)} async-done(((bf16[2,144,1280]{2,1,0:T(8,128)(2,1)}), bf16[2,144,5120]{2,1,0:T(8,128)(2,1)}) %all-gather.4.cloned.1.call-update) | async-done | bytes 2949136 | tf_op jit(solution)/shard_map/all_gather | solution.py:80
  48.1 2.5 convert_reduce_fusion
  50.6 2.9 fusion.11
  53.5 1.6 fusion.14
  55.2 1.6 copy-done.2
  56.8 2.5 convolution_convert_fusion
  59.3 1.3 reshape_reshape.3
  60.6 6.8 %multiply_reduce_fusion = (f32[288]{0:T(512)S(1)}, f32[288,640]{1,0:T(8,128)S(1)}) fusion(bf16[288,5120]{1,0:T(8,128)(2,1)} %bitcast.69, bf16[5120,640]{1,0:T(8,128)(2,1)} %param.15), kind=kOutput, calls=%fused_computation.41 | convolution fusion | flops 1887805184 | bytes 10241152 | tf_op jit(solution)/shard_map/dot_general | solution.py:90
  67.4 5.5 %multiply_reduce_fusion.1 = (f32[288]{0:T(512)S(1)}, f32[288,640]{1,0:T(8,128)S(1)}) fusion(bf16[288,5120]{1,0:T(8,128)(2,1)S(1)} %bitcast.70, bf16[5120,640]{1,0:T(8,128)(2,1)} %param.14), kind=kOutput, calls=%fused_computation.43 | convolution fusion | flops 1887805184 | bytes 10241152 | tf_op jit(solution)/shard_map/dot_general | solution.py:89
  72.9 6.8 %all-reduce = (f32[288]{0:T(512)S(1)}, f32[288]{0:T(512)S(1)}) all-reduce(f32[288]{0:T(512)S(1)} %get-tuple-element.34, f32[288]{0:T(512)S(1)} %get-tuple-element.36), channel_id=1, replica_groups=mesh['patch'=32,'tp'=4] {'tp'}, use_global_device_ids=true, to_apply=%region_3.4 | all-reduce | flops 576 | bytes 4608 | tf_op jit(solution)/shard_map/psum | solution.py:94
  79.8 0.1 multiply_multiply_fusion.1
  79.9 0.1 reshape.235
  80.1 0.1 multiply_multiply_fusion
  80.2 1.2 reshape.237
  81.4 0.7 fusion.54
  82.0 0.3 fusion.55
  82.3 0.3 pad_maximum_fusion
  82.6 1.1 concatenate.20
  83.7 1.0 maximum_negate_fusion
  84.7 1.1 neg.15
  86.0 0.3 fusion.52
  86.2 2.5 add_convert_fusion.2
  88.7 1.2 concatenate.23
  89.9 1.2 neg.17
  91.1 2.9 add_convert_fusion
  93.9 0.4 fusion.58
  94.3 0.2 fusion.15
  94.6 83.0 %all-gather.6.cloned.1.call-done = bf16[2,4608,640]{2,0,1:T(2,128)(2,1)} async-done(((bf16[2,144,640]{2,0,1:T(2,128)(2,1)}), bf16[2,4608,640]{2,0,1:T(2,128)(2,1)}) %all-gather.6.cloned.1.call-update) | async-done | bytes 11796496 | tf_op jit(solution)/shard_map/all_gather | solution.py:128
  177.5 29.4 %copy.41 = bf16[2,4608,640]{1,2,0:T(8,128)(2,1)} copy(bf16[2,4608,640]{2,0,1:T(2,128)(2,1)} %all-gather.6.cloned.1.call-done) | data formatting | bytes 23592960 | tf_op jit(solution)/shard_map/all_gather | solution.py:128
  207.0 13.7 %fusion = (f32[2,5,144]{2,1,0:T(8,128)S(1)}, f32[2,5,144,4608]{3,2,1,0:T(8,128)}) fusion(pred[4608]{0:T(1024)(128)(4,1)S(1)} %fusion.34, bf16[2,4608,5,128]{1,3,2,0:T(8,128)(2,1)} %bitcast.61, bf16[2,144,5,128]{3,2,1,0:T(8,128)(2,1)S(1)} %get-tuple-element.21), kind=kOutput, calls=%fused_computation.2 | convolution fusion | flops 1718598272 | bytes 38717568 | tf_op jit(solution)/shard_map/bqhd,bkhd->bhqk/dot_general | solution.py:134
  220.7 11.9 %fusion.1 = f32[2,5,144]{2,1,0:T(8,128)S(1)} fusion(f32[2,5,144,4608]{3,2,1,0:T(8,128)} %get-tuple-element.41, f32[2,5,144]{2,1,0:T(8,128)S(1)} %max.18, pred[4608]{0:T(1024)(128)(4,1)S(1)} %fusion.34), kind=kLoop, calls=%fused_computation.3 | loop fusion | flops 26540640 | bytes 26558208 | tf_op jit(solution)/shard_map/reduce_sum | solution.py:143
  232.5 71.5 %all-gather.8.cloned.1.call-done = bf16[2,4608,640]{2,0,1:T(2,128)(2,1)} async-done(((bf16[2,144,640]{2,0,1:T(2,128)(2,1)}), bf16[2,4608,640]{2,0,1:T(2,128)(2,1)}) %all-gather.8.cloned.1.call-update) | async-done | bytes 11796496 | tf_op jit(solution)/shard_map/all_gather | solution.py:129
  304.0 29.4 %copy.45 = bf16[2,4608,640]{1,2,0:T(8,128)(2,1)} copy(bf16[2,4608,640]{2,0,1:T(2,128)(2,1)} %all-gather.8.cloned.1.call-done) | data formatting | bytes 23592960 | tf_op jit(solution)/shard_map/all_gather | solution.py:129
  333.4 19.8 %fusion.20 = f32[2,144,5,128]{3,1,2,0:T(8,128)S(1)} fusion(bf16[2,4608,5,128]{1,3,2,0:T(8,128)(2,1)} %bitcast.67, f32[2,5,144,4608]{3,2,1,0:T(8,128)} %get-tuple-element.41, f32[2,5,144]{2,1,0:T(8,128)S(1)} %max.18, pred[4608]{0:T(1024)(128)(4,1)S(1)} %fusion.34), kind=kOutput, calls=%fused_computation.28 | convolution fusion | flops 1725235200 | bytes 39086208 | tf_op jit(solution)/shard_map/bhqk,bkhd->bhqd/dot_general | solution.py:144
  353.3 0.8 fusion.24
  354.1 0.8 copy.75
  (51 shorter events, 0.8 us)
Async XLA Ops:
  7.2 9.4 %copy-start.6 = (f32[2,5120]{1,0:T(2,128)S(1)}, f32[2,5120]{1,0:T(2,128)}, u32[]{:S(2)}) copy-start(f32[2,5120]{1,0:T(2,128)} %param.12) | copy-start | bytes 122884
  7.2 9.5 %copy-start.7 = (f32[2,5120]{1,0:T(2,128)S(1)}, f32[2,5120]{1,0:T(2,128)}, u32[]{:S(2)}) copy-start(f32[2,5120]{1,0:T(2,128)} %param.13) | copy-start | bytes 122884
  7.2 40.9 %all-gather.4.cloned.1.call-start = ((), (), s32[]{:S(2)}) async-start(), calls=%async_computation | async-start | bytes 3686400 | tf_op jit(solution)/shard_map/all_gather | solution.py:80
  7.9 169.6 %all-gather.6.cloned.1.call-start = ((), (), s32[]{:S(2)}) async-start(), calls=%async_computation.1 | async-start | bytes 12165120 | tf_op jit(solution)/shard_map/all_gather | solution.py:128
  10.0 294.0 %all-gather.8.cloned.1.call-start = ((), (), s32[]{:S(2)}) async-start(), calls=%async_computation.2 | async-start | bytes 12165120 | tf_op jit(solution)/shard_map/all_gather | solution.py:129
  48.1 5.4 %copy-start = (bf16[2,144,5120]{2,1,0:T(8,128)(2,1)S(1)}, bf16[2,144,5120]{2,1,0:T(8,128)(2,1)}, u32[]{:S(2)}) copy-start(bf16[2,144,5120]{2,1,0:T(8,128)(2,1)} %all-gather.4.cloned.1.call-done) | copy-start | bytes 8847364
  48.1 5.4 %copy-start.1 = (f32[144,5120]{1,0:T(8,128)S(1)}, f32[144,5120]{1,0:T(8,128)}, u32[]{:S(2)}) copy-start(f32[144,5120]{1,0:T(8,128)} %get-tuple-element.33) | copy-start | bytes 8847364
  50.6 6.2 %slice-start = ((s8[6553600]{0:T(1024)(128)(4,1)}), s8[4194304]{0:T(1024)(128)(4,1)S(1)}, s32[]{:S(2)}) async-start(s8[6553600]{0:T(1024)(128)(4,1)} %bitcast.81), calls=%async_computation.3 | async-start | bytes 8388608
  53.5 3.3 slice-start.1
  55.2 1.7 copy-start.2
  59.3 1.3 copy-start.5
  60.6 6.8 %copy-start.3 = (bf16[2,144,5120]{2,1,0:T(8,128)(2,1)S(1)}, bf16[2,144,5120]{2,1,0:T(8,128)(2,1)}, u32[]{:S(2)}) copy-start(bf16[2,144,5120]{2,1,0:T(8,128)(2,1)} %copy-done.2) | copy-start | bytes 8847364
  67.4 12.4 %copy-start.8 = (f32[640]{0:T(1024)S(1)}, f32[640]{0:T(1024)}, u32[]{:S(2)}) copy-start(f32[640]{0:T(1024)} %param.17) | copy-start | bytes 7684
  67.4 12.6 %copy-start.9 = (f32[640]{0:T(1024)S(1)}, f32[640]{0:T(1024)}, u32[]{:S(2)}) copy-start(f32[640]{0:T(1024)} %param.18) | copy-start | bytes 7684
  82.3 3.9 %copy-start.11 = (pred[640]{0:T(1024)(128)(4,1)S(1)}, pred[640]{0:T(1024)(128)(4,1)}, u32[]{:S(2)}) copy-start(pred[640]{0:T(1024)(128)(4,1)} %fusion.37) | copy-start | bytes 1924
  85.9 5.1 %copy-start.10 = (pred[5,128]{1,0:T(8,128)(4,1)S(1)}, pred[5,128]{1,0:T(8,128)(4,1)}, u32[]{:S(2)}) copy-start(pred[5,128]{1,0:T(8,128)(4,1)} %fusion.36) | copy-start | bytes 1924
  333.4 19.8 %copy-start.4 = (bf16[2,144,5,128]{3,2,1,0:T(8,128)(2,1)S(1)}, bf16[2,144,5,128]{3,2,1,0:T(8,128)(2,1)}, u32[]{:S(2)}) copy-start(bf16[2,144,5,128]{3,2,1,0:T(8,128)(2,1)} %reshape_reshape.3) | copy-start | bytes 1105924
Sparse Core Ops, SparseCore 0:
  9.7 38.3 all-gather.3
  51.1 126.3 all-gather.5
  181.2 122.8 all-gather.7
where the time goes:
time: 364 us; the launch traced here: 361 us
  waiting for transfers between devices  184 us (51%)
  local copies, waits for them, and re-layouts  76 us (21%)
  matrix products  49.5 us (14%)
  other arithmetic  30.6 us (8%)
  between operations  14.1 us (4%)
  blocking collectives  6.83 us (2%)
    all_gather x1, waiting for transfers between devices, shards(): part_keys = lax.all_gather(stale_keys, 'patch', axis=1, tiled=True)  83 us
    all_gather x1, waiting for transfers between devices, shards(): part_values = lax.all_gather(stale_values, 'patch', axis=1, tiled=True)  71.5 us
    all_gather x1, local copies, waits for them, and re-layouts, shards(): part_keys = lax.all_gather(stale_keys, 'patch', axis=1, tiled=True)  29.4 us
    all_gather x1, local copies, waits for them, and re-layouts, shards(): part_values = lax.all_gather(stale_values, 'patch', axis=1, tiled=True)  29.4 us
    all_gather x1, waiting for transfers between devices, shards(): whole = lax.all_gather(hidden, 'tp', axis=2, tiled=True).astype(jnp.float32)  29.1 us
    dot_general x1, matrix products, shards(): jnp.einsum('bhqk,bkhd->bhqd', block_probs.astype(jnp.bfloat16), value_blo...  19.8 us
    dot_general x1, matrix products, shards(): jnp.einsum('bqhd,bkhd->bhqk', query_heads, key_block, preferred_element_t...  13.7 us
    reduce_sum x1, other arithmetic, shards(): new_sum = row_sum * rescale + jnp.sum(block_probs, axis=-1)  11.9 us
  transfers between devices with their start and end apart: 3, of which 3 were waited for; matrix products, arithmetic and copies ran while one was open for 29% of the time, Pallas kernels for 0%

commit v1 on v0

v1 whole, which is shorter than its diff:
```python
import functools
import math

import jax
import jax.numpy as jnp
import numpy as np
from jax import lax
from jax.experimental import pallas as pl
from jax.experimental.pallas import tpu as pltpu
from jax.sharding import PartitionSpec as P

D = 5120
HEADS = 20
HD = 128
FRAMES = 3
GRID_W = 48
EPS = 1e-06
MASKED = -1e30
NY, NX, NZ = 4, 4, 2
TP = 4
N_PATCH = NY * NX * NZ
TOK = 144
B = 2
ROWS = B * TOK
LOCAL_HEADS = 5
WIDTH = LOCAL_HEADS * HD
CHUNK = D // TP
STAT_LANES = 384
PIECE = 5 * TOK
MSG_ROWS = 2 * TOK + 16
SCORE_SCALE = math.log2(math.e) / math.sqrt(HD)
F32 = jnp.float32
BF16 = jnp.bfloat16
AXES = ("patch", "tp")


def params(mib):
    return pltpu.CompilerParams(vmem_limit_bytes=mib * 1024 * 1024)


def vmem():
    return pl.BlockSpec(memory_space=pltpu.VMEM)


def smem():
    return pl.BlockSpec(memory_space=pltpu.SMEM)


def linear(u, v, z_hi, z_lo, core):
    y, x = (u, v) if core == 0 else (v, u)
    return ((y * NX + x) * NZ + z_hi) * TP + z_lo * 2 + core


def places():
    return [
        (u, v, h, l, c)
        for u in range(4)
        for v in range(4)
        for h in range(2)
        for l in range(2)
        for c in range(2)
    ]


def permute(value, move):
    return lax.ppermute(value, AXES, [(linear(*p), linear(*move(*p))) for p in places()])


def swap_pair(value):
    return permute(value, lambda u, v, h, l, c: (u, v ^ 1, h, l, c))


def swap_v(value):
    return permute(value, lambda u, v, h, l, c: (u, v ^ 3, h, l, c))


def swap_z_hi(value):
    return permute(value, lambda u, v, h, l, c: (u, v, 1 - h, l, c))


def swap_tp(value, z, core):
    return permute(value, lambda u, v, h, l, c: (u, v, h, l ^ z, c) if not core else swapped(u, v, h, l ^ z, c))


def swapped(u, v, h, l, c):
    return v, u, h, l, 1 - c


def exchange(value):
    groups = []
    for c in range(2):
        for l in range(2):
            for h in range(2):
                for pair in ((0, 1), (3, 2)):
                    groups.append([linear(u, v, h, l, c) for v in pair for u in range(4)])
    return lax.all_to_all(value, AXES, 0, 0, axis_index_groups=groups)


def frequencies():
    half_dim = HD // 2
    third_dim = half_dim // 3
    frame_pairs = half_dim - 2 * third_dim
    pair = np.arange(HD) // 2
    offset = np.where(
        pair < frame_pairs,
        pair,
        np.where(pair < frame_pairs + third_dim, pair - frame_pairs, pair - frame_pairs - third_dim),
    )
    width = np.where(pair < frame_pairs, 2 * frame_pairs, 2 * third_dim)
    return np.exp(-math.log(10000.0) * 2.0 * offset / width).astype(np.float32).reshape(1, HD)


def columns_to_rows(first, second):
    lane = lax.broadcasted_iota(jnp.int32, (ROWS, 128), 1)
    both = jnp.where(lane == 0, first, jnp.where(lane == 1, second, 0.0))
    padded = jnp.concatenate([both, jnp.zeros((STAT_LANES - ROWS, 128), F32)], axis=0)
    return padded.T[0:8]


def row_to_column(row):
    return jnp.broadcast_to(row, (128, STAT_LANES)).T[0:ROWS]


def stats_kernel(hidden_ref, out_ref):
    part = hidden_ref[...].astype(F32)
    mean = jnp.sum(part, axis=1, keepdims=True) * (1.0 / CHUNK)
    centered = part - mean
    deviation = jnp.sum(centered * centered, axis=1, keepdims=True)
    out_ref[...] = columns_to_rows(mean, deviation)


def row_stats(hidden_rows):
    return pl.pallas_call(
        stats_kernel,
        out_shape=jax.ShapeDtypeStruct((8, STAT_LANES), F32),
        in_specs=[vmem()],
        out_specs=vmem(),
        compiler_params=params(16),
        cost_estimate=pl.CostEstimate(
            flops=4 * ROWS * CHUNK, bytes_accessed=2 * ROWS * CHUNK, transcendentals=0
        ),
        name="row_stats",
    )(hidden_rows)


def prepare_kernel(s_ref, place_hbm, freq, key_hbm, value_hbm, *refs):
    refs = refs[3:]
    send, last_own, last_send, cond, cos, sin, places_s, place_ref, key_ref, value_ref, sems = refs
    copies = [
        pltpu.make_async_copy(source, target, sems.at[n])
        for n, (source, target) in enumerate(
            ((key_hbm, key_ref), (value_hbm, value_ref), (place_hbm, place_ref))
        )
    ]
    for copy in copies:
        copy.start()
    copies[2].wait()
    for row in range(TOK):
        places_s[row : row + 1] = jnp.full((1, HD), place_ref[row], jnp.int32)
    place = places_s[...]
    frame_tok = TOK * N_PATCH // FRAMES
    frame = jnp.where(place >= frame_tok, 1, 0) + jnp.where(place >= 2 * frame_tok, 1, 0)
    within = place - frame * frame_tok
    grid_row = ((within.astype(F32) + 0.5) * (1.0 / GRID_W)).astype(jnp.int32)
    grid_col = within - grid_row * GRID_W
    lane = lax.broadcasted_iota(jnp.int32, (TOK, HD), 1)
    third = 2 * (HD // 6)
    frame_lanes = HD - 2 * third
    position = jnp.where(
        lane < frame_lanes, frame, jnp.where(lane < frame_lanes + third, grid_row, grid_col)
    )
    angles = position.astype(F32) * freq[...]
    cos[...] = jnp.cos(angles)
    sine = jnp.sin(angles)
    sin[...] = jnp.where(lane % 2 == 0, -sine, sine)
    flag = jnp.where((frame == 0) | (frame == FRAMES - 1), 1.0, 0.0)
    cond[0:TOK] = flag
    cond[TOK:ROWS] = flag
    own = s_ref[0]
    for n, ref in enumerate((key_ref, value_ref)):
        copies[n].wait()
        for s in range(B):
            for head in range(4):
                send[s * 4 + head, n] = ref[s, :, head * HD : (head + 1) * HD]
        last_own[n] = ref[own, :, 4 * HD :]
        last_send[n] = ref[1 - own, :, 4 * HD :]


def prepare(s, token_place, stale_keys, stale_values, after):
    table = jax.ShapeDtypeStruct((TOK, HD), F32)
    last = jax.ShapeDtypeStruct((2, TOK, HD), BF16)
    hbm = pl.BlockSpec(memory_space=pltpu.HBM)
    return pl.pallas_call(
        prepare_kernel,
        out_shape=[
            jax.ShapeDtypeStruct((8, 2, TOK, HD), BF16),
            last,
            last,
            jax.ShapeDtypeStruct((ROWS, HD), F32),
            table,
            table,
        ],
        in_specs=[smem(), hbm, vmem(), hbm, hbm] + [pl.BlockSpec(memory_space=pl.ANY)] * 3,
        out_specs=[vmem()] * 6,
        scratch_shapes=[
            pltpu.VMEM((TOK, HD), jnp.int32),
            pltpu.SMEM((TOK,), jnp.int32),
            pltpu.VMEM((B, TOK, WIDTH), BF16),
            pltpu.VMEM((B, TOK, WIDTH), BF16),
            pltpu.SemaphoreType.DMA((3,)),
        ],
        compiler_params=params(58),
        cost_estimate=pl.CostEstimate(
            flops=100 * TOK * HD, bytes_accessed=8 * ROWS * WIDTH, transcendentals=0
        ),
        name="prepare",
    )(s, token_place, jnp.asarray(frequencies()), stale_keys, stale_values, *after)


def assemble_kernel(s_ref, arrived, last_own, last_other, first, second):
    own = s_ref[0]
    for n in range(2):
        for u in range(4):
            first[n, u * TOK : (u + 1) * TOK] = arrived[u, n]
            second[n, u * TOK : (u + 1) * TOK] = arrived[4 + u, n]
        mine, other = last_own[n], last_other[n]
        first[n, 4 * TOK :] = jnp.where(own == 0, mine, other)
        second[n, 4 * TOK :] = jnp.where(own == 0, other, mine)


def assemble(s, arrived, last_own, last_other):
    shape = jax.ShapeDtypeStruct((2, PIECE, HD), BF16)
    return pl.pallas_call(
        assemble_kernel,
        out_shape=[shape, shape],
        in_specs=[smem()] + [vmem()] * 3,
        out_specs=[vmem()] * 2,
        compiler_params=params(32),
        cost_estimate=pl.CostEstimate(
            flops=0, bytes_accessed=16 * PIECE * HD, transcendentals=0
        ),
        name="assemble",
    )(s, arrived, last_own, last_other)


def merged_stats(refs):
    means = [ref[0:1] for ref in refs]
    mean = (means[0] + means[1] + means[2] + means[3]) * 0.25
    total = jnp.zeros_like(mean)
    for ref, one in zip(refs, means):
        total = total + (ref[1:2] + CHUNK * (one - mean) * (one - mean))
    return mean, lax.rsqrt(total * (1.0 / D) + EPS)


def project_kernel(count, first, last, *refs):
    t_ref = refs[0]
    chunks = refs[1 : 1 + count]
    cond, shift, scale, w_q, w_k, w_v, s0, s1, s2, s3 = refs[1 + count : 11 + count]
    rest = list(refs[11 + count :])
    acc_in = None if first else rest.pop(0)
    if last:
        q_out, k_out, v_out, sq_out, buffer, sems = rest
    else:
        acc, buffer, sems = rest
    copies = {}
    for c in range(count):
        row = pl.multiple_of(t_ref[c] * CHUNK, CHUNK)
        for n, weight in enumerate((w_q, w_k, w_v)):
            copies[c, n] = pltpu.make_async_copy(
                weight.at[pl.ds(row, CHUNK)], buffer.at[c, n], sems.at[c, n]
            )
            copies[c, n].start()
    mean, rstd = merged_stats((s0, s1, s2, s3))
    mean = row_to_column(mean)[:, 0:1]
    rstd = row_to_column(rstd)[:, 0:1]
    conditioned = cond[:, 0:1] > 0.5
    totals = [None] * 3
    for c in range(count):
        cols = pl.ds(pl.multiple_of(t_ref[c] * CHUNK, CHUNK), CHUNK)
        part = chunks[c][...].astype(F32)
        gain = jnp.where(conditioned, scale[1:2, cols], scale[0:1, cols])
        bias = jnp.where(conditioned, shift[1:2, cols], shift[0:1, cols])
        modded = ((part - mean) * rstd * (1.0 + gain) + bias).astype(BF16)
        for n in range(3):
            columns = slice(n * WIDTH, (n + 1) * WIDTH)
            copies[c, n].wait()
            product = jnp.dot(modded, buffer[c, n], preferred_element_type=F32)
            if c == 0 and not first:
                product = product + acc_in[:, columns]
            if last:
                totals[n] = product
            elif c == 0:
                acc[:, columns] = product
            else:
                acc[:, columns] += product
    if last:
        query, key, value = totals
        q_out[...] = query
        k_out[...] = key
        v_out[...] = value.astype(BF16)
        sq_out[...] = columns_to_rows(
            jnp.sum(query * query, axis=1, keepdims=True),
            jnp.sum(key * key, axis=1, keepdims=True),
        )


def project(name, blocks, chunks, cond, shift, scale, weights, stats, acc=None, last=False):
    count = len(chunks)
    hbm = pl.BlockSpec(memory_space=pltpu.HBM)
    in_specs = [smem()] + [vmem()] * (count + 3) + [hbm] * 3 + [vmem()] * 4
    args = [blocks, *chunks, cond, shift, scale, *weights, *stats]
    if acc is not None:
        in_specs.append(vmem())
        args.append(acc)
    if last:
        out_shape = [
            jax.ShapeDtypeStruct((ROWS, WIDTH), F32),
            jax.ShapeDtypeStruct((ROWS, WIDTH), F32),
            jax.ShapeDtypeStruct((ROWS, WIDTH), BF16),
            jax.ShapeDtypeStruct((8, STAT_LANES), F32),
        ]
        out_specs = [vmem()] * 4
    else:
        out_shape = jax.ShapeDtypeStruct((ROWS, 3 * WIDTH), F32)
        out_specs = vmem()
    return pl.pallas_call(
        functools.partial(project_kernel, count, acc is None, last),
        out_shape=out_shape,
        in_specs=in_specs,
        out_specs=out_specs,
        scratch_shapes=[
            pltpu.VMEM((count, 3, CHUNK, WIDTH), BF16),
            pltpu.SemaphoreType.DMA((count, 3)),
        ],
        compiler_params=params(58),
        cost_estimate=pl.CostEstimate(
            flops=2 * ROWS * count * CHUNK * 3 * WIDTH,
            bytes_accessed=2 * count * CHUNK * 3 * WIDTH,
            transcendentals=0,
        ),
        name=name,
    )(*args)


def rope_kernel(q_ref, k_ref, squares, qg, kg, cos, sin, q_all, k_all, send):
    total = squares[0] + squares[1] + squares[2] + squares[3]
    inverse = lax.rsqrt(total * (1.0 / (HEADS * HD)) + EPS)
    even = lax.broadcasted_iota(jnp.int32, (ROWS, HD), 1) % 2 == 0
    cos_rows = jnp.concatenate([cos[...], cos[...]], axis=0)
    sin_rows = jnp.concatenate([sin[...], sin[...]], axis=0)

    def rotate(ref, column, gain, cols):
        part = ref[:, cols] * column * gain[cols].reshape(1, HD)
        swap = jnp.where(even, pltpu.roll(part, HD - 1, 1), pltpu.roll(part, 1, 1))
        return (part * cos_rows + swap * sin_rows).astype(BF16)

    q_column = row_to_column(inverse[0:1])
    k_column = row_to_column(inverse[1:2])
    for head in range(LOCAL_HEADS):
        cols = slice(head * HD, (head + 1) * HD)
        query = rotate(q_ref, q_column, qg, cols)
        q_all[:, cols] = query
        for s in range(B):
            rows = query[s * TOK : (s + 1) * TOK]
            if head < 4:
                send[s * 4 + head, 0] = rows
            else:
                for u in range(4):
                    send[s * 4 + u, 1] = rows
        k_all[:, cols] = rotate(k_ref, k_column, kg, cols)


def norm_rope(query, key, squares, q_gain, k_gain, cos, sin):
    flat = jax.ShapeDtypeStruct((ROWS, WIDTH), BF16)
    return pl.pallas_call(
        rope_kernel,
        out_shape=[flat, flat, jax.ShapeDtypeStruct((8, 2, TOK, HD), BF16)],
        in_specs=[vmem()] * 7,
        out_specs=[vmem()] * 3,
        compiler_params=params(32),
        cost_estimate=pl.CostEstimate(
            flops=20 * ROWS * WIDTH, bytes_accessed=16 * ROWS * WIDTH, transcendentals=0
        ),
        name="norm_rope",
    )(query, key, squares, q_gain, k_gain, cos, sin)


def scores_of(query, keys):
    return lax.dot_general(query, keys, (((1,), (1,)), ((), ())), preferred_element_type=F32)


def fresh_kernel(q_ref, k_ref, v_ref, out_ref, lse_ref):
    for s in range(B):
        rows = slice(s * TOK, (s + 1) * TOK)
        for head in range(LOCAL_HEADS):
            cols = slice(head * HD, (head + 1) * HD)
            scores = scores_of(q_ref[rows, cols], k_ref[rows, cols])
            top = jnp.max(scores, axis=1, keepdims=True)
            probs = jnp.exp2((scores - top) * SCORE_SCALE)
            total = jnp.sum(probs, axis=1, keepdims=True)
            out = jnp.dot(probs.astype(BF16), v_ref[rows, cols], preferred_element_type=F32)
            out_ref[head, s] = out / total
            lse_ref[head, s] = jnp.broadcast_to(top * SCORE_SCALE + jnp.log2(total), (TOK, HD))


def fresh_attention(query, key, value):
    shape = jax.ShapeDtypeStruct((LOCAL_HEADS, B, TOK, HD), F32)
    return pl.pallas_call(
        fresh_kernel,
        out_shape=[shape, shape],
        in_specs=[vmem()] * 3,
        out_specs=[vmem()] * 2,
        compiler_params=params(32),
        cost_estimate=pl.CostEstimate(
            flops=4 * ROWS * TOK * WIDTH,
            bytes_accessed=14 * ROWS * WIDTH,
            transcendentals=ROWS * TOK * LOCAL_HEADS,
        ),
        name="fresh_attention",
    )(query, key, value)


TILE = 2 * TOK
GROUP = 16
PER_PIECE = 4 * TOK
KEYS = 4 * PER_PIECE
KEYS_LAST = 4 * TOK


def stale_kernel(far, u_ref, queries, *refs):
    pieces = refs[0:4]
    if far:
        near_out, near_lse, _, msg_ref = refs[4:8]
    else:
        out_ref, lse_ref = refs[4:6]
    lse_s, k_main, v_main, k_last, v_last, scores_s, probs_s, sems = refs[-8:]
    copies = []
    for n, piece in enumerate(pieces):
        main, last = pl.ds(n * PER_PIECE, PER_PIECE), pl.ds(n * TOK, TOK)
        head, tail = pl.ds(0, PER_PIECE), pl.ds(PER_PIECE, TOK)
        for kind, part, target, rows in (
            (0, head, k_main, main),
            (1, head, v_main, main),
            (0, tail, k_last, last),
            (1, tail, v_last, last),
        ):
            copy = pltpu.make_async_copy(
                piece.at[kind, part], target.at[rows], sems.at[len(copies)]
            )
            copy.start()
            copies.append(copy)
    for copy in copies:
        copy.wait()

    jobs = [(tile, e) for tile in range(4) for e in range(2)]

    def score(i):
        tile, e = jobs[i]
        count = KEYS_LAST if e else KEYS
        query = jnp.concatenate([queries[2 * tile, e], queries[2 * tile + 1, e]], axis=0)
        out = scores_s.at[i % 2]
        out[:, 0:count] = scores_of(query, k_last[...] if e else k_main[...])
        if far:
            return
        for n in range(2):
            block = 2 * tile + n
            rows = slice(n * TOK, (n + 1) * TOK)
            if not e:
                out[rows, block * TOK : (block + 1) * TOK] = jnp.full((TOK, TOK), MASKED, F32)
            else:
                lane = lax.broadcasted_iota(jnp.int32, (TOK, 384), 1)
                low = block // 4 * TOK
                own = (lane >= low) & (lane < low + TOK) & (u_ref[0] == block % 4)
                out[rows, 0:384] = jnp.where(own, MASKED, out[rows, 0:384])

    def softmax(i):
        count = KEYS_LAST if jobs[i][1] else KEYS
        tops, totals = [], []
        for row in range(0, TILE, GROUP):
            rows = slice(row, row + GROUP)
            part = scores_s[i % 2, rows, 0:count]
            top = jnp.max(part, axis=1, keepdims=True)
            probs = jnp.exp2((part - top) * SCORE_SCALE)
            totals.append(jnp.sum(probs, axis=1, keepdims=True))
            tops.append(top)
            probs_s[i % 2, rows, 0:count] = probs.astype(BF16)
        return jnp.concatenate(tops, axis=0), jnp.concatenate(totals, axis=0)

    def finish(i, top, total):
        tile, e = jobs[i]
        count = KEYS_LAST if e else KEYS
        values = v_last[...] if e else v_main[...]
        out = jnp.dot(probs_s[i % 2, :, 0:count], values, preferred_element_type=F32) / total
        lse = top * SCORE_SCALE + jnp.log2(total)
        rows = slice(tile * TILE, (tile + 1) * TILE)
        if not far:
            out_ref[e, rows] = out
            lse_ref[e, rows] = jnp.broadcast_to(lse, (TILE, HD))
            return
        lse_near = near_lse[e, rows][:, 0:1]
        high = jnp.maximum(lse, lse_near)
        weight, weight_near = jnp.exp2(lse - high), jnp.exp2(lse_near - high)
        both = weight + weight_near
        out = (out * weight + near_out[e, rows] * weight_near) / both
        lse_s[e, rows] = jnp.broadcast_to(high + jnp.log2(both), (TILE, HD))
        for n in range(2):
            msg_ref[2 * tile + n, e * TOK : (e + 1) * TOK] = out[n * TOK : (n + 1) * TOK].astype(BF16)

    score(0)
    for i in range(len(jobs)):
        if i + 1 < len(jobs):
            score(i + 1)
        finish(i, *softmax(i))
    if far:
        lane = lax.broadcasted_iota(jnp.int32, (HD, HD), 1)
        table = jnp.zeros((HD, HD), F32)
        rest_rows = jnp.zeros((2 * HD - TOK, HD), F32)
        for block in range(8):
            for e in range(2):
                at = block * TOK
                first = lse_s[e, at : at + HD]
                rest = jnp.concatenate([lse_s[e, at + HD : at + TOK], rest_rows], axis=0)
                table = jnp.where(lane == block * 4 + e * 2, first, table)
                table = jnp.where(lane == block * 4 + e * 2 + 1, rest, table)
        flat = table.T
        for block in range(8):
            part = flat[block * 4 : block * 4 + 4]
            high = part.astype(BF16).astype(F32)
            middle = (part - high).astype(BF16).astype(F32)
            low = part - high - middle
            stack = jnp.concatenate([high, middle, low, jnp.zeros((4, HD), F32)], axis=0)
            msg_ref[block, 2 * TOK : MSG_ROWS] = stack.astype(BF16)


def stale_attention(u, queries, pieces, near=None, after=None):
    far = near is not None
    args = [u, queries, *pieces]
    hbm = pl.BlockSpec(memory_space=pltpu.HBM)
    in_specs = [smem(), vmem()] + [hbm] * 4
    state = jax.ShapeDtypeStruct((2, 8 * TOK, HD), F32)
    if far:
        args += [*near, after]
        in_specs += [vmem()] * 2 + [pl.BlockSpec(memory_space=pl.ANY)]
        out_shape = jax.ShapeDtypeStruct((8, MSG_ROWS, HD), BF16)
        out_specs = vmem()
    else:
        out_shape = [state, state]
        out_specs = [vmem()] * 2
    work = 8 * TOK * (KEYS + KEYS_LAST)
    return pl.pallas_call(
        functools.partial(stale_kernel, far),
        out_shape=out_shape,
        in_specs=in_specs,
        out_specs=out_specs,
        scratch_shapes=[
            pltpu.VMEM((2, 8 * TOK, HD), F32),
            pltpu.VMEM((KEYS, HD), BF16),
            pltpu.VMEM((KEYS, HD), BF16),
            pltpu.VMEM((KEYS_LAST, HD), BF16),
            pltpu.VMEM((KEYS_LAST, HD), BF16),
            pltpu.VMEM((2, TILE, KEYS), F32),
            pltpu.VMEM((2, TILE, KEYS), BF16),
            pltpu.SemaphoreType.DMA((16,)),
        ],
        compiler_params=params(40),
        cost_estimate=pl.CostEstimate(
            flops=4 * work * HD, bytes_accessed=4 * (KEYS + KEYS_LAST) * HD, transcendentals=work
        ),
        name="far_attention" if far else "near_attention",
    )(*args)


def merge_kernel(fresh_out, fresh_lse, msgs, out_ref):
    rows = []
    for block in range(8):
        stack = msgs[block, 2 * TOK : MSG_ROWS].astype(F32)
        rows.append(stack[0:4] + stack[4:8] + stack[8:12])
    table = jnp.concatenate(rows + [jnp.zeros((HD - 32, HD), F32)], axis=0).T

    def message(block, e):
        at = block * 4 + e * 2
        lse = jnp.concatenate([table[:, at : at + 1], table[0 : TOK - HD, at + 1 : at + 2]], axis=0)
        return msgs[block, e * TOK : (e + 1) * TOK].astype(F32), lse

    def combine(parts):
        top = parts[0][1]
        for _, lse in parts[1:]:
            top = jnp.maximum(top, lse)
        total = out = None
        for value, lse in parts:
            weight = jnp.exp2(lse - top)
            term = value * weight
            total = weight if total is None else total + weight
            out = term if out is None else out + term
        return (out / total).astype(BF16)

    for s in range(B):
        for head in range(LOCAL_HEADS):
            parts = [(fresh_out[head, s], fresh_lse[head, s][:, 0:1])]
            if head < 4:
                parts.append(message(s * 4 + head, 0))
            else:
                parts += [message(s * 4 + u, 1) for u in range(4)]
            out_ref[s, :, head * HD : (head + 1) * HD] = combine(parts)


def merge(fresh_out, fresh_lse, msgs):
    return pl.pallas_call(
        merge_kernel,
        out_shape=jax.ShapeDtypeStruct((B, TOK, WIDTH), BF16),
        in_specs=[vmem()] * 3,
        out_specs=vmem(),
        compiler_params=params(32),
        cost_estimate=pl.CostEstimate(
            flops=10 * ROWS * WIDTH, bytes_accessed=14 * ROWS * WIDTH, transcendentals=0
        ),
        name="merge",
    )(fresh_out, fresh_lse, msgs)


def shards(
    hidden,
    mod_shift,
    mod_scale,
    w_query,
    w_key,
    w_value,
    q_gain,
    k_gain,
    token_place,
    stale_keys,
    stale_values,
):
    patch = lax.axis_index("patch")
    tp = lax.axis_index("tp")
    y = patch // (NX * NZ)
    x = (patch // NZ) % NX
    u = jnp.where(tp % 2 == 0, y, x).astype(jnp.int32).reshape(1)
    v = jnp.where(tp % 2 == 0, x, y).astype(jnp.int32).reshape(1)
    s = (v ^ (v >> 1)) & 1

    own_rows = hidden.reshape(ROWS, CHUNK)
    z_rows = swap_tp(own_rows, 1, 0)
    core_rows = swap_tp(own_rows, 0, 1)

    own_stats = row_stats(own_rows)
    stats = [own_stats] + [swap_tp(own_stats, z, c) for z, c in ((0, 1), (1, 0), (1, 1))]

    send, last_own, last_send, cond, cos, sin = prepare(
        s, token_place, stale_keys, stale_values, stats[1:]
    )
    near = assemble(s, exchange(send), last_own, swap_pair(last_send))
    near_all = [*near, *[swap_v(piece) for piece in near]]

    weights = (w_query, w_key, w_value)
    block = lambda flip: (tp ^ flip).astype(jnp.int32).reshape(1)
    blocks = jnp.concatenate([block(0), block(1)])
    same = (cond, mod_shift, mod_scale, weights, stats)
    acc = project("project_chip", blocks, [own_rows, core_rows], *same)

    *near, z_rows = lax.optimization_barrier((*near, z_rows))
    cross_rows = swap_tp(z_rows, 0, 1)
    far = [swap_z_hi(piece) for piece in near]
    far_all = [*far, *[swap_v(piece) for piece in far]]
    acc = project("project_z", block(2), [z_rows], *same, acc=acc)
    query, key, fresh_values, own_sq = project(
        "project_cross", block(3), [cross_rows], *same, acc=acc, last=True
    )

    squares = lax.all_to_all(jnp.broadcast_to(own_sq, (TP, 8, STAT_LANES)), "tp", 0, 0)
    q_all, fresh_keys, send = norm_rope(query, key, squares, q_gain, k_gain, cos, sin)
    queries = exchange(send)
    fresh_out, fresh_lse = fresh_attention(q_all, fresh_keys, fresh_values)

    partial = stale_attention(u, queries, near_all)
    msgs = exchange(stale_attention(u, queries, far_all, near=partial, after=fresh_lse))
    attended = merge(fresh_out, fresh_lse, msgs)
    return (
        attended,
        fresh_keys.reshape(B, TOK, WIDTH),
        fresh_values.reshape(B, TOK, WIDTH),
    )


def solution(mesh):
    in_specs = (
        P(None, "patch", "tp"),
        P(),
        P(),
        P(None, "tp"),
        P(None, "tp"),
        P(None, "tp"),
        P("tp"),
        P("tp"),
        P("patch"),
        P(None, "patch", "tp"),
        P(None, "patch", "tp"),
    )
    out_specs = (P(None, "patch", "tp"), P(None, "patch", "tp"), P(None, "patch", "tp"))
    return jax.shard_map(shards, mesh=mesh, in_specs=in_specs, out_specs=out_specs, check_vma=False)
```

time: 364 us -> 137 us (0.38)
  waiting for transfers between devices: 184 us -> 28.4 us
  local copies, waits for them, and re-layouts: 76 us -> 8.05 us
  Pallas kernels: 0 us -> 50.6 us
  matrix products: 49.5 us -> 0 us
  other arithmetic: 30.6 us -> 0.61 us
  starting transfers between devices: 0.12 us -> 25.8 us
  blocking collectives: 6.83 us -> 21.5 us
  between operations: 14.1 us -> 0.82 us
    all_gather x3 -> x0, waiting for transfers between devices: 184 us -> none  [the longest x1 83 us: shards(): part_keys = lax.all_gather(stale_keys, 'patch', axis=1, tiled=True)]
    all_gather x2 -> x0, local copies, waits for them, and re-layouts: 58.8 us -> none  [the longest x1 29.4 us: shards(): part_keys = lax.all_gather(stale_keys, 'patch', axis=1, tiled=True)]
    pallas_call x0 -> x11, Pallas kernels: none -> 50.6 us  [the longest x3 24.7 us: project(): pl.pallas_call(functools.partial(project_kernel, count, acc is None, last...]
    dot_general x7 -> x0, matrix products: 49.5 us -> none  [the longest x1 19.8 us: shards(): jnp.einsum('bhqk,bkhd->bhqd', block_probs.astype(jnp.bfloat16), value_blo...]
    ppermute x0 -> x13, waiting for transfers between devices: none -> 27.1 us  [permute(): lax.ppermute(value, AXES, [(linear(*p), linear(*move(*p))) for p in place...]
    all_to_all x0 -> x2, blocking collectives: none -> 21.5 us  [the longest x1 14.8 us: exchange(): return lax.all_to_all(value, AXES, 0, 0, axis_index_groups=groups)]
    reduce_sum x4 -> x0, other arithmetic: 17.5 us -> none  [the longest x1 11.9 us: shards(): new_sum = row_sum * rescale + jnp.sum(block_probs, axis=-1)]
    ppermute x0 -> x13, starting transfers between devices: none -> 16.4 us  [permute(): lax.ppermute(value, AXES, [(linear(*p), linear(*move(*p))) for p in place...]
  transfers between devices with their start and end apart: 3 -> 15, of which waited for: 3 -> 6; matrix products, arithmetic and copies ran while one was open for 29% -> 1% of each run, Pallas kernels for 0% -> 28%
where the time goes in v1:
time: 137 us; the launch traced here: 136 us
  Pallas kernels  50.6 us (37%)
  waiting for transfers between devices  28.4 us (21%)
  starting transfers between devices  25.8 us (19%)
  blocking collectives  21.5 us (16%)
  local copies, waits for them, and re-layouts  8.05 us (6%)
    ppermute x13, waiting for transfers between devices, permute(): lax.ppermute(value, AXES, [(linear(*p), linear(*move(*p))) for p in place...  27.1 us
    pallas_call x3, Pallas kernels, project(): pl.pallas_call(functools.partial(project_kernel, count, acc is None, last...  24.7 us
    ppermute x13, starting transfers between devices, permute(): lax.ppermute(value, AXES, [(linear(*p), linear(*move(*p))) for p in place...  16.4 us
    pallas_call x2, Pallas kernels, stale_attention(): pl.pallas_call(functools.partial(stale_kernel, far), out_shape=out_shape,...  15.3 us
    all_to_all x1, blocking collectives, exchange(): return lax.all_to_all(value, AXES, 0, 0, axis_index_groups=groups)  14.8 us
    all_to_all x2, starting transfers between devices, exchange(): return lax.all_to_all(value, AXES, 0, 0, axis_index_groups=groups)  9.4 us
    unnamed x32, local copies, waits for them, and re-layouts  7.33 us
    all_to_all x1, blocking collectives, shards(): lax.all_to_all(jnp.broadcast_to(own_sq, (TP, 8, STAT_LANES)), 'tp', 0, 0)  6.64 us
  transfers between devices with their start and end apart: 15, of which 6 were waited for; matrix products, arithmetic and copies ran while one was open for 1% of the time, Pallas kernels for 28%

profile of v1, /device:TPU:0, one launch (start us, length us, event | category | flops | bytes accessed | tf_op | source)
XLA Modules:
  0.0 135.8 jit_solution(3143529298815461708)
XLA Ops:
  0.6 2.1 %collective-permute-start.4 = (bf16[288,1280]{1,0:T(8,128)(2,1)}, bf16[288,1280]{1,0:T(8,128)(2,1)}, u32[]{:S(2)}, u32[]{:S(2)}) collective-permute-start(bf16[288,1280]{1,0:T(8,128)(2,1)} %bitcast.9), channel_id=1, source_target_pairs={{0,2},{1,3},{2,0},{3,1},{4,6},{5,7},{6,4},{7,5},{8,10},{33,35},{10... | collective-permute-start | bytes 2211848 | tf_op jit(solution)/shard_map/ppermute | solution.py:66
  2.7 1.1 copy-done
  3.9 0.4 row_stats.1.refs_9_.refs_8_
  4.3 0.1 collective-permute-start
  4.4 0.1 collective-permute-start.1
  4.5 1.8 %collective-permute-start.2 = (f32[8,384]{1,0:T(8,128)S(1)}, f32[8,384]{1,0:T(8,128)S(1)}, u32[]{:S(2)}, u32[]{:S(2)}) collective-permute-start(f32[8,384]{1,0:T(8,128)S(1)} %row_stats.1.refs_9_.refs_8_), channel_id=1, source_target_pairs={{0,3},{1,2},{2,1},{3,0},{4,7},{5,6},{6,5},{7,4},{8,11},{33,34},{10... | collective-permute-start | bytes 36872 | tf_op jit(solution)/shard_map/ppermute | solution.py:66
  6.2 0.0 collective-permute-done.refs_0_.refs_10_.refs_9_
  6.2 13.6 %collective-permute-done.1.refs_1_.refs_11_.refs_10_ = f32[8,384]{1,0:T(8,128)S(1)} collective-permute-done((f32[8,384]{1,0:T(8,128)S(1)}, f32[8,384]{1,0:T(8,128)S(1)}, u32[]{:S(2)}, u32[]{:S(2)}) %collective-permute-start.1) | collective-permute-done | bytes 12320 | tf_op jit(solution)/shard_map/ppermute | solution.py:66
  19.8 0.0 collective-permute-done.2.refs_2_.refs_12_.refs_11_
  19.8 0.6 copy-done.14
  20.4 0.6 copy-done.15
  21.0 2.9 %prepare.1 = (bf16[8,2,144,128]{3,2,1,0:T(8,128)(2,1)}, bf16[2,144,128]{2,1,0:T(8,128)(2,1)}, bf16[2,144,128]{2,1,0:T(8,128)(2,1)}, f32[288,128]{1,0:T(8,128)}, f32[144,128]{1,0:T(8,128)}, /*index=5*/f32[144,128]{1,0:T(8,128)}) custom-call(s32[1]{0:T(128)S(6)} %and.28.s_ref, s32[144]{0:T(256)} %place_hbm.1, f32[1,128]{1,0:T(1,128)} %constant.62.clone.freq, ...), custom_call_target="tpu_custom_call" | custom-call | flops 1843200 | bytes 1474560 | tf_op jit(solution)/shard_map/prepare/pallas_call | solution.py:193
  23.9 5.4 %all-to-all-start = ((bf16[8,2,144,128]{3,2,1,0:T(8,128)(2,1)}), bf16[8,2,144,128]{3,2,1,0:T(8,128)(2,1)S(1)}, u32[]{:S(2)}, u32[]{:S(2)}) async-start(bf16[8,2,144,128]{3,2,1,0:T(8,128)(2,1)} %get-tuple-element.25), calls=%async_computation | async-start | bytes 1179648 | tf_op jit(solution)/shard_map/all_to_all | solution.py:96
  29.3 0.1 collective-permute-start.6
  29.4 2.0 %collective-permute-start.3 = (bf16[2,144,128]{2,1,0:T(8,128)(2,1)}, bf16[2,144,128]{2,1,0:T(8,128)(2,1)S(1)}, u32[]{:S(2)}, u32[]{:S(2)}) collective-permute-start(bf16[2,144,128]{2,1,0:T(8,128)(2,1)} %get-tuple-element.27), channel_id=1, source_target_pairs={{0,8},{1,33},{2,10},{3,35},{4,12},{5,37},{6,14},{7,39},{8,0},{33,1... | collective-permute-start | bytes 221192 | tf_op jit(solution)/shard_map/ppermute | solution.py:66
  31.4 7.3 %collective-permute-done.3.last_other = bf16[2,144,128]{2,1,0:T(8,128)(2,1)S(1)} collective-permute-done((bf16[2,144,128]{2,1,0:T(8,128)(2,1)}, bf16[2,144,128]{2,1,0:T(8,128)(2,1)S(1)}, u32[]{:S(2)}, u32[]{:S(2)}) %collective-permute-start.3) | collective-permute-done | bytes 73760 | tf_op jit(solution)/shard_map/ppermute | solution.py:66
  38.7 1.4 all-to-all-done.arrived
  40.0 0.9 copy-done.9
  40.9 0.1 assemble.1
  41.0 0.1 collective-permute-start.5
  41.1 0.6 pad_add_fusion.refs_0_
  41.7 3.7 %collective-permute-start.8 = (bf16[2,720,128]{2,1,0:T(8,128)(2,1)S(1)}, bf16[2,720,128]{2,1,0:T(8,128)(2,1)}, u32[]{:S(2)}, u32[]{:S(2)}) collective-permute-start(bf16[2,720,128]{2,1,0:T(8,128)(2,1)S(1)} %get-tuple-element.44.refs_1_), channel_id=1, source_target_pairs={{0,4},{1,5},{2,6},{3,7},{4,0},{5,1},{6,2},{7,3},{8,12},{33,37},{10... | collective-permute-start | bytes 1105928 | tf_op jit(solution)/shard_map/ppermute | solution.py:66
  45.4 0.0 collective-permute-start.7
  45.5 0.9 copy-done.12
  46.3 10.2 %project_chip.1.refs_12_ = f32[288,1920]{1,0:T(8,128)} custom-call(s32[2]{0:T(128)} %pad_add_fusion.refs_0_, bf16[288,1280]{1,0:T(8,128)(2,1)} %bitcast.10, bf16[288,1280]{1,0:T(8,128)(2,1)} %copy-done.12, f32[288,128]{1,0:T(8,128)} %get-tuple-element.31.refs_3_.refs_2_, f32[2,5120]{1,0:T(2,128)} %refs_3_.3, f32[2,5120]{1,0:T(2,128)} %refs_4_.5, ...), custom_call_target="tpu_custom_call" | custom-call | flops 2831155200 | bytes 9830400 | tf_op jit(solution)/shard_map/project_chip/pallas_call | solution.py:326
  56.6 7.5 %project_z.1.refs_12_ = f32[288,1920]{1,0:T(8,128)} custom-call(s32[1]{0:T(128)} %bitcast.3.refs_0_, bf16[288,1280]{1,0:T(8,128)(2,1)} %collective-permute-done.4.refs_1_, f32[288,128]{1,0:T(8,128)} %get-tuple-element.31.refs_3_.refs_2_, f32[2,5120]{1,0:T(2,128)} %refs_3_.3, f32[2,5120]{1,0:T(2,128)} %refs_4_.5, bf16[5120,640]{1,0:T(8,128)(2,1)} %refs_5_.5, ...), custom_call_target="tpu_custom_call" | custom-call | flops 1415577600 | bytes 4915200 | tf_op jit(solution)/shard_map/project_z/pallas_call | solution.py:326
  64.1 0.0 copy-start.10
  64.1 0.0 copy-start.11
  64.1 7.0 %project_cross.1 = (f32[288,640]{1,0:T(8,128)}, f32[288,640]{1,0:T(8,128)}, bf16[288,640]{1,0:T(8,128)(2,1)}, f32[8,384]{1,0:T(8,128)}) custom-call(s32[1]{0:T(128)} %bitcast.refs_0_, bf16[288,1280]{1,0:T(8,128)(2,1)} %collective-permute-done.5.refs_1_, f32[288,128]{1,0:T(8,128)} %get-tuple-element.31.refs_3_.refs_2_, f32[2,5120]{1,0:T(2,128)} %refs_3_.3, ...), custom_call_target="tpu_custom_call" | custom-call | flops 1415577600 | bytes 4915200 | tf_op jit(solution)/shard_map/project_cross/pallas_call | solution.py:326
  71.1 0.7 broadcast_in_dim.3
  71.8 6.6 %all_to_all.20.squares = f32[4,8,384]{2,1,0:T(8,128)S(1)} all-to-all(f32[4,8,384]{2,1,0:T(8,128)S(1)} %broadcast_in_dim.3), channel_id=1, replica_groups=mesh['patch'=32,'tp'=4] {'tp'}, dimensions={0} | all-to-all | bytes 98304 | tf_op jit(solution)/shard_map/all_to_all | solution.py:670
  78.4 1.1 copy-done.2
  79.6 1.1 copy-done.3
  80.7 1.8 %norm_rope.1 = (bf16[288,640]{1,0:T(8,128)(2,1)S(1)}, bf16[288,640]{1,0:T(8,128)(2,1)}, bf16[8,2,144,128]{3,2,1,0:T(8,128)(2,1)}) custom-call(f32[288,640]{1,0:T(8,128)S(1)} %copy-done.2, f32[288,640]{1,0:T(8,128)S(1)} %copy-done.3, f32[4,8,384]{2,1,0:T(8,128)S(1)} %all_to_all.20.squares, f32[640]{0:T(1024)S(1)} %copy-done.10, f32[640]{0:T(1024)S(1)} %copy-done.11, ...), custom_call_target="tpu_custom_call" | custom-call | flops 3686400 | bytes 2949120 | tf_op jit(solution)/shard_map/norm_rope/pallas_call | solution.py:375
  82.5 4.0 %all-to-all-start.2 = ((bf16[8,2,144,128]{3,2,1,0:T(8,128)(2,1)}), bf16[8,2,144,128]{3,2,1,0:T(8,128)(2,1)S(1)}, u32[]{:S(2)}, u32[]{:S(2)}) async-start(bf16[8,2,144,128]{3,2,1,0:T(8,128)(2,1)} %get-tuple-element.42), calls=%async_computation.2 | async-start | bytes 1179648 | tf_op jit(solution)/shard_map/all_to_all | solution.py:96
  86.5 1.4 %collective-permute-start.11 = (bf16[2,720,128]{2,1,0:T(8,128)(2,1)S(1)}, bf16[2,720,128]{2,1,0:T(8,128)(2,1)}, u32[]{:S(2)}, u32[]{:S(2)}) collective-permute-start(bf16[2,720,128]{2,1,0:T(8,128)(2,1)S(1)} %get-tuple-element.43.refs_0_), channel_id=1, source_target_pairs={{0,24},{1,97},{2,26},{3,99},{4,28},{5,101},{6,30},{7,103},{8,16},{... | collective-permute-start | bytes 1105928 | tf_op jit(solution)/shard_map/ppermute | solution.py:66
  87.9 1.9 %collective-permute-start.12 = (bf16[2,720,128]{2,1,0:T(8,128)(2,1)S(1)}, bf16[2,720,128]{2,1,0:T(8,128)(2,1)}, u32[]{:S(2)}, u32[]{:S(2)}) collective-permute-start(bf16[2,720,128]{2,1,0:T(8,128)(2,1)S(1)} %get-tuple-element.44.refs_1_), channel_id=1, source_target_pairs={{0,24},{1,97},{2,26},{3,99},{4,28},{5,101},{6,30},{7,103},{8,16},{... | collective-permute-start | bytes 1105928 | tf_op jit(solution)/shard_map/ppermute | solution.py:66
  89.7 1.4 %collective-permute-start.10 = (bf16[2,720,128]{2,1,0:T(8,128)(2,1)}, bf16[2,720,128]{2,1,0:T(8,128)(2,1)}, u32[]{:S(2)}, u32[]{:S(2)}) collective-permute-start(bf16[2,720,128]{2,1,0:T(8,128)(2,1)} %collective-permute-done.8.refs_1_), channel_id=1, source_target_pairs={{0,24},{1,97},{2,26},{3,99},{4,28},{5,101},{6,30},{7,103},{8,16},{... | collective-permute-start | bytes 1105928 | tf_op jit(solution)/shard_map/ppermute | solution.py:66
  91.1 1.9 %collective-permute-start.9 = (bf16[2,720,128]{2,1,0:T(8,128)(2,1)}, bf16[2,720,128]{2,1,0:T(8,128)(2,1)}, u32[]{:S(2)}, u32[]{:S(2)}) collective-permute-start(bf16[2,720,128]{2,1,0:T(8,128)(2,1)} %collective-permute-done.7.refs_0_), channel_id=1, source_target_pairs={{0,24},{1,97},{2,26},{3,99},{4,28},{5,101},{6,30},{7,103},{8,16},{... | collective-permute-start | bytes 1105928 | tf_op jit(solution)/shard_map/ppermute | solution.py:66
  93.0 1.0 copy-done.5
  94.0 1.0 fresh_attention.1
  94.9 1.9 %collective-permute-done.11.refs_2_ = bf16[2,720,128]{2,1,0:T(8,128)(2,1)} collective-permute-done((bf16[2,720,128]{2,1,0:T(8,128)(2,1)S(1)}, bf16[2,720,128]{2,1,0:T(8,128)(2,1)}, u32[]{:S(2)}, u32[]{:S(2)}) %collective-permute-start.11) | collective-permute-done | bytes 368672 | tf_op jit(solution)/shard_map/ppermute | solution.py:66
  96.9 3.9 %collective-permute-done.12.refs_3_ = bf16[2,720,128]{2,1,0:T(8,128)(2,1)} collective-permute-done((bf16[2,720,128]{2,1,0:T(8,128)(2,1)S(1)}, bf16[2,720,128]{2,1,0:T(8,128)(2,1)}, u32[]{:S(2)}, u32[]{:S(2)}) %collective-permute-start.12) | collective-permute-done | bytes 368672 | tf_op jit(solution)/shard_map/ppermute | solution.py:66
  100.8 7.5 %near_attention.1 = (f32[2,1152,128]{2,1,0:T(8,128)S(1)}, f32[2,1152,128]{2,1,0:T(8,128)S(1)}) custom-call(s32[1]{0:T(128)} %bitcast.6.u_ref, bf16[8,2,144,128]{3,2,1,0:T(8,128)(2,1)S(1)} %all-to-all-done.2.queries, bf16[2,720,128]{2,1,0:T(8,128)(2,1)S(1)} %get-tuple-element.43.refs_0_, bf16[2,720,128]{2,1,0:T(8,128)(2,1)S(1)} %get-tuple-element.44.refs_1_, ...), custom_call_target="tpu_custom_call" | custom-call | flops 1698693120 | bytes 1474560 | tf_op jit(solution)/shard_map/near_attention/pallas_call | solution.py:550
  108.4 0.3 collective-permute-done.9.refs_2_
  108.7 7.7 %far_attention.1 = bf16[8,304,128]{2,1,0:T(8,128)(2,1)S(1)} custom-call(s32[1]{0:T(128)} %bitcast.6.u_ref, bf16[8,2,144,128]{3,2,1,0:T(8,128)(2,1)S(1)} %all-to-all-done.2.queries, bf16[2,720,128]{2,1,0:T(8,128)(2,1)} %collective-permute-done.7.refs_0_, bf16[2,720,128]{2,1,0:T(8,128)(2,1)} %collective-permute-done.8.refs_1_, ...), custom_call_target="tpu_custom_call" | custom-call | flops 1698693120 | bytes 1474560 | tf_op jit(solution)/shard_map/far_attention/pallas_call | solution.py:550
  116.4 14.8 %all_to_all.21.msgs = bf16[8,304,128]{2,1,0:T(8,128)(2,1)S(1)} all-to-all(bf16[8,304,128]{2,1,0:T(8,128)(2,1)S(1)} %far_attention.1), channel_id=1, replica_groups={{0,32,64,96,8,40,72,104},{24,56,88,120,16,48,80,112},{4,36,68,100,12,44..., dimensions={0} | all-to-all | bytes 1245184 | tf_op jit(solution)/shard_map/all_to_all | solution.py:96
  131.3 4.5 %merge.1 = bf16[2,144,640]{2,1,0:T(8,128)(2,1)} custom-call(f32[5,2,144,128]{3,2,1,0:T(8,128)S(1)} %get-tuple-element.40.fresh_out, f32[5,2,144,128]{3,2,1,0:T(8,128)S(1)} %get-tuple-element.41.refs_6_.fresh_lse, bf16[8,304,128]{2,1,0:T(8,128)(2,1)S(1)} %all_to_all.21.msgs), custom_call_target="tpu_custom_call" | custom-call | flops 1843200 | bytes 2580480 | tf_op jit(solution)/shard_map/merge/pallas_call | solution.py:608
  (29 shorter events, 0.1 us)
Async XLA Ops:
  0.6 40.4 %collective-permute-start.4 = (bf16[288,1280]{1,0:T(8,128)(2,1)}, bf16[288,1280]{1,0:T(8,128)(2,1)}, u32[]{:S(2)}, u32[]{:S(2)}) collective-permute-start(bf16[288,1280]{1,0:T(8,128)(2,1)} %bitcast.9), channel_id=1, source_target_pairs={{0,2},{1,3},{2,0},{3,1},{4,6},{5,7},{6,4},{7,5},{8,10},{33,35},{10... | collective-permute-start | bytes 2211848 | tf_op jit(solution)/shard_map/ppermute | solution.py:66
  2.7 1.1 copy-start
  3.9 25.5 %copy-start.1 = (bf16[2,144,1280]{2,1,0:T(8,128)(2,1)S(1)}, bf16[2,144,1280]{2,1,0:T(8,128)(2,1)}, u32[]{:S(2)}) copy-start(bf16[2,144,1280]{2,1,0:T(8,128)(2,1)} %param.12) | copy-start | bytes 2211844
  4.3 41.1 %copy-start.6 = (f32[8,384]{1,0:T(8,128)}, f32[8,384]{1,0:T(8,128)S(1)}, u32[]{:S(2)}) copy-start(f32[8,384]{1,0:T(8,128)S(1)} %row_stats.1.refs_9_.refs_8_) | copy-start | bytes 36868
  4.3 1.9 %collective-permute-start = (f32[8,384]{1,0:T(8,128)S(1)}, f32[8,384]{1,0:T(8,128)S(1)}, u32[]{:S(2)}, u32[]{:S(2)}) collective-permute-start(f32[8,384]{1,0:T(8,128)S(1)} %row_stats.1.refs_9_.refs_8_), channel_id=1, source_target_pairs={{0,1},{1,0},{2,3},{3,2},{4,5},{5,4},{6,7},{7,6},{8,9},{33,32},{10,... | collective-permute-start | bytes 36872 | tf_op jit(solution)/shard_map/ppermute | solution.py:66
  4.4 15.4 %collective-permute-start.1 = (f32[8,384]{1,0:T(8,128)S(1)}, f32[8,384]{1,0:T(8,128)S(1)}, u32[]{:S(2)}, u32[]{:S(2)}) collective-permute-start(f32[8,384]{1,0:T(8,128)S(1)} %row_stats.1.refs_9_.refs_8_), channel_id=1, source_target_pairs={{0,2},{1,3},{2,0},{3,1},{4,6},{5,7},{6,4},{7,5},{8,10},{33,35},{10... | collective-permute-start | bytes 36872 | tf_op jit(solution)/shard_map/ppermute | solution.py:66
  4.5 15.3 %collective-permute-start.2 = (f32[8,384]{1,0:T(8,128)S(1)}, f32[8,384]{1,0:T(8,128)S(1)}, u32[]{:S(2)}, u32[]{:S(2)}) collective-permute-start(f32[8,384]{1,0:T(8,128)S(1)} %row_stats.1.refs_9_.refs_8_), channel_id=1, source_target_pairs={{0,3},{1,2},{2,1},{3,0},{4,7},{5,6},{6,5},{7,4},{8,11},{33,34},{10... | collective-permute-start | bytes 36872 | tf_op jit(solution)/shard_map/ppermute | solution.py:66
  6.2 13.6 %copy-start.13 = (f32[8,384]{1,0:T(8,128)}, f32[8,384]{1,0:T(8,128)S(1)}, u32[]{:S(2)}) copy-start(f32[8,384]{1,0:T(8,128)S(1)} %collective-permute-done.refs_0_.refs_10_.refs_9_) | copy-start | bytes 36868
  19.8 0.6 copy-start.14
  20.4 0.6 copy-start.15
  23.9 16.1 %all-to-all-start = ((bf16[8,2,144,128]{3,2,1,0:T(8,128)(2,1)}), bf16[8,2,144,128]{3,2,1,0:T(8,128)(2,1)S(1)}, u32[]{:S(2)}, u32[]{:S(2)}) async-start(bf16[8,2,144,128]{3,2,1,0:T(8,128)(2,1)} %get-tuple-element.25), calls=%async_computation | async-start | bytes 1179648 | tf_op jit(solution)/shard_map/all_to_all | solution.py:96
  29.3 16.1 %collective-permute-start.6 = (bf16[288,1280]{1,0:T(8,128)(2,1)S(1)}, bf16[288,1280]{1,0:T(8,128)(2,1)S(1)}, u32[]{:S(2)}, u32[]{:S(2)}) collective-permute-start(bf16[288,1280]{1,0:T(8,128)(2,1)S(1)} %bitcast.12), channel_id=1, source_target_pairs={{0,1},{1,0},{2,3},{3,2},{4,5},{5,4},{6,7},{7,6},{8,9},{33,32},{10,... | collective-permute-start | bytes 2211848 | tf_op jit(solution)/shard_map/ppermute | solution.py:66
  29.4 9.3 %collective-permute-start.3 = (bf16[2,144,128]{2,1,0:T(8,128)(2,1)}, bf16[2,144,128]{2,1,0:T(8,128)(2,1)S(1)}, u32[]{:S(2)}, u32[]{:S(2)}) collective-permute-start(bf16[2,144,128]{2,1,0:T(8,128)(2,1)} %get-tuple-element.27), channel_id=1, source_target_pairs={{0,8},{1,33},{2,10},{3,35},{4,12},{5,37},{6,14},{7,39},{8,0},{33,1... | collective-permute-start | bytes 221192 | tf_op jit(solution)/shard_map/ppermute | solution.py:66
  40.0 0.9 copy-start.9
  41.0 23.0 %collective-permute-start.5 = (bf16[288,1280]{1,0:T(8,128)(2,1)}, bf16[288,1280]{1,0:T(8,128)(2,1)}, u32[]{:S(2)}, u32[]{:S(2)}) collective-permute-start(bf16[288,1280]{1,0:T(8,128)(2,1)} %collective-permute-done.4.refs_1_), channel_id=1, source_target_pairs={{0,1},{1,0},{2,3},{3,2},{4,5},{5,4},{6,7},{7,6},{8,9},{33,32},{10,... | collective-permute-start | bytes 2211848 | tf_op jit(solution)/shard_map/ppermute | solution.py:66
  41.7 48.0 %collective-permute-start.8 = (bf16[2,720,128]{2,1,0:T(8,128)(2,1)S(1)}, bf16[2,720,128]{2,1,0:T(8,128)(2,1)}, u32[]{:S(2)}, u32[]{:S(2)}) collective-permute-start(bf16[2,720,128]{2,1,0:T(8,128)(2,1)S(1)} %get-tuple-element.44.refs_1_), channel_id=1, source_target_pairs={{0,4},{1,5},{2,6},{3,7},{4,0},{5,1},{6,2},{7,3},{8,12},{33,37},{10... | collective-permute-start | bytes 1105928 | tf_op jit(solution)/shard_map/ppermute | solution.py:66
  45.4 45.7 %collective-permute-start.7 = (bf16[2,720,128]{2,1,0:T(8,128)(2,1)S(1)}, bf16[2,720,128]{2,1,0:T(8,128)(2,1)}, u32[]{:S(2)}, u32[]{:S(2)}) collective-permute-start(bf16[2,720,128]{2,1,0:T(8,128)(2,1)S(1)} %get-tuple-element.43.refs_0_), channel_id=1, source_target_pairs={{0,4},{1,5},{2,6},{3,7},{4,0},{5,1},{6,2},{7,3},{8,12},{33,37},{10... | collective-permute-start | bytes 1105928 | tf_op jit(solution)/shard_map/ppermute | solution.py:66
  45.5 0.9 copy-start.12
  64.1 14.4 %copy-start.7 = (f32[144,128]{1,0:T(8,128)S(1)}, f32[144,128]{1,0:T(8,128)}, u32[]{:S(2)}) copy-start(f32[144,128]{1,0:T(8,128)} %get-tuple-element.35.cos) | copy-start | bytes 221188
  64.1 14.4 %copy-start.8 = (f32[144,128]{1,0:T(8,128)S(1)}, f32[144,128]{1,0:T(8,128)}, u32[]{:S(2)}) copy-start(f32[144,128]{1,0:T(8,128)} %get-tuple-element.36.sin) | copy-start | bytes 221188
  64.1 14.3 %copy-start.10 = (f32[640]{0:T(1024)S(1)}, f32[640]{0:T(1024)}, u32[]{:S(2)}) copy-start(f32[640]{0:T(1024)} %qg.1) | copy-start | bytes 7684
  64.1 14.3 %copy-start.11 = (f32[640]{0:T(1024)S(1)}, f32[640]{0:T(1024)}, u32[]{:S(2)}) copy-start(f32[640]{0:T(1024)} %kg.1) | copy-start | bytes 7684
  78.4 1.1 copy-start.2
  79.6 1.1 copy-start.3
  80.7 12.3 %copy-start.4 = (bf16[288,640]{1,0:T(8,128)(2,1)S(1)}, bf16[288,640]{1,0:T(8,128)(2,1)}, u32[]{:S(2)}) copy-start(bf16[288,640]{1,0:T(8,128)(2,1)} %get-tuple-element.39.v_ref) | copy-start | bytes 1105924
  82.5 18.3 %all-to-all-start.2 = ((bf16[8,2,144,128]{3,2,1,0:T(8,128)(2,1)}), bf16[8,2,144,128]{3,2,1,0:T(8,128)(2,1)S(1)}, u32[]{:S(2)}, u32[]{:S(2)}) async-start(bf16[8,2,144,128]{3,2,1,0:T(8,128)(2,1)} %get-tuple-element.42), calls=%async_computation.2 | async-start | bytes 1179648 | tf_op jit(solution)/shard_map/all_to_all | solution.py:96
  86.5 10.4 %collective-permute-start.11 = (bf16[2,720,128]{2,1,0:T(8,128)(2,1)S(1)}, bf16[2,720,128]{2,1,0:T(8,128)(2,1)}, u32[]{:S(2)}, u32[]{:S(2)}) collective-permute-start(bf16[2,720,128]{2,1,0:T(8,128)(2,1)S(1)} %get-tuple-element.43.refs_0_), channel_id=1, source_target_pairs={{0,24},{1,97},{2,26},{3,99},{4,28},{5,101},{6,30},{7,103},{8,16},{... | collective-permute-start | bytes 1105928 | tf_op jit(solution)/shard_map/ppermute | solution.py:66
  87.9 12.9 %collective-permute-start.12 = (bf16[2,720,128]{2,1,0:T(8,128)(2,1)S(1)}, bf16[2,720,128]{2,1,0:T(8,128)(2,1)}, u32[]{:S(2)}, u32[]{:S(2)}) collective-permute-start(bf16[2,720,128]{2,1,0:T(8,128)(2,1)S(1)} %get-tuple-element.44.refs_1_), channel_id=1, source_target_pairs={{0,24},{1,97},{2,26},{3,99},{4,28},{5,101},{6,30},{7,103},{8,16},{... | collective-permute-start | bytes 1105928 | tf_op jit(solution)/shard_map/ppermute | solution.py:66
  89.7 18.6 %collective-permute-start.10 = (bf16[2,720,128]{2,1,0:T(8,128)(2,1)}, bf16[2,720,128]{2,1,0:T(8,128)(2,1)}, u32[]{:S(2)}, u32[]{:S(2)}) collective-permute-start(bf16[2,720,128]{2,1,0:T(8,128)(2,1)} %collective-permute-done.8.refs_1_), channel_id=1, source_target_pairs={{0,24},{1,97},{2,26},{3,99},{4,28},{5,101},{6,30},{7,103},{8,16},{... | collective-permute-start | bytes 1105928 | tf_op jit(solution)/shard_map/ppermute | solution.py:66
  91.1 17.6 %collective-permute-start.9 = (bf16[2,720,128]{2,1,0:T(8,128)(2,1)}, bf16[2,720,128]{2,1,0:T(8,128)(2,1)}, u32[]{:S(2)}, u32[]{:S(2)}) collective-permute-start(bf16[2,720,128]{2,1,0:T(8,128)(2,1)} %collective-permute-done.7.refs_0_), channel_id=1, source_target_pairs={{0,24},{1,97},{2,26},{3,99},{4,28},{5,101},{6,30},{7,103},{8,16},{... | collective-permute-start | bytes 1105928 | tf_op jit(solution)/shard_map/ppermute | solution.py:66
  93.0 1.0 copy-start.5

commit v2 on v1

v2 whole, which is shorter than its diff:
```python
import functools
import math

import jax
import jax.numpy as jnp
import numpy as np
from jax import lax
from jax.experimental import pallas as pl
from jax.experimental.pallas import tpu as pltpu
from jax.sharding import PartitionSpec as P

D = 5120
HEADS = 20
HD = 128
FRAMES = 3
GRID_W = 48
EPS = 1e-06
MASKED = -1e30
NY, NX, NZ = 4, 4, 2
TP = 4
N_PATCH = NY * NX * NZ
TOK = 144
B = 2
ROWS = B * TOK
LOCAL_HEADS = 5
WIDTH = LOCAL_HEADS * HD
CHUNK = D // TP
STAT_LANES = 384
PIECE = 5 * TOK
MSG_ROWS = 2 * TOK + 16
SCORE_SCALE = math.log2(math.e) / math.sqrt(HD)
F32 = jnp.float32
BF16 = jnp.bfloat16
AXES = ("patch", "tp")
VMEM_MIB = 40


def params(mib):
    return pltpu.CompilerParams(vmem_limit_bytes=mib * 1024 * 1024)


def vmem():
    return pl.BlockSpec(memory_space=pltpu.VMEM)


def smem():
    return pl.BlockSpec(memory_space=pltpu.SMEM)


def linear(u, v, z_hi, z_lo, core):
    y, x = (u, v) if core == 0 else (v, u)
    return ((y * NX + x) * NZ + z_hi) * TP + z_lo * 2 + core


def places():
    return [
        (u, v, h, l, c)
        for u in range(4)
        for v in range(4)
        for h in range(2)
        for l in range(2)
        for c in range(2)
    ]


def permute(value, move):
    return lax.ppermute(value, AXES, [(linear(*p), linear(*move(*p))) for p in places()])


def to_peer(value, p, k):
    return permute(value, lambda u, v, h, l, c: ((u + k) % 4, v ^ p, h, l, c))


def swap_v(value):
    return permute(value, lambda u, v, h, l, c: (u, v ^ 3, h, l, c))


def swap_z_hi(value):
    return permute(value, lambda u, v, h, l, c: (u, v, 1 - h, l, c))


def swap_tp(value, z, core):
    if core:
        return permute(value, lambda u, v, h, l, c: (v, u, h, l ^ z, 1 - c))
    return permute(value, lambda u, v, h, l, c: (u, v, h, l ^ z, c))


def frequencies():
    half_dim = HD // 2
    third_dim = half_dim // 3
    frame_pairs = half_dim - 2 * third_dim
    pair = np.arange(HD) // 2
    offset = np.where(
        pair < frame_pairs,
        pair,
        np.where(pair < frame_pairs + third_dim, pair - frame_pairs, pair - frame_pairs - third_dim),
    )
    width = np.where(pair < frame_pairs, 2 * frame_pairs, 2 * third_dim)
    return np.exp(-math.log(10000.0) * 2.0 * offset / width).astype(np.float32).reshape(1, HD)


def columns_to_rows(first, second):
    lane = lax.broadcasted_iota(jnp.int32, (ROWS, 128), 1)
    both = jnp.where(lane == 0, first, jnp.where(lane == 1, second, 0.0))
    padded = jnp.concatenate([both, jnp.zeros((STAT_LANES - ROWS, 128), F32)], axis=0)
    return padded.T[0:8]


def row_to_column(row):
    return jnp.broadcast_to(row, (128, STAT_LANES)).T[0:ROWS]


def stats_kernel(hidden_hbm, out_ref, hidden_ref, sem):
    copy = pltpu.make_async_copy(hidden_hbm, hidden_ref, sem.at[0])
    copy.start()
    copy.wait()
    part = hidden_ref[...].astype(F32)
    mean = jnp.sum(part, axis=1, keepdims=True) * (1.0 / CHUNK)
    centered = part - mean
    deviation = jnp.sum(centered * centered, axis=1, keepdims=True)
    out_ref[...] = columns_to_rows(mean, deviation)


def row_stats(hidden_rows):
    return pl.pallas_call(
        stats_kernel,
        out_shape=jax.ShapeDtypeStruct((8, STAT_LANES), F32),
        in_specs=[pl.BlockSpec(memory_space=pltpu.HBM)],
        out_specs=vmem(),
        scratch_shapes=[pltpu.VMEM((ROWS, CHUNK), BF16), pltpu.SemaphoreType.DMA((1,))],
        compiler_params=params(VMEM_MIB),
        cost_estimate=pl.CostEstimate(
            flops=4 * ROWS * CHUNK, bytes_accessed=2 * ROWS * CHUNK, transcendentals=0
        ),
        name="row_stats",
    )(hidden_rows)


def pack_kernel(u_ref, key_hbm, value_hbm, *refs):
    outs, sems = refs[0:5], refs[5]
    copies = []
    for k in range(5):
        head = lax.rem(u_ref[0] + k, 4) if k < 4 else 4
        cols = pl.ds(pl.multiple_of(head * HD, HD), HD)
        for n, source in enumerate((key_hbm, value_hbm)):
            for s in range(B):
                copy = pltpu.make_async_copy(
                    source.at[s, :, cols], outs[k].at[s, n], sems.at[len(copies)]
                )
                copy.start()
                copies.append(copy)
    for copy in copies:
        copy.wait()


def pack_stale(u, stale_keys, stale_values):
    hbm = pl.BlockSpec(memory_space=pltpu.HBM)
    return pl.pallas_call(
        pack_kernel,
        out_shape=[jax.ShapeDtypeStruct((B, 2, TOK, HD), BF16)] * 5,
        in_specs=[smem(), hbm, hbm],
        out_specs=[vmem()] * 5,
        scratch_shapes=[pltpu.SemaphoreType.DMA((20,))],
        compiler_params=params(VMEM_MIB),
        cost_estimate=pl.CostEstimate(
            flops=0, bytes_accessed=8 * ROWS * WIDTH, transcendentals=0
        ),
        name="pack_stale",
    )(u, stale_keys, stale_values)


def tables_kernel(place_hbm, freq, after, cond, cos, sin, places_s, place_ref, sem):
    copy = pltpu.make_async_copy(place_hbm, place_ref, sem.at[0])
    copy.start()
    copy.wait()
    for row in range(TOK):
        places_s[row : row + 1] = jnp.full((1, HD), place_ref[row], jnp.int32)
    place = places_s[...]
    frame_tok = TOK * N_PATCH // FRAMES
    frame = jnp.where(place >= frame_tok, 1, 0) + jnp.where(place >= 2 * frame_tok, 1, 0)
    within = place - frame * frame_tok
    grid_row = ((within.astype(F32) + 0.5) * (1.0 / GRID_W)).astype(jnp.int32)
    grid_col = within - grid_row * GRID_W
    lane = lax.broadcasted_iota(jnp.int32, (TOK, HD), 1)
    third = 2 * (HD // 6)
    frame_lanes = HD - 2 * third
    position = jnp.where(
        lane < frame_lanes, frame, jnp.where(lane < frame_lanes + third, grid_row, grid_col)
    )
    angles = position.astype(F32) * freq[...]
    cos[...] = jnp.cos(angles)
    sine = jnp.sin(angles)
    sin[...] = jnp.where(lane % 2 == 0, -sine, sine)
    flag = jnp.where((frame == 0) | (frame == FRAMES - 1), 1.0, 0.0)
    cond[0:TOK] = flag
    cond[TOK:ROWS] = flag


def tables(token_place, after):
    table = jax.ShapeDtypeStruct((TOK, HD), F32)
    return pl.pallas_call(
        tables_kernel,
        out_shape=[jax.ShapeDtypeStruct((ROWS, HD), F32), table, table],
        in_specs=[
            pl.BlockSpec(memory_space=pltpu.HBM),
            vmem(),
            pl.BlockSpec(memory_space=pl.ANY),
        ],
        out_specs=[vmem()] * 3,
        scratch_shapes=[
            pltpu.VMEM((TOK, HD), jnp.int32),
            pltpu.SMEM((TOK,), jnp.int32),
            pltpu.SemaphoreType.DMA((1,)),
        ],
        compiler_params=params(VMEM_MIB),
        cost_estimate=pl.CostEstimate(
            flops=100 * TOK * HD, bytes_accessed=16 * TOK * HD, transcendentals=0
        ),
        name="tables",
    )(token_place, jnp.asarray(frequencies()), after)


def assemble_kernel(s_ref, *refs):
    parts, outs = refs[0:5], refs[5:7]
    for p in range(2):
        s = s_ref[0] if p == 0 else 1 - s_ref[0]
        for n in range(2):
            for r in range(5):
                outs[p][n, r * TOK : (r + 1) * TOK] = parts[r][s, n]


def assemble(s, parts):
    shape = jax.ShapeDtypeStruct((2, PIECE, HD), BF16)
    return pl.pallas_call(
        assemble_kernel,
        out_shape=[shape, shape],
        in_specs=[smem()] + [vmem()] * 5,
        out_specs=[vmem()] * 2,
        compiler_params=params(VMEM_MIB),
        cost_estimate=pl.CostEstimate(
            flops=0, bytes_accessed=16 * PIECE * HD, transcendentals=0
        ),
        name="assemble",
    )(s, *parts)


def merged_stats(refs):
    means = [ref[0:1] for ref in refs]
    mean = (means[0] + means[1] + means[2] + means[3]) * 0.25
    total = jnp.zeros_like(mean)
    for ref, one in zip(refs, means):
        total = total + (ref[1:2] + CHUNK * (one - mean) * (one - mean))
    return mean, lax.rsqrt(total * (1.0 / D) + EPS)


def project_kernel(count, unread, first, last, *refs):
    t_ref = refs[0]
    chunks = refs[1 : 1 + count]
    cond, shift, scale, w_q, w_k, w_v, s0, s1, s2, s3 = refs[1 + count : 11 + count]
    rest = list(refs[11 + count :])
    acc_in = None if first else rest.pop(0)
    rest = rest[unread:]
    if last:
        q_out, k_out, v_out, sq_out, buffer, sems = rest
    else:
        acc, buffer, sems = rest
    copies = {}
    for c in range(count):
        row = pl.multiple_of(t_ref[c] * CHUNK, CHUNK)
        for n, weight in enumerate((w_q, w_k, w_v)):
            copies[c, n] = pltpu.make_async_copy(
                weight.at[pl.ds(row, CHUNK)], buffer.at[c, n], sems.at[c, n]
            )
            copies[c, n].start()
    mean, rstd = merged_stats((s0, s1, s2, s3))
    mean = row_to_column(mean)[:, 0:1]
    rstd = row_to_column(rstd)[:, 0:1]
    conditioned = cond[:, 0:1] > 0.5
    totals = [None] * 3
    for c in range(count):
        cols = pl.ds(pl.multiple_of(t_ref[c] * CHUNK, CHUNK), CHUNK)
        part = chunks[c][...].astype(F32)
        gain = jnp.where(conditioned, scale[1:2, cols], scale[0:1, cols])
        bias = jnp.where(conditioned, shift[1:2, cols], shift[0:1, cols])
        modded = ((part - mean) * rstd * (1.0 + gain) + bias).astype(BF16)
        for n in range(3):
            columns = slice(n * WIDTH, (n + 1) * WIDTH)
            copies[c, n].wait()
            product = jnp.dot(modded, buffer[c, n], preferred_element_type=F32)
            if c == 0 and not first:
                product = product + acc_in[:, columns]
            if last:
                totals[n] = product
            elif c == 0:
                acc[:, columns] = product
            else:
                acc[:, columns] += product
    if last:
        query, key, value = totals
        q_out[...] = query
        k_out[...] = key
        v_out[...] = value.astype(BF16)
        sq_out[...] = columns_to_rows(
            jnp.sum(query * query, axis=1, keepdims=True),
            jnp.sum(key * key, axis=1, keepdims=True),
        )


def project(name, blocks, chunks, cond, shift, scale, weights, stats, acc=None, last=False, after=()):
    count = len(chunks)
    hbm = pl.BlockSpec(memory_space=pltpu.HBM)
    in_specs = [smem()] + [vmem()] * (count + 3) + [hbm] * 3 + [vmem()] * 4
    args = [blocks, *chunks, cond, shift, scale, *weights, *stats]
    if acc is not None:
        in_specs.append(vmem())
        args.append(acc)
    in_specs += [pl.BlockSpec(memory_space=pl.ANY)] * len(after)
    args += after
    if last:
        out_shape = [
            jax.ShapeDtypeStruct((ROWS, WIDTH), F32),
            jax.ShapeDtypeStruct((ROWS, WIDTH), F32),
            jax.ShapeDtypeStruct((ROWS, WIDTH), BF16),
            jax.ShapeDtypeStruct((8, STAT_LANES), F32),
        ]
        out_specs = [vmem()] * 4
    else:
        out_shape = jax.ShapeDtypeStruct((ROWS, 3 * WIDTH), F32)
        out_specs = vmem()
    return pl.pallas_call(
        functools.partial(project_kernel, count, len(after), acc is None, last),
        out_shape=out_shape,
        in_specs=in_specs,
        out_specs=out_specs,
        scratch_shapes=[
            pltpu.VMEM((count, 3, CHUNK, WIDTH), BF16),
            pltpu.SemaphoreType.DMA((count, 3)),
        ],
        compiler_params=params(VMEM_MIB),
        cost_estimate=pl.CostEstimate(
            flops=2 * ROWS * count * CHUNK * 3 * WIDTH,
            bytes_accessed=2 * count * CHUNK * 3 * WIDTH,
            transcendentals=0,
        ),
        name=name,
    )(*args)


def rope_kernel(u_ref, s_ref, q_ref, k_ref, s0, s1, s2, s3, qg, kg, cos, sin, k_all, *refs):
    sends, q_rot = refs[0:8], refs[8]
    total = s0[...] + s1[...] + s2[...] + s3[...]
    inverse = lax.rsqrt(total * (1.0 / (HEADS * HD)) + EPS)
    even = lax.broadcasted_iota(jnp.int32, (ROWS, HD), 1) % 2 == 0
    cos_rows = jnp.concatenate([cos[...], cos[...]], axis=0)
    sin_rows = jnp.concatenate([sin[...], sin[...]], axis=0)

    def rotate(ref, column, gain, cols):
        part = ref[:, cols] * column * gain[cols].reshape(1, HD)
        swap = jnp.where(even, pltpu.roll(part, HD - 1, 1), pltpu.roll(part, 1, 1))
        return (part * cos_rows + swap * sin_rows).astype(BF16)

    q_column = row_to_column(inverse[0:1])
    k_column = row_to_column(inverse[1:2])
    for head in range(LOCAL_HEADS):
        cols = slice(head * HD, (head + 1) * HD)
        query = rotate(q_ref, q_column, qg, cols)
        for s in range(B):
            q_rot[head, s] = query[s * TOK : (s + 1) * TOK]
        k_all[:, cols] = rotate(k_ref, k_column, kg, cols)
    for p in range(2):
        s = s_ref[0] if p == 0 else 1 - s_ref[0]
        for k in range(4):
            sends[4 * p + k][0] = q_rot[lax.rem(u_ref[0] + k, 4), s]
            sends[4 * p + k][1] = q_rot[4, s]


def norm_rope(u, s, query, key, squares, q_gain, k_gain, cos, sin):
    send = jax.ShapeDtypeStruct((2, TOK, HD), BF16)
    return pl.pallas_call(
        rope_kernel,
        out_shape=[jax.ShapeDtypeStruct((ROWS, WIDTH), BF16)] + [send] * 8,
        in_specs=[smem()] * 2 + [vmem()] * 10,
        out_specs=[vmem()] * 9,
        scratch_shapes=[pltpu.VMEM((LOCAL_HEADS, B, TOK, HD), BF16)],
        compiler_params=params(VMEM_MIB),
        cost_estimate=pl.CostEstimate(
            flops=20 * ROWS * WIDTH, bytes_accessed=16 * ROWS * WIDTH, transcendentals=0
        ),
        name="norm_rope",
    )(u, s, query, key, *squares, q_gain, k_gain, cos, sin)


def scores_of(query, keys):
    return lax.dot_general(query, keys, (((1,), (1,)), ((), ())), preferred_element_type=F32)


def to_rows(blocks):
    lane = lax.broadcasted_iota(jnp.int32, (HD, HD), 1)
    table = jnp.zeros((HD, HD), F32)
    empty = jnp.zeros((2 * HD - TOK, HD), F32)
    for n, block in enumerate(blocks):
        rest = jnp.concatenate([block[HD:TOK], empty], axis=0)
        table = jnp.where(lane == 2 * n, block[0:HD], table)
        table = jnp.where(lane == 2 * n + 1, rest, table)
    return table.T


FRESH_ROWS = 24


def fresh_kernel(u_ref, s_ref, k_ref, v_ref, *refs):
    queries, (out_ref, rows_ref) = refs[0:8], refs[8:10]
    lses = []
    for p in range(2):
        s = s_ref[0] if p == 0 else 1 - s_ref[0]
        rows = pl.ds(pl.multiple_of(s * TOK, TOK), TOK)
        for k in range(LOCAL_HEADS):
            head = lax.rem(u_ref[0] + k, 4) if k < 4 else 4
            cols = pl.ds(pl.multiple_of(head * HD, HD), HD)
            query = queries[4 * p + k][0] if k < 4 else queries[4 * p][1]
            scores = scores_of(query, k_ref[rows, cols])
            top = jnp.max(scores, axis=1, keepdims=True)
            probs = jnp.exp2((scores - top) * SCORE_SCALE)
            total = jnp.sum(probs, axis=1, keepdims=True)
            out = jnp.dot(probs.astype(BF16), v_ref[rows, cols], preferred_element_type=F32)
            out_ref[p, k] = out / total
            lses.append(jnp.broadcast_to(top * SCORE_SCALE + jnp.log2(total), (TOK, HD)))
    rows_ref[...] = to_rows(lses)[0:FRESH_ROWS]


def fresh_attention(u, s, key, value, queries):
    return pl.pallas_call(
        fresh_kernel,
        out_shape=[
            jax.ShapeDtypeStruct((B, LOCAL_HEADS, TOK, HD), F32),
            jax.ShapeDtypeStruct((FRESH_ROWS, HD), F32),
        ],
        in_specs=[smem()] * 2 + [vmem()] * 10,
        out_specs=[vmem()] * 2,
        compiler_params=params(VMEM_MIB),
        cost_estimate=pl.CostEstimate(
            flops=4 * ROWS * TOK * WIDTH,
            bytes_accessed=14 * ROWS * WIDTH,
            transcendentals=ROWS * TOK * LOCAL_HEADS,
        ),
        name="fresh_attention",
    )(u, s, key, value, *queries)


TILE = 2 * TOK
GROUP = 16
PER_PIECE = 4 * TOK
KEYS = 4 * PER_PIECE
KEYS_LAST = 4 * TOK
SPLIT = 768


def stale_kernel(far, count, *refs):
    queries, pieces = refs[0:count], refs[count : count + 4]
    rest = refs[count + 4 :]
    if far:
        near_out, near_lse = rest[0:2]
        msgs = rest[3 : 3 + count]
    else:
        out_ref, lse_ref = rest[0:2]
    lse_s, acc_s, k_main, v_main, k_last, v_last, scores_s, probs_s, sems = rest[-9:]
    copies = []
    for n, piece in enumerate(pieces):
        main, last = pl.ds(n * PER_PIECE, PER_PIECE), pl.ds(n * TOK, TOK)
        head, tail = pl.ds(0, PER_PIECE), pl.ds(PER_PIECE, TOK)
        for kind, part, target, rows in (
            (0, head, k_main, main),
            (0, tail, k_last, last),
            (1, head, v_main, main),
            (1, tail, v_last, last),
        ):
            copy = pltpu.make_async_copy(
                piece.at[kind, part], target.at[rows], sems.at[len(copies)]
            )
            copy.start()
            copies.append(copy)
    for copy in copies:
        copy.wait()

    jobs = [(tile, e) for e in range(2) for tile in range(count // 2)]

    def size(i):
        return KEYS_LAST if jobs[i][1] else KEYS

    def score_steps(i):
        tile, e = jobs[i]
        keys = k_last if e else k_main
        out = scores_s.at[i % 2]

        def step(at, end):
            query = jnp.concatenate([queries[2 * tile][e], queries[2 * tile + 1][e]], axis=0)
            out[:, at:end] = scores_of(query, keys[at:end])

        def hide():
            for n in range(2):
                block = 2 * tile + n
                rows = slice(n * TOK, (n + 1) * TOK)
                p, r = block // 4, block % 4
                if not e:
                    at = (p * 4 + r) * TOK
                elif r == 0:
                    at = p * TOK
                else:
                    continue
                out[rows, at : at + TOK] = jnp.full((TOK, TOK), MASKED, F32)

        steps = []
        for at in range(0, size(i), SPLIT):
            steps.append(functools.partial(step, at, min(at + SPLIT, size(i))))
        return steps if far else steps + [hide]

    def softmax_steps(i, tops, totals):
        def step(row):
            rows = slice(row, row + GROUP)
            part = scores_s[i % 2, rows, 0 : size(i)]
            top = jnp.max(part, axis=1, keepdims=True)
            probs = jnp.exp2((part - top) * SCORE_SCALE)
            totals.append(jnp.sum(probs, axis=1, keepdims=True))
            tops.append(top)
            probs_s[i % 2, rows, 0 : size(i)] = probs.astype(BF16)

        return [functools.partial(step, row) for row in range(0, TILE, GROUP)]

    def product_steps(i, tops, totals):
        tile, e = jobs[i]
        values = v_last if e else v_main

        def step(at, end):
            part = jnp.dot(probs_s[i % 2, :, at:end], values[at:end], preferred_element_type=F32)
            acc_s[...] = part if at == 0 else acc_s[...] + part

        def finish():
            top, total = jnp.concatenate(tops, axis=0), jnp.concatenate(totals, axis=0)
            out = acc_s[...] / total
            lse = top * SCORE_SCALE + jnp.log2(total)
            rows = slice(tile * TILE, (tile + 1) * TILE)
            if not far:
                for n in range(2):
                    block = 2 * tile + n
                    half = slice(n * TOK, (n + 1) * TOK)
                    out_ref[block // 4, block % 4, e] = out[half]
                    lse_ref[block // 4, block % 4, e] = jnp.broadcast_to(lse[half], (TOK, HD))
                return
            for n in range(2):
                block = 2 * tile + n
                half = slice(n * TOK, (n + 1) * TOK)
                lse_near = near_lse[block // 4, block % 4, e][:, 0:1]
                high = jnp.maximum(lse[half], lse_near)
                weight, weight_near = jnp.exp2(lse[half] - high), jnp.exp2(lse_near - high)
                both = weight + weight_near
                value = (out[half] * weight + near_out[block // 4, block % 4, e] * weight_near) / both
                lse_s[block, e] = jnp.broadcast_to(high + jnp.log2(both), (TOK, HD))
                msgs[block][e * TOK : (e + 1) * TOK] = value.astype(BF16)

        steps = []
        for at in range(0, size(i), SPLIT):
            steps.append(functools.partial(step, at, min(at + SPLIT, size(i))))
        return steps + [finish]

    def weave(*lists):
        order = []
        for steps in lists:
            order += [((n + 0.5) / len(steps), step) for n, step in enumerate(steps)]
        for _, step in sorted(order, key=lambda entry: entry[0]):
            step()

    weave(score_steps(0))
    pending = None
    for i in range(len(jobs)):
        tops, totals = [], []
        lists = [softmax_steps(i, tops, totals)]
        if i + 1 < len(jobs):
            lists.append(score_steps(i + 1))
        if pending is not None:
            lists.append(pending)
        weave(*lists)
        pending = product_steps(i, tops, totals)
    weave(pending)

    if far:
        flat = to_rows([lse_s[block, e] for block in range(count) for e in range(2)])
        for block in range(count):
            part = flat[block * 4 : block * 4 + 4]
            high = part.astype(BF16).astype(F32)
            middle = (part - high).astype(BF16).astype(F32)
            low = part - high - middle
            stack = jnp.concatenate([high, middle, low, jnp.zeros((4, HD), F32)], axis=0)
            msgs[block][2 * TOK : MSG_ROWS] = stack.astype(BF16)


def stale_attention(queries, pieces, near=None, after=None):
    far = near is not None
    count = len(queries)
    args = [*queries, *pieces]
    hbm = pl.BlockSpec(memory_space=pltpu.HBM)
    in_specs = [vmem()] * count + [hbm] * 4
    if far:
        args += [*near, after]
        in_specs += [vmem(), vmem(), pl.BlockSpec(memory_space=pl.ANY)]
        out_shape = [jax.ShapeDtypeStruct((MSG_ROWS, HD), BF16)] * count
    else:
        out_shape = [jax.ShapeDtypeStruct((B, 4, 2, TOK, HD), F32)] * 2
    work = count * TOK * (KEYS + KEYS_LAST)
    return pl.pallas_call(
        functools.partial(stale_kernel, far, count),
        out_shape=out_shape,
        in_specs=in_specs,
        out_specs=[vmem()] * len(out_shape),
        scratch_shapes=[
            pltpu.VMEM((8, 2, TOK, HD), F32),
            pltpu.VMEM((TILE, HD), F32),
            pltpu.VMEM((KEYS, HD), BF16),
            pltpu.VMEM((KEYS, HD), BF16),
            pltpu.VMEM((KEYS_LAST, HD), BF16),
            pltpu.VMEM((KEYS_LAST, HD), BF16),
            pltpu.VMEM((2, TILE, KEYS), F32),
            pltpu.VMEM((2, TILE, KEYS), BF16),
            pltpu.SemaphoreType.DMA((16,)),
        ],
        compiler_params=params(VMEM_MIB),
        cost_estimate=pl.CostEstimate(
            flops=4 * work * HD, bytes_accessed=4 * (KEYS + KEYS_LAST) * HD, transcendentals=work
        ),
        name="far_attention" if far else "near_attention",
    )(*args)


def merge_kernel(u_ref, s_ref, fresh_out, fresh_rows, *refs):
    msgs, out_ref = refs[0:8], refs[8]
    lses = []
    for msg in msgs:
        stack = msg[2 * TOK : MSG_ROWS].astype(F32)
        lses.append(stack[0:4] + stack[4:8] + stack[8:12])
    weights, jobs = [], []
    for p in range(2):
        for k in range(LOCAL_HEADS):
            at = (p * LOCAL_HEADS + k) * 2
            parts = [(None, fresh_rows[at : at + 2])]
            if k < 4:
                parts.append((4 * p + k, lses[4 * p + k][0:2]))
            else:
                parts += [(4 * p + n, lses[4 * p + n][2:4]) for n in range(4)]
            top = parts[0][1]
            for _, lse in parts[1:]:
                top = jnp.maximum(top, lse)
            raw = [jnp.exp2(lse - top) for _, lse in parts]
            total = sum(raw[1:], raw[0])
            jobs.append((p, k, [(source, len(weights) + n) for n, (source, _) in enumerate(parts)]))
            weights += [one / total for one in raw]
    filler = jnp.zeros((HD - 2 * len(weights), HD), F32)
    table = jnp.concatenate(weights + [filler], axis=0).T
    for p, k, parts in jobs:
        s = s_ref[0] if p == 0 else 1 - s_ref[0]
        head = lax.rem(u_ref[0] + k, 4) if k < 4 else 4
        out = [None, None]
        for source, n in parts:
            for half, rows in enumerate((slice(0, HD), slice(HD, TOK))):
                if source is None:
                    value = fresh_out[p, k, rows]
                else:
                    at = 0 if k < 4 else TOK
                    value = msgs[source][at + rows.start : at + rows.stop].astype(F32)
                column = table[0 : rows.stop - rows.start, 2 * n + half : 2 * n + half + 1]
                term = value * column
                out[half] = term if out[half] is None else out[half] + term
        cols = pl.ds(pl.multiple_of(head * HD, HD), HD)
        out_ref[s, :, cols] = jnp.concatenate(out, axis=0).astype(BF16)


def merge(u, s, fresh_out, fresh_rows, msgs):
    return pl.pallas_call(
        merge_kernel,
        out_shape=jax.ShapeDtypeStruct((B, TOK, WIDTH), BF16),
        in_specs=[smem()] * 2 + [vmem()] * 10,
        out_specs=vmem(),
        compiler_params=params(VMEM_MIB),
        cost_estimate=pl.CostEstimate(
            flops=10 * ROWS * WIDTH, bytes_accessed=14 * ROWS * WIDTH, transcendentals=0
        ),
        name="merge",
    )(u, s, fresh_out, fresh_rows, *msgs)


def shards(
    hidden,
    mod_shift,
    mod_scale,
    w_query,
    w_key,
    w_value,
    q_gain,
    k_gain,
    token_place,
    stale_keys,
    stale_values,
):
    patch = lax.axis_index("patch")
    tp = lax.axis_index("tp")
    y = patch // (NX * NZ)
    x = (patch // NZ) % NX
    u = jnp.where(tp % 2 == 0, y, x).astype(jnp.int32).reshape(1)
    v = jnp.where(tp % 2 == 0, x, y).astype(jnp.int32).reshape(1)
    s = (v ^ (v >> 1)) & 1

    own_rows = hidden.reshape(ROWS, CHUNK)
    own_stats = row_stats(own_rows)
    stats = [own_stats] + [swap_tp(own_stats, z, c) for z, c in ((1, 0), (1, 1), (0, 1))]
    own_rows, *stats = lax.optimization_barrier((own_rows, *stats))
    z_rows = swap_tp(own_rows, 1, 0)
    core_rows = swap_tp(own_rows, 0, 1)

    packed = pack_stale(u, stale_keys, stale_values)
    arrived = [packed[0]] + [to_peer(packed[4 - r], 0, 4 - r) for r in range(1, 4)]
    near, other = assemble(s, [*arrived, packed[4]])
    near = [near, to_peer(other, 1, 0)]
    near_all = [*near, *[swap_v(piece) for piece in near]]
    cond, cos, sin = tables(token_place, other)

    weights = (w_query, w_key, w_value)
    block = lambda flip: (tp ^ flip).astype(jnp.int32).reshape(1)
    blocks = jnp.concatenate([block(0), block(1)])
    same = (cond, mod_shift, mod_scale, weights, stats)
    acc = project("project_chip", blocks, [own_rows, core_rows], *same)

    *near, z_rows, acc = lax.optimization_barrier((*near, z_rows, acc))
    cross_rows = swap_tp(z_rows, 0, 1)
    far = [swap_z_hi(piece) for piece in near]
    acc = project("project_z", block(2), [z_rows], *same, acc=acc, after=near_all[2:])
    query, key, fresh_values, own_sq = project(
        "project_cross", block(3), [cross_rows], *same, acc=acc, last=True
    )

    squares = [own_sq] + [swap_tp(own_sq, z, c) for z, c in ((1, 0), (1, 1), (0, 1))]
    fresh_keys, *sends = norm_rope(u, s, query, key, squares, q_gain, k_gain, cos, sin)
    queries = [None] * 8
    queries[0] = sends[0]
    for p, r in ((0, 1), (0, 3), (1, 0), (0, 2), (1, 1), (1, 3), (1, 2)):
        k = (4 - r) % 4
        queries[4 * p + r] = to_peer(sends[4 * p + k], p, k)
    fresh_out, fresh_rows = fresh_attention(u, s, fresh_keys, fresh_values, sends)

    far_second, *queries = lax.optimization_barrier((far[1], *queries))
    far_all = [far[0], far_second, swap_v(far[0]), swap_v(far_second)]
    partial = stale_attention(queries, near_all)
    outs = stale_attention(queries, far_all, near=partial, after=fresh_rows)
    returned = [outs[0]] + [None] * 7
    for p, k in ((1, 0), (1, 1), (1, 3), (1, 2), (0, 1), (0, 3), (0, 2)):
        r = (4 - k) % 4
        returned[4 * p + k] = to_peer(outs[4 * p + r], p, r)
    attended = merge(u, s, fresh_out, fresh_rows, returned)
    return (
        attended,
        fresh_keys.reshape(B, TOK, WIDTH),
        fresh_values.reshape(B, TOK, WIDTH),
    )


def solution(mesh):
    in_specs = (
        P(None, "patch", "tp"),
        P(),
        P(),
        P(None, "tp"),
        P(None, "tp"),
        P(None, "tp"),
        P("tp"),
        P("tp"),
        P("patch"),
        P(None, "patch", "tp"),
        P(None, "patch", "tp"),
    )
    out_specs = (P(None, "patch", "tp"), P(None, "patch", "tp"), P(None, "patch", "tp"))
    return jax.shard_map(shards, mesh=mesh, in_specs=in_specs, out_specs=out_specs, check_vma=False)
```

time: 137 us -> 125 us (0.912)
  blocking collectives: 21.5 us -> 0 us
  starting transfers between devices: 25.8 us -> 42.6 us
  Pallas kernels: 50.6 us -> 40.6 us
  local copies, waits for them, and re-layouts: 8.05 us -> 15.8 us
  waiting for transfers between devices: 28.4 us -> 24.5 us
    ppermute x13 -> x33, starting transfers between devices: 16.4 us -> 42.6 us  [permute(): lax.ppermute(value, AXES, [(linear(*p), linear(*move(*p))) for p in place...]
    all_to_all x2 -> x0, blocking collectives: 21.5 us -> none  [the longest x1 14.8 us: exchange(): return lax.all_to_all(value, AXES, 0, 0, axis_index_groups=groups)]
    all_to_all x2 -> x0, starting transfers between devices: 9.4 us -> none  [exchange(): return lax.all_to_all(value, AXES, 0, 0, axis_index_groups=groups)]
    pallas_call x8 -> x9, Pallas kernels: 45.6 us -> 36.7 us  [the longest x3 17.5 us: project(): pl.pallas_call(functools.partial(project_kernel, count, len(after), acc i...]
    unnamed x32 -> x52, local copies, waits for them, and re-layouts: 7.33 us -> 15.8 us
    pallas_call x1, Pallas kernels: 4.47 us -> 1.55 us  [merge(): pl.pallas_call(merge_kernel, out_shape=jax.ShapeDtypeStruct((B, TOK, WIDT...]
    ppermute x13 -> x33, waiting for transfers between devices: 27.1 us -> 24.5 us  [permute(): lax.ppermute(value, AXES, [(linear(*p), linear(*move(*p))) for p in place...]
  transfers between devices with their start and end apart: 15 -> 33, of which waited for: 6 -> 13; matrix products, arithmetic and copies ran while one was open for 1% -> 0% of each run, Pallas kernels for 28% -> 24%
where the time goes in v2:
time: 125 us
  starting transfers between devices  42.6 us (34%)
  Pallas kernels  40.6 us (32%)
  waiting for transfers between devices  24.5 us (20%)
  local copies, waits for them, and re-layouts  15.8 us (13%)
    ppermute x33, starting transfers between devices, permute(): lax.ppermute(value, AXES, [(linear(*p), linear(*move(*p))) for p in place...  42.6 us
    ppermute x33, waiting for transfers between devices, permute(): lax.ppermute(value, AXES, [(linear(*p), linear(*move(*p))) for p in place...  24.5 us
    pallas_call x3, Pallas kernels, project(): pl.pallas_call(functools.partial(project_kernel, count, len(after), acc i...  17.5 us
    unnamed x52, local copies, waits for them, and re-layouts  15.8 us
    pallas_call x2, Pallas kernels, stale_attention(): pl.pallas_call(functools.partial(stale_kernel, far, count), out_shape=out...  15.1 us
  transfers between devices with their start and end apart: 33, of which 13 were waited for; matrix products, arithmetic and copies ran while one was open for 0% of the time, Pallas kernels for 24%

profile of v2, /device:TPU:0, one launch (start us, length us, event | category | flops | bytes accessed | tf_op | source)
XLA Modules:
  0.0 124.5 jit_solution(3772671515498035140)
XLA Ops:
  0.7 1.6 %row_stats.1.refs_9_.refs_8_ = f32[8,384]{1,0:T(8,128)S(1)} custom-call(bf16[288,1280]{1,0:T(8,128)(2,1)} %bitcast.3.hidden_hbm.refs_1_), custom_call_target="tpu_custom_call" | custom-call | flops 1474560 | bytes 737280 | tf_op jit(solution)/shard_map/row_stats/pallas_call | solution.py:125
  2.2 2.1 %collective-permute-start.4 = (f32[8,384]{1,0:T(8,128)S(1)}, f32[8,384]{1,0:T(8,128)S(1)}, u32[]{:S(2)}, u32[]{:S(2)}) collective-permute-start(f32[8,384]{1,0:T(8,128)S(1)} %row_stats.1.refs_9_.refs_8_), channel_id=1, source_target_pairs={{0,2},{1,3},{2,0},{3,1},{4,6},{5,7},{6,4},{7,5},{8,10},{33,35},{10... | collective-permute-start | bytes 36872 | tf_op jit(solution)/shard_map/ppermute | solution.py:67
  4.5 1.5 %collective-permute-done.4.refs_10_.refs_9_ = f32[8,384]{1,0:T(8,128)S(1)} collective-permute-done((f32[8,384]{1,0:T(8,128)S(1)}, f32[8,384]{1,0:T(8,128)S(1)}, u32[]{:S(2)}, u32[]{:S(2)}) %collective-permute-start.4) | collective-permute-done | bytes 12320 | tf_op jit(solution)/shard_map/ppermute | solution.py:67
  6.0 1.4 %collective-permute-done.5.refs_11_.refs_10_ = f32[8,384]{1,0:T(8,128)S(1)} collective-permute-done((f32[8,384]{1,0:T(8,128)S(1)}, f32[8,384]{1,0:T(8,128)S(1)}, u32[]{:S(2)}, u32[]{:S(2)}) %collective-permute-start.5) | collective-permute-done | bytes 12320 | tf_op jit(solution)/shard_map/ppermute | solution.py:67
  8.2 1.0 copy-done.6
  9.2 1.0 copy-done.7
  10.6 3.1 %collective-permute-start = (bf16[2,2,144,128]{3,2,1,0:T(8,128)(2,1)S(1)}, bf16[2,2,144,128]{3,2,1,0:T(8,128)(2,1)S(1)}, u32[]{:S(2)}, u32[]{:S(2)}) collective-permute-start(bf16[2,2,144,128]{3,2,1,0:T(8,128)(2,1)S(1)} %get-tuple-element.57), channel_id=1, source_target_pairs={{0,96},{1,25},{2,98},{3,27},{4,100},{5,29},{6,102},{7,31},{8,104},... | collective-permute-start | bytes 442376 | tf_op jit(solution)/shard_map/ppermute | solution.py:67
  14.3 1.0 collective-permute-start.2
  15.3 2.7 %collective-permute-done.refs_1_ = bf16[2,2,144,128]{3,2,1,0:T(8,128)(2,1)S(1)} collective-permute-done((bf16[2,2,144,128]{3,2,1,0:T(8,128)(2,1)S(1)}, bf16[2,2,144,128]{3,2,1,0:T(8,128)(2,1)S(1)}, u32[]{:S(2)}, u32[]{:S(2)}) %collective-permute-start) | collective-permute-done | bytes 147488 | tf_op jit(solution)/shard_map/ppermute | solution.py:67
  17.9 2.5 %collective-permute-done.1.refs_2_ = bf16[2,2,144,128]{3,2,1,0:T(8,128)(2,1)S(1)} collective-permute-done((bf16[2,2,144,128]{3,2,1,0:T(8,128)(2,1)S(1)}, bf16[2,2,144,128]{3,2,1,0:T(8,128)(2,1)S(1)}, u32[]{:S(2)}, u32[]{:S(2)}) %collective-permute-start.1) | collective-permute-done | bytes 147488 | tf_op jit(solution)/shard_map/ppermute | solution.py:67
  20.4 1.5 %collective-permute-done.2.refs_3_ = bf16[2,2,144,128]{3,2,1,0:T(8,128)(2,1)S(1)} collective-permute-done((bf16[2,2,144,128]{3,2,1,0:T(8,128)(2,1)S(1)}, bf16[2,2,144,128]{3,2,1,0:T(8,128)(2,1)S(1)}, u32[]{:S(2)}, u32[]{:S(2)}) %collective-permute-start.2) | collective-permute-done | bytes 147488 | tf_op jit(solution)/shard_map/ppermute | solution.py:67
  22.7 1.5 %collective-permute-start.3 = (bf16[2,720,128]{2,1,0:T(8,128)(2,1)S(1)}, bf16[2,720,128]{2,1,0:T(8,128)(2,1)}, u32[]{:S(2)}, u32[]{:S(2)}) collective-permute-start(bf16[2,720,128]{2,1,0:T(8,128)(2,1)S(1)} %get-tuple-element.62.after), channel_id=1, source_target_pairs={{0,8},{1,33},{2,10},{3,35},{4,12},{5,37},{6,14},{7,39},{8,0},{33,1... | collective-permute-start | bytes 1105928 | tf_op jit(solution)/shard_map/ppermute | solution.py:67
  24.2 0.9 tables.1
  26.4 0.9 copy-done.2
  27.4 2.9 %copy-done = bf16[5120,640]{1,0:T(8,128)(2,1)S(1)} copy-done((bf16[5120,640]{1,0:T(8,128)(2,1)S(1)}, bf16[5120,640]{1,0:T(8,128)(2,1)}, u32[]{:S(2)}) %copy-start) | copy-done | bytes 6553624
  30.2 1.1 copy-done.3
  31.3 8.2 %project_chip.1.refs_12_ = f32[288,1920]{1,0:T(8,128)S(1)} custom-call(s32[2]{0:T(128)S(1)} %pad_add_fusion.refs_0_, bf16[288,1280]{1,0:T(8,128)(2,1)} %bitcast.3.hidden_hbm.refs_1_, bf16[288,1280]{1,0:T(8,128)(2,1)S(1)} %copy-done.3, f32[288,128]{1,0:T(8,128)S(1)} %get-tuple-element.64.refs_3_.refs_2_, f32[2,5120]{1,0:T(2,128)S(1)} %copy-done.4, ...), custom_call_target="tpu_custom_call" | custom-call | flops 2831155200 | bytes 9830400 | tf_op jit(solution)/shard_map/project_chip/pallas_call | solution.py:330
  39.7 2.2 %collective-permute-start.10 = (bf16[2,720,128]{2,1,0:T(8,128)(2,1)}, bf16[2,720,128]{2,1,0:T(8,128)(2,1)S(1)}, u32[]{:S(2)}, u32[]{:S(2)}) collective-permute-start(bf16[2,720,128]{2,1,0:T(8,128)(2,1)} %get-tuple-element.97.refs_8_), channel_id=1, source_target_pairs={{0,24},{1,97},{2,26},{3,99},{4,28},{5,101},{6,30},{7,103},{8,16},{... | collective-permute-start | bytes 1105928 | tf_op jit(solution)/shard_map/ppermute | solution.py:67
  41.9 1.1 collective-permute-start.11
  43.0 3.6 %collective-permute-start.15 = (bf16[2,720,128]{2,1,0:T(8,128)(2,1)}, bf16[2,720,128]{2,1,0:T(8,128)(2,1)}, u32[]{:S(2)}, u32[]{:S(2)}) collective-permute-start(bf16[2,720,128]{2,1,0:T(8,128)(2,1)} %collective-permute-done.3.refs_9_), channel_id=1, source_target_pairs={{0,4},{1,5},{2,6},{3,7},{4,0},{5,1},{6,2},{7,3},{8,12},{33,37},{10... | collective-permute-start | bytes 1105928 | tf_op jit(solution)/shard_map/ppermute | solution.py:67
  46.7 2.1 %collective-permute-done.10.refs_13_.refs_10_ = bf16[2,720,128]{2,1,0:T(8,128)(2,1)S(1)} collective-permute-done((bf16[2,720,128]{2,1,0:T(8,128)(2,1)}, bf16[2,720,128]{2,1,0:T(8,128)(2,1)S(1)}, u32[]{:S(2)}, u32[]{:S(2)}) %collective-permute-start.10) | collective-permute-done | bytes 368672 | tf_op jit(solution)/shard_map/ppermute | solution.py:67
  48.7 4.1 %collective-permute-done.11.refs_14_.refs_11_ = bf16[2,720,128]{2,1,0:T(8,128)(2,1)} collective-permute-done((bf16[2,720,128]{2,1,0:T(8,128)(2,1)}, bf16[2,720,128]{2,1,0:T(8,128)(2,1)}, u32[]{:S(2)}, u32[]{:S(2)}) %collective-permute-start.11) | collective-permute-done | bytes 368672 | tf_op jit(solution)/shard_map/ppermute | solution.py:67
  52.8 2.9 %copy-done.1 = bf16[5120,640]{1,0:T(8,128)(2,1)S(1)} copy-done((bf16[5120,640]{1,0:T(8,128)(2,1)S(1)}, bf16[5120,640]{1,0:T(8,128)(2,1)}, u32[]{:S(2)}) %copy-start.1) | copy-done | bytes 6553624
  58.5 3.6 %project_z.1.refs_12_ = f32[288,1920]{1,0:T(8,128)S(1)} custom-call(s32[1]{0:T(128)} %bitcast.6.refs_0_, bf16[288,1280]{1,0:T(8,128)(2,1)S(1)} %collective-permute-done.7.refs_1_, f32[288,128]{1,0:T(8,128)S(1)} %get-tuple-element.64.refs_3_.refs_2_, f32[2,5120]{1,0:T(2,128)S(1)} %copy-done.4, f32[2,5120]{1,0:T(2,128)S(1)} %copy-done.5, ...), custom_call_target="tpu_custom_call" | custom-call | flops 1415577600 | bytes 4915200 | tf_op jit(solution)/shard_map/project_z/pallas_call | solution.py:330
  62.2 5.7 %project_cross.1 = (f32[288,640]{1,0:T(8,128)S(1)}, f32[288,640]{1,0:T(8,128)S(1)}, bf16[288,640]{1,0:T(8,128)(2,1)}, f32[8,384]{1,0:T(8,128)S(1)}) custom-call(s32[1]{0:T(128)} %bitcast.2.refs_0_, bf16[288,1280]{1,0:T(8,128)(2,1)} %collective-permute-done.9.refs_1_, f32[288,128]{1,0:T(8,128)S(1)} %get-tuple-element.64.refs_3_.refs_2_, ...), custom_call_target="tpu_custom_call" | custom-call | flops 1415577600 | bytes 4915200 | tf_op jit(solution)/shard_map/project_cross/pallas_call | solution.py:330
  67.8 1.5 %collective-permute-start.12 = (f32[8,384]{1,0:T(8,128)S(1)}, f32[8,384]{1,0:T(8,128)S(1)}, u32[]{:S(2)}, u32[]{:S(2)}) collective-permute-start(f32[8,384]{1,0:T(8,128)S(1)} %get-tuple-element.73.s0), channel_id=1, source_target_pairs={{0,2},{1,3},{2,0},{3,1},{4,6},{5,7},{6,4},{7,5},{8,10},{33,35},{10... | collective-permute-start | bytes 36872 | tf_op jit(solution)/shard_map/ppermute | solution.py:67
  70.1 1.6 %collective-permute-done.12.s1 = f32[8,384]{1,0:T(8,128)S(1)} collective-permute-done((f32[8,384]{1,0:T(8,128)S(1)}, f32[8,384]{1,0:T(8,128)S(1)}, u32[]{:S(2)}, u32[]{:S(2)}) %collective-permute-start.12) | collective-permute-done | bytes 12320 | tf_op jit(solution)/shard_map/ppermute | solution.py:67
  72.5 1.8 %norm_rope.1 = (bf16[288,640]{1,0:T(8,128)(2,1)}, bf16[2,144,128]{2,1,0:T(8,128)(2,1)S(1)}, bf16[2,144,128]{2,1,0:T(8,128)(2,1)S(1)}, bf16[2,144,128]{2,1,0:T(8,...) custom-call(s32[1]{0:T(128)} %bitcast.u_ref, ...), custom_call_target="tpu_custom_call" | custom-call | flops 3686400 | bytes 2949120 | tf_op jit(solution)/shard_map/norm_rope/pallas_call | solution.py:379
  75.5 1.3 %collective-permute-start.18 = (bf16[2,144,128]{2,1,0:T(8,128)(2,1)S(1)}, bf16[2,144,128]{2,1,0:T(8,128)(2,1)S(1)}, u32[]{:S(2)}, u32[]{:S(2)}) collective-permute-start(bf16[2,144,128]{2,1,0:T(8,128)(2,1)S(1)} %get-tuple-element.79.refs_1_), channel_id=1, source_target_pairs={{0,32},{1,9},{2,34},{3,11},{4,36},{5,13},{6,38},{7,15},{8,40},{33,... | collective-permute-start | bytes 221192 | tf_op jit(solution)/shard_map/ppermute | solution.py:67
  76.8 3.7 %collective-permute-start.20 = (bf16[2,144,128]{2,1,0:T(8,128)(2,1)S(1)}, bf16[2,144,128]{2,1,0:T(8,128)(2,1)S(1)}, u32[]{:S(2)}, u32[]{:S(2)}) collective-permute-start(bf16[2,144,128]{2,1,0:T(8,128)(2,1)S(1)} %get-tuple-element.85.refs_7_), channel_id=1, source_target_pairs={{0,104},{1,57},{2,106},{3,59},{4,108},{5,61},{6,110},{7,63},{8,96}... | collective-permute-start | bytes 221192 | tf_op jit(solution)/shard_map/ppermute | solution.py:67
  80.5 1.5 %collective-permute-start.21 = (bf16[2,144,128]{2,1,0:T(8,128)(2,1)S(1)}, bf16[2,144,128]{2,1,0:T(8,128)(2,1)S(1)}, u32[]{:S(2)}, u32[]{:S(2)}) collective-permute-start(bf16[2,144,128]{2,1,0:T(8,128)(2,1)S(1)} %get-tuple-element.84.refs_6_), channel_id=1, source_target_pairs={{0,72},{1,49},{2,74},{3,51},{4,76},{5,53},{6,78},{7,55},{8,64},{33... | collective-permute-start | bytes 221192 | tf_op jit(solution)/shard_map/ppermute | solution.py:67
  82.0 2.2 %collective-permute-start.22 = (bf16[2,144,128]{2,1,0:T(8,128)(2,1)S(1)}, bf16[2,144,128]{2,1,0:T(8,128)(2,1)S(1)}, u32[]{:S(2)}, u32[]{:S(2)}) collective-permute-start(bf16[2,144,128]{2,1,0:T(8,128)(2,1)S(1)} %get-tuple-element.83.refs_5_), channel_id=1, source_target_pairs={{0,40},{1,41},{2,42},{3,43},{4,44},{5,45},{6,46},{7,47},{8,32},{33... | collective-permute-start | bytes 221192 | tf_op jit(solution)/shard_map/ppermute | solution.py:67
  84.3 2.1 %collective-permute-start.24 = (bf16[2,720,128]{2,1,0:T(8,128)(2,1)}, bf16[2,720,128]{2,1,0:T(8,128)(2,1)S(1)}, u32[]{:S(2)}, u32[]{:S(2)}) collective-permute-start(bf16[2,720,128]{2,1,0:T(8,128)(2,1)} %collective-permute-done.23.refs_8_), channel_id=1, source_target_pairs={{0,24},{1,97},{2,26},{3,99},{4,28},{5,101},{6,30},{7,103},{8,16},{... | collective-permute-start | bytes 1105928 | tf_op jit(solution)/shard_map/ppermute | solution.py:67
  86.4 1.2 %collective-permute-done.21.refs_6_ = bf16[2,144,128]{2,1,0:T(8,128)(2,1)S(1)} collective-permute-done((bf16[2,144,128]{2,1,0:T(8,128)(2,1)S(1)}, bf16[2,144,128]{2,1,0:T(8,128)(2,1)S(1)}, u32[]{:S(2)}, u32[]{:S(2)}) %collective-permute-start.21) | collective-permute-done | bytes 73760 | tf_op jit(solution)/shard_map/ppermute | solution.py:67
  87.6 0.9 collective-permute-done.22.refs_7_
  88.5 2.1 %collective-permute-start.25 = (bf16[2,720,128]{2,1,0:T(8,128)(2,1)}, bf16[2,720,128]{2,1,0:T(8,128)(2,1)S(1)}, u32[]{:S(2)}, u32[]{:S(2)}) collective-permute-start(bf16[2,720,128]{2,1,0:T(8,128)(2,1)} %collective-permute-done.15.refs_9_), channel_id=1, source_target_pairs={{0,24},{1,97},{2,26},{3,99},{4,28},{5,101},{6,30},{7,103},{8,16},{... | collective-permute-start | bytes 1105928 | tf_op jit(solution)/shard_map/ppermute | solution.py:67
  90.6 1.0 copy-done.8
  91.6 1.0 copy-done.9
  92.6 1.0 fresh_attention.1
  93.7 7.1 %near_attention.1 = (f32[2,4,2,144,128]{4,3,2,1,0:T(8,128)S(1)}, f32[2,4,2,144,128]{4,3,2,1,0:T(8,128)S(1)}) custom-call(bf16[2,144,128]{2,1,0:T(8,128)(2,1)S(1)} %get-tuple-element.89.refs_0_, bf16[2,144,128]{2,1,0:T(8,128)(2,1)S(1)} %collective-permute-done.16.refs_1_, bf16[2,144,128]{2,1,0:T(8,128)(2,1)S(1)} %collective-permute-done.17.refs_2_, ...), custom_call_target="tpu_custom_call" | custom-call | flops 1698693120 | bytes 1474560 | tf_op jit(solution)/shard_map/near_attention/pallas_call | solution.py:609
  100.8 7.9 %far_attention.1 = (bf16[304,128]{1,0:T(8,128)(2,1)S(1)}, bf16[304,128]{1,0:T(8,128)(2,1)S(1)}, bf16[304,128]{1,0:T(8,128)(2,1)S(1)}, bf16[304,128]{1,0:T(8,128)...) custom-call(bf16[2,144,128]{2,1,0:T(8,128)(2,1)S(1)} %get-tuple-elem, ...), custom_call_target="tpu_custom_call" | custom-call | flops 1698693120 | bytes 1474560 | tf_op jit(solution)/shard_map/far_attention/pallas_call | solution.py:609
  108.8 0.9 collective-permute-start.26
  111.9 3.3 %collective-permute-start.30 = (bf16[304,128]{1,0:T(8,128)(2,1)S(1)}, bf16[304,128]{1,0:T(8,128)(2,1)S(1)}, u32[]{:S(2)}, u32[]{:S(2)}) collective-permute-start(bf16[304,128]{1,0:T(8,128)(2,1)S(1)} %get-tuple-element.106), channel_id=1, source_target_pairs={{0,104},{1,57},{2,106},{3,59},{4,108},{5,61},{6,110},{7,63},{8,96}... | collective-permute-start | bytes 233480 | tf_op jit(solution)/shard_map/ppermute | solution.py:67
  115.2 1.3 %collective-permute-start.31 = (bf16[304,128]{1,0:T(8,128)(2,1)S(1)}, bf16[304,128]{1,0:T(8,128)(2,1)S(1)}, u32[]{:S(2)}, u32[]{:S(2)}) collective-permute-start(bf16[304,128]{1,0:T(8,128)(2,1)S(1)} %get-tuple-element.107), channel_id=1, source_target_pairs={{0,72},{1,49},{2,74},{3,51},{4,76},{5,53},{6,78},{7,55},{8,64},{33... | collective-permute-start | bytes 233480 | tf_op jit(solution)/shard_map/ppermute | solution.py:67
  116.5 2.3 %collective-permute-start.32 = (bf16[304,128]{1,0:T(8,128)(2,1)S(1)}, bf16[304,128]{1,0:T(8,128)(2,1)S(1)}, u32[]{:S(2)}, u32[]{:S(2)}) collective-permute-start(bf16[304,128]{1,0:T(8,128)(2,1)S(1)} %get-tuple-element.108), channel_id=1, source_target_pairs={{0,40},{1,41},{2,42},{3,43},{4,44},{5,45},{6,46},{7,47},{8,32},{33... | collective-permute-start | bytes 233480 | tf_op jit(solution)/shard_map/ppermute | solution.py:67
  118.8 3.2 %collective-permute-done.31.refs_6_ = bf16[304,128]{1,0:T(8,128)(2,1)S(1)} collective-permute-done((bf16[304,128]{1,0:T(8,128)(2,1)S(1)}, bf16[304,128]{1,0:T(8,128)(2,1)S(1)}, u32[]{:S(2)}, u32[]{:S(2)}) %collective-permute-start.31) | collective-permute-done | bytes 77856 | tf_op jit(solution)/shard_map/ppermute | solution.py:67
  122.0 1.0 collective-permute-done.32.refs_7_
  123.0 1.6 %merge.1 = bf16[2,144,640]{2,1,0:T(8,128)(2,1)} custom-call(s32[1]{0:T(128)} %bitcast.u_ref, s32[1]{0:T(128)S(6)} %and.28.s_ref, f32[2,5,144,128]{3,2,1,0:T(8,128)S(1)} %get-tuple-element.86.fresh_out, f32[24,128]{1,0:T(8,128)S(1)} %get-tuple-element.87.refs_14_.fresh_rows, bf16[304,128]{1,0:T(8,128)(2,1)S(1)} %get-tuple-element.101.refs_0_, ...), custom_call_target="tpu_custom_call" | custom-call | flops 1843200 | bytes 2580480 | tf_op jit(solution)/shard_map/merge/pallas_call | solution.py:676
  (83 shorter events, 12.1 us)
Async XLA Ops:
  0.6 23.6 %copy-start.25 = (f32[1,128]{1,0:T(1,128)S(1)}, f32[1,128]{1,0:T(1,128)}, u32[]{:S(2)}) copy-start(f32[1,128]{1,0:T(1,128)} %constant.62.clone.freq) | copy-start | bytes 1540
  0.6 23.6 %copy-start.24 = (s32[144]{0:T(256)S(1)}, s32[144]{0:T(256)}, u32[]{:S(2)}) copy-start(s32[144]{0:T(256)} %place_hbm.1) | copy-start | bytes 1732
  0.7 26.7 %copy-start.4 = (f32[2,5120]{1,0:T(2,128)S(1)}, f32[2,5120]{1,0:T(2,128)}, u32[]{:S(2)}) copy-start(f32[2,5120]{1,0:T(2,128)} %refs_3_.3) | copy-start | bytes 122884
  0.7 26.7 %copy-start.5 = (f32[2,5120]{1,0:T(2,128)S(1)}, f32[2,5120]{1,0:T(2,128)}, u32[]{:S(2)}) copy-start(f32[2,5120]{1,0:T(2,128)} %refs_4_.5) | copy-start | bytes 122884
  2.2 37.3 %copy-start.10 = (f32[8,384]{1,0:T(8,128)}, f32[8,384]{1,0:T(8,128)S(1)}, u32[]{:S(2)}) copy-start(f32[8,384]{1,0:T(8,128)S(1)} %row_stats.1.refs_9_.refs_8_) | copy-start | bytes 36868
  2.2 3.8 %collective-permute-start.4 = (f32[8,384]{1,0:T(8,128)S(1)}, f32[8,384]{1,0:T(8,128)S(1)}, u32[]{:S(2)}, u32[]{:S(2)}) collective-permute-start(f32[8,384]{1,0:T(8,128)S(1)} %row_stats.1.refs_9_.refs_8_), channel_id=1, source_target_pairs={{0,2},{1,3},{2,0},{3,1},{4,6},{5,7},{6,4},{7,5},{8,10},{33,35},{10... | collective-permute-start | bytes 36872 | tf_op jit(solution)/shard_map/ppermute | solution.py:67
  4.3 3.1 %collective-permute-start.5 = (f32[8,384]{1,0:T(8,128)S(1)}, f32[8,384]{1,0:T(8,128)S(1)}, u32[]{:S(2)}, u32[]{:S(2)}) collective-permute-start(f32[8,384]{1,0:T(8,128)S(1)} %row_stats.1.refs_9_.refs_8_), channel_id=1, source_target_pairs={{0,3},{1,2},{2,1},{3,0},{4,7},{5,6},{6,5},{7,4},{8,11},{33,34},{10... | collective-permute-start | bytes 36872 | tf_op jit(solution)/shard_map/ppermute | solution.py:67
  4.3 3.1 %collective-permute-start.6 = (f32[8,384]{1,0:T(8,128)S(1)}, f32[8,384]{1,0:T(8,128)S(1)}, u32[]{:S(2)}, u32[]{:S(2)}) collective-permute-start(f32[8,384]{1,0:T(8,128)S(1)} %row_stats.1.refs_9_.refs_8_), channel_id=1, source_target_pairs={{0,1},{1,0},{2,3},{3,2},{4,5},{5,4},{6,7},{7,6},{8,9},{33,32},{10,... | collective-permute-start | bytes 36872 | tf_op jit(solution)/shard_map/ppermute | solution.py:67
  6.0 33.6 %copy-start.12 = (f32[8,384]{1,0:T(8,128)}, f32[8,384]{1,0:T(8,128)S(1)}, u32[]{:S(2)}) copy-start(f32[8,384]{1,0:T(8,128)S(1)} %collective-permute-done.4.refs_10_.refs_9_) | copy-start | bytes 36868
  7.5 32.1 %copy-start.14 = (f32[8,384]{1,0:T(8,128)}, f32[8,384]{1,0:T(8,128)S(1)}, u32[]{:S(2)}) copy-start(f32[8,384]{1,0:T(8,128)S(1)} %collective-permute-done.5.refs_11_.refs_10_) | copy-start | bytes 36868
  7.5 32.1 %copy-start.16 = (f32[8,384]{1,0:T(8,128)}, f32[8,384]{1,0:T(8,128)S(1)}, u32[]{:S(2)}) copy-start(f32[8,384]{1,0:T(8,128)S(1)} %collective-permute-done.6.refs_12_.refs_11_) | copy-start | bytes 36868
  7.5 19.0 %collective-permute-start.8 = (bf16[288,1280]{1,0:T(8,128)(2,1)}, bf16[288,1280]{1,0:T(8,128)(2,1)S(1)}, u32[]{:S(2)}, u32[]{:S(2)}) collective-permute-start(bf16[288,1280]{1,0:T(8,128)(2,1)} %bitcast.3.hidden_hbm.refs_1_), channel_id=1, source_target_pairs={{0,1},{1,0},{2,3},{3,2},{4,5},{5,4},{6,7},{7,6},{8,9},{33,32},{10,... | collective-permute-start | bytes 2211848 | tf_op jit(solution)/shard_map/ppermute | solution.py:67
  7.5 32.1 %collective-permute-start.7 = (bf16[288,1280]{1,0:T(8,128)(2,1)}, bf16[288,1280]{1,0:T(8,128)(2,1)S(1)}, u32[]{:S(2)}, u32[]{:S(2)}) collective-permute-start(bf16[288,1280]{1,0:T(8,128)(2,1)} %bitcast.3.hidden_hbm.refs_1_), channel_id=1, source_target_pairs={{0,2},{1,3},{2,0},{3,1},{4,6},{5,7},{6,4},{7,5},{8,10},{33,35},{10... | collective-permute-start | bytes 2211848 | tf_op jit(solution)/shard_map/ppermute | solution.py:67
  10.6 7.4 %collective-permute-start = (bf16[2,2,144,128]{3,2,1,0:T(8,128)(2,1)S(1)}, bf16[2,2,144,128]{3,2,1,0:T(8,128)(2,1)S(1)}, u32[]{:S(2)}, u32[]{:S(2)}) collective-permute-start(bf16[2,2,144,128]{3,2,1,0:T(8,128)(2,1)S(1)} %get-tuple-element.57), channel_id=1, source_target_pairs={{0,96},{1,25},{2,98},{3,27},{4,100},{5,29},{6,102},{7,31},{8,104},... | collective-permute-start | bytes 442376 | tf_op jit(solution)/shard_map/ppermute | solution.py:67
  13.7 6.8 %collective-permute-start.1 = (bf16[2,2,144,128]{3,2,1,0:T(8,128)(2,1)S(1)}, bf16[2,2,144,128]{3,2,1,0:T(8,128)(2,1)S(1)}, u32[]{:S(2)}, u32[]{:S(2)}) collective-permute-start(bf16[2,2,144,128]{3,2,1,0:T(8,128)(2,1)S(1)} %get-tuple-element.58), channel_id=1, source_target_pairs={{0,64},{1,17},{2,66},{3,19},{4,68},{5,21},{6,70},{7,23},{8,72},{33... | collective-permute-start | bytes 442376 | tf_op jit(solution)/shard_map/ppermute | solution.py:67
  14.3 7.6 %collective-permute-start.2 = (bf16[2,2,144,128]{3,2,1,0:T(8,128)(2,1)S(1)}, bf16[2,2,144,128]{3,2,1,0:T(8,128)(2,1)S(1)}, u32[]{:S(2)}, u32[]{:S(2)}) collective-permute-start(bf16[2,2,144,128]{3,2,1,0:T(8,128)(2,1)S(1)} %get-tuple-element.59), channel_id=1, source_target_pairs={{0,32},{1,9},{2,34},{3,11},{4,36},{5,13},{6,38},{7,15},{8,40},{33,... | collective-permute-start | bytes 442376 | tf_op jit(solution)/shard_map/ppermute | solution.py:67
  22.7 16.9 %collective-permute-start.3 = (bf16[2,720,128]{2,1,0:T(8,128)(2,1)S(1)}, bf16[2,720,128]{2,1,0:T(8,128)(2,1)}, u32[]{:S(2)}, u32[]{:S(2)}) collective-permute-start(bf16[2,720,128]{2,1,0:T(8,128)(2,1)S(1)} %get-tuple-element.62.after), channel_id=1, source_target_pairs={{0,8},{1,33},{2,10},{3,35},{4,12},{5,37},{6,14},{7,39},{8,0},{33,1... | collective-permute-start | bytes 1105928 | tf_op jit(solution)/shard_map/ppermute | solution.py:67
  27.4 2.9 %copy-start = (bf16[5120,640]{1,0:T(8,128)(2,1)S(1)}, bf16[5120,640]{1,0:T(8,128)(2,1)}, u32[]{:S(2)}) copy-start(bf16[5120,640]{1,0:T(8,128)(2,1)} %refs_5_.5) | copy-start | bytes 19660804
  30.2 1.1 copy-start.3
  39.6 22.5 %collective-permute-start.9 = (bf16[288,1280]{1,0:T(8,128)(2,1)S(1)}, bf16[288,1280]{1,0:T(8,128)(2,1)}, u32[]{:S(2)}, u32[]{:S(2)}) collective-permute-start(bf16[288,1280]{1,0:T(8,128)(2,1)S(1)} %collective-permute-done.7.refs_1_), channel_id=1, source_target_pairs={{0,1},{1,0},{2,3},{3,2},{4,5},{5,4},{6,7},{7,6},{8,9},{33,32},{10,... | collective-permute-start | bytes 2211848 | tf_op jit(solution)/shard_map/ppermute | solution.py:67
  39.7 9.0 %collective-permute-start.10 = (bf16[2,720,128]{2,1,0:T(8,128)(2,1)}, bf16[2,720,128]{2,1,0:T(8,128)(2,1)S(1)}, u32[]{:S(2)}, u32[]{:S(2)}) collective-permute-start(bf16[2,720,128]{2,1,0:T(8,128)(2,1)} %get-tuple-element.97.refs_8_), channel_id=1, source_target_pairs={{0,24},{1,97},{2,26},{3,99},{4,28},{5,101},{6,30},{7,103},{8,16},{... | collective-permute-start | bytes 1105928 | tf_op jit(solution)/shard_map/ppermute | solution.py:67
  41.9 10.9 %collective-permute-start.11 = (bf16[2,720,128]{2,1,0:T(8,128)(2,1)}, bf16[2,720,128]{2,1,0:T(8,128)(2,1)}, u32[]{:S(2)}, u32[]{:S(2)}) collective-permute-start(bf16[2,720,128]{2,1,0:T(8,128)(2,1)} %collective-permute-done.3.refs_9_), channel_id=1, source_target_pairs={{0,24},{1,97},{2,26},{3,99},{4,28},{5,101},{6,30},{7,103},{8,16},{... | collective-permute-start | bytes 1105928 | tf_op jit(solution)/shard_map/ppermute | solution.py:67
  43.0 33.8 %collective-permute-start.15 = (bf16[2,720,128]{2,1,0:T(8,128)(2,1)}, bf16[2,720,128]{2,1,0:T(8,128)(2,1)}, u32[]{:S(2)}, u32[]{:S(2)}) collective-permute-start(bf16[2,720,128]{2,1,0:T(8,128)(2,1)} %collective-permute-done.3.refs_9_), channel_id=1, source_target_pairs={{0,4},{1,5},{2,6},{3,7},{4,0},{5,1},{6,2},{7,3},{8,12},{33,37},{10... | collective-permute-start | bytes 1105928 | tf_op jit(solution)/shard_map/ppermute | solution.py:67
  46.6 30.2 %collective-permute-start.23 = (bf16[2,720,128]{2,1,0:T(8,128)(2,1)}, bf16[2,720,128]{2,1,0:T(8,128)(2,1)}, u32[]{:S(2)}, u32[]{:S(2)}) collective-permute-start(bf16[2,720,128]{2,1,0:T(8,128)(2,1)} %get-tuple-element.97.refs_8_), channel_id=1, source_target_pairs={{0,4},{1,5},{2,6},{3,7},{4,0},{5,1},{6,2},{7,3},{8,12},{33,37},{10... | collective-permute-start | bytes 1105928 | tf_op jit(solution)/shard_map/ppermute | solution.py:67
  52.8 2.9 %copy-start.1 = (bf16[5120,640]{1,0:T(8,128)(2,1)S(1)}, bf16[5120,640]{1,0:T(8,128)(2,1)}, u32[]{:S(2)}) copy-start(bf16[5120,640]{1,0:T(8,128)(2,1)} %refs_5_.5) | copy-start | bytes 19660804
  62.1 10.4 %copy-start.19 = (f32[144,128]{1,0:T(8,128)S(1)}, f32[144,128]{1,0:T(8,128)}, u32[]{:S(2)}) copy-start(f32[144,128]{1,0:T(8,128)} %copy-done.18) | copy-start | bytes 221188
  62.1 10.3 %copy-start.21 = (f32[144,128]{1,0:T(8,128)S(1)}, f32[144,128]{1,0:T(8,128)}, u32[]{:S(2)}) copy-start(f32[144,128]{1,0:T(8,128)} %copy-done.20) | copy-start | bytes 221188
  62.1 10.3 %copy-start.22 = (f32[640]{0:T(1024)S(1)}, f32[640]{0:T(1024)}, u32[]{:S(2)}) copy-start(f32[640]{0:T(1024)} %qg.1) | copy-start | bytes 7684
  62.2 10.3 %copy-start.23 = (f32[640]{0:T(1024)S(1)}, f32[640]{0:T(1024)}, u32[]{:S(2)}) copy-start(f32[640]{0:T(1024)} %kg.1) | copy-start | bytes 7684
  67.8 3.8 %collective-permute-start.12 = (f32[8,384]{1,0:T(8,128)S(1)}, f32[8,384]{1,0:T(8,128)S(1)}, u32[]{:S(2)}, u32[]{:S(2)}) collective-permute-start(f32[8,384]{1,0:T(8,128)S(1)} %get-tuple-element.73.s0), channel_id=1, source_target_pairs={{0,2},{1,3},{2,0},{3,1},{4,6},{5,7},{6,4},{7,5},{8,10},{33,35},{10... | collective-permute-start | bytes 36872 | tf_op jit(solution)/shard_map/ppermute | solution.py:67
  69.4 3.1 %collective-permute-start.13 = (f32[8,384]{1,0:T(8,128)S(1)}, f32[8,384]{1,0:T(8,128)S(1)}, u32[]{:S(2)}, u32[]{:S(2)}) collective-permute-start(f32[8,384]{1,0:T(8,128)S(1)} %get-tuple-element.73.s0), channel_id=1, source_target_pairs={{0,3},{1,2},{2,1},{3,0},{4,7},{5,6},{6,5},{7,4},{8,11},{33,34},{10... | collective-permute-start | bytes 36872 | tf_op jit(solution)/shard_map/ppermute | solution.py:67
  69.4 3.1 %collective-permute-start.14 = (f32[8,384]{1,0:T(8,128)S(1)}, f32[8,384]{1,0:T(8,128)S(1)}, u32[]{:S(2)}, u32[]{:S(2)}) collective-permute-start(f32[8,384]{1,0:T(8,128)S(1)} %get-tuple-element.73.s0), channel_id=1, source_target_pairs={{0,1},{1,0},{2,3},{3,2},{4,5},{5,4},{6,7},{7,6},{8,9},{33,32},{10,... | collective-permute-start | bytes 36872 | tf_op jit(solution)/shard_map/ppermute | solution.py:67
  74.3 6.2 %collective-permute-start.16 = (bf16[2,144,128]{2,1,0:T(8,128)(2,1)S(1)}, bf16[2,144,128]{2,1,0:T(8,128)(2,1)S(1)}, u32[]{:S(2)}, u32[]{:S(2)}) collective-permute-start(bf16[2,144,128]{2,1,0:T(8,128)(2,1)S(1)} %get-tuple-element.81.refs_3_), channel_id=1, source_target_pairs={{0,96},{1,25},{2,98},{3,27},{4,100},{5,29},{6,102},{7,31},{8,104},... | collective-permute-start | bytes 221192 | tf_op jit(solution)/shard_map/ppermute | solution.py:67
  74.9 7.2 %collective-permute-start.17 = (bf16[2,144,128]{2,1,0:T(8,128)(2,1)S(1)}, bf16[2,144,128]{2,1,0:T(8,128)(2,1)S(1)}, u32[]{:S(2)}, u32[]{:S(2)}) collective-permute-start(bf16[2,144,128]{2,1,0:T(8,128)(2,1)S(1)} %get-tuple-element.80.refs_2_), channel_id=1, source_target_pairs={{0,64},{1,17},{2,66},{3,19},{4,68},{5,21},{6,70},{7,23},{8,72},{33... | collective-permute-start | bytes 221192 | tf_op jit(solution)/shard_map/ppermute | solution.py:67
  75.5 8.8 %collective-permute-start.18 = (bf16[2,144,128]{2,1,0:T(8,128)(2,1)S(1)}, bf16[2,144,128]{2,1,0:T(8,128)(2,1)S(1)}, u32[]{:S(2)}, u32[]{:S(2)}) collective-permute-start(bf16[2,144,128]{2,1,0:T(8,128)(2,1)S(1)} %get-tuple-element.79.refs_1_), channel_id=1, source_target_pairs={{0,32},{1,9},{2,34},{3,11},{4,36},{5,13},{6,38},{7,15},{8,40},{33,... | collective-permute-start | bytes 221192 | tf_op jit(solution)/shard_map/ppermute | solution.py:67
  76.8 9.6 %collective-permute-start.19 = (bf16[2,144,128]{2,1,0:T(8,128)(2,1)S(1)}, bf16[2,144,128]{2,1,0:T(8,128)(2,1)S(1)}, u32[]{:S(2)}, u32[]{:S(2)}) collective-permute-start(bf16[2,144,128]{2,1,0:T(8,128)(2,1)S(1)} %get-tuple-element.82.refs_4_), channel_id=1, source_target_pairs={{0,8},{1,33},{2,10},{3,35},{4,12},{5,37},{6,14},{7,39},{8,0},{33,1... | collective-permute-start | bytes 221192 | tf_op jit(solution)/shard_map/ppermute | solution.py:67
  76.8 9.6 %collective-permute-start.20 = (bf16[2,144,128]{2,1,0:T(8,128)(2,1)S(1)}, bf16[2,144,128]{2,1,0:T(8,128)(2,1)S(1)}, u32[]{:S(2)}, u32[]{:S(2)}) collective-permute-start(bf16[2,144,128]{2,1,0:T(8,128)(2,1)S(1)} %get-tuple-element.85.refs_7_), channel_id=1, source_target_pairs={{0,104},{1,57},{2,106},{3,59},{4,108},{5,61},{6,110},{7,63},{8,96}... | collective-permute-start | bytes 221192 | tf_op jit(solution)/shard_map/ppermute | solution.py:67
  80.5 7.1 %collective-permute-start.21 = (bf16[2,144,128]{2,1,0:T(8,128)(2,1)S(1)}, bf16[2,144,128]{2,1,0:T(8,128)(2,1)S(1)}, u32[]{:S(2)}, u32[]{:S(2)}) collective-permute-start(bf16[2,144,128]{2,1,0:T(8,128)(2,1)S(1)} %get-tuple-element.84.refs_6_), channel_id=1, source_target_pairs={{0,72},{1,49},{2,74},{3,51},{4,76},{5,53},{6,78},{7,55},{8,64},{33... | collective-permute-start | bytes 221192 | tf_op jit(solution)/shard_map/ppermute | solution.py:67
  82.0 6.5 %collective-permute-start.22 = (bf16[2,144,128]{2,1,0:T(8,128)(2,1)S(1)}, bf16[2,144,128]{2,1,0:T(8,128)(2,1)S(1)}, u32[]{:S(2)}, u32[]{:S(2)}) collective-permute-start(bf16[2,144,128]{2,1,0:T(8,128)(2,1)S(1)} %get-tuple-element.83.refs_5_), channel_id=1, source_target_pairs={{0,40},{1,41},{2,42},{3,43},{4,44},{5,45},{6,46},{7,47},{8,32},{33... | collective-permute-start | bytes 221192 | tf_op jit(solution)/shard_map/ppermute | solution.py:67
  84.3 16.5 %collective-permute-start.24 = (bf16[2,720,128]{2,1,0:T(8,128)(2,1)}, bf16[2,720,128]{2,1,0:T(8,128)(2,1)S(1)}, u32[]{:S(2)}, u32[]{:S(2)}) collective-permute-start(bf16[2,720,128]{2,1,0:T(8,128)(2,1)} %collective-permute-done.23.refs_8_), channel_id=1, source_target_pairs={{0,24},{1,97},{2,26},{3,99},{4,28},{5,101},{6,30},{7,103},{8,16},{... | collective-permute-start | bytes 1105928 | tf_op jit(solution)/shard_map/ppermute | solution.py:67
  88.5 12.3 %collective-permute-start.25 = (bf16[2,720,128]{2,1,0:T(8,128)(2,1)}, bf16[2,720,128]{2,1,0:T(8,128)(2,1)S(1)}, u32[]{:S(2)}, u32[]{:S(2)}) collective-permute-start(bf16[2,720,128]{2,1,0:T(8,128)(2,1)} %collective-permute-done.15.refs_9_), channel_id=1, source_target_pairs={{0,24},{1,97},{2,26},{3,99},{4,28},{5,101},{6,30},{7,103},{8,16},{... | collective-permute-start | bytes 1105928 | tf_op jit(solution)/shard_map/ppermute | solution.py:67
  108.8 6.4 %collective-permute-start.26 = (bf16[304,128]{1,0:T(8,128)(2,1)S(1)}, bf16[304,128]{1,0:T(8,128)(2,1)S(1)}, u32[]{:S(2)}, u32[]{:S(2)}) collective-permute-start(bf16[304,128]{1,0:T(8,128)(2,1)S(1)} %get-tuple-element.102), channel_id=1, source_target_pairs={{0,96},{1,25},{2,98},{3,27},{4,100},{5,29},{6,102},{7,31},{8,104},... | collective-permute-start | bytes 233480 | tf_op jit(solution)/shard_map/ppermute | solution.py:67
  109.6 6.8 %collective-permute-start.27 = (bf16[304,128]{1,0:T(8,128)(2,1)S(1)}, bf16[304,128]{1,0:T(8,128)(2,1)S(1)}, u32[]{:S(2)}, u32[]{:S(2)}) collective-permute-start(bf16[304,128]{1,0:T(8,128)(2,1)S(1)} %get-tuple-element.103), channel_id=1, source_target_pairs={{0,64},{1,17},{2,66},{3,19},{4,68},{5,21},{6,70},{7,23},{8,72},{33... | collective-permute-start | bytes 233480 | tf_op jit(solution)/shard_map/ppermute | solution.py:67
  110.5 8.3 %collective-permute-start.28 = (bf16[304,128]{1,0:T(8,128)(2,1)S(1)}, bf16[304,128]{1,0:T(8,128)(2,1)S(1)}, u32[]{:S(2)}, u32[]{:S(2)}) collective-permute-start(bf16[304,128]{1,0:T(8,128)(2,1)S(1)} %get-tuple-element.104), channel_id=1, source_target_pairs={{0,32},{1,9},{2,34},{3,11},{4,36},{5,13},{6,38},{7,15},{8,40},{33,... | collective-permute-start | bytes 233480 | tf_op jit(solution)/shard_map/ppermute | solution.py:67
  111.3 7.5 %collective-permute-start.29 = (bf16[304,128]{1,0:T(8,128)(2,1)S(1)}, bf16[304,128]{1,0:T(8,128)(2,1)S(1)}, u32[]{:S(2)}, u32[]{:S(2)}) collective-permute-start(bf16[304,128]{1,0:T(8,128)(2,1)S(1)} %get-tuple-element.105), channel_id=1, source_target_pairs={{0,8},{1,33},{2,10},{3,35},{4,12},{5,37},{6,14},{7,39},{8,0},{33,1... | collective-permute-start | bytes 233480 | tf_op jit(solution)/shard_map/ppermute | solution.py:67
  111.9 6.9 %collective-permute-start.30 = (bf16[304,128]{1,0:T(8,128)(2,1)S(1)}, bf16[304,128]{1,0:T(8,128)(2,1)S(1)}, u32[]{:S(2)}, u32[]{:S(2)}) collective-permute-start(bf16[304,128]{1,0:T(8,128)(2,1)S(1)} %get-tuple-element.106), channel_id=1, source_target_pairs={{0,104},{1,57},{2,106},{3,59},{4,108},{5,61},{6,110},{7,63},{8,96}... | collective-permute-start | bytes 233480 | tf_op jit(solution)/shard_map/ppermute | solution.py:67
  115.2 6.8 %collective-permute-start.31 = (bf16[304,128]{1,0:T(8,128)(2,1)S(1)}, bf16[304,128]{1,0:T(8,128)(2,1)S(1)}, u32[]{:S(2)}, u32[]{:S(2)}) collective-permute-start(bf16[304,128]{1,0:T(8,128)(2,1)S(1)} %get-tuple-element.107), channel_id=1, source_target_pairs={{0,72},{1,49},{2,74},{3,51},{4,76},{5,53},{6,78},{7,55},{8,64},{33... | collective-permute-start | bytes 233480 | tf_op jit(solution)/shard_map/ppermute | solution.py:67
  116.5 6.5 %collective-permute-start.32 = (bf16[304,128]{1,0:T(8,128)(2,1)S(1)}, bf16[304,128]{1,0:T(8,128)(2,1)S(1)}, u32[]{:S(2)}, u32[]{:S(2)}) collective-permute-start(bf16[304,128]{1,0:T(8,128)(2,1)S(1)} %get-tuple-element.108), channel_id=1, source_target_pairs={{0,40},{1,41},{2,42},{3,43},{4,44},{5,45},{6,46},{7,47},{8,32},{33... | collective-permute-start | bytes 233480 | tf_op jit(solution)/shard_map/ppermute | solution.py:67
  (11 other events, 8.9 us)

commit v3 on v2

v3 whole, which is shorter than its diff:
```python
import functools
import math

import jax
import jax.numpy as jnp
import numpy as np
from jax import lax
from jax.experimental import pallas as pl
from jax.experimental.pallas import tpu as pltpu
from jax.sharding import PartitionSpec as P

D = 5120
HEADS = 20
HD = 128
FRAMES = 3
GRID_W = 48
EPS = 1e-06
MASKED = -1e30
NY, NX, NZ = 4, 4, 2
TP = 4
N_PATCH = NY * NX * NZ
TOK = 144
B = 2
ROWS = B * TOK
LOCAL_HEADS = 5
WIDTH = LOCAL_HEADS * HD
CHUNK = D // TP
STAT_LANES = 384
PIECE = 5 * TOK
MSG_ROWS = 2 * TOK + 16
SCORE_SCALE = math.log2(math.e) / math.sqrt(HD)
F32 = jnp.float32
BF16 = jnp.bfloat16
AXES = ("patch", "tp")
VMEM_MIB = 40


def params(mib):
    return pltpu.CompilerParams(vmem_limit_bytes=mib * 1024 * 1024)


def vmem():
    return pl.BlockSpec(memory_space=pltpu.VMEM)


def smem():
    return pl.BlockSpec(memory_space=pltpu.SMEM)


def linear(u, v, z_hi, z_lo, core):
    y, x = (u, v) if core == 0 else (v, u)
    return ((y * NX + x) * NZ + z_hi) * TP + z_lo * 2 + core


def places():
    return [
        (u, v, h, l, c)
        for u in range(4)
        for v in range(4)
        for h in range(2)
        for l in range(2)
        for c in range(2)
    ]


def permute(value, move):
    return lax.ppermute(value, AXES, [(linear(*p), linear(*move(*p))) for p in places()])


def shift_u(value, k):
    return permute(value, lambda u, v, h, l, c: ((u + k) % 4, v, h, l, c))


def shift_v(value, k):
    return permute(value, lambda u, v, h, l, c: (u, (v + k) % 4, h, l, c))


def swap_z_hi(value):
    return permute(value, lambda u, v, h, l, c: (u, v, 1 - h, l, c))


def swap_tp(value, z, core):
    if core:
        return permute(value, lambda u, v, h, l, c: (v, u, h, l ^ z, 1 - c))
    return permute(value, lambda u, v, h, l, c: (u, v, h, l ^ z, c))


def frequencies():
    half_dim = HD // 2
    third_dim = half_dim // 3
    frame_pairs = half_dim - 2 * third_dim
    pair = np.arange(HD) // 2
    offset = np.where(
        pair < frame_pairs,
        pair,
        np.where(pair < frame_pairs + third_dim, pair - frame_pairs, pair - frame_pairs - third_dim),
    )
    width = np.where(pair < frame_pairs, 2 * frame_pairs, 2 * third_dim)
    return np.exp(-math.log(10000.0) * 2.0 * offset / width).astype(np.float32).reshape(1, HD)


def columns_to_rows(first, second):
    lane = lax.broadcasted_iota(jnp.int32, (ROWS, 128), 1)
    both = jnp.where(lane == 0, first, jnp.where(lane == 1, second, 0.0))
    padded = jnp.concatenate([both, jnp.zeros((STAT_LANES - ROWS, 128), F32)], axis=0)
    return padded.T[0:8]


def row_to_column(row):
    return jnp.broadcast_to(row, (128, STAT_LANES)).T[0:ROWS]


def pack_kernel(u_ref, key_ref, value_ref, *outs):
    for k in range(5):
        head = lax.rem(u_ref[0] + k, 4) if k < 4 else 4
        cols = pl.ds(pl.multiple_of(head * HD, HD), HD)
        for n, source in enumerate((key_ref, value_ref)):
            for s in range(B):
                outs[k][s, n] = source[s, :, cols]


def pack_stale(u, stale_keys, stale_values):
    return pl.pallas_call(
        pack_kernel,
        out_shape=[jax.ShapeDtypeStruct((B, 2, TOK, HD), BF16)] * 5,
        in_specs=[smem(), vmem(), vmem()],
        out_specs=[vmem()] * 5,
        compiler_params=params(VMEM_MIB),
        cost_estimate=pl.CostEstimate(
            flops=0, bytes_accessed=8 * ROWS * WIDTH, transcendentals=0
        ),
        name="pack_stale",
    )(u, stale_keys, stale_values)


def tables_kernel(place_hbm, freq, after, cond, cos, sin, places_s, place_ref, sem):
    copy = pltpu.make_async_copy(place_hbm, place_ref, sem.at[0])
    copy.start()
    copy.wait()
    for row in range(TOK):
        places_s[row : row + 1] = jnp.full((1, HD), place_ref[row], jnp.int32)
    place = places_s[...]
    frame_tok = TOK * N_PATCH // FRAMES
    frame = jnp.where(place >= frame_tok, 1, 0) + jnp.where(place >= 2 * frame_tok, 1, 0)
    within = place - frame * frame_tok
    grid_row = ((within.astype(F32) + 0.5) * (1.0 / GRID_W)).astype(jnp.int32)
    grid_col = within - grid_row * GRID_W
    lane = lax.broadcasted_iota(jnp.int32, (TOK, HD), 1)
    third = 2 * (HD // 6)
    frame_lanes = HD - 2 * third
    position = jnp.where(
        lane < frame_lanes, frame, jnp.where(lane < frame_lanes + third, grid_row, grid_col)
    )
    angles = position.astype(F32) * freq[...]
    cos[...] = jnp.cos(angles)
    sine = jnp.sin(angles)
    sin[...] = jnp.where(lane % 2 == 0, -sine, sine)
    flag = jnp.where((frame == 0) | (frame == FRAMES - 1), 1.0, 0.0)
    cond[0:TOK] = flag
    cond[TOK:ROWS] = flag


def tables(token_place, after):
    table = jax.ShapeDtypeStruct((TOK, HD), F32)
    return pl.pallas_call(
        tables_kernel,
        out_shape=[jax.ShapeDtypeStruct((ROWS, HD), F32), table, table],
        in_specs=[
            pl.BlockSpec(memory_space=pltpu.HBM),
            vmem(),
            pl.BlockSpec(memory_space=pl.ANY),
        ],
        out_specs=[vmem()] * 3,
        scratch_shapes=[
            pltpu.VMEM((TOK, HD), jnp.int32),
            pltpu.SMEM((TOK,), jnp.int32),
            pltpu.SemaphoreType.DMA((1,)),
        ],
        compiler_params=params(VMEM_MIB),
        cost_estimate=pl.CostEstimate(
            flops=100 * TOK * HD, bytes_accessed=16 * TOK * HD, transcendentals=0
        ),
        name="tables",
    )(token_place, jnp.asarray(frequencies()), after)


def assemble_kernel(*refs):
    parts, out = refs[0:5], refs[5]
    for s in range(B):
        for n in range(2):
            for r in range(5):
                out[s, n, r * TOK : (r + 1) * TOK] = parts[r][s, n]


def assemble(parts):
    return pl.pallas_call(
        assemble_kernel,
        out_shape=jax.ShapeDtypeStruct((B, 2, PIECE, HD), BF16),
        in_specs=[vmem()] * 5,
        out_specs=vmem(),
        compiler_params=params(VMEM_MIB),
        cost_estimate=pl.CostEstimate(
            flops=0, bytes_accessed=16 * PIECE * HD, transcendentals=0
        ),
        name="assemble",
    )(*parts)


def modulate_kernel(t_ref, h0, h1, h2, h3, cond, shift, scale, out_ref):
    chunks = (h0, h1, h2, h3)
    total = jnp.zeros((ROWS, 1), F32)
    for chunk in chunks:
        total = total + jnp.sum(chunk[...].astype(F32), axis=1, keepdims=True)
    mean = total * (1.0 / D)
    deviation = jnp.zeros((ROWS, 1), F32)
    for chunk in chunks:
        centered = chunk[...].astype(F32) - mean
        deviation = deviation + jnp.sum(centered * centered, axis=1, keepdims=True)
    rstd = lax.rsqrt(deviation * (1.0 / D) + EPS)
    conditioned = cond[:, 0:1] > 0.5
    for c in range(TP):
        cols = pl.ds(pl.multiple_of(t_ref[c] * CHUNK, CHUNK), CHUNK)
        part = chunks[c][...].astype(F32)
        gain = jnp.where(conditioned, scale[1:2, cols], scale[0:1, cols])
        bias = jnp.where(conditioned, shift[1:2, cols], shift[0:1, cols])
        out_ref[:, cols] = ((part - mean) * rstd * (1.0 + gain) + bias).astype(BF16)


def modulate(blocks, chunks, cond, shift, scale):
    return pl.pallas_call(
        modulate_kernel,
        out_shape=jax.ShapeDtypeStruct((ROWS, D), BF16),
        in_specs=[smem()] + [vmem()] * 7,
        out_specs=vmem(),
        compiler_params=params(VMEM_MIB),
        cost_estimate=pl.CostEstimate(
            flops=12 * ROWS * D, bytes_accessed=4 * ROWS * D, transcendentals=0
        ),
        name="modulate",
    )(blocks, *chunks, cond, shift, scale)


def squares_kernel(q_ref, k_ref, out_ref):
    query, key = q_ref[...], k_ref[...]
    out_ref[...] = columns_to_rows(
        jnp.sum(query * query, axis=1, keepdims=True),
        jnp.sum(key * key, axis=1, keepdims=True),
    )


def sum_squares(query, key):
    return pl.pallas_call(
        squares_kernel,
        out_shape=jax.ShapeDtypeStruct((8, STAT_LANES), F32),
        in_specs=[vmem()] * 2,
        out_specs=vmem(),
        compiler_params=params(VMEM_MIB),
        cost_estimate=pl.CostEstimate(
            flops=4 * ROWS * WIDTH, bytes_accessed=8 * ROWS * WIDTH, transcendentals=0
        ),
        name="sum_squares",
    )(query, key)


def rope_kernel(u_ref, q_ref, k_ref, s0, s1, s2, s3, qg, kg, cos, sin, k_all, *refs):
    sends, q_rot = refs[0:4], refs[4]
    total = s0[...] + s1[...] + s2[...] + s3[...]
    inverse = lax.rsqrt(total * (1.0 / (HEADS * HD)) + EPS)
    even = lax.broadcasted_iota(jnp.int32, (ROWS, HD), 1) % 2 == 0
    cos_rows = jnp.concatenate([cos[...], cos[...]], axis=0)
    sin_rows = jnp.concatenate([sin[...], sin[...]], axis=0)

    def rotate(ref, column, gain, cols):
        part = ref[:, cols] * column * gain[cols].reshape(1, HD)
        swap = jnp.where(even, pltpu.roll(part, HD - 1, 1), pltpu.roll(part, 1, 1))
        return (part * cos_rows + swap * sin_rows).astype(BF16)

    q_column = row_to_column(inverse[0:1])
    k_column = row_to_column(inverse[1:2])
    for head in range(LOCAL_HEADS):
        cols = slice(head * HD, (head + 1) * HD)
        query = rotate(q_ref, q_column, qg, cols)
        for s in range(B):
            q_rot[head, s] = query[s * TOK : (s + 1) * TOK]
        k_all[:, cols] = rotate(k_ref, k_column, kg, cols)
    for k in range(4):
        for s in range(B):
            sends[k][s, 0] = q_rot[lax.rem(u_ref[0] + k, 4), s]
            sends[k][s, 1] = q_rot[4, s]


def norm_rope(u, query, key, squares, q_gain, k_gain, cos, sin):
    send = jax.ShapeDtypeStruct((B, 2, TOK, HD), BF16)
    flat = jax.ShapeDtypeStruct((ROWS, WIDTH), BF16)
    return pl.pallas_call(
        rope_kernel,
        out_shape=[flat] + [send] * 4,
        in_specs=[smem()] + [vmem()] * 10,
        out_specs=[vmem()] * 5,
        scratch_shapes=[pltpu.VMEM((LOCAL_HEADS, B, TOK, HD), BF16)],
        compiler_params=params(VMEM_MIB),
        cost_estimate=pl.CostEstimate(
            flops=20 * ROWS * WIDTH, bytes_accessed=16 * ROWS * WIDTH, transcendentals=0
        ),
        name="norm_rope",
    )(u, query, key, *squares, q_gain, k_gain, cos, sin)


def scores_of(query, keys):
    return lax.dot_general(query, keys, (((1,), (1,)), ((), ())), preferred_element_type=F32)


def to_rows(blocks):
    lane = lax.broadcasted_iota(jnp.int32, (HD, HD), 1)
    table = jnp.zeros((HD, HD), F32)
    empty = jnp.zeros((2 * HD - TOK, HD), F32)
    for n, block in enumerate(blocks):
        rest = jnp.concatenate([block[HD:TOK], empty], axis=0)
        table = jnp.where(lane == 2 * n, block[0:HD], table)
        table = jnp.where(lane == 2 * n + 1, rest, table)
    return table.T


FRESH_ROWS = 24


def fresh_kernel(u_ref, k_ref, v_ref, *refs):
    queries, (out_ref, rows_ref) = refs[0:4], refs[4:6]
    lses = []
    for s in range(B):
        rows = slice(s * TOK, (s + 1) * TOK)
        for k in range(LOCAL_HEADS):
            head = lax.rem(u_ref[0] + k, 4) if k < 4 else 4
            cols = pl.ds(pl.multiple_of(head * HD, HD), HD)
            query = queries[k][s, 0] if k < 4 else queries[0][s, 1]
            scores = scores_of(query, k_ref[rows, cols])
            top = jnp.max(scores, axis=1, keepdims=True)
            probs = jnp.exp2((scores - top) * SCORE_SCALE)
            total = jnp.sum(probs, axis=1, keepdims=True)
            out = jnp.dot(probs.astype(BF16), v_ref[rows, cols], preferred_element_type=F32)
            out_ref[s, k] = out / total
            lses.append(jnp.broadcast_to(top * SCORE_SCALE + jnp.log2(total), (TOK, HD)))
    rows_ref[...] = to_rows(lses)[0:FRESH_ROWS]


def fresh_attention(u, key, value, queries):
    return pl.pallas_call(
        fresh_kernel,
        out_shape=[
            jax.ShapeDtypeStruct((B, LOCAL_HEADS, TOK, HD), F32),
            jax.ShapeDtypeStruct((FRESH_ROWS, HD), F32),
        ],
        in_specs=[smem()] + [vmem()] * 6,
        out_specs=[vmem()] * 2,
        compiler_params=params(VMEM_MIB),
        cost_estimate=pl.CostEstimate(
            flops=4 * ROWS * TOK * WIDTH,
            bytes_accessed=14 * ROWS * WIDTH,
            transcendentals=ROWS * TOK * LOCAL_HEADS,
        ),
        name="fresh_attention",
    )(u, key, value, *queries)


TILE = 2 * TOK
GROUP = 16
PER_PIECE = 4 * TOK
KEYS = 4 * PER_PIECE
KEYS_LAST = 4 * TOK
SPLIT = 768


def stale_kernel(far, *refs):
    queries = refs[0:4]
    pieces, rest = refs[4:8], refs[8:]
    if far:
        near_out, near_lse = rest[0:2]
        msgs = rest[3:7]
    else:
        out_ref, lse_ref = rest[0:2]
    lse_s, acc_s, k_main, v_main, k_last, v_last, scores_s, probs_s, sems = rest[-9:]
    copies = ([], [])
    for s in range(B):
        for n in range(4):
            piece = pieces[n].at[s]
            main, last = pl.ds(n * PER_PIECE, PER_PIECE), pl.ds(n * TOK, TOK)
            head, tail = pl.ds(0, PER_PIECE), pl.ds(PER_PIECE, TOK)
            for kind, part, target, rows in (
                (0, head, k_main, main),
                (0, tail, k_last, last),
                (1, head, v_main, main),
                (1, tail, v_last, last),
            ):
                copy = pltpu.make_async_copy(
                    piece.at[kind, part], target.at[s, rows], sems.at[s, len(copies[s])]
                )
                copy.start()
                copies[s].append(copy)

    jobs = [(s, e, tile) for s in range(B) for e in range(2) for tile in range(2)]

    def size(i):
        return KEYS_LAST if jobs[i][1] else KEYS

    def score_steps(i):
        s, e, tile = jobs[i]
        keys = k_last if e else k_main
        out = scores_s.at[i % 2]

        def arrive():
            for copy in copies[s]:
                copy.wait()

        def step(at, end):
            query = jnp.concatenate([queries[2 * tile][s, e], queries[2 * tile + 1][s, e]], axis=0)
            out[:, at:end] = scores_of(query, keys[s, at:end])

        def hide():
            for n in range(2):
                r = 2 * tile + n
                rows = slice(n * TOK, (n + 1) * TOK)
                if e and r:
                    continue
                out[rows, r * TOK : (r + 1) * TOK] = jnp.full((TOK, TOK), MASKED, F32)

        steps = [] if i % 4 else [arrive]
        for at in range(0, size(i), SPLIT):
            steps.append(functools.partial(step, at, min(at + SPLIT, size(i))))
        return steps if far else steps + [hide]

    def softmax_steps(i, tops, totals):
        def step(row):
            rows = slice(row, row + GROUP)
            part = scores_s[i % 2, rows, 0 : size(i)]
            top = jnp.max(part, axis=1, keepdims=True)
            probs = jnp.exp2((part - top) * SCORE_SCALE)
            totals.append(jnp.sum(probs, axis=1, keepdims=True))
            tops.append(top)
            probs_s[i % 2, rows, 0 : size(i)] = probs.astype(BF16)

        return [functools.partial(step, row) for row in range(0, TILE, GROUP)]

    def product_steps(i, tops, totals):
        s, e, tile = jobs[i]
        values = v_last if e else v_main

        def step(at, end):
            part = jnp.dot(
                probs_s[i % 2, :, at:end], values[s, at:end], preferred_element_type=F32
            )
            acc_s[...] = part if at == 0 else acc_s[...] + part

        def finish():
            top, total = jnp.concatenate(tops, axis=0), jnp.concatenate(totals, axis=0)
            out = acc_s[...] / total
            lse = top * SCORE_SCALE + jnp.log2(total)
            for n in range(2):
                r = 2 * tile + n
                half = slice(n * TOK, (n + 1) * TOK)
                if not far:
                    out_ref[s, r, e] = out[half]
                    lse_ref[s, r, e] = jnp.broadcast_to(lse[half], (TOK, HD))
                    continue
                lse_near = near_lse[s, r, e][:, 0:1]
                high = jnp.maximum(lse[half], lse_near)
                weight, weight_near = jnp.exp2(lse[half] - high), jnp.exp2(lse_near - high)
                both = weight + weight_near
                value = (out[half] * weight + near_out[s, r, e] * weight_near) / both
                lse_s[s, r, e] = jnp.broadcast_to(high + jnp.log2(both), (TOK, HD))
                msgs[r][s, e * TOK : (e + 1) * TOK] = value.astype(BF16)

        steps = []
        for at in range(0, size(i), SPLIT):
            steps.append(functools.partial(step, at, min(at + SPLIT, size(i))))
        return steps + [finish]

    def weave(*lists):
        order = []
        for steps in lists:
            order += [((n + 0.5) / len(steps), step) for n, step in enumerate(steps)]
        for _, step in sorted(order, key=lambda entry: entry[0]):
            step()

    weave(score_steps(0))
    pending = None
    for i in range(len(jobs)):
        tops, totals = [], []
        lists = [softmax_steps(i, tops, totals)]
        if i + 1 < len(jobs):
            lists.append(score_steps(i + 1))
        if pending is not None:
            lists.append(pending)
        weave(*lists)
        pending = product_steps(i, tops, totals)
    weave(pending)

    if far:
        order = [(r, s) for r in range(4) for s in range(B)]
        flat = to_rows([lse_s[s, r, e] for r, s in order for e in range(2)])
        for n, (r, s) in enumerate(order):
            part = flat[n * 4 : n * 4 + 4]
            high = part.astype(BF16).astype(F32)
            middle = (part - high).astype(BF16).astype(F32)
            low = part - high - middle
            stack = jnp.concatenate([high, middle, low, jnp.zeros((4, HD), F32)], axis=0)
            msgs[r][s, 2 * TOK : MSG_ROWS] = stack.astype(BF16)


def stale_attention(queries, pieces, near=None, after=None):
    far = near is not None
    args = [*queries, *pieces]
    hbm = pl.BlockSpec(memory_space=pltpu.HBM)
    in_specs = [vmem()] * 4 + [hbm] * len(pieces)
    if far:
        args += [*near, after]
        in_specs += [vmem(), vmem(), pl.BlockSpec(memory_space=pl.ANY)]
        out_shape = [jax.ShapeDtypeStruct((B, MSG_ROWS, HD), BF16)] * 4
    else:
        out_shape = [jax.ShapeDtypeStruct((B, 4, 2, TOK, HD), F32)] * 2
    work = B * 4 * TOK * (KEYS + KEYS_LAST)
    return pl.pallas_call(
        functools.partial(stale_kernel, far),
        out_shape=out_shape,
        in_specs=in_specs,
        out_specs=[vmem()] * len(out_shape),
        scratch_shapes=[
            pltpu.VMEM((B, 4, 2, TOK, HD), F32),
            pltpu.VMEM((TILE, HD), F32),
            pltpu.VMEM((B, KEYS, HD), BF16),
            pltpu.VMEM((B, KEYS, HD), BF16),
            pltpu.VMEM((B, KEYS_LAST, HD), BF16),
            pltpu.VMEM((B, KEYS_LAST, HD), BF16),
            pltpu.VMEM((2, TILE, KEYS), F32),
            pltpu.VMEM((2, TILE, KEYS), BF16),
            pltpu.SemaphoreType.DMA((B, 16)),
        ],
        compiler_params=params(VMEM_MIB),
        cost_estimate=pl.CostEstimate(
            flops=4 * work * HD, bytes_accessed=8 * (KEYS + KEYS_LAST) * HD, transcendentals=work
        ),
        name="far_attention" if far else "near_attention",
    )(*args)


def merge_kernel(u_ref, fresh_out, fresh_rows, *refs):
    msgs, out_ref = refs[0:4], refs[4]
    lses = {}
    for k in range(4):
        for s in range(B):
            stack = msgs[k][s, 2 * TOK : MSG_ROWS].astype(F32)
            lses[s, k] = stack[0:4] + stack[4:8] + stack[8:12]
    weights, jobs = [], []
    for s in range(B):
        for k in range(LOCAL_HEADS):
            at = (s * LOCAL_HEADS + k) * 2
            parts = [(None, fresh_rows[at : at + 2])]
            if k < 4:
                parts.append((k, lses[s, k][0:2]))
            else:
                parts += [(n, lses[s, n][2:4]) for n in range(4)]
            top = parts[0][1]
            for _, lse in parts[1:]:
                top = jnp.maximum(top, lse)
            raw = [jnp.exp2(lse - top) for _, lse in parts]
            total = sum(raw[1:], raw[0])
            jobs.append((s, k, [(source, len(weights) + n) for n, (source, _) in enumerate(parts)]))
            weights += [one / total for one in raw]
    filler = jnp.zeros((HD - 2 * len(weights), HD), F32)
    table = jnp.concatenate(weights + [filler], axis=0).T
    for s, k, parts in jobs:
        head = lax.rem(u_ref[0] + k, 4) if k < 4 else 4
        out = [None, None]
        for source, n in parts:
            for half, rows in enumerate((slice(0, HD), slice(HD, TOK))):
                if source is None:
                    value = fresh_out[s, k, rows]
                else:
                    at = 0 if k < 4 else TOK
                    value = msgs[source][s, at + rows.start : at + rows.stop].astype(F32)
                column = table[0 : rows.stop - rows.start, 2 * n + half : 2 * n + half + 1]
                term = value * column
                out[half] = term if out[half] is None else out[half] + term
        cols = pl.ds(pl.multiple_of(head * HD, HD), HD)
        out_ref[s, :, cols] = jnp.concatenate(out, axis=0).astype(BF16)


def merge(u, fresh_out, fresh_rows, msgs):
    return pl.pallas_call(
        merge_kernel,
        out_shape=jax.ShapeDtypeStruct((B, TOK, WIDTH), BF16),
        in_specs=[smem()] + [vmem()] * 6,
        out_specs=vmem(),
        compiler_params=params(VMEM_MIB),
        cost_estimate=pl.CostEstimate(
            flops=10 * ROWS * WIDTH, bytes_accessed=14 * ROWS * WIDTH, transcendentals=0
        ),
        name="merge",
    )(u, fresh_out, fresh_rows, *msgs)


def gather_v(piece):
    return [piece, shift_v(piece, 3), shift_v(piece, 1), shift_v(piece, 2)]


def shards(
    hidden,
    mod_shift,
    mod_scale,
    w_query,
    w_key,
    w_value,
    q_gain,
    k_gain,
    token_place,
    stale_keys,
    stale_values,
):
    patch = lax.axis_index("patch")
    tp = lax.axis_index("tp")
    y = patch // (NX * NZ)
    x = (patch // NZ) % NX
    u = jnp.where(tp % 2 == 0, y, x).astype(jnp.int32).reshape(1)
    own_rows = hidden.reshape(ROWS, CHUNK)
    z_rows = swap_tp(own_rows, 1, 0)
    core_rows = swap_tp(own_rows, 0, 1)

    packed = pack_stale(u, stale_keys, stale_values)
    arrived = [packed[0]] + [shift_u(packed[4 - r], 4 - r) for r in range(1, 4)]
    near = assemble([*arrived, packed[4]])
    near_all = gather_v(near)
    far = swap_z_hi(near)
    cond, cos, sin = tables(token_place, near)

    z_rows, cond = lax.optimization_barrier((z_rows, cond))
    cross_rows = swap_tp(z_rows, 0, 1)
    blocks = jnp.stack([tp, tp ^ 1, tp ^ 2, tp ^ 3]).astype(jnp.int32)
    rows = [own_rows, core_rows, z_rows, cross_rows]
    modded = modulate(blocks, rows, cond, mod_shift, mod_scale)
    query = jnp.dot(modded, w_query, preferred_element_type=F32)
    key = jnp.dot(modded, w_key, preferred_element_type=F32)
    fresh_values = jnp.dot(modded, w_value, preferred_element_type=F32).astype(BF16)
    own_sq = sum_squares(query, key)
    own_sq, *near_all = lax.optimization_barrier((own_sq, *near_all))
    squares = [own_sq] + [swap_tp(own_sq, z, c) for z, c in ((1, 0), (1, 1), (0, 1))]
    fresh_keys, *sends = norm_rope(u, query, key, squares, q_gain, k_gain, cos, sin)
    queries = [sends[0]] + [shift_u(sends[4 - r], 4 - r) for r in (1, 3, 2)]
    queries = [queries[0], queries[1], queries[3], queries[2]]
    fresh_out, fresh_rows = fresh_attention(u, fresh_keys, fresh_values, sends)

    far, fresh_rows, *queries = lax.optimization_barrier((far, fresh_rows, *queries))
    far_all = gather_v(far)
    partial = stale_attention(queries, near_all)
    outs = stale_attention(queries, far_all, near=partial, after=fresh_rows)
    returned = [outs[0]] + [shift_u(outs[4 - k], 4 - k) for k in range(1, 4)]
    attended = merge(u, fresh_out, fresh_rows, returned)
    return (
        attended,
        fresh_keys.reshape(B, TOK, WIDTH),
        fresh_values.reshape(B, TOK, WIDTH),
    )


def solution(mesh):
    in_specs = (
        P(None, "patch", "tp"),
        P(),
        P(),
        P(None, "tp"),
        P(None, "tp"),
        P(None, "tp"),
        P("tp"),
        P("tp"),
        P("patch"),
        P(None, "patch", "tp"),
        P(None, "patch", "tp"),
    )
    out_specs = (P(None, "patch", "tp"), P(None, "patch", "tp"), P(None, "patch", "tp"))
    return jax.shard_map(shards, mesh=mesh, in_specs=in_specs, out_specs=out_specs, check_vma=False)
```

time: 125 us -> 105 us (0.84)
  starting transfers between devices: 42.6 us -> 29.3 us
  matrix products: 0 us -> 10.6 us
  Pallas kernels: 40.6 us -> 30.4 us
  local copies, waits for them, and re-layouts: 15.8 us -> 6.02 us
  waiting for transfers between devices: 24.5 us -> 27.1 us
    ppermute x33 -> x22, starting transfers between devices: 42.6 us -> 29.3 us  [permute(): lax.ppermute(value, AXES, [(linear(*p), linear(*move(*p))) for p in place...]
    dot_general x0 -> x3, matrix products: none -> 10.6 us  [the longest x1 5.54 us: shards(): query = jnp.dot(modded, w_query, preferred_element_type=F32)]
    pallas_call x8 -> x6, Pallas kernels: 36.7 us -> 26.7 us  [the longest x2 20.2 us: stale_attention(): pl.pallas_call(functools.partial(stale_kernel, far), out_shape=out_shape,...]
    unnamed x52 -> x30, local copies, waits for them, and re-layouts: 15.8 us -> 6.02 us
    ppermute x33 -> x22, waiting for transfers between devices: 24.5 us -> 27.1 us  [permute(): lax.ppermute(value, AXES, [(linear(*p), linear(*move(*p))) for p in place...]
  transfers between devices with their start and end apart: 33 -> 22, of which waited for: 13 -> 12; matrix products, arithmetic and copies ran while one was open for 0% -> 10% of each run, Pallas kernels for 24% -> 18%
where the time goes in v3:
time: 105 us; the launch traced here: 104 us
  Pallas kernels  30.4 us (29%)
  starting transfers between devices  29.3 us (28%)
  waiting for transfers between devices  27.1 us (26%)
  matrix products  10.6 us (10%)
  local copies, waits for them, and re-layouts  6.02 us (6%)
    ppermute x22, starting transfers between devices, permute(): lax.ppermute(value, AXES, [(linear(*p), linear(*move(*p))) for p in place...  29.3 us
    ppermute x22, waiting for transfers between devices, permute(): lax.ppermute(value, AXES, [(linear(*p), linear(*move(*p))) for p in place...  27.1 us
    pallas_call x2, Pallas kernels, stale_attention(): pl.pallas_call(functools.partial(stale_kernel, far), out_shape=out_shape,...  20.2 us
    unnamed x30, local copies, waits for them, and re-layouts  6.02 us
    dot_general x1, matrix products, shards(): query = jnp.dot(modded, w_query, preferred_element_type=F32)  5.54 us
    pallas_call x1, Pallas kernels, modulate(): pl.pallas_call(modulate_kernel, out_shape=jax.ShapeDtypeStruct((ROWS, D),...  4.44 us
    dot_general x1, matrix products, shards(): jnp.dot(modded, w_value, preferred_element_type=F32).astype(BF16)  2.55 us
    dot_general x1, matrix products, shards(): key = jnp.dot(modded, w_key, preferred_element_type=F32)  2.54 us
  transfers between devices with their start and end apart: 22, of which 12 were waited for; matrix products, arithmetic and copies ran while one was open for 10% of the time, Pallas kernels for 18%

profile of v3, /device:TPU:0, one launch (start us, length us, event | category | flops | bytes accessed | tf_op | source)
XLA Modules:
  0.0 104.4 jit_solution(1815453137642579488)
XLA Ops:
  0.6 2.1 %collective-permute-start.1 = (bf16[288,1280]{1,0:T(8,128)(2,1)}, bf16[288,1280]{1,0:T(8,128)(2,1)S(1)}, u32[]{:S(2)}, u32[]{:S(2)}) collective-permute-start(bf16[288,1280]{1,0:T(8,128)(2,1)} %bitcast.14), channel_id=1, source_target_pairs={{0,2},{1,3},{2,0},{3,1},{4,6},{5,7},{6,4},{7,5},{8,10},{33,35},{10... | collective-permute-start | bytes 2211848 | tf_op jit(solution)/shard_map/ppermute | solution.py:67
  2.7 1.0 copy-done.1
  3.7 1.0 copy-done.2
  4.8 3.1 %collective-permute-start.2 = (bf16[2,2,144,128]{3,2,1,0:T(8,128)(2,1)S(1)}, bf16[2,2,144,128]{3,2,1,0:T(8,128)(2,1)S(1)}, u32[]{:S(2)}, u32[]{:S(2)}) collective-permute-start(bf16[2,2,144,128]{3,2,1,0:T(8,128)(2,1)S(1)} %get-tuple-element.38), channel_id=1, source_target_pairs={{0,96},{1,25},{2,98},{3,27},{4,100},{5,29},{6,102},{7,31},{8,104},... | collective-permute-start | bytes 442376 | tf_op jit(solution)/shard_map/ppermute | solution.py:67
  7.9 0.6 collective-permute-start.3
  8.5 1.0 collective-permute-start.4
  9.5 2.7 %collective-permute-done.2.refs_1_ = bf16[2,2,144,128]{3,2,1,0:T(8,128)(2,1)S(1)} collective-permute-done((bf16[2,2,144,128]{3,2,1,0:T(8,128)(2,1)S(1)}, bf16[2,2,144,128]{3,2,1,0:T(8,128)(2,1)S(1)}, u32[]{:S(2)}, u32[]{:S(2)}) %collective-permute-start.2) | collective-permute-done | bytes 147488 | tf_op jit(solution)/shard_map/ppermute | solution.py:67
  12.2 2.5 %collective-permute-done.3.refs_2_ = bf16[2,2,144,128]{3,2,1,0:T(8,128)(2,1)S(1)} collective-permute-done((bf16[2,2,144,128]{3,2,1,0:T(8,128)(2,1)S(1)}, bf16[2,2,144,128]{3,2,1,0:T(8,128)(2,1)S(1)}, u32[]{:S(2)}, u32[]{:S(2)}) %collective-permute-start.3) | collective-permute-done | bytes 147488 | tf_op jit(solution)/shard_map/ppermute | solution.py:67
  14.7 1.5 %collective-permute-done.4.refs_3_ = bf16[2,2,144,128]{3,2,1,0:T(8,128)(2,1)S(1)} collective-permute-done((bf16[2,2,144,128]{3,2,1,0:T(8,128)(2,1)S(1)}, bf16[2,2,144,128]{3,2,1,0:T(8,128)(2,1)S(1)}, u32[]{:S(2)}, u32[]{:S(2)}) %collective-permute-start.4) | collective-permute-done | bytes 147488 | tf_op jit(solution)/shard_map/ppermute | solution.py:67
  16.2 0.7 copy-done.9
  16.9 0.7 copy-done.10
  17.5 0.9 tables.1
  18.5 1.0 collective-permute-done.1.h2
  19.5 2.8 %collective-permute-start.6 = (bf16[2,2,720,128]{3,2,1,0:T(8,128)(2,1)S(1)}, bf16[2,2,720,128]{3,2,1,0:T(8,128)(2,1)S(1)}, u32[]{:S(2)}, u32[]{:S(2)}) collective-permute-start(bf16[2,2,720,128]{3,2,1,0:T(8,128)(2,1)S(1)} %assemble.1.after.refs_4_), channel_id=1, source_target_pairs={{0,24},{1,97},{2,26},{3,99},{4,28},{5,101},{6,30},{7,103},{8,0},{3... | collective-permute-start | bytes 2211848 | tf_op jit(solution)/shard_map/ppermute | solution.py:67
  22.3 2.3 %collective-permute-start.8 = (bf16[2,2,720,128]{3,2,1,0:T(8,128)(2,1)S(1)}, bf16[2,2,720,128]{3,2,1,0:T(8,128)(2,1)S(1)}, u32[]{:S(2)}, u32[]{:S(2)}) collective-permute-start(bf16[2,2,720,128]{3,2,1,0:T(8,128)(2,1)S(1)} %assemble.1.after.refs_4_), channel_id=1, source_target_pairs={{0,16},{1,65},{2,18},{3,67},{4,20},{5,69},{6,22},{7,71},{8,24},{33... | collective-permute-start | bytes 2211848 | tf_op jit(solution)/shard_map/ppermute | solution.py:67
  24.6 3.7 %collective-permute-start.12 = (bf16[2,2,720,128]{3,2,1,0:T(8,128)(2,1)S(1)}, bf16[2,2,720,128]{3,2,1,0:T(8,128)(2,1)S(1)}, u32[]{:S(2)}, u32[]{:S(2)}) collective-permute-start(bf16[2,2,720,128]{3,2,1,0:T(8,128)(2,1)S(1)} %assemble.1.after.refs_4_), channel_id=1, source_target_pairs={{0,4},{1,5},{2,6},{3,7},{4,0},{5,1},{6,2},{7,3},{8,12},{33,37},{10... | collective-permute-start | bytes 2211848 | tf_op jit(solution)/shard_map/ppermute | solution.py:67
  28.3 1.1 %copy-done = bf16[2,144,1280]{2,1,0:T(8,128)(2,1)S(1)} copy-done((bf16[2,144,1280]{2,1,0:T(8,128)(2,1)S(1)}, bf16[2,144,1280]{2,1,0:T(8,128)(2,1)}, u32[]{:S(2)}) %copy-start) | copy-done | bytes 737304
  29.4 0.8 copy-done.5
  30.2 0.8 copy-done.6
  30.9 4.4 %modulate.1 = bf16[288,5120]{1,0:T(8,128)(2,1)S(1)} custom-call(s32[4]{0:T(128)S(1)} %pad_add_fusion.t_ref, bf16[288,1280]{1,0:T(8,128)(2,1)S(1)} %bitcast.16, bf16[288,1280]{1,0:T(8,128)(2,1)S(1)} %collective-permute-done.h1, bf16[288,1280]{1,0:T(8,128)(2,1)S(1)} %collective-permute-done.1.h2, bf16[288,1280]{1,0:T(8,128)(2,1)S(1)} %collective-permute-done.5.h3, ...), custom_call_target="tpu_custom_call" | custom-call | flops 17694720 | bytes 5898240 | tf_op jit(solution)/shard_map/modulate/pallas_call | solution.py:230
  35.4 5.5 %fusion.q_ref = f32[288,640]{1,0:T(8,128)S(1)} fusion(bf16[288,5120]{1,0:T(8,128)(2,1)S(1)} %modulate.1, bf16[5120,640]{1,0:T(8,128)(2,1)} %param.15), kind=kOutput, calls=%fused_computation.2 | convolution fusion | flops 1887436800 | bytes 10240000 | tf_op jit(solution)/shard_map/dot_general | solution.py:639
  41.0 2.5 %fusion.1.k_ref = f32[288,640]{1,0:T(8,128)S(1)} fusion(bf16[288,5120]{1,0:T(8,128)(2,1)S(1)} %modulate.1, bf16[5120,640]{1,0:T(8,128)(2,1)S(1)} %bitcast.20), kind=kOutput, calls=%fused_computation.3 | convolution fusion | flops 1887436800 | bytes 10240000 | tf_op jit(solution)/shard_map/dot_general | solution.py:640
  43.8 0.2 collective-permute-start.10
  44.1 1.0 collective-permute-start.11
  45.0 1.0 collective-permute-start.9
  46.0 1.0 collective-permute-done.10.s2
  47.0 1.7 %collective-permute-done.9.s1 = f32[8,384]{1,0:T(8,128)S(1)} collective-permute-done((f32[8,384]{1,0:T(8,128)S(1)}, f32[8,384]{1,0:T(8,128)S(1)}, u32[]{:S(2)}, u32[]{:S(2)}) %collective-permute-start.9) | collective-permute-done | bytes 12320 | tf_op jit(solution)/shard_map/ppermute | solution.py:67
  48.7 1.8 %norm_rope.1 = (bf16[288,640]{1,0:T(8,128)(2,1)}, bf16[2,2,144,128]{3,2,1,0:T(8,128)(2,1)S(1)}, bf16[2,2,144,128]{3,2,1,0:T(8,128)(2,1)S(1)}, bf16[2,2,144,128]{...) custom-call(s32[1]{0:T(128)} %bitcast.u_ref, f32[288,640]{1,0:T(8,128)S(1)} %fusion.q_ref, f32[288,640]{1,0:T(8,128)S(1)} %fusion.1.k_ref, ...), custom_call_target="tpu_custom_call" | custom-call | flops 3686400 | bytes 2949120 | tf_op jit(solution)/shard_map/norm_rope/pallas_call | solution.py:295
  50.5 3.0 %collective-permute-start.13 = (bf16[2,2,144,128]{3,2,1,0:T(8,128)(2,1)S(1)}, bf16[2,2,144,128]{3,2,1,0:T(8,128)(2,1)S(1)}, u32[]{:S(2)}, u32[]{:S(2)}) collective-permute-start(bf16[2,2,144,128]{3,2,1,0:T(8,128)(2,1)S(1)} %get-tuple-element.52.refs_3_), channel_id=1, source_target_pairs={{0,96},{1,25},{2,98},{3,27},{4,100},{5,29},{6,102},{7,31},{8,104},... | collective-permute-start | bytes 442376 | tf_op jit(solution)/shard_map/ppermute | solution.py:67
  53.5 0.6 collective-permute-start.14
  54.2 1.0 collective-permute-start.15
  55.2 2.5 %convolution_convert_fusion.v_ref = bf16[288,640]{1,0:T(8,128)(2,1)S(1)} fusion(bf16[288,5120]{1,0:T(8,128)(2,1)S(1)} %modulate.1, bf16[5120,640]{1,0:T(8,128)(2,1)S(1)} %bitcast.22), kind=kOutput, calls=%fused_computation | convolution fusion | flops 1887621120 | bytes 9871360 | tf_op jit(solution)/shard_map/dot_general | solution.py:641
  57.7 1.0 %fresh_attention.1 = (f32[2,5,144,128]{3,2,1,0:T(8,128)S(1)}, f32[24,128]{1,0:T(8,128)S(1)}) custom-call(s32[1]{0:T(128)} %bitcast.u_ref, bf16[288,640]{1,0:T(8,128)(2,1)S(1)} %copy-done.3, bf16[288,640]{1,0:T(8,128)(2,1)S(1)} %convolution_convert_fusion.v_ref, bf16[2,2,144,128]{3,2,1,0:T(8,128)(2,1)S(1)} %get-tuple-element.56.refs_0_, ...), custom_call_target="tpu_custom_call" | custom-call | flops 106168320 | bytes 2580480 | tf_op jit(solution)/shard_map/fresh_attention/pallas_call | solution.py:347
  58.8 1.5 %collective-permute-done.14.refs_2_ = bf16[2,2,144,128]{3,2,1,0:T(8,128)(2,1)S(1)} collective-permute-done((bf16[2,2,144,128]{3,2,1,0:T(8,128)(2,1)S(1)}, bf16[2,2,144,128]{3,2,1,0:T(8,128)(2,1)S(1)}, u32[]{:S(2)}, u32[]{:S(2)}) %collective-permute-start.14) | collective-permute-done | bytes 147488 | tf_op jit(solution)/shard_map/ppermute | solution.py:67
  60.3 1.5 %collective-permute-done.15.refs_3_ = bf16[2,2,144,128]{3,2,1,0:T(8,128)(2,1)S(1)} collective-permute-done((bf16[2,2,144,128]{3,2,1,0:T(8,128)(2,1)S(1)}, bf16[2,2,144,128]{3,2,1,0:T(8,128)(2,1)S(1)}, u32[]{:S(2)}, u32[]{:S(2)}) %collective-permute-start.15) | collective-permute-done | bytes 147488 | tf_op jit(solution)/shard_map/ppermute | solution.py:67
  61.8 1.1 %collective-permute-start.16 = (bf16[2,2,720,128]{3,2,1,0:T(8,128)(2,1)S(1)}, bf16[2,2,720,128]{3,2,1,0:T(8,128)(2,1)S(1)}, u32[]{:S(2)}, u32[]{:S(2)}) collective-permute-start(bf16[2,2,720,128]{3,2,1,0:T(8,128)(2,1)S(1)} %collective-permute-done.12.refs_4_), channel_id=1, source_target_pairs={{0,24},{1,97},{2,26},{3,99},{4,28},{5,101},{6,30},{7,103},{8,0},{3... | collective-permute-start | bytes 2211848 | tf_op jit(solution)/shard_map/ppermute | solution.py:67
  62.9 0.9 collective-permute-start.17
  63.8 1.8 %collective-permute-start.18 = (bf16[2,2,720,128]{3,2,1,0:T(8,128)(2,1)S(1)}, bf16[2,2,720,128]{3,2,1,0:T(8,128)(2,1)S(1)}, u32[]{:S(2)}, u32[]{:S(2)}) collective-permute-start(bf16[2,2,720,128]{3,2,1,0:T(8,128)(2,1)S(1)} %collective-permute-done.12.refs_4_), channel_id=1, source_target_pairs={{0,16},{1,65},{2,18},{3,67},{4,20},{5,69},{6,22},{7,71},{8,24},{33... | collective-permute-start | bytes 2211848 | tf_op jit(solution)/shard_map/ppermute | solution.py:67
  65.6 9.9 %near_attention.1 = (f32[2,4,2,144,128]{4,3,2,1,0:T(8,128)S(1)}, f32[2,4,2,144,128]{4,3,2,1,0:T(8,128)S(1)}) custom-call(bf16[2,2,144,128]{3,2,1,0:T(8,128)(2,1)S(1)} %get-tuple-element.56.refs_0_, bf16[2,2,144,128]{3,2,1,0:T(8,128)(2,1)S(1)} %collective-permute-done.13.refs_1_, bf16[2,2,144,128]{3,2,1,0:T(8,128)(2,1)S(1)} %collective-permute-done.14.refs_2_, ...), custom_call_target="tpu_custom_call" | custom-call | flops 1698693120 | bytes 2949120 | tf_op jit(solution)/shard_map/near_attention/pallas_call | solution.py:521
  75.6 7.9 %collective-permute-done.17.refs_6_ = bf16[2,2,720,128]{3,2,1,0:T(8,128)(2,1)S(1)} collective-permute-done((bf16[2,2,720,128]{3,2,1,0:T(8,128)(2,1)S(1)}, bf16[2,2,720,128]{3,2,1,0:T(8,128)(2,1)S(1)}, u32[]{:S(2)}, u32[]{:S(2)}) %collective-permute-start.17) | collective-permute-done | bytes 737312 | tf_op jit(solution)/shard_map/ppermute | solution.py:67
  83.5 10.3 %far_attention.1 = (bf16[2,304,128]{2,1,0:T(8,128)(2,1)S(1)}, bf16[2,304,128]{2,1,0:T(8,128)(2,1)S(1)}, bf16[2,304,128]{2,1,0:T(8,128)(2,1)S(1)}, bf16[2,304,128]{2,1,0:T(8,128)(2,1)S(1)}) custom-call(bf16[2,2,144,128]{3,2,1,0:T(8,128)(2,1)S(1)} %get-tuple-element.56.refs_0_, bf16[2,2,144,128]{3,2,1,0:T(8,128)(2,1)S(1)} %collective-permute-done.13.refs_1_, ...), custom_call_target="tpu_custom_call" | custom-call | flops 1698693120 | bytes 2949120 | tf_op jit(solution)/shard_map/far_attention/pallas_call | solution.py:521
  93.8 0.6 collective-permute-start.19
  94.5 1.6 %collective-permute-start.20 = (bf16[2,304,128]{2,1,0:T(8,128)(2,1)S(1)}, bf16[2,304,128]{2,1,0:T(8,128)(2,1)S(1)}, u32[]{:S(2)}, u32[]{:S(2)}) collective-permute-start(bf16[2,304,128]{2,1,0:T(8,128)(2,1)S(1)} %get-tuple-element.69), channel_id=1, source_target_pairs={{0,64},{1,17},{2,66},{3,19},{4,68},{5,21},{6,70},{7,23},{8,72},{33... | collective-permute-start | bytes 466952 | tf_op jit(solution)/shard_map/ppermute | solution.py:67
  96.1 0.9 collective-permute-start.21
  96.9 2.2 %collective-permute-done.19.refs_1_ = bf16[2,304,128]{2,1,0:T(8,128)(2,1)S(1)} collective-permute-done((bf16[2,304,128]{2,1,0:T(8,128)(2,1)S(1)}, bf16[2,304,128]{2,1,0:T(8,128)(2,1)S(1)}, u32[]{:S(2)}, u32[]{:S(2)}) %collective-permute-start.19) | collective-permute-done | bytes 155680 | tf_op jit(solution)/shard_map/ppermute | solution.py:67
  99.1 2.1 %collective-permute-done.20.refs_2_ = bf16[2,304,128]{2,1,0:T(8,128)(2,1)S(1)} collective-permute-done((bf16[2,304,128]{2,1,0:T(8,128)(2,1)S(1)}, bf16[2,304,128]{2,1,0:T(8,128)(2,1)S(1)}, u32[]{:S(2)}, u32[]{:S(2)}) %collective-permute-start.20) | collective-permute-done | bytes 155680 | tf_op jit(solution)/shard_map/ppermute | solution.py:67
  101.2 1.6 %collective-permute-done.21.refs_3_ = bf16[2,304,128]{2,1,0:T(8,128)(2,1)S(1)} collective-permute-done((bf16[2,304,128]{2,1,0:T(8,128)(2,1)S(1)}, bf16[2,304,128]{2,1,0:T(8,128)(2,1)S(1)}, u32[]{:S(2)}, u32[]{:S(2)}) %collective-permute-start.21) | collective-permute-done | bytes 155680 | tf_op jit(solution)/shard_map/ppermute | solution.py:67
  102.9 1.5 %merge.1 = bf16[2,144,640]{2,1,0:T(8,128)(2,1)} custom-call(s32[1]{0:T(128)} %bitcast.u_ref, f32[2,5,144,128]{3,2,1,0:T(8,128)S(1)} %get-tuple-element.53.fresh_out, f32[24,128]{1,0:T(8,128)S(1)} %get-tuple-element.55.refs_10_.fresh_rows, bf16[2,304,128]{2,1,0:T(8,128)(2,1)S(1)} %get-tuple-element.67.refs_0_, ...), custom_call_target="tpu_custom_call" | custom-call | flops 1843200 | bytes 2580480 | tf_op jit(solution)/shard_map/merge/pallas_call | solution.py:588
  (42 shorter events, 0.6 us)
Async XLA Ops:
  0.6 18.8 %collective-permute-start.1 = (bf16[288,1280]{1,0:T(8,128)(2,1)}, bf16[288,1280]{1,0:T(8,128)(2,1)S(1)}, u32[]{:S(2)}, u32[]{:S(2)}) collective-permute-start(bf16[288,1280]{1,0:T(8,128)(2,1)} %bitcast.14), channel_id=1, source_target_pairs={{0,2},{1,3},{2,0},{3,1},{4,6},{5,7},{6,4},{7,5},{8,10},{33,35},{10... | collective-permute-start | bytes 2211848 | tf_op jit(solution)/shard_map/ppermute | solution.py:67
  2.7 1.0 copy-start.1
  3.7 1.0 copy-start.2
  4.8 7.4 %collective-permute-start.2 = (bf16[2,2,144,128]{3,2,1,0:T(8,128)(2,1)S(1)}, bf16[2,2,144,128]{3,2,1,0:T(8,128)(2,1)S(1)}, u32[]{:S(2)}, u32[]{:S(2)}) collective-permute-start(bf16[2,2,144,128]{3,2,1,0:T(8,128)(2,1)S(1)} %get-tuple-element.38), channel_id=1, source_target_pairs={{0,96},{1,25},{2,98},{3,27},{4,100},{5,29},{6,102},{7,31},{8,104},... | collective-permute-start | bytes 442376 | tf_op jit(solution)/shard_map/ppermute | solution.py:67
  7.9 6.8 %collective-permute-start.3 = (bf16[2,2,144,128]{3,2,1,0:T(8,128)(2,1)S(1)}, bf16[2,2,144,128]{3,2,1,0:T(8,128)(2,1)S(1)}, u32[]{:S(2)}, u32[]{:S(2)}) collective-permute-start(bf16[2,2,144,128]{3,2,1,0:T(8,128)(2,1)S(1)} %get-tuple-element.39), channel_id=1, source_target_pairs={{0,64},{1,17},{2,66},{3,19},{4,68},{5,21},{6,70},{7,23},{8,72},{33... | collective-permute-start | bytes 442376 | tf_op jit(solution)/shard_map/ppermute | solution.py:67
  8.5 7.6 %collective-permute-start.4 = (bf16[2,2,144,128]{3,2,1,0:T(8,128)(2,1)S(1)}, bf16[2,2,144,128]{3,2,1,0:T(8,128)(2,1)S(1)}, u32[]{:S(2)}, u32[]{:S(2)}) collective-permute-start(bf16[2,2,144,128]{3,2,1,0:T(8,128)(2,1)S(1)} %get-tuple-element.40), channel_id=1, source_target_pairs={{0,32},{1,9},{2,34},{3,11},{4,36},{5,13},{6,38},{7,15},{8,40},{33,... | collective-permute-start | bytes 442376 | tf_op jit(solution)/shard_map/ppermute | solution.py:67
  9.5 15.0 %collective-permute-start = (bf16[288,1280]{1,0:T(8,128)(2,1)}, bf16[288,1280]{1,0:T(8,128)(2,1)S(1)}, u32[]{:S(2)}, u32[]{:S(2)}) collective-permute-start(bf16[288,1280]{1,0:T(8,128)(2,1)} %bitcast.15), channel_id=1, source_target_pairs={{0,1},{1,0},{2,3},{3,2},{4,5},{5,4},{6,7},{7,6},{8,9},{33,32},{10,... | collective-permute-start | bytes 2211848 | tf_op jit(solution)/shard_map/ppermute | solution.py:67
  16.2 0.7 copy-start.9
  16.9 0.7 copy-start.10
  19.4 8.8 %collective-permute-start.5 = (bf16[288,1280]{1,0:T(8,128)(2,1)S(1)}, bf16[288,1280]{1,0:T(8,128)(2,1)S(1)}, u32[]{:S(2)}, u32[]{:S(2)}) collective-permute-start(bf16[288,1280]{1,0:T(8,128)(2,1)S(1)} %collective-permute-done.1.h2), channel_id=1, source_target_pairs={{0,1},{1,0},{2,3},{3,2},{4,5},{5,4},{6,7},{7,6},{8,9},{33,32},{10,... | collective-permute-start | bytes 2211848 | tf_op jit(solution)/shard_map/ppermute | solution.py:67
  19.5 24.3 %collective-permute-start.6 = (bf16[2,2,720,128]{3,2,1,0:T(8,128)(2,1)S(1)}, bf16[2,2,720,128]{3,2,1,0:T(8,128)(2,1)S(1)}, u32[]{:S(2)}, u32[]{:S(2)}) collective-permute-start(bf16[2,2,720,128]{3,2,1,0:T(8,128)(2,1)S(1)} %assemble.1.after.refs_4_), channel_id=1, source_target_pairs={{0,24},{1,97},{2,26},{3,99},{4,28},{5,101},{6,30},{7,103},{8,0},{3... | collective-permute-start | bytes 2211848 | tf_op jit(solution)/shard_map/ppermute | solution.py:67
  22.3 21.5 %collective-permute-start.7 = (bf16[2,2,720,128]{3,2,1,0:T(8,128)(2,1)S(1)}, bf16[2,2,720,128]{3,2,1,0:T(8,128)(2,1)S(1)}, u32[]{:S(2)}, u32[]{:S(2)}) collective-permute-start(bf16[2,2,720,128]{3,2,1,0:T(8,128)(2,1)S(1)} %assemble.1.after.refs_4_), channel_id=1, source_target_pairs={{0,8},{1,33},{2,10},{3,35},{4,12},{5,37},{6,14},{7,39},{8,16},{33,... | collective-permute-start | bytes 2211848 | tf_op jit(solution)/shard_map/ppermute | solution.py:67
  22.3 21.6 %collective-permute-start.8 = (bf16[2,2,720,128]{3,2,1,0:T(8,128)(2,1)S(1)}, bf16[2,2,720,128]{3,2,1,0:T(8,128)(2,1)S(1)}, u32[]{:S(2)}, u32[]{:S(2)}) collective-permute-start(bf16[2,2,720,128]{3,2,1,0:T(8,128)(2,1)S(1)} %assemble.1.after.refs_4_), channel_id=1, source_target_pairs={{0,16},{1,65},{2,18},{3,67},{4,20},{5,69},{6,22},{7,71},{8,24},{33... | collective-permute-start | bytes 2211848 | tf_op jit(solution)/shard_map/ppermute | solution.py:67
  24.6 34.2 %collective-permute-start.12 = (bf16[2,2,720,128]{3,2,1,0:T(8,128)(2,1)S(1)}, bf16[2,2,720,128]{3,2,1,0:T(8,128)(2,1)S(1)}, u32[]{:S(2)}, u32[]{:S(2)}) collective-permute-start(bf16[2,2,720,128]{3,2,1,0:T(8,128)(2,1)S(1)} %assemble.1.after.refs_4_), channel_id=1, source_target_pairs={{0,4},{1,5},{2,6},{3,7},{4,0},{5,1},{6,2},{7,3},{8,12},{33,37},{10... | collective-permute-start | bytes 2211848 | tf_op jit(solution)/shard_map/ppermute | solution.py:67
  28.3 1.1 %copy-start = (bf16[2,144,1280]{2,1,0:T(8,128)(2,1)S(1)}, bf16[2,144,1280]{2,1,0:T(8,128)(2,1)}, u32[]{:S(2)}) copy-start(bf16[2,144,1280]{2,1,0:T(8,128)(2,1)} %param.12) | copy-start | bytes 2211844
  29.4 0.8 copy-start.5
  30.1 0.8 copy-start.6
  30.9 10.0 %slice-start = ((s8[6553600]{0:T(1024)(128)(4,1)}), s8[4194304]{0:T(1024)(128)(4,1)S(1)}, s32[]{:S(2)}) async-start(s8[6553600]{0:T(1024)(128)(4,1)} %bitcast.19), calls=%async_computation | async-start | bytes 8388608
  35.4 5.6 %slice-start.1 = ((s8[6553600]{0:T(1024)(128)(4,1)}), s8[2359296]{0:T(1024)(128)(4,1)S(1)}, s32[]{:S(2)}) async-start(s8[6553600]{0:T(1024)(128)(4,1)} %bitcast.19), calls=%async_computation.1 | async-start | bytes 4718592
  35.4 19.8 %slice-start.2 = ((s8[6553600]{0:T(1024)(128)(4,1)}), s8[4194304]{0:T(1024)(128)(4,1)S(1)}, s32[]{:S(2)}) async-start(s8[6553600]{0:T(1024)(128)(4,1)} %bitcast.21), calls=%async_computation.2 | async-start | bytes 8388608
  41.0 7.7 %copy-start.7 = (f32[640]{0:T(1024)S(1)}, f32[640]{0:T(1024)}, u32[]{:S(2)}) copy-start(f32[640]{0:T(1024)} %qg.1) | copy-start | bytes 7684
  41.0 7.7 %copy-start.8 = (f32[640]{0:T(1024)S(1)}, f32[640]{0:T(1024)}, u32[]{:S(2)}) copy-start(f32[640]{0:T(1024)} %kg.1) | copy-start | bytes 7684
  41.0 14.1 %slice-start.3 = ((s8[6553600]{0:T(1024)(128)(4,1)}), s8[2359296]{0:T(1024)(128)(4,1)S(1)}, s32[]{:S(2)}) async-start(s8[6553600]{0:T(1024)(128)(4,1)} %bitcast.21), calls=%async_computation.3 | async-start | bytes 4718592
  43.8 3.2 %collective-permute-start.10 = (f32[8,384]{1,0:T(8,128)S(1)}, f32[8,384]{1,0:T(8,128)S(1)}, u32[]{:S(2)}, u32[]{:S(2)}) collective-permute-start(f32[8,384]{1,0:T(8,128)S(1)} %sum_squares.1.s0), channel_id=1, source_target_pairs={{0,3},{1,2},{2,1},{3,0},{4,7},{5,6},{6,5},{7,4},{8,11},{33,34},{10... | collective-permute-start | bytes 36872 | tf_op jit(solution)/shard_map/ppermute | solution.py:67
  44.1 3.0 %collective-permute-start.11 = (f32[8,384]{1,0:T(8,128)S(1)}, f32[8,384]{1,0:T(8,128)S(1)}, u32[]{:S(2)}, u32[]{:S(2)}) collective-permute-start(f32[8,384]{1,0:T(8,128)S(1)} %sum_squares.1.s0), channel_id=1, source_target_pairs={{0,1},{1,0},{2,3},{3,2},{4,5},{5,4},{6,7},{7,6},{8,9},{33,32},{10,... | collective-permute-start | bytes 36872 | tf_op jit(solution)/shard_map/ppermute | solution.py:67
  45.0 3.7 %collective-permute-start.9 = (f32[8,384]{1,0:T(8,128)S(1)}, f32[8,384]{1,0:T(8,128)S(1)}, u32[]{:S(2)}, u32[]{:S(2)}) collective-permute-start(f32[8,384]{1,0:T(8,128)S(1)} %sum_squares.1.s0), channel_id=1, source_target_pairs={{0,2},{1,3},{2,0},{3,1},{4,6},{5,7},{6,4},{7,5},{8,10},{33,35},{10... | collective-permute-start | bytes 36872 | tf_op jit(solution)/shard_map/ppermute | solution.py:67
  50.5 8.3 %collective-permute-start.13 = (bf16[2,2,144,128]{3,2,1,0:T(8,128)(2,1)S(1)}, bf16[2,2,144,128]{3,2,1,0:T(8,128)(2,1)S(1)}, u32[]{:S(2)}, u32[]{:S(2)}) collective-permute-start(bf16[2,2,144,128]{3,2,1,0:T(8,128)(2,1)S(1)} %get-tuple-element.52.refs_3_), channel_id=1, source_target_pairs={{0,96},{1,25},{2,98},{3,27},{4,100},{5,29},{6,102},{7,31},{8,104},... | collective-permute-start | bytes 442376 | tf_op jit(solution)/shard_map/ppermute | solution.py:67
  53.5 6.8 %collective-permute-start.14 = (bf16[2,2,144,128]{3,2,1,0:T(8,128)(2,1)S(1)}, bf16[2,2,144,128]{3,2,1,0:T(8,128)(2,1)S(1)}, u32[]{:S(2)}, u32[]{:S(2)}) collective-permute-start(bf16[2,2,144,128]{3,2,1,0:T(8,128)(2,1)S(1)} %get-tuple-element.51.refs_2_), channel_id=1, source_target_pairs={{0,64},{1,17},{2,66},{3,19},{4,68},{5,21},{6,70},{7,23},{8,72},{33... | collective-permute-start | bytes 442376 | tf_op jit(solution)/shard_map/ppermute | solution.py:67
  54.2 3.6 %copy-start.3 = (bf16[288,640]{1,0:T(8,128)(2,1)S(1)}, bf16[288,640]{1,0:T(8,128)(2,1)}, u32[]{:S(2)}) copy-start(bf16[288,640]{1,0:T(8,128)(2,1)} %get-tuple-element.48.k_ref) | copy-start | bytes 1105924
  54.2 7.6 %collective-permute-start.15 = (bf16[2,2,144,128]{3,2,1,0:T(8,128)(2,1)S(1)}, bf16[2,2,144,128]{3,2,1,0:T(8,128)(2,1)S(1)}, u32[]{:S(2)}, u32[]{:S(2)}) collective-permute-start(bf16[2,2,144,128]{3,2,1,0:T(8,128)(2,1)S(1)} %get-tuple-element.50.refs_1_), channel_id=1, source_target_pairs={{0,32},{1,9},{2,34},{3,11},{4,36},{5,13},{6,38},{7,15},{8,40},{33,... | collective-permute-start | bytes 442376 | tf_op jit(solution)/shard_map/ppermute | solution.py:67
  57.7 36.1 %copy-start.4 = (bf16[288,640]{1,0:T(8,128)(2,1)}, bf16[288,640]{1,0:T(8,128)(2,1)S(1)}, u32[]{:S(2)}) copy-start(bf16[288,640]{1,0:T(8,128)(2,1)S(1)} %convolution_convert_fusion.v_ref) | copy-start | bytes 1105924
  61.8 13.8 %collective-permute-start.16 = (bf16[2,2,720,128]{3,2,1,0:T(8,128)(2,1)S(1)}, bf16[2,2,720,128]{3,2,1,0:T(8,128)(2,1)S(1)}, u32[]{:S(2)}, u32[]{:S(2)}) collective-permute-start(bf16[2,2,720,128]{3,2,1,0:T(8,128)(2,1)S(1)} %collective-permute-done.12.refs_4_), channel_id=1, source_target_pairs={{0,24},{1,97},{2,26},{3,99},{4,28},{5,101},{6,30},{7,103},{8,0},{3... | collective-permute-start | bytes 2211848 | tf_op jit(solution)/shard_map/ppermute | solution.py:67
  62.9 20.6 %collective-permute-start.17 = (bf16[2,2,720,128]{3,2,1,0:T(8,128)(2,1)S(1)}, bf16[2,2,720,128]{3,2,1,0:T(8,128)(2,1)S(1)}, u32[]{:S(2)}, u32[]{:S(2)}) collective-permute-start(bf16[2,2,720,128]{3,2,1,0:T(8,128)(2,1)S(1)} %collective-permute-done.12.refs_4_), channel_id=1, source_target_pairs={{0,8},{1,33},{2,10},{3,35},{4,12},{5,37},{6,14},{7,39},{8,16},{33,... | collective-permute-start | bytes 2211848 | tf_op jit(solution)/shard_map/ppermute | solution.py:67
  63.8 19.7 %collective-permute-start.18 = (bf16[2,2,720,128]{3,2,1,0:T(8,128)(2,1)S(1)}, bf16[2,2,720,128]{3,2,1,0:T(8,128)(2,1)S(1)}, u32[]{:S(2)}, u32[]{:S(2)}) collective-permute-start(bf16[2,2,720,128]{3,2,1,0:T(8,128)(2,1)S(1)} %collective-permute-done.12.refs_4_), channel_id=1, source_target_pairs={{0,16},{1,65},{2,18},{3,67},{4,20},{5,69},{6,22},{7,71},{8,24},{33... | collective-permute-start | bytes 2211848 | tf_op jit(solution)/shard_map/ppermute | solution.py:67
  93.8 5.3 %collective-permute-start.19 = (bf16[2,304,128]{2,1,0:T(8,128)(2,1)S(1)}, bf16[2,304,128]{2,1,0:T(8,128)(2,1)S(1)}, u32[]{:S(2)}, u32[]{:S(2)}) collective-permute-start(bf16[2,304,128]{2,1,0:T(8,128)(2,1)S(1)} %get-tuple-element.68), channel_id=1, source_target_pairs={{0,96},{1,25},{2,98},{3,27},{4,100},{5,29},{6,102},{7,31},{8,104},... | collective-permute-start | bytes 466952 | tf_op jit(solution)/shard_map/ppermute | solution.py:67
  94.5 6.8 %collective-permute-start.20 = (bf16[2,304,128]{2,1,0:T(8,128)(2,1)S(1)}, bf16[2,304,128]{2,1,0:T(8,128)(2,1)S(1)}, u32[]{:S(2)}, u32[]{:S(2)}) collective-permute-start(bf16[2,304,128]{2,1,0:T(8,128)(2,1)S(1)} %get-tuple-element.69), channel_id=1, source_target_pairs={{0,64},{1,17},{2,66},{3,19},{4,68},{5,21},{6,70},{7,23},{8,72},{33... | collective-permute-start | bytes 466952 | tf_op jit(solution)/shard_map/ppermute | solution.py:67
  96.1 6.8 %collective-permute-start.21 = (bf16[2,304,128]{2,1,0:T(8,128)(2,1)S(1)}, bf16[2,304,128]{2,1,0:T(8,128)(2,1)S(1)}, u32[]{:S(2)}, u32[]{:S(2)}) collective-permute-start(bf16[2,304,128]{2,1,0:T(8,128)(2,1)S(1)} %get-tuple-element.70), channel_id=1, source_target_pairs={{0,32},{1,9},{2,34},{3,11},{4,36},{5,13},{6,38},{7,15},{8,40},{33,... | collective-permute-start | bytes 466952 | tf_op jit(solution)/shard_map/ppermute | solution.py:67

commit v4 on v3

--- a/solution.py
+++ b/solution.py
@@ -32,7 +32,9 @@
 F32 = jnp.float32
 BF16 = jnp.bfloat16
 AXES = ("patch", "tp")
-VMEM_MIB = 40
+GROUP = 16
+VMEM_MIB = 24
+ATTENTION_MIB = 34
 
 
 def params(mib):
@@ -71,8 +73,13 @@
     return permute(value, lambda u, v, h, l, c: ((u + k) % 4, v, h, l, c))
 
 
-def shift_v(value, k):
-    return permute(value, lambda u, v, h, l, c: (u, (v + k) % 4, h, l, c))
+def swap_v(value, mask):
+    return permute(value, lambda u, v, h, l, c: (u, v ^ mask, h, l, c))
+
+
+def exchange_u(values):
+    came = {r: shift_u(values[4 - r], 4 - r) for r in (2, 1, 3)}
+    return [values[0], came[1], came[2], came[3]]
 
 
 def swap_z_hi(value):
@@ -133,7 +140,8 @@
     )(u, stale_keys, stale_values)
 
 
-def tables_kernel(place_hbm, freq, after, cond, cos, sin, places_s, place_ref, sem):
+def tables_kernel(place_hbm, freq, rows, shift, scale, after, *refs):
+    cond, cos, sin, mod, rows_out, places_s, place_ref, sem = refs
     copy = pltpu.make_async_copy(place_hbm, place_ref, sem.at[0])
     copy.start()
     copy.wait()
@@ -158,19 +166,26 @@
     flag = jnp.where((frame == 0) | (frame == FRAMES - 1), 1.0, 0.0)
     cond[0:TOK] = flag
     cond[TOK:ROWS] = flag
-
-
-def tables(token_place, after):
+    mod[0:2] = 1.0 + scale[...]
+    mod[2:4] = shift[...]
+    rows_out[...] = rows[...]
+
+
+def tables(token_place, rows, shift, scale, after):
     table = jax.ShapeDtypeStruct((TOK, HD), F32)
     return pl.pallas_call(
         tables_kernel,
-        out_shape=[jax.ShapeDtypeStruct((ROWS, HD), F32), table, table],
-        in_specs=[
-            pl.BlockSpec(memory_space=pltpu.HBM),
-            vmem(),
-            pl.BlockSpec(memory_space=pl.ANY),
+        out_shape=[
+            jax.ShapeDtypeStruct((ROWS, HD), F32),
+            table,
+            table,
+            jax.ShapeDtypeStruct((4, D), F32),
+            jax.ShapeDtypeStruct((ROWS, CHUNK), BF16),
         ],
-        out_specs=[vmem()] * 3,
+        in_specs=[pl.BlockSpec(memory_space=pltpu.HBM)]
+        + [vmem()] * 4
+        + [pl.BlockSpec(memory_space=pl.ANY)],
+        out_specs=[vmem()] * 5,
         scratch_shapes=[
             pltpu.VMEM((TOK, HD), jnp.int32),
             pltpu.SMEM((TOK,), jnp.int32),
@@ -178,10 +193,10 @@
         ],
         compiler_params=params(VMEM_MIB),
         cost_estimate=pl.CostEstimate(
-            flops=100 * TOK * HD, bytes_accessed=16 * TOK * HD, transcendentals=0
+            flops=100 * TOK * HD, bytes_accessed=40_000_000, transcendentals=0
         ),
         name="tables",
-    )(token_place, jnp.asarray(frequencies()), after)
+    )(token_place, jnp.asarray(frequencies()), rows, shift, scale, after)
 
 
 def assemble_kernel(*refs):
@@ -206,38 +221,40 @@
     )(*parts)
 
 
-def modulate_kernel(t_ref, h0, h1, h2, h3, cond, shift, scale, out_ref):
+def modulate_kernel(t_ref, h0, h1, h2, h3, cond, mod, out_ref):
     chunks = (h0, h1, h2, h3)
-    total = jnp.zeros((ROWS, 1), F32)
-    for chunk in chunks:
-        total = total + jnp.sum(chunk[...].astype(F32), axis=1, keepdims=True)
-    mean = total * (1.0 / D)
-    deviation = jnp.zeros((ROWS, 1), F32)
-    for chunk in chunks:
-        centered = chunk[...].astype(F32) - mean
-        deviation = deviation + jnp.sum(centered * centered, axis=1, keepdims=True)
-    rstd = lax.rsqrt(deviation * (1.0 / D) + EPS)
-    conditioned = cond[:, 0:1] > 0.5
-    for c in range(TP):
-        cols = pl.ds(pl.multiple_of(t_ref[c] * CHUNK, CHUNK), CHUNK)
-        part = chunks[c][...].astype(F32)
-        gain = jnp.where(conditioned, scale[1:2, cols], scale[0:1, cols])
-        bias = jnp.where(conditioned, shift[1:2, cols], shift[0:1, cols])
-        out_ref[:, cols] = ((part - mean) * rstd * (1.0 + gain) + bias).astype(BF16)
-
-
-def modulate(blocks, chunks, cond, shift, scale):
+    for row in range(0, ROWS, GROUP):
+        rows = slice(row, row + GROUP)
+        total = jnp.zeros((GROUP, 1), F32)
+        for chunk in chunks:
+            total = total + jnp.sum(chunk[rows].astype(F32), axis=1, keepdims=True)
+        mean = total * (1.0 / D)
+        deviation = jnp.zeros((GROUP, 1), F32)
+        for chunk in chunks:
+            centered = chunk[rows].astype(F32) - mean
+            deviation = deviation + jnp.sum(centered * centered, axis=1, keepdims=True)
+        rstd = lax.rsqrt(deviation * (1.0 / D) + EPS)
+        conditioned = cond[rows, 0:1] > 0.5
+        for c in range(TP):
+            cols = pl.ds(pl.multiple_of(t_ref[c] * CHUNK, CHUNK), CHUNK)
+            gain = jnp.where(conditioned, mod[1:2, cols], mod[0:1, cols])
+            bias = jnp.where(conditioned, mod[3:4, cols], mod[2:3, cols])
+            normed = (chunks[c][rows].astype(F32) - mean) * rstd
+            out_ref[rows, cols] = (normed * gain + bias).astype(BF16)
+
+
+def modulate(blocks, chunks, cond, mod):
     return pl.pallas_call(
         modulate_kernel,
         out_shape=jax.ShapeDtypeStruct((ROWS, D), BF16),
-        in_specs=[smem()] + [vmem()] * 7,
+        in_specs=[smem()] + [vmem()] * 6,
         out_specs=vmem(),
         compiler_params=params(VMEM_MIB),
         cost_estimate=pl.CostEstimate(
-            flops=12 * ROWS * D, bytes_accessed=4 * ROWS * D, transcendentals=0
+            flops=12 * ROWS * D, bytes_accessed=20_000_000, transcendentals=0
         ),
         name="modulate",
-    )(blocks, *chunks, cond, shift, scale)
+    )(blocks, *chunks, cond, mod)
 
 
 def squares_kernel(q_ref, k_ref, out_ref):
@@ -363,7 +380,6 @@
 
 
 TILE = 2 * TOK
-GROUP = 16
 PER_PIECE = 4 * TOK
 KEYS = 4 * PER_PIECE
 KEYS_LAST = 4 * TOK
@@ -378,24 +394,7 @@
         msgs = rest[3:7]
     else:
         out_ref, lse_ref = rest[0:2]
-    lse_s, acc_s, k_main, v_main, k_last, v_last, scores_s, probs_s, sems = rest[-9:]
-    copies = ([], [])
-    for s in range(B):
-        for n in range(4):
-            piece = pieces[n].at[s]
-            main, last = pl.ds(n * PER_PIECE, PER_PIECE), pl.ds(n * TOK, TOK)
-            head, tail = pl.ds(0, PER_PIECE), pl.ds(PER_PIECE, TOK)
-            for kind, part, target, rows in (
-                (0, head, k_main, main),
-                (0, tail, k_last, last),
-                (1, head, v_main, main),
-                (1, tail, v_last, last),
-            ):
-                copy = pltpu.make_async_copy(
-                    piece.at[kind, part], target.at[s, rows], sems.at[s, len(copies[s])]
-                )
-                copy.start()
-                copies[s].append(copy)
+    lse_s, acc_s, k_main, v_main, k_last, v_last, scores_s, probs_s = rest[-8:]
 
     jobs = [(s, e, tile) for s in range(B) for e in range(2) for tile in range(2)]
 
@@ -408,8 +407,13 @@
         out = scores_s.at[i % 2]
 
         def arrive():
-            for copy in copies[s]:
-                copy.wait()
+            for n, piece in enumerate(pieces):
+                main = slice(n * PER_PIECE, (n + 1) * PER_PIECE)
+                last = slice(n * TOK, (n + 1) * TOK)
+                k_main[s, main] = piece[s, 0, 0:PER_PIECE]
+                k_last[s, last] = piece[s, 0, PER_PIECE:PIECE]
+                v_main[s, main] = piece[s, 1, 0:PER_PIECE]
+                v_last[s, last] = piece[s, 1, PER_PIECE:PIECE]
 
         def step(at, end):
             query = jnp.concatenate([queries[2 * tile][s, e], queries[2 * tile + 1][s, e]], axis=0)
@@ -509,8 +513,7 @@
 def stale_attention(queries, pieces, near=None, after=None):
     far = near is not None
     args = [*queries, *pieces]
-    hbm = pl.BlockSpec(memory_space=pltpu.HBM)
-    in_specs = [vmem()] * 4 + [hbm] * len(pieces)
+    in_specs = [vmem()] * 8
     if far:
         args += [*near, after]
         in_specs += [vmem(), vmem(), pl.BlockSpec(memory_space=pl.ANY)]
@@ -532,9 +535,8 @@
             pltpu.VMEM((B, KEYS_LAST, HD), BF16),
             pltpu.VMEM((2, TILE, KEYS), F32),
             pltpu.VMEM((2, TILE, KEYS), BF16),
-            pltpu.SemaphoreType.DMA((B, 16)),
         ],
-        compiler_params=params(VMEM_MIB),
+        compiler_params=params(ATTENTION_MIB),
         cost_estimate=pl.CostEstimate(
             flops=4 * work * HD, bytes_accessed=8 * (KEYS + KEYS_LAST) * HD, transcendentals=work
         ),
@@ -598,10 +600,6 @@
     )(u, fresh_out, fresh_rows, *msgs)
 
 
-def gather_v(piece):
-    return [piece, shift_v(piece, 3), shift_v(piece, 1), shift_v(piece, 2)]
-
-
 def shards(
     hidden,
     mod_shift,
@@ -625,33 +623,36 @@
     core_rows = swap_tp(own_rows, 0, 1)
 
     packed = pack_stale(u, stale_keys, stale_values)
-    arrived = [packed[0]] + [shift_u(packed[4 - r], 4 - r) for r in range(1, 4)]
+    arrived = exchange_u(packed)
     near = assemble([*arrived, packed[4]])
-    near_all = gather_v(near)
+    near_one, near_three = swap_v(near, 1), swap_v(near, 3)
     far = swap_z_hi(near)
-    cond, cos, sin = tables(token_place, near)
+    cond, cos, sin, mod, own_rows = tables(token_place, own_rows, mod_shift, mod_scale, near)
 
     z_rows, cond = lax.optimization_barrier((z_rows, cond))
     cross_rows = swap_tp(z_rows, 0, 1)
     blocks = jnp.stack([tp, tp ^ 1, tp ^ 2, tp ^ 3]).astype(jnp.int32)
-    rows = [own_rows, core_rows, z_rows, cross_rows]
-    modded = modulate(blocks, rows, cond, mod_shift, mod_scale)
+    modded = modulate(blocks, [own_rows, core_rows, z_rows, cross_rows], cond, mod)
     query = jnp.dot(modded, w_query, preferred_element_type=F32)
     key = jnp.dot(modded, w_key, preferred_element_type=F32)
     fresh_values = jnp.dot(modded, w_value, preferred_element_type=F32).astype(BF16)
     own_sq = sum_squares(query, key)
-    own_sq, *near_all = lax.optimization_barrier((own_sq, *near_all))
-    squares = [own_sq] + [swap_tp(own_sq, z, c) for z, c in ((1, 0), (1, 1), (0, 1))]
+    own_sq, near_one, near_three = lax.optimization_barrier((own_sq, near_one, near_three))
+    squares = [own_sq] + [swap_tp(own_sq, z, c) for z, c in ((1, 1), (1, 0), (0, 1))]
+    near_two = swap_v(near_one, 3)
     fresh_keys, *sends = norm_rope(u, query, key, squares, q_gain, k_gain, cos, sin)
-    queries = [sends[0]] + [shift_u(sends[4 - r], 4 - r) for r in (1, 3, 2)]
-    queries = [queries[0], queries[1], queries[3], queries[2]]
+    far, near_two, *sends = lax.optimization_barrier((far, near_two, *sends))
+    far_one, far_three = swap_v(far, 1), swap_v(far, 3)
+    queries = exchange_u(sends)
     fresh_out, fresh_rows = fresh_attention(u, fresh_keys, fresh_values, sends)
 
-    far, fresh_rows, *queries = lax.optimization_barrier((far, fresh_rows, *queries))
-    far_all = gather_v(far)
-    partial = stale_attention(queries, near_all)
-    outs = stale_attention(queries, far_all, near=partial, after=fresh_rows)
-    returned = [outs[0]] + [shift_u(outs[4 - k], 4 - k) for k in range(1, 4)]
+    far_one, fresh_rows, *queries = lax.optimization_barrier((far_one, fresh_rows, *queries))
+    far_two = swap_v(far_one, 3)
+    partial = stale_attention(queries, [near, near_one, near_three, near_two])
+    outs = stale_attention(
+        queries, [far, far_one, far_three, far_two], near=partial, after=fresh_rows
+    )
+    returned = exchange_u(outs)
     attended = merge(u, fresh_out, fresh_rows, returned)
     return (
         attended,

time: 105 us -> 100 us (0.952)
  Pallas kernels: 30.4 us -> 23.1 us
  waiting for transfers between devices: 27.1 us -> 29 us
    pallas_call x2, Pallas kernels: 20.2 us -> 11.9 us  [stale_attention(): pl.pallas_call(functools.partial(stale_kernel, far), out_shape=out_shape,...]
    ppermute x22, waiting for transfers between devices: 27.1 us -> 29 us  [permute(): lax.ppermute(value, AXES, [(linear(*p), linear(*move(*p))) for p in place...]
    pallas_call x1, Pallas kernels: 4.44 us -> 5.5 us  [modulate(): pl.pallas_call(modulate_kernel, out_shape=jax.ShapeDtypeStruct((ROWS, D),...]
  transfers between devices with their start and end apart: 22 -> 22, of which waited for: 12 -> 13; matrix products, arithmetic and copies ran while one was open for 10% -> 10% of each run, Pallas kernels for 18% -> 15%
where the time goes in v4:
time: 100 us; the launch traced here: 99.7 us
  starting transfers between devices  30.2 us (30%)
  waiting for transfers between devices  29 us (29%)
  Pallas kernels  23.1 us (23%)
  matrix products  10.3 us (10%)
  local copies, waits for them, and re-layouts  6.02 us (6%)
    ppermute x22, starting transfers between devices, permute(): lax.ppermute(value, AXES, [(linear(*p), linear(*move(*p))) for p in place...  30.2 us
    ppermute x22, waiting for transfers between devices, permute(): lax.ppermute(value, AXES, [(linear(*p), linear(*move(*p))) for p in place...  29 us
    pallas_call x2, Pallas kernels, stale_attention(): pl.pallas_call(functools.partial(stale_kernel, far), out_shape=out_shape,...  11.9 us
    unnamed x30, local copies, waits for them, and re-layouts  6.02 us
    pallas_call x1, Pallas kernels, modulate(): pl.pallas_call(modulate_kernel, out_shape=jax.ShapeDtypeStruct((ROWS, D),...  5.5 us
    dot_general x1, matrix products, shards(): query = jnp.dot(modded, w_query, preferred_element_type=F32)  5.45 us
    dot_general x1, matrix products, shards(): jnp.dot(modded, w_value, preferred_element_type=F32).astype(BF16)  2.44 us
    dot_general x1, matrix products, shards(): key = jnp.dot(modded, w_key, preferred_element_type=F32)  2.43 us
  transfers between devices with their start and end apart: 22, of which 13 were waited for; matrix products, arithmetic and copies ran while one was open for 10% of the time, Pallas kernels for 15%

profile of v4, /device:TPU:0, one launch (start us, length us, event | category | flops | bytes accessed | tf_op | source)
XLA Modules:
  0.0 99.7 jit_solution(9954504248612977186)
XLA Ops:
  0.6 2.1 %collective-permute-start.4 = (bf16[288,1280]{1,0:T(8,128)(2,1)}, bf16[288,1280]{1,0:T(8,128)(2,1)S(1)}, u32[]{:S(2)}, u32[]{:S(2)}) collective-permute-start(bf16[288,1280]{1,0:T(8,128)(2,1)} %bitcast.14), channel_id=1, source_target_pairs={{0,2},{1,3},{2,0},{3,1},{4,6},{5,7},{6,4},{7,5},{8,10},{33,35},{10... | collective-permute-start | bytes 2211848 | tf_op jit(solution)/shard_map/ppermute | solution.py:69
  2.7 1.0 copy-done.1
  3.7 1.0 copy-done.2
  4.8 3.1 %collective-permute-start = (bf16[2,2,144,128]{3,2,1,0:T(8,128)(2,1)S(1)}, bf16[2,2,144,128]{3,2,1,0:T(8,128)(2,1)S(1)}, u32[]{:S(2)}, u32[]{:S(2)}) collective-permute-start(bf16[2,2,144,128]{3,2,1,0:T(8,128)(2,1)S(1)} %get-tuple-element.44), channel_id=1, source_target_pairs={{0,96},{1,25},{2,98},{3,27},{4,100},{5,29},{6,102},{7,31},{8,104},... | collective-permute-start | bytes 442376 | tf_op jit(solution)/shard_map/ppermute | solution.py:69
  7.9 0.6 collective-permute-start.1
  8.5 1.0 collective-permute-start.2
  9.5 2.7 %collective-permute-done.refs_1_ = bf16[2,2,144,128]{3,2,1,0:T(8,128)(2,1)S(1)} collective-permute-done((bf16[2,2,144,128]{3,2,1,0:T(8,128)(2,1)S(1)}, bf16[2,2,144,128]{3,2,1,0:T(8,128)(2,1)S(1)}, u32[]{:S(2)}, u32[]{:S(2)}) %collective-permute-start) | collective-permute-done | bytes 147488 | tf_op jit(solution)/shard_map/ppermute | solution.py:69
  12.2 2.5 %collective-permute-done.1.refs_2_ = bf16[2,2,144,128]{3,2,1,0:T(8,128)(2,1)S(1)} collective-permute-done((bf16[2,2,144,128]{3,2,1,0:T(8,128)(2,1)S(1)}, bf16[2,2,144,128]{3,2,1,0:T(8,128)(2,1)S(1)}, u32[]{:S(2)}, u32[]{:S(2)}) %collective-permute-start.1) | collective-permute-done | bytes 147488 | tf_op jit(solution)/shard_map/ppermute | solution.py:69
  14.7 1.5 %collective-permute-done.2.refs_3_ = bf16[2,2,144,128]{3,2,1,0:T(8,128)(2,1)S(1)} collective-permute-done((bf16[2,2,144,128]{3,2,1,0:T(8,128)(2,1)S(1)}, bf16[2,2,144,128]{3,2,1,0:T(8,128)(2,1)S(1)}, u32[]{:S(2)}, u32[]{:S(2)}) %collective-permute-start.2) | collective-permute-done | bytes 147488 | tf_op jit(solution)/shard_map/ppermute | solution.py:69
  16.2 1.1 %copy-done = bf16[2,144,1280]{2,1,0:T(8,128)(2,1)S(1)} copy-done((bf16[2,144,1280]{2,1,0:T(8,128)(2,1)S(1)}, bf16[2,144,1280]{2,1,0:T(8,128)(2,1)}, u32[]{:S(2)}) %copy-start) | copy-done | bytes 737304
  17.3 0.8 copy-done.5
  18.1 0.8 copy-done.6
  18.9 0.7 copy-done.9
  19.5 0.7 copy-done.10
  20.2 0.9 tables.1
  21.3 1.5 %collective-permute-start.6 = (bf16[2,2,720,128]{3,2,1,0:T(8,128)(2,1)S(1)}, bf16[2,2,720,128]{3,2,1,0:T(8,128)(2,1)S(1)}, u32[]{:S(2)}, u32[]{:S(2)}) collective-permute-start(bf16[2,2,720,128]{3,2,1,0:T(8,128)(2,1)S(1)} %assemble.1.after.refs_4_), channel_id=1, source_target_pairs={{0,8},{1,33},{2,10},{3,35},{4,12},{5,37},{6,14},{7,39},{8,0},{33,1... | collective-permute-start | bytes 2211848 | tf_op jit(solution)/shard_map/ppermute | solution.py:69
  22.9 2.1 %collective-permute-start.7 = (bf16[2,2,720,128]{3,2,1,0:T(8,128)(2,1)S(1)}, bf16[2,2,720,128]{3,2,1,0:T(8,128)(2,1)S(1)}, u32[]{:S(2)}, u32[]{:S(2)}) collective-permute-start(bf16[2,2,720,128]{3,2,1,0:T(8,128)(2,1)S(1)} %assemble.1.after.refs_4_), channel_id=1, source_target_pairs={{0,24},{1,97},{2,26},{3,99},{4,28},{5,101},{6,30},{7,103},{8,16},{... | collective-permute-start | bytes 2211848 | tf_op jit(solution)/shard_map/ppermute | solution.py:69
  24.9 3.6 %collective-permute-start.11 = (bf16[2,2,720,128]{3,2,1,0:T(8,128)(2,1)S(1)}, bf16[2,2,720,128]{3,2,1,0:T(8,128)(2,1)S(1)}, u32[]{:S(2)}, u32[]{:S(2)}) collective-permute-start(bf16[2,2,720,128]{3,2,1,0:T(8,128)(2,1)S(1)} %assemble.1.after.refs_4_), channel_id=1, source_target_pairs={{0,4},{1,5},{2,6},{3,7},{4,0},{5,1},{6,2},{7,3},{8,12},{33,37},{10... | collective-permute-start | bytes 2211848 | tf_op jit(solution)/shard_map/ppermute | solution.py:69
  28.5 5.5 %modulate.1 = bf16[288,5120]{1,0:T(8,128)(2,1)S(1)} custom-call(s32[4]{0:T(128)S(1)} %pad_add_fusion.t_ref, bf16[288,1280]{1,0:T(8,128)(2,1)S(1)} %get-tuple-element.48.h0, bf16[288,1280]{1,0:T(8,128)(2,1)S(1)} %collective-permute-done.3.h1, bf16[288,1280]{1,0:T(8,128)(2,1)S(1)} %collective-permute-done.4.h2, bf16[288,1280]{1,0:T(8,128)(2,1)} %collective-permute-done.5.h3, ...), custom_call_target="tpu_custom_call" | custom-call | flops 17694720 | bytes 20000000 | tf_op jit(solution)/shard_map/modulate/pallas_call | solution.py:247
  34.1 5.4 %fusion.q_ref = f32[288,640]{1,0:T(8,128)S(1)} fusion(bf16[288,5120]{1,0:T(8,128)(2,1)S(1)} %modulate.1, bf16[5120,640]{1,0:T(8,128)(2,1)} %param.15), kind=kOutput, calls=%fused_computation.2 | convolution fusion | flops 1887436800 | bytes 10240000 | tf_op jit(solution)/shard_map/dot_general | solution.py:636
  39.6 2.4 %fusion.1.k_ref = f32[288,640]{1,0:T(8,128)S(1)} fusion(bf16[288,5120]{1,0:T(8,128)(2,1)S(1)} %modulate.1, bf16[5120,640]{1,0:T(8,128)(2,1)S(1)} %bitcast.20), kind=kOutput, calls=%fused_computation.3 | convolution fusion | flops 1887436800 | bytes 10240000 | tf_op jit(solution)/shard_map/dot_general | solution.py:637
  42.0 0.2 sum_squares.1.s0
  42.3 1.2 %collective-permute-start.12 = (bf16[2,2,720,128]{3,2,1,0:T(8,128)(2,1)S(1)}, bf16[2,2,720,128]{3,2,1,0:T(8,128)(2,1)S(1)}, u32[]{:S(2)}, u32[]{:S(2)}) collective-permute-start(bf16[2,2,720,128]{3,2,1,0:T(8,128)(2,1)S(1)} %collective-permute-done.6.refs_5_), channel_id=1, source_target_pairs={{0,24},{1,97},{2,26},{3,99},{4,28},{5,101},{6,30},{7,103},{8,16},{... | collective-permute-start | bytes 2211848 | tf_op jit(solution)/shard_map/ppermute | solution.py:69
  43.5 2.1 %collective-permute-start.9 = (f32[8,384]{1,0:T(8,128)S(1)}, f32[8,384]{1,0:T(8,128)S(1)}, u32[]{:S(2)}, u32[]{:S(2)}) collective-permute-start(f32[8,384]{1,0:T(8,128)S(1)} %sum_squares.1.s0), channel_id=1, source_target_pairs={{0,2},{1,3},{2,0},{3,1},{4,6},{5,7},{6,4},{7,5},{8,10},{33,35},{10... | collective-permute-start | bytes 36872 | tf_op jit(solution)/shard_map/ppermute | solution.py:69
  45.6 1.0 collective-permute-done.8.s1
  46.6 0.8 collective-permute-done.9.s2
  47.4 1.8 %norm_rope.1 = (bf16[288,640]{1,0:T(8,128)(2,1)}, bf16[2,2,144,128]{3,2,1,0:T(8,128)(2,1)S(1)}, bf16[2,2,144,128]{3,2,1,0:T(8,128)(2,1)S(1)}, bf16[2,2,144,128]{...) custom-call(s32[1]{0:T(128)} %bitcast.u_ref, f32[288,640]{1,0:T(8,128)S(1)} %fusion.q_ref, f32[288,640]{1,0:T(8,128)S(1)} %fusion.1.k_ref, ...), custom_call_target="tpu_custom_call" | custom-call | flops 3686400 | bytes 2949120 | tf_op jit(solution)/shard_map/norm_rope/pallas_call | solution.py:312
  49.2 5.8 %collective-permute-done.12.refs_7_ = bf16[2,2,720,128]{3,2,1,0:T(8,128)(2,1)S(1)} collective-permute-done((bf16[2,2,720,128]{3,2,1,0:T(8,128)(2,1)S(1)}, bf16[2,2,720,128]{3,2,1,0:T(8,128)(2,1)S(1)}, u32[]{:S(2)}, u32[]{:S(2)}) %collective-permute-start.12) | collective-permute-done | bytes 737312 | tf_op jit(solution)/shard_map/ppermute | solution.py:69
  55.0 1.3 %collective-permute-start.14 = (bf16[2,2,144,128]{3,2,1,0:T(8,128)(2,1)S(1)}, bf16[2,2,144,128]{3,2,1,0:T(8,128)(2,1)S(1)}, u32[]{:S(2)}, u32[]{:S(2)}) collective-permute-start(bf16[2,2,144,128]{3,2,1,0:T(8,128)(2,1)S(1)} %get-tuple-element.65.refs_3_), channel_id=1, source_target_pairs={{0,96},{1,25},{2,98},{3,27},{4,100},{5,29},{6,102},{7,31},{8,104},... | collective-permute-start | bytes 442376 | tf_op jit(solution)/shard_map/ppermute | solution.py:69
  56.3 0.6 collective-permute-start.15
  56.9 1.0 collective-permute-start.16
  57.9 2.4 %convolution_convert_fusion.v_ref = bf16[288,640]{1,0:T(8,128)(2,1)S(1)} fusion(bf16[288,5120]{1,0:T(8,128)(2,1)S(1)} %modulate.1, bf16[5120,640]{1,0:T(8,128)(2,1)S(1)} %bitcast.22), kind=kOutput, calls=%fused_computation | convolution fusion | flops 1887621120 | bytes 9871360 | tf_op jit(solution)/shard_map/dot_general | solution.py:638
  60.4 1.2 %collective-permute-start.17 = (bf16[2,2,720,128]{3,2,1,0:T(8,128)(2,1)S(1)}, bf16[2,2,720,128]{3,2,1,0:T(8,128)(2,1)S(1)}, u32[]{:S(2)}, u32[]{:S(2)}) collective-permute-start(bf16[2,2,720,128]{3,2,1,0:T(8,128)(2,1)S(1)} %collective-permute-done.11.refs_4_), channel_id=1, source_target_pairs={{0,24},{1,97},{2,26},{3,99},{4,28},{5,101},{6,30},{7,103},{8,16},{... | collective-permute-start | bytes 2211848 | tf_op jit(solution)/shard_map/ppermute | solution.py:69
  61.6 1.0 %fresh_attention.1 = (f32[2,5,144,128]{3,2,1,0:T(8,128)S(1)}, f32[24,128]{1,0:T(8,128)S(1)}) custom-call(s32[1]{0:T(128)} %bitcast.u_ref, bf16[288,640]{1,0:T(8,128)(2,1)S(1)} %copy-done.3, bf16[288,640]{1,0:T(8,128)(2,1)S(1)} %convolution_convert_fusion.v_ref, bf16[2,2,144,128]{3,2,1,0:T(8,128)(2,1)S(1)} %get-tuple-element.70.refs_0_, ...), custom_call_target="tpu_custom_call" | custom-call | flops 106168320 | bytes 2580480 | tf_op jit(solution)/shard_map/fresh_attention/pallas_call | solution.py:364
  62.6 2.0 %collective-permute-done.15.refs_2_ = bf16[2,2,144,128]{3,2,1,0:T(8,128)(2,1)S(1)} collective-permute-done((bf16[2,2,144,128]{3,2,1,0:T(8,128)(2,1)S(1)}, bf16[2,2,144,128]{3,2,1,0:T(8,128)(2,1)S(1)}, u32[]{:S(2)}, u32[]{:S(2)}) %collective-permute-start.15) | collective-permute-done | bytes 147488 | tf_op jit(solution)/shard_map/ppermute | solution.py:69
  64.6 1.6 %collective-permute-done.16.refs_3_ = bf16[2,2,144,128]{3,2,1,0:T(8,128)(2,1)S(1)} collective-permute-done((bf16[2,2,144,128]{3,2,1,0:T(8,128)(2,1)S(1)}, bf16[2,2,144,128]{3,2,1,0:T(8,128)(2,1)S(1)}, u32[]{:S(2)}, u32[]{:S(2)}) %collective-permute-start.16) | collective-permute-done | bytes 147488 | tf_op jit(solution)/shard_map/ppermute | solution.py:69
  66.2 0.3 collective-permute-done.13.refs_5_
  66.5 4.0 %collective-permute-start.18 = (bf16[2,2,720,128]{3,2,1,0:T(8,128)(2,1)S(1)}, bf16[2,2,720,128]{3,2,1,0:T(8,128)(2,1)S(1)}, u32[]{:S(2)}, u32[]{:S(2)}) collective-permute-start(bf16[2,2,720,128]{3,2,1,0:T(8,128)(2,1)S(1)} %collective-permute-done.13.refs_5_), channel_id=1, source_target_pairs={{0,24},{1,97},{2,26},{3,99},{4,28},{5,101},{6,30},{7,103},{8,16},{... | collective-permute-start | bytes 2211848 | tf_op jit(solution)/shard_map/ppermute | solution.py:69
  70.4 5.6 %near_attention.1 = (f32[2,4,2,144,128]{4,3,2,1,0:T(8,128)S(1)}, f32[2,4,2,144,128]{4,3,2,1,0:T(8,128)S(1)}) custom-call(bf16[2,2,144,128]{3,2,1,0:T(8,128)(2,1)S(1)} %get-tuple-element.70.refs_0_, bf16[2,2,144,128]{3,2,1,0:T(8,128)(2,1)S(1)} %collective-permute-done.14.refs_1_, bf16[2,2,144,128]{3,2,1,0:T(8,128)(2,1)S(1)} %collective-permute-done.15.refs_2_, ...), custom_call_target="tpu_custom_call" | custom-call | flops 1698693120 | bytes 2949120 | tf_op jit(solution)/shard_map/near_attention/pallas_call | solution.py:524
  76.0 5.0 %collective-permute-done.18.refs_7_ = bf16[2,2,720,128]{3,2,1,0:T(8,128)(2,1)S(1)} collective-permute-done((bf16[2,2,720,128]{3,2,1,0:T(8,128)(2,1)S(1)}, bf16[2,2,720,128]{3,2,1,0:T(8,128)(2,1)S(1)}, u32[]{:S(2)}, u32[]{:S(2)}) %collective-permute-start.18) | collective-permute-done | bytes 737312 | tf_op jit(solution)/shard_map/ppermute | solution.py:69
  81.0 6.3 %far_attention.1 = (bf16[2,304,128]{2,1,0:T(8,128)(2,1)S(1)}, bf16[2,304,128]{2,1,0:T(8,128)(2,1)S(1)}, bf16[2,304,128]{2,1,0:T(8,128)(2,1)S(1)}, bf16[2,304,128]{2,1,0:T(8,128)(2,1)S(1)}) custom-call(bf16[2,2,144,128]{3,2,1,0:T(8,128)(2,1)S(1)} %get-tuple-element.70.refs_0_, bf16[2,2,144,128]{3,2,1,0:T(8,128)(2,1)S(1)} %collective-permute-done.14.refs_1_, ...), custom_call_target="tpu_custom_call" | custom-call | flops 1698693120 | bytes 2949120 | tf_op jit(solution)/shard_map/far_attention/pallas_call | solution.py:524
  87.4 2.3 %collective-permute-start.19 = (bf16[2,304,128]{2,1,0:T(8,128)(2,1)S(1)}, bf16[2,304,128]{2,1,0:T(8,128)(2,1)S(1)}, u32[]{:S(2)}, u32[]{:S(2)}) collective-permute-start(bf16[2,304,128]{2,1,0:T(8,128)(2,1)S(1)} %get-tuple-element.80), channel_id=1, source_target_pairs={{0,96},{1,25},{2,98},{3,27},{4,100},{5,29},{6,102},{7,31},{8,104},... | collective-permute-start | bytes 466952 | tf_op jit(solution)/shard_map/ppermute | solution.py:69
  89.7 1.7 %collective-permute-start.20 = (bf16[2,304,128]{2,1,0:T(8,128)(2,1)S(1)}, bf16[2,304,128]{2,1,0:T(8,128)(2,1)S(1)}, u32[]{:S(2)}, u32[]{:S(2)}) collective-permute-start(bf16[2,304,128]{2,1,0:T(8,128)(2,1)S(1)} %get-tuple-element.81), channel_id=1, source_target_pairs={{0,64},{1,17},{2,66},{3,19},{4,68},{5,21},{6,70},{7,23},{8,72},{33... | collective-permute-start | bytes 466952 | tf_op jit(solution)/shard_map/ppermute | solution.py:69
  91.4 0.8 collective-permute-start.21
  92.2 0.5 collective-permute-done.19.refs_1_
  92.7 3.8 %collective-permute-done.20.refs_2_ = bf16[2,304,128]{2,1,0:T(8,128)(2,1)S(1)} collective-permute-done((bf16[2,304,128]{2,1,0:T(8,128)(2,1)S(1)}, bf16[2,304,128]{2,1,0:T(8,128)(2,1)S(1)}, u32[]{:S(2)}, u32[]{:S(2)}) %collective-permute-start.20) | collective-permute-done | bytes 155680 | tf_op jit(solution)/shard_map/ppermute | solution.py:69
  96.5 1.6 %collective-permute-done.21.refs_3_ = bf16[2,304,128]{2,1,0:T(8,128)(2,1)S(1)} collective-permute-done((bf16[2,304,128]{2,1,0:T(8,128)(2,1)S(1)}, bf16[2,304,128]{2,1,0:T(8,128)(2,1)S(1)}, u32[]{:S(2)}, u32[]{:S(2)}) %collective-permute-start.21) | collective-permute-done | bytes 155680 | tf_op jit(solution)/shard_map/ppermute | solution.py:69
  98.1 1.5 %merge.1 = bf16[2,144,640]{2,1,0:T(8,128)(2,1)} custom-call(s32[1]{0:T(128)} %bitcast.u_ref, f32[2,5,144,128]{3,2,1,0:T(8,128)S(1)} %get-tuple-element.66.fresh_out, f32[24,128]{1,0:T(8,128)S(1)} %get-tuple-element.69.refs_10_.fresh_rows, bf16[2,304,128]{2,1,0:T(8,128)(2,1)S(1)} %get-tuple-element.79.refs_0_, ...), custom_call_target="tpu_custom_call" | custom-call | flops 1843200 | bytes 2580480 | tf_op jit(solution)/shard_map/merge/pallas_call | solution.py:590
  (42 shorter events, 0.4 us)
Async XLA Ops:
  0.6 20.5 %collective-permute-start.4 = (bf16[288,1280]{1,0:T(8,128)(2,1)}, bf16[288,1280]{1,0:T(8,128)(2,1)S(1)}, u32[]{:S(2)}, u32[]{:S(2)}) collective-permute-start(bf16[288,1280]{1,0:T(8,128)(2,1)} %bitcast.14), channel_id=1, source_target_pairs={{0,2},{1,3},{2,0},{3,1},{4,6},{5,7},{6,4},{7,5},{8,10},{33,35},{10... | collective-permute-start | bytes 2211848 | tf_op jit(solution)/shard_map/ppermute | solution.py:69
  2.7 1.0 copy-start.1
  3.7 1.0 copy-start.2
  4.8 7.4 %collective-permute-start = (bf16[2,2,144,128]{3,2,1,0:T(8,128)(2,1)S(1)}, bf16[2,2,144,128]{3,2,1,0:T(8,128)(2,1)S(1)}, u32[]{:S(2)}, u32[]{:S(2)}) collective-permute-start(bf16[2,2,144,128]{3,2,1,0:T(8,128)(2,1)S(1)} %get-tuple-element.44), channel_id=1, source_target_pairs={{0,96},{1,25},{2,98},{3,27},{4,100},{5,29},{6,102},{7,31},{8,104},... | collective-permute-start | bytes 442376 | tf_op jit(solution)/shard_map/ppermute | solution.py:69
  7.9 6.8 %collective-permute-start.1 = (bf16[2,2,144,128]{3,2,1,0:T(8,128)(2,1)S(1)}, bf16[2,2,144,128]{3,2,1,0:T(8,128)(2,1)S(1)}, u32[]{:S(2)}, u32[]{:S(2)}) collective-permute-start(bf16[2,2,144,128]{3,2,1,0:T(8,128)(2,1)S(1)} %get-tuple-element.45), channel_id=1, source_target_pairs={{0,64},{1,17},{2,66},{3,19},{4,68},{5,21},{6,70},{7,23},{8,72},{33... | collective-permute-start | bytes 442376 | tf_op jit(solution)/shard_map/ppermute | solution.py:69
  8.5 7.6 %collective-permute-start.2 = (bf16[2,2,144,128]{3,2,1,0:T(8,128)(2,1)S(1)}, bf16[2,2,144,128]{3,2,1,0:T(8,128)(2,1)S(1)}, u32[]{:S(2)}, u32[]{:S(2)}) collective-permute-start(bf16[2,2,144,128]{3,2,1,0:T(8,128)(2,1)S(1)} %get-tuple-element.46), channel_id=1, source_target_pairs={{0,32},{1,9},{2,34},{3,11},{4,36},{5,13},{6,38},{7,15},{8,40},{33,... | collective-permute-start | bytes 442376 | tf_op jit(solution)/shard_map/ppermute | solution.py:69
  9.5 19.0 %collective-permute-start.3 = (bf16[288,1280]{1,0:T(8,128)(2,1)}, bf16[288,1280]{1,0:T(8,128)(2,1)S(1)}, u32[]{:S(2)}, u32[]{:S(2)}) collective-permute-start(bf16[288,1280]{1,0:T(8,128)(2,1)} %bitcast.15), channel_id=1, source_target_pairs={{0,1},{1,0},{2,3},{3,2},{4,5},{5,4},{6,7},{7,6},{8,9},{33,32},{10,... | collective-permute-start | bytes 2211848 | tf_op jit(solution)/shard_map/ppermute | solution.py:69
  16.2 1.1 %copy-start = (bf16[2,144,1280]{2,1,0:T(8,128)(2,1)S(1)}, bf16[2,144,1280]{2,1,0:T(8,128)(2,1)}, u32[]{:S(2)}) copy-start(bf16[2,144,1280]{2,1,0:T(8,128)(2,1)} %param.12) | copy-start | bytes 2211844
  17.3 0.8 copy-start.5
  18.1 0.8 copy-start.6
  18.9 0.7 copy-start.9
  19.5 0.7 copy-start.10
  21.2 7.4 %collective-permute-start.5 = (bf16[288,1280]{1,0:T(8,128)(2,1)S(1)}, bf16[288,1280]{1,0:T(8,128)(2,1)}, u32[]{:S(2)}, u32[]{:S(2)}) collective-permute-start(bf16[288,1280]{1,0:T(8,128)(2,1)S(1)} %collective-permute-done.4.h2), channel_id=1, source_target_pairs={{0,1},{1,0},{2,3},{3,2},{4,5},{5,4},{6,7},{7,6},{8,9},{33,32},{10,... | collective-permute-start | bytes 2211848 | tf_op jit(solution)/shard_map/ppermute | solution.py:69
  21.3 20.9 %collective-permute-start.6 = (bf16[2,2,720,128]{3,2,1,0:T(8,128)(2,1)S(1)}, bf16[2,2,720,128]{3,2,1,0:T(8,128)(2,1)S(1)}, u32[]{:S(2)}, u32[]{:S(2)}) collective-permute-start(bf16[2,2,720,128]{3,2,1,0:T(8,128)(2,1)S(1)} %assemble.1.after.refs_4_), channel_id=1, source_target_pairs={{0,8},{1,33},{2,10},{3,35},{4,12},{5,37},{6,14},{7,39},{8,0},{33,1... | collective-permute-start | bytes 2211848 | tf_op jit(solution)/shard_map/ppermute | solution.py:69
  22.9 19.4 %collective-permute-start.7 = (bf16[2,2,720,128]{3,2,1,0:T(8,128)(2,1)S(1)}, bf16[2,2,720,128]{3,2,1,0:T(8,128)(2,1)S(1)}, u32[]{:S(2)}, u32[]{:S(2)}) collective-permute-start(bf16[2,2,720,128]{3,2,1,0:T(8,128)(2,1)S(1)} %assemble.1.after.refs_4_), channel_id=1, source_target_pairs={{0,24},{1,97},{2,26},{3,99},{4,28},{5,101},{6,30},{7,103},{8,16},{... | collective-permute-start | bytes 2211848 | tf_op jit(solution)/shard_map/ppermute | solution.py:69
  24.9 24.3 %collective-permute-start.11 = (bf16[2,2,720,128]{3,2,1,0:T(8,128)(2,1)S(1)}, bf16[2,2,720,128]{3,2,1,0:T(8,128)(2,1)S(1)}, u32[]{:S(2)}, u32[]{:S(2)}) collective-permute-start(bf16[2,2,720,128]{3,2,1,0:T(8,128)(2,1)S(1)} %assemble.1.after.refs_4_), channel_id=1, source_target_pairs={{0,4},{1,5},{2,6},{3,7},{4,0},{5,1},{6,2},{7,3},{8,12},{33,37},{10... | collective-permute-start | bytes 2211848 | tf_op jit(solution)/shard_map/ppermute | solution.py:69
  28.5 11.0 %slice-start = ((s8[6553600]{0:T(1024)(128)(4,1)}), s8[4194304]{0:T(1024)(128)(4,1)S(1)}, s32[]{:S(2)}) async-start(s8[6553600]{0:T(1024)(128)(4,1)} %bitcast.19), calls=%async_computation | async-start | bytes 8388608
  34.1 5.5 %slice-start.1 = ((s8[6553600]{0:T(1024)(128)(4,1)}), s8[2359296]{0:T(1024)(128)(4,1)S(1)}, s32[]{:S(2)}) async-start(s8[6553600]{0:T(1024)(128)(4,1)} %bitcast.19), calls=%async_computation.1 | async-start | bytes 4718592
  34.1 23.8 %slice-start.2 = ((s8[6553600]{0:T(1024)(128)(4,1)}), s8[4194304]{0:T(1024)(128)(4,1)S(1)}, s32[]{:S(2)}) async-start(s8[6553600]{0:T(1024)(128)(4,1)} %bitcast.21), calls=%async_computation.2 | async-start | bytes 8388608
  39.6 7.9 %copy-start.7 = (f32[640]{0:T(1024)S(1)}, f32[640]{0:T(1024)}, u32[]{:S(2)}) copy-start(f32[640]{0:T(1024)} %qg.1) | copy-start | bytes 7684
  39.6 7.8 %copy-start.8 = (f32[640]{0:T(1024)S(1)}, f32[640]{0:T(1024)}, u32[]{:S(2)}) copy-start(f32[640]{0:T(1024)} %kg.1) | copy-start | bytes 7684
  39.6 18.3 %slice-start.3 = ((s8[6553600]{0:T(1024)(128)(4,1)}), s8[2359296]{0:T(1024)(128)(4,1)S(1)}, s32[]{:S(2)}) async-start(s8[6553600]{0:T(1024)(128)(4,1)} %bitcast.21), calls=%async_computation.3 | async-start | bytes 4718592
  42.3 12.7 %collective-permute-start.12 = (bf16[2,2,720,128]{3,2,1,0:T(8,128)(2,1)S(1)}, bf16[2,2,720,128]{3,2,1,0:T(8,128)(2,1)S(1)}, u32[]{:S(2)}, u32[]{:S(2)}) collective-permute-start(bf16[2,2,720,128]{3,2,1,0:T(8,128)(2,1)S(1)} %collective-permute-done.6.refs_5_), channel_id=1, source_target_pairs={{0,24},{1,97},{2,26},{3,99},{4,28},{5,101},{6,30},{7,103},{8,16},{... | collective-permute-start | bytes 2211848 | tf_op jit(solution)/shard_map/ppermute | solution.py:69
  43.5 2.1 %collective-permute-start.10 = (f32[8,384]{1,0:T(8,128)S(1)}, f32[8,384]{1,0:T(8,128)S(1)}, u32[]{:S(2)}, u32[]{:S(2)}) collective-permute-start(f32[8,384]{1,0:T(8,128)S(1)} %sum_squares.1.s0), channel_id=1, source_target_pairs={{0,1},{1,0},{2,3},{3,2},{4,5},{5,4},{6,7},{7,6},{8,9},{33,32},{10,... | collective-permute-start | bytes 36872 | tf_op jit(solution)/shard_map/ppermute | solution.py:69
  43.5 3.1 %collective-permute-start.8 = (f32[8,384]{1,0:T(8,128)S(1)}, f32[8,384]{1,0:T(8,128)S(1)}, u32[]{:S(2)}, u32[]{:S(2)}) collective-permute-start(f32[8,384]{1,0:T(8,128)S(1)} %sum_squares.1.s0), channel_id=1, source_target_pairs={{0,3},{1,2},{2,1},{3,0},{4,7},{5,6},{6,5},{7,4},{8,11},{33,34},{10... | collective-permute-start | bytes 36872 | tf_op jit(solution)/shard_map/ppermute | solution.py:69
  43.5 3.9 %collective-permute-start.9 = (f32[8,384]{1,0:T(8,128)S(1)}, f32[8,384]{1,0:T(8,128)S(1)}, u32[]{:S(2)}, u32[]{:S(2)}) collective-permute-start(f32[8,384]{1,0:T(8,128)S(1)} %sum_squares.1.s0), channel_id=1, source_target_pairs={{0,2},{1,3},{2,0},{3,1},{4,6},{5,7},{6,4},{7,5},{8,10},{33,35},{10... | collective-permute-start | bytes 36872 | tf_op jit(solution)/shard_map/ppermute | solution.py:69
  55.0 6.6 %copy-start.3 = (bf16[288,640]{1,0:T(8,128)(2,1)S(1)}, bf16[288,640]{1,0:T(8,128)(2,1)}, u32[]{:S(2)}) copy-start(bf16[288,640]{1,0:T(8,128)(2,1)} %get-tuple-element.56.k_ref) | copy-start | bytes 1105924
  55.0 11.5 %collective-permute-start.13 = (bf16[2,2,720,128]{3,2,1,0:T(8,128)(2,1)S(1)}, bf16[2,2,720,128]{3,2,1,0:T(8,128)(2,1)S(1)}, u32[]{:S(2)}, u32[]{:S(2)}) collective-permute-start(bf16[2,2,720,128]{3,2,1,0:T(8,128)(2,1)S(1)} %collective-permute-done.11.refs_4_), channel_id=1, source_target_pairs={{0,8},{1,33},{2,10},{3,35},{4,12},{5,37},{6,14},{7,39},{8,0},{33,1... | collective-permute-start | bytes 2211848 | tf_op jit(solution)/shard_map/ppermute | solution.py:69
  55.0 7.6 %collective-permute-start.14 = (bf16[2,2,144,128]{3,2,1,0:T(8,128)(2,1)S(1)}, bf16[2,2,144,128]{3,2,1,0:T(8,128)(2,1)S(1)}, u32[]{:S(2)}, u32[]{:S(2)}) collective-permute-start(bf16[2,2,144,128]{3,2,1,0:T(8,128)(2,1)S(1)} %get-tuple-element.65.refs_3_), channel_id=1, source_target_pairs={{0,96},{1,25},{2,98},{3,27},{4,100},{5,29},{6,102},{7,31},{8,104},... | collective-permute-start | bytes 442376 | tf_op jit(solution)/shard_map/ppermute | solution.py:69
  56.3 8.3 %collective-permute-start.15 = (bf16[2,2,144,128]{3,2,1,0:T(8,128)(2,1)S(1)}, bf16[2,2,144,128]{3,2,1,0:T(8,128)(2,1)S(1)}, u32[]{:S(2)}, u32[]{:S(2)}) collective-permute-start(bf16[2,2,144,128]{3,2,1,0:T(8,128)(2,1)S(1)} %get-tuple-element.64.refs_2_), channel_id=1, source_target_pairs={{0,64},{1,17},{2,66},{3,19},{4,68},{5,21},{6,70},{7,23},{8,72},{33... | collective-permute-start | bytes 442376 | tf_op jit(solution)/shard_map/ppermute | solution.py:69
  56.9 9.3 %collective-permute-start.16 = (bf16[2,2,144,128]{3,2,1,0:T(8,128)(2,1)S(1)}, bf16[2,2,144,128]{3,2,1,0:T(8,128)(2,1)S(1)}, u32[]{:S(2)}, u32[]{:S(2)}) collective-permute-start(bf16[2,2,144,128]{3,2,1,0:T(8,128)(2,1)S(1)} %get-tuple-element.63.refs_1_), channel_id=1, source_target_pairs={{0,32},{1,9},{2,34},{3,11},{4,36},{5,13},{6,38},{7,15},{8,40},{33,... | collective-permute-start | bytes 442376 | tf_op jit(solution)/shard_map/ppermute | solution.py:69
  60.3 27.0 %copy-start.4 = (bf16[288,640]{1,0:T(8,128)(2,1)}, bf16[288,640]{1,0:T(8,128)(2,1)S(1)}, u32[]{:S(2)}) copy-start(bf16[288,640]{1,0:T(8,128)(2,1)S(1)} %convolution_convert_fusion.v_ref) | copy-start | bytes 1105924
  60.4 15.7 %collective-permute-start.17 = (bf16[2,2,720,128]{3,2,1,0:T(8,128)(2,1)S(1)}, bf16[2,2,720,128]{3,2,1,0:T(8,128)(2,1)S(1)}, u32[]{:S(2)}, u32[]{:S(2)}) collective-permute-start(bf16[2,2,720,128]{3,2,1,0:T(8,128)(2,1)S(1)} %collective-permute-done.11.refs_4_), channel_id=1, source_target_pairs={{0,24},{1,97},{2,26},{3,99},{4,28},{5,101},{6,30},{7,103},{8,16},{... | collective-permute-start | bytes 2211848 | tf_op jit(solution)/shard_map/ppermute | solution.py:69
  66.5 14.5 %collective-permute-start.18 = (bf16[2,2,720,128]{3,2,1,0:T(8,128)(2,1)S(1)}, bf16[2,2,720,128]{3,2,1,0:T(8,128)(2,1)S(1)}, u32[]{:S(2)}, u32[]{:S(2)}) collective-permute-start(bf16[2,2,720,128]{3,2,1,0:T(8,128)(2,1)S(1)} %collective-permute-done.13.refs_5_), channel_id=1, source_target_pairs={{0,24},{1,97},{2,26},{3,99},{4,28},{5,101},{6,30},{7,103},{8,16},{... | collective-permute-start | bytes 2211848 | tf_op jit(solution)/shard_map/ppermute | solution.py:69
  87.4 5.3 %collective-permute-start.19 = (bf16[2,304,128]{2,1,0:T(8,128)(2,1)S(1)}, bf16[2,304,128]{2,1,0:T(8,128)(2,1)S(1)}, u32[]{:S(2)}, u32[]{:S(2)}) collective-permute-start(bf16[2,304,128]{2,1,0:T(8,128)(2,1)S(1)} %get-tuple-element.80), channel_id=1, source_target_pairs={{0,96},{1,25},{2,98},{3,27},{4,100},{5,29},{6,102},{7,31},{8,104},... | collective-permute-start | bytes 466952 | tf_op jit(solution)/shard_map/ppermute | solution.py:69
  89.7 6.8 %collective-permute-start.20 = (bf16[2,304,128]{2,1,0:T(8,128)(2,1)S(1)}, bf16[2,304,128]{2,1,0:T(8,128)(2,1)S(1)}, u32[]{:S(2)}, u32[]{:S(2)}) collective-permute-start(bf16[2,304,128]{2,1,0:T(8,128)(2,1)S(1)} %get-tuple-element.81), channel_id=1, source_target_pairs={{0,64},{1,17},{2,66},{3,19},{4,68},{5,21},{6,70},{7,23},{8,72},{33... | collective-permute-start | bytes 466952 | tf_op jit(solution)/shard_map/ppermute | solution.py:69
  91.4 6.7 %collective-permute-start.21 = (bf16[2,304,128]{2,1,0:T(8,128)(2,1)S(1)}, bf16[2,304,128]{2,1,0:T(8,128)(2,1)S(1)}, u32[]{:S(2)}, u32[]{:S(2)}) collective-permute-start(bf16[2,304,128]{2,1,0:T(8,128)(2,1)S(1)} %get-tuple-element.82), channel_id=1, source_target_pairs={{0,32},{1,9},{2,34},{3,11},{4,36},{5,13},{6,38},{7,15},{8,40},{33,... | collective-permute-start | bytes 466952 | tf_op jit(solution)/shard_map/ppermute | solution.py:69

commit v5 on v4

--- a/solution.py
+++ b/solution.py
@@ -193,7 +193,7 @@
         ],
         compiler_params=params(VMEM_MIB),
         cost_estimate=pl.CostEstimate(
-            flops=100 * TOK * HD, bytes_accessed=40_000_000, transcendentals=0
+            flops=100 * TOK * HD, bytes_accessed=1_000_000, transcendentals=0
         ),
         name="tables",
     )(token_place, jnp.asarray(frequencies()), rows, shift, scale, after)
@@ -221,25 +221,29 @@
     )(*parts)
 
 
+def lane_sum(parts):
+    total = None
+    for part in parts:
+        for at in range(0, part.shape[1], HD):
+            piece = part[:, at : at + HD]
+            total = piece if total is None else total + piece
+    return jnp.sum(total, axis=1, keepdims=True)
+
+
 def modulate_kernel(t_ref, h0, h1, h2, h3, cond, mod, out_ref):
     chunks = (h0, h1, h2, h3)
     for row in range(0, ROWS, GROUP):
         rows = slice(row, row + GROUP)
-        total = jnp.zeros((GROUP, 1), F32)
-        for chunk in chunks:
-            total = total + jnp.sum(chunk[rows].astype(F32), axis=1, keepdims=True)
-        mean = total * (1.0 / D)
-        deviation = jnp.zeros((GROUP, 1), F32)
-        for chunk in chunks:
-            centered = chunk[rows].astype(F32) - mean
-            deviation = deviation + jnp.sum(centered * centered, axis=1, keepdims=True)
+        lanes = [chunk[rows].astype(F32) for chunk in chunks]
+        mean = lane_sum([(lanes[0] + lanes[1]) + (lanes[2] + lanes[3])]) * (1.0 / D)
+        deviation = lane_sum([(part - mean) * (part - mean) for part in lanes])
         rstd = lax.rsqrt(deviation * (1.0 / D) + EPS)
         conditioned = cond[rows, 0:1] > 0.5
         for c in range(TP):
             cols = pl.ds(pl.multiple_of(t_ref[c] * CHUNK, CHUNK), CHUNK)
             gain = jnp.where(conditioned, mod[1:2, cols], mod[0:1, cols])
             bias = jnp.where(conditioned, mod[3:4, cols], mod[2:3, cols])
-            normed = (chunks[c][rows].astype(F32) - mean) * rstd
+            normed = (lanes[c] - mean) * rstd
             out_ref[rows, cols] = (normed * gain + bias).astype(BF16)
 
 
@@ -251,7 +255,7 @@
         out_specs=vmem(),
         compiler_params=params(VMEM_MIB),
         cost_estimate=pl.CostEstimate(
-            flops=12 * ROWS * D, bytes_accessed=20_000_000, transcendentals=0
+            flops=12 * ROWS * D, bytes_accessed=45_000_000, transcendentals=0
         ),
         name="modulate",
     )(blocks, *chunks, cond, mod)
@@ -625,29 +629,29 @@
     packed = pack_stale(u, stale_keys, stale_values)
     arrived = exchange_u(packed)
     near = assemble([*arrived, packed[4]])
+    cond, cos, sin, mod, own_rows = tables(token_place, own_rows, mod_shift, mod_scale, near)
     near_one, near_three = swap_v(near, 1), swap_v(near, 3)
     far = swap_z_hi(near)
-    cond, cos, sin, mod, own_rows = tables(token_place, own_rows, mod_shift, mod_scale, near)
 
     z_rows, cond = lax.optimization_barrier((z_rows, cond))
     cross_rows = swap_tp(z_rows, 0, 1)
+    near_two = swap_v(near_one, 3)
     blocks = jnp.stack([tp, tp ^ 1, tp ^ 2, tp ^ 3]).astype(jnp.int32)
     modded = modulate(blocks, [own_rows, core_rows, z_rows, cross_rows], cond, mod)
     query = jnp.dot(modded, w_query, preferred_element_type=F32)
     key = jnp.dot(modded, w_key, preferred_element_type=F32)
     fresh_values = jnp.dot(modded, w_value, preferred_element_type=F32).astype(BF16)
     own_sq = sum_squares(query, key)
-    own_sq, near_one, near_three = lax.optimization_barrier((own_sq, near_one, near_three))
+    own_sq, near_three = lax.optimization_barrier((own_sq, near_three))
     squares = [own_sq] + [swap_tp(own_sq, z, c) for z, c in ((1, 1), (1, 0), (0, 1))]
-    near_two = swap_v(near_one, 3)
+    near_two, *squares = lax.optimization_barrier((near_two, *squares))
+    far_two = swap_z_hi(near_two)
     fresh_keys, *sends = norm_rope(u, query, key, squares, q_gain, k_gain, cos, sin)
-    far, near_two, *sends = lax.optimization_barrier((far, near_two, *sends))
-    far_one, far_three = swap_v(far, 1), swap_v(far, 3)
     queries = exchange_u(sends)
     fresh_out, fresh_rows = fresh_attention(u, fresh_keys, fresh_values, sends)
-
-    far_one, fresh_rows, *queries = lax.optimization_barrier((far_one, fresh_rows, *queries))
-    far_two = swap_v(far_one, 3)
+    far, *queries = lax.optimization_barrier((far, *queries))
+    far_one, far_three = swap_v(far, 1), swap_v(far, 3)
+
     partial = stale_attention(queries, [near, near_one, near_three, near_two])
     outs = stale_attention(
         queries, [far, far_one, far_three, far_two], near=partial, after=fresh_rows

time: 100 us -> 90.5 us (0.905)
  waiting for transfers between devices: 29 us -> 20.6 us
  starting transfers between devices: 30.2 us -> 29.1 us
    ppermute x22, waiting for transfers between devices: 29 us -> 20.6 us  [permute(): lax.ppermute(value, AXES, [(linear(*p), linear(*move(*p))) for p in place...]
    dot_general x1, matrix products: 5.45 us -> 2.43 us  [shards(): query = jnp.dot(modded, w_query, preferred_element_type=F32)]
    dot_general x1, matrix products: 2.43 us -> 5.44 us  [shards(): key = jnp.dot(modded, w_key, preferred_element_type=F32)]
    pallas_call x1, Pallas kernels: 5.5 us -> 4.24 us  [modulate(): pl.pallas_call(modulate_kernel, out_shape=jax.ShapeDtypeStruct((ROWS, D),...]
    pallas_call x2, Pallas kernels: 11.9 us -> 13.1 us  [stale_attention(): pl.pallas_call(functools.partial(stale_kernel, far), out_shape=out_shape,...]
    ppermute x22, starting transfers between devices: 30.2 us -> 29.1 us  [permute(): lax.ppermute(value, AXES, [(linear(*p), linear(*move(*p))) for p in place...]
  transfers between devices with their start and end apart: 22 -> 22, of which waited for: 13 -> 11; matrix products, arithmetic and copies ran while one was open for 10% -> 12% of each run, Pallas kernels for 15% -> 17%
where the time goes in v5:
time: 90.5 us; the launch traced here: 90.1 us
  starting transfers between devices  29.1 us (32%)
  Pallas kernels  23.1 us (26%)
  waiting for transfers between devices  20.6 us (23%)
  matrix products  10.3 us (11%)
  local copies, waits for them, and re-layouts  6.03 us (7%)
    ppermute x22, starting transfers between devices, permute(): lax.ppermute(value, AXES, [(linear(*p), linear(*move(*p))) for p in place...  29.1 us
    ppermute x22, waiting for transfers between devices, permute(): lax.ppermute(value, AXES, [(linear(*p), linear(*move(*p))) for p in place...  20.6 us
    pallas_call x2, Pallas kernels, stale_attention(): pl.pallas_call(functools.partial(stale_kernel, far), out_shape=out_shape,...  13.1 us
    unnamed x30, local copies, waits for them, and re-layouts  6.03 us
    dot_general x1, matrix products, shards(): key = jnp.dot(modded, w_key, preferred_element_type=F32)  5.44 us
    pallas_call x1, Pallas kernels, modulate(): pl.pallas_call(modulate_kernel, out_shape=jax.ShapeDtypeStruct((ROWS, D),...  4.24 us
    dot_general x1, matrix products, shards(): jnp.dot(modded, w_value, preferred_element_type=F32).astype(BF16)  2.44 us
    dot_general x1, matrix products, shards(): query = jnp.dot(modded, w_query, preferred_element_type=F32)  2.43 us
  transfers between devices with their start and end apart: 22, of which 11 were waited for; matrix products, arithmetic and copies ran while one was open for 12% of the time, Pallas kernels for 17%

profile of v5, /device:TPU:0, one launch (start us, length us, event | category | flops | bytes accessed | tf_op | source)
XLA Modules:
  0.0 90.1 jit_solution(9366509304393190087)
XLA Ops:
  0.6 2.1 %collective-permute-start.4 = (bf16[288,1280]{1,0:T(8,128)(2,1)}, bf16[288,1280]{1,0:T(8,128)(2,1)S(1)}, u32[]{:S(2)}, u32[]{:S(2)}) collective-permute-start(bf16[288,1280]{1,0:T(8,128)(2,1)} %bitcast.14), channel_id=1, source_target_pairs={{0,2},{1,3},{2,0},{3,1},{4,6},{5,7},{6,4},{7,5},{8,10},{33,35},{10... | collective-permute-start | bytes 2211848 | tf_op jit(solution)/shard_map/ppermute | solution.py:69
  2.7 1.0 %copy-done.1 = bf16[2,144,640]{2,1,0:T(8,128)(2,1)S(1)} copy-done((bf16[2,144,640]{2,1,0:T(8,128)(2,1)S(1)}, bf16[2,144,640]{2,1,0:T(8,128)(2,1)}, u32[]{:S(2)}) %copy-start.1) | copy-done | bytes 368664
  3.7 1.0 %copy-done.2 = bf16[2,144,640]{2,1,0:T(8,128)(2,1)S(1)} copy-done((bf16[2,144,640]{2,1,0:T(8,128)(2,1)S(1)}, bf16[2,144,640]{2,1,0:T(8,128)(2,1)}, u32[]{:S(2)}) %copy-start.2) | copy-done | bytes 368664
  4.7 0.1 pack_stale.1
  4.8 3.1 %collective-permute-start = (bf16[2,2,144,128]{3,2,1,0:T(8,128)(2,1)S(1)}, bf16[2,2,144,128]{3,2,1,0:T(8,128)(2,1)S(1)}, u32[]{:S(2)}, u32[]{:S(2)}) collective-permute-start(bf16[2,2,144,128]{3,2,1,0:T(8,128)(2,1)S(1)} %get-tuple-element.41), channel_id=1, source_target_pairs={{0,96},{1,25},{2,98},{3,27},{4,100},{5,29},{6,102},{7,31},{8,104},... | collective-permute-start | bytes 442376 | tf_op jit(solution)/shard_map/ppermute | solution.py:69
  7.9 0.6 collective-permute-start.1
  8.5 1.0 %collective-permute-start.2 = (bf16[2,2,144,128]{3,2,1,0:T(8,128)(2,1)S(1)}, bf16[2,2,144,128]{3,2,1,0:T(8,128)(2,1)S(1)}, u32[]{:S(2)}, u32[]{:S(2)}) collective-permute-start(bf16[2,2,144,128]{3,2,1,0:T(8,128)(2,1)S(1)} %get-tuple-element.43), channel_id=1, source_target_pairs={{0,32},{1,9},{2,34},{3,11},{4,36},{5,13},{6,38},{7,15},{8,40},{33,... | collective-permute-start | bytes 442376 | tf_op jit(solution)/shard_map/ppermute | solution.py:69
  9.5 2.7 %collective-permute-done.refs_1_ = bf16[2,2,144,128]{3,2,1,0:T(8,128)(2,1)S(1)} collective-permute-done((bf16[2,2,144,128]{3,2,1,0:T(8,128)(2,1)S(1)}, bf16[2,2,144,128]{3,2,1,0:T(8,128)(2,1)S(1)}, u32[]{:S(2)}, u32[]{:S(2)}) %collective-permute-start) | collective-permute-done | bytes 147488 | tf_op jit(solution)/shard_map/ppermute | solution.py:69
  12.2 2.5 %collective-permute-done.1.refs_2_ = bf16[2,2,144,128]{3,2,1,0:T(8,128)(2,1)S(1)} collective-permute-done((bf16[2,2,144,128]{3,2,1,0:T(8,128)(2,1)S(1)}, bf16[2,2,144,128]{3,2,1,0:T(8,128)(2,1)S(1)}, u32[]{:S(2)}, u32[]{:S(2)}) %collective-permute-start.1) | collective-permute-done | bytes 147488 | tf_op jit(solution)/shard_map/ppermute | solution.py:69
  14.7 1.5 %collective-permute-done.2.refs_3_ = bf16[2,2,144,128]{3,2,1,0:T(8,128)(2,1)S(1)} collective-permute-done((bf16[2,2,144,128]{3,2,1,0:T(8,128)(2,1)S(1)}, bf16[2,2,144,128]{3,2,1,0:T(8,128)(2,1)S(1)}, u32[]{:S(2)}, u32[]{:S(2)}) %collective-permute-start.2) | collective-permute-done | bytes 147488 | tf_op jit(solution)/shard_map/ppermute | solution.py:69
  16.2 1.6 %collective-permute-start.6 = (bf16[2,2,720,128]{3,2,1,0:T(8,128)(2,1)S(1)}, bf16[2,2,720,128]{3,2,1,0:T(8,128)(2,1)}, u32[]{:S(2)}, u32[]{:S(2)}) collective-permute-start(bf16[2,2,720,128]{3,2,1,0:T(8,128)(2,1)S(1)} %assemble.1.after.refs_4_), channel_id=1, source_target_pairs={{0,8},{1,33},{2,10},{3,35},{4,12},{5,37},{6,14},{7,39},{8,0},{33,1... | collective-permute-start | bytes 2211848 | tf_op jit(solution)/shard_map/ppermute | solution.py:69
  17.8 1.1 %copy-done = bf16[2,144,1280]{2,1,0:T(8,128)(2,1)S(1)} copy-done((bf16[2,144,1280]{2,1,0:T(8,128)(2,1)S(1)}, bf16[2,144,1280]{2,1,0:T(8,128)(2,1)}, u32[]{:S(2)}) %copy-start) | copy-done | bytes 737304
  18.9 0.8 copy-done.5
  19.7 0.8 copy-done.6
  20.4 0.7 copy-done.9
  21.1 0.7 copy-done.10
  21.8 0.9 %tables.1 = (f32[288,128]{1,0:T(8,128)S(1)}, f32[144,128]{1,0:T(8,128)S(1)}, f32[144,128]{1,0:T(8,128)S(1)}, f32[4,5120]{1,0:T(4,128)S(1)}, bf16[288,1280]{1,0:T(8,128)(2,1)S(1)}) custom-call(s32[144]{0:T(256)S(1)} %copy-done.9, f32[1,128]{1,0:T(1,128)S(1)} %copy-done.10, bf16[288,1280]{1,0:T(8,128)(2,1)S(1)} %bitcast.16, f32[2,5120]{1,0:T(2,128)S(1)} %copy-done.5, ...), custom_call_target="tpu_custom_call" | custom-call | flops 1843200 | bytes 1000000 | tf_op jit(solution)/shard_map/tables/pallas_call | solution.py:176
  22.7 0.1 collective-permute-start.5
  22.9 3.6 %collective-permute-start.12 = (bf16[2,2,720,128]{3,2,1,0:T(8,128)(2,1)S(1)}, bf16[2,2,720,128]{3,2,1,0:T(8,128)(2,1)S(1)}, u32[]{:S(2)}, u32[]{:S(2)}) collective-permute-start(bf16[2,2,720,128]{3,2,1,0:T(8,128)(2,1)S(1)} %assemble.1.after.refs_4_), channel_id=1, source_target_pairs={{0,4},{1,5},{2,6},{3,7},{4,0},{5,1},{6,2},{7,3},{8,12},{33,37},{10... | collective-permute-start | bytes 2211848 | tf_op jit(solution)/shard_map/ppermute | solution.py:69
  26.5 2.1 %collective-permute-start.8 = (bf16[2,2,720,128]{3,2,1,0:T(8,128)(2,1)S(1)}, bf16[2,2,720,128]{3,2,1,0:T(8,128)(2,1)S(1)}, u32[]{:S(2)}, u32[]{:S(2)}) collective-permute-start(bf16[2,2,720,128]{3,2,1,0:T(8,128)(2,1)S(1)} %assemble.1.after.refs_4_), channel_id=1, source_target_pairs={{0,24},{1,97},{2,26},{3,99},{4,28},{5,101},{6,30},{7,103},{8,16},{... | collective-permute-start | bytes 2211848 | tf_op jit(solution)/shard_map/ppermute | solution.py:69
  28.6 2.0 %collective-permute-start.7 = (bf16[2,2,720,128]{3,2,1,0:T(8,128)(2,1)}, bf16[2,2,720,128]{3,2,1,0:T(8,128)(2,1)S(1)}, u32[]{:S(2)}, u32[]{:S(2)}) collective-permute-start(bf16[2,2,720,128]{3,2,1,0:T(8,128)(2,1)} %collective-permute-done.6.refs_5_), channel_id=1, source_target_pairs={{0,24},{1,97},{2,26},{3,99},{4,28},{5,101},{6,30},{7,103},{8,16},{... | collective-permute-start | bytes 2211848 | tf_op jit(solution)/shard_map/ppermute | solution.py:69
  30.6 4.2 %modulate.1 = bf16[288,5120]{1,0:T(8,128)(2,1)S(1)} custom-call(s32[4]{0:T(128)S(1)} %pad_add_fusion.t_ref, bf16[288,1280]{1,0:T(8,128)(2,1)S(1)} %get-tuple-element.45.h0, bf16[288,1280]{1,0:T(8,128)(2,1)S(1)} %collective-permute-done.3.h1, bf16[288,1280]{1,0:T(8,128)(2,1)S(1)} %collective-permute-done.4.h2, bf16[288,1280]{1,0:T(8,128)(2,1)} %collective-permute-done.5.h3, ...), custom_call_target="tpu_custom_call" | custom-call | flops 17694720 | bytes 45000000 | tf_op jit(solution)/shard_map/modulate/pallas_call | solution.py:251
  34.9 5.4 %fusion.1.k_ref = f32[288,640]{1,0:T(8,128)S(1)} fusion(bf16[288,5120]{1,0:T(8,128)(2,1)S(1)} %modulate.1, bf16[5120,640]{1,0:T(8,128)(2,1)} %param.16), kind=kOutput, calls=%fused_computation.3 | convolution fusion | flops 1887436800 | bytes 10240000 | tf_op jit(solution)/shard_map/dot_general | solution.py:642
  40.4 2.4 %fusion.q_ref = f32[288,640]{1,0:T(8,128)S(1)} fusion(bf16[288,5120]{1,0:T(8,128)(2,1)S(1)} %modulate.1, bf16[5120,640]{1,0:T(8,128)(2,1)S(1)} %bitcast.20), kind=kOutput, calls=%fused_computation.2 | convolution fusion | flops 1887436800 | bytes 10240000 | tf_op jit(solution)/shard_map/dot_general | solution.py:641
  42.8 0.2 sum_squares.1.s0
  43.1 0.2 collective-permute-start.10
  43.3 1.7 %collective-permute-start.9 = (f32[8,384]{1,0:T(8,128)S(1)}, f32[8,384]{1,0:T(8,128)S(1)}, u32[]{:S(2)}, u32[]{:S(2)}) collective-permute-start(f32[8,384]{1,0:T(8,128)S(1)} %sum_squares.1.s0), channel_id=1, source_target_pairs={{0,3},{1,2},{2,1},{3,0},{4,7},{5,6},{6,5},{7,4},{8,11},{33,34},{10... | collective-permute-start | bytes 36872 | tf_op jit(solution)/shard_map/ppermute | solution.py:69
  45.0 1.9 %collective-permute-done.10.s2 = f32[8,384]{1,0:T(8,128)S(1)} collective-permute-done((f32[8,384]{1,0:T(8,128)S(1)}, f32[8,384]{1,0:T(8,128)S(1)}, u32[]{:S(2)}, u32[]{:S(2)}) %collective-permute-start.10) | collective-permute-done | bytes 12320 | tf_op jit(solution)/shard_map/ppermute | solution.py:69
  46.9 0.2 collective-permute-done.7.refs_7_
  47.1 1.8 %norm_rope.1 = (bf16[288,640]{1,0:T(8,128)(2,1)}, bf16[2,2,144,128]{3,2,1,0:T(8,128)(2,1)S(1)}, bf16[2,2,144,128]{3,2,1,0:T(8,128)(2,1)S(1)}, bf16[2,2,144,128]{...) custom-call(s32[1]{0:T(128)} %bitcast.u_ref, f32[288,640]{1,0:T(8,128)S(1)} %fusion.q_ref, f32[288,640]{1,0:T(8,128)S(1)} %fusion.1.k_ref, ...), custom_call_target="tpu_custom_call" | custom-call | flops 3686400 | bytes 2949120 | tf_op jit(solution)/shard_map/norm_rope/pallas_call | solution.py:316
  48.9 2.0 %collective-permute-start.14 = (bf16[2,2,144,128]{3,2,1,0:T(8,128)(2,1)S(1)}, bf16[2,2,144,128]{3,2,1,0:T(8,128)(2,1)S(1)}, u32[]{:S(2)}, u32[]{:S(2)}) collective-permute-start(bf16[2,2,144,128]{3,2,1,0:T(8,128)(2,1)S(1)} %get-tuple-element.60.refs_2_), channel_id=1, source_target_pairs={{0,64},{1,17},{2,66},{3,19},{4,68},{5,21},{6,70},{7,23},{8,72},{33... | collective-permute-start | bytes 442376 | tf_op jit(solution)/shard_map/ppermute | solution.py:69
  50.9 1.2 %collective-permute-start.13 = (bf16[2,2,144,128]{3,2,1,0:T(8,128)(2,1)S(1)}, bf16[2,2,144,128]{3,2,1,0:T(8,128)(2,1)S(1)}, u32[]{:S(2)}, u32[]{:S(2)}) collective-permute-start(bf16[2,2,144,128]{3,2,1,0:T(8,128)(2,1)S(1)} %get-tuple-element.61.refs_3_), channel_id=1, source_target_pairs={{0,96},{1,25},{2,98},{3,27},{4,100},{5,29},{6,102},{7,31},{8,104},... | collective-permute-start | bytes 442376 | tf_op jit(solution)/shard_map/ppermute | solution.py:69
  52.1 3.4 %collective-permute-start.18 = (bf16[2,2,720,128]{3,2,1,0:T(8,128)(2,1)S(1)}, bf16[2,2,720,128]{3,2,1,0:T(8,128)(2,1)S(1)}, u32[]{:S(2)}, u32[]{:S(2)}) collective-permute-start(bf16[2,2,720,128]{3,2,1,0:T(8,128)(2,1)S(1)} %collective-permute-done.7.refs_7_), channel_id=1, source_target_pairs={{0,4},{1,5},{2,6},{3,7},{4,0},{5,1},{6,2},{7,3},{8,12},{33,37},{10... | collective-permute-start | bytes 2211848 | tf_op jit(solution)/shard_map/ppermute | solution.py:69
  55.6 1.3 %collective-permute-done.15.refs_3_ = bf16[2,2,144,128]{3,2,1,0:T(8,128)(2,1)S(1)} collective-permute-done((bf16[2,2,144,128]{3,2,1,0:T(8,128)(2,1)S(1)}, bf16[2,2,144,128]{3,2,1,0:T(8,128)(2,1)S(1)}, u32[]{:S(2)}, u32[]{:S(2)}) %collective-permute-start.15) | collective-permute-done | bytes 147488 | tf_op jit(solution)/shard_map/ppermute | solution.py:69
  56.8 0.9 collective-permute-done.13.refs_1_
  57.7 2.1 %collective-permute-start.17 = (bf16[2,2,720,128]{3,2,1,0:T(8,128)(2,1)S(1)}, bf16[2,2,720,128]{3,2,1,0:T(8,128)(2,1)S(1)}, u32[]{:S(2)}, u32[]{:S(2)}) collective-permute-start(bf16[2,2,720,128]{3,2,1,0:T(8,128)(2,1)S(1)} %collective-permute-done.12.refs_4_), channel_id=1, source_target_pairs={{0,24},{1,97},{2,26},{3,99},{4,28},{5,101},{6,30},{7,103},{8,16},{... | collective-permute-start | bytes 2211848 | tf_op jit(solution)/shard_map/ppermute | solution.py:69
  59.8 2.4 %convolution_convert_fusion.v_ref = bf16[288,640]{1,0:T(8,128)(2,1)S(1)} fusion(bf16[288,5120]{1,0:T(8,128)(2,1)S(1)} %modulate.1, bf16[5120,640]{1,0:T(8,128)(2,1)S(1)} %bitcast.22), kind=kOutput, calls=%fused_computation | convolution fusion | flops 1887621120 | bytes 9871360 | tf_op jit(solution)/shard_map/dot_general | solution.py:643
  62.3 1.0 %fresh_attention.1 = (f32[2,5,144,128]{3,2,1,0:T(8,128)S(1)}, f32[24,128]{1,0:T(8,128)S(1)}) custom-call(s32[1]{0:T(128)} %bitcast.u_ref, bf16[288,640]{1,0:T(8,128)(2,1)S(1)} %copy-done.3, bf16[288,640]{1,0:T(8,128)(2,1)S(1)} %convolution_convert_fusion.v_ref, bf16[2,2,144,128]{3,2,1,0:T(8,128)(2,1)S(1)} %get-tuple-element.64.refs_0_, ...), custom_call_target="tpu_custom_call" | custom-call | flops 106168320 | bytes 2580480 | tf_op jit(solution)/shard_map/fresh_attention/pallas_call | solution.py:368
  63.3 6.6 %near_attention.1 = (f32[2,4,2,144,128]{4,3,2,1,0:T(8,128)S(1)}, f32[2,4,2,144,128]{4,3,2,1,0:T(8,128)S(1)}) custom-call(bf16[2,2,144,128]{3,2,1,0:T(8,128)(2,1)S(1)} %get-tuple-element.64.refs_0_, bf16[2,2,144,128]{3,2,1,0:T(8,128)(2,1)S(1)} %collective-permute-done.13.refs_1_, bf16[2,2,144,128]{3,2,1,0:T(8,128)(2,1)S(1)} %collective-permute-done.14.refs_2_, ...), custom_call_target="tpu_custom_call" | custom-call | flops 1698693120 | bytes 2949120 | tf_op jit(solution)/shard_map/near_attention/pallas_call | solution.py:528
  70.0 2.4 %collective-permute-done.18.refs_7_ = bf16[2,2,720,128]{3,2,1,0:T(8,128)(2,1)S(1)} collective-permute-done((bf16[2,2,720,128]{3,2,1,0:T(8,128)(2,1)S(1)}, bf16[2,2,720,128]{3,2,1,0:T(8,128)(2,1)S(1)}, u32[]{:S(2)}, u32[]{:S(2)}) %collective-permute-start.18) | collective-permute-done | bytes 737312 | tf_op jit(solution)/shard_map/ppermute | solution.py:69
  72.4 6.5 %far_attention.1 = (bf16[2,304,128]{2,1,0:T(8,128)(2,1)S(1)}, bf16[2,304,128]{2,1,0:T(8,128)(2,1)S(1)}, bf16[2,304,128]{2,1,0:T(8,128)(2,1)S(1)}, bf16[2,304,128]{2,1,0:T(8,128)(2,1)S(1)}) custom-call(bf16[2,2,144,128]{3,2,1,0:T(8,128)(2,1)S(1)} %get-tuple-element.64.refs_0_, bf16[2,2,144,128]{3,2,1,0:T(8,128)(2,1)S(1)} %collective-permute-done.13.refs_1_, ...), custom_call_target="tpu_custom_call" | custom-call | flops 1698693120 | bytes 2949120 | tf_op jit(solution)/shard_map/far_attention/pallas_call | solution.py:528
  78.9 1.3 %collective-permute-start.19 = (bf16[2,304,128]{2,1,0:T(8,128)(2,1)S(1)}, bf16[2,304,128]{2,1,0:T(8,128)(2,1)S(1)}, u32[]{:S(2)}, u32[]{:S(2)}) collective-permute-start(bf16[2,304,128]{2,1,0:T(8,128)(2,1)S(1)} %get-tuple-element.74), channel_id=1, source_target_pairs={{0,96},{1,25},{2,98},{3,27},{4,100},{5,29},{6,102},{7,31},{8,104},... | collective-permute-start | bytes 466952 | tf_op jit(solution)/shard_map/ppermute | solution.py:69
  80.2 0.1 collective-permute-start.20
  80.4 0.8 collective-permute-start.21
  81.2 3.0 %collective-permute-done.19.refs_1_ = bf16[2,304,128]{2,1,0:T(8,128)(2,1)S(1)} collective-permute-done((bf16[2,304,128]{2,1,0:T(8,128)(2,1)S(1)}, bf16[2,304,128]{2,1,0:T(8,128)(2,1)S(1)}, u32[]{:S(2)}, u32[]{:S(2)}) %collective-permute-start.19) | collective-permute-done | bytes 155680 | tf_op jit(solution)/shard_map/ppermute | solution.py:69
  84.2 2.9 %collective-permute-done.20.refs_2_ = bf16[2,304,128]{2,1,0:T(8,128)(2,1)S(1)} collective-permute-done((bf16[2,304,128]{2,1,0:T(8,128)(2,1)S(1)}, bf16[2,304,128]{2,1,0:T(8,128)(2,1)S(1)}, u32[]{:S(2)}, u32[]{:S(2)}) %collective-permute-start.20) | collective-permute-done | bytes 155680 | tf_op jit(solution)/shard_map/ppermute | solution.py:69
  87.1 1.5 %collective-permute-done.21.refs_3_ = bf16[2,304,128]{2,1,0:T(8,128)(2,1)S(1)} collective-permute-done((bf16[2,304,128]{2,1,0:T(8,128)(2,1)S(1)}, bf16[2,304,128]{2,1,0:T(8,128)(2,1)S(1)}, u32[]{:S(2)}, u32[]{:S(2)}) %collective-permute-start.21) | collective-permute-done | bytes 155680 | tf_op jit(solution)/shard_map/ppermute | solution.py:69
  88.6 1.5 %merge.1 = bf16[2,144,640]{2,1,0:T(8,128)(2,1)} custom-call(s32[1]{0:T(128)} %bitcast.u_ref, f32[2,5,144,128]{3,2,1,0:T(8,128)S(1)} %get-tuple-element.62.fresh_out, f32[24,128]{1,0:T(8,128)S(1)} %get-tuple-element.63.refs_10_.fresh_rows, bf16[2,304,128]{2,1,0:T(8,128)(2,1)S(1)} %get-tuple-element.73.refs_0_, ...), custom_call_target="tpu_custom_call" | custom-call | flops 1843200 | bytes 2580480 | tf_op jit(solution)/shard_map/merge/pallas_call | solution.py:594
  (42 shorter events, 0.3 us)
Async XLA Ops:
  0.6 22.1 %collective-permute-start.4 = (bf16[288,1280]{1,0:T(8,128)(2,1)}, bf16[288,1280]{1,0:T(8,128)(2,1)S(1)}, u32[]{:S(2)}, u32[]{:S(2)}) collective-permute-start(bf16[288,1280]{1,0:T(8,128)(2,1)} %bitcast.14), channel_id=1, source_target_pairs={{0,2},{1,3},{2,0},{3,1},{4,6},{5,7},{6,4},{7,5},{8,10},{33,35},{10... | collective-permute-start | bytes 2211848 | tf_op jit(solution)/shard_map/ppermute | solution.py:69
  2.7 1.0 %copy-start.1 = (bf16[2,144,640]{2,1,0:T(8,128)(2,1)S(1)}, bf16[2,144,640]{2,1,0:T(8,128)(2,1)}, u32[]{:S(2)}) copy-start(bf16[2,144,640]{2,1,0:T(8,128)(2,1)} %key_ref.1) | copy-start | bytes 1105924
  3.7 1.0 %copy-start.2 = (bf16[2,144,640]{2,1,0:T(8,128)(2,1)S(1)}, bf16[2,144,640]{2,1,0:T(8,128)(2,1)}, u32[]{:S(2)}) copy-start(bf16[2,144,640]{2,1,0:T(8,128)(2,1)} %value_ref.1) | copy-start | bytes 1105924
  4.8 7.4 %collective-permute-start = (bf16[2,2,144,128]{3,2,1,0:T(8,128)(2,1)S(1)}, bf16[2,2,144,128]{3,2,1,0:T(8,128)(2,1)S(1)}, u32[]{:S(2)}, u32[]{:S(2)}) collective-permute-start(bf16[2,2,144,128]{3,2,1,0:T(8,128)(2,1)S(1)} %get-tuple-element.41), channel_id=1, source_target_pairs={{0,96},{1,25},{2,98},{3,27},{4,100},{5,29},{6,102},{7,31},{8,104},... | collective-permute-start | bytes 442376 | tf_op jit(solution)/shard_map/ppermute | solution.py:69
  7.9 6.8 %collective-permute-start.1 = (bf16[2,2,144,128]{3,2,1,0:T(8,128)(2,1)S(1)}, bf16[2,2,144,128]{3,2,1,0:T(8,128)(2,1)S(1)}, u32[]{:S(2)}, u32[]{:S(2)}) collective-permute-start(bf16[2,2,144,128]{3,2,1,0:T(8,128)(2,1)S(1)} %get-tuple-element.42), channel_id=1, source_target_pairs={{0,64},{1,17},{2,66},{3,19},{4,68},{5,21},{6,70},{7,23},{8,72},{33... | collective-permute-start | bytes 442376 | tf_op jit(solution)/shard_map/ppermute | solution.py:69
  8.5 7.6 %collective-permute-start.2 = (bf16[2,2,144,128]{3,2,1,0:T(8,128)(2,1)S(1)}, bf16[2,2,144,128]{3,2,1,0:T(8,128)(2,1)S(1)}, u32[]{:S(2)}, u32[]{:S(2)}) collective-permute-start(bf16[2,2,144,128]{3,2,1,0:T(8,128)(2,1)S(1)} %get-tuple-element.43), channel_id=1, source_target_pairs={{0,32},{1,9},{2,34},{3,11},{4,36},{5,13},{6,38},{7,15},{8,40},{33,... | collective-permute-start | bytes 442376 | tf_op jit(solution)/shard_map/ppermute | solution.py:69
  9.5 21.1 %collective-permute-start.3 = (bf16[288,1280]{1,0:T(8,128)(2,1)}, bf16[288,1280]{1,0:T(8,128)(2,1)S(1)}, u32[]{:S(2)}, u32[]{:S(2)}) collective-permute-start(bf16[288,1280]{1,0:T(8,128)(2,1)} %bitcast.15), channel_id=1, source_target_pairs={{0,1},{1,0},{2,3},{3,2},{4,5},{5,4},{6,7},{7,6},{8,9},{33,32},{10,... | collective-permute-start | bytes 2211848 | tf_op jit(solution)/shard_map/ppermute | solution.py:69
  16.2 12.4 %collective-permute-start.6 = (bf16[2,2,720,128]{3,2,1,0:T(8,128)(2,1)S(1)}, bf16[2,2,720,128]{3,2,1,0:T(8,128)(2,1)}, u32[]{:S(2)}, u32[]{:S(2)}) collective-permute-start(bf16[2,2,720,128]{3,2,1,0:T(8,128)(2,1)S(1)} %assemble.1.after.refs_4_), channel_id=1, source_target_pairs={{0,8},{1,33},{2,10},{3,35},{4,12},{5,37},{6,14},{7,39},{8,0},{33,1... | collective-permute-start | bytes 2211848 | tf_op jit(solution)/shard_map/ppermute | solution.py:69
  17.8 1.1 %copy-start = (bf16[2,144,1280]{2,1,0:T(8,128)(2,1)S(1)}, bf16[2,144,1280]{2,1,0:T(8,128)(2,1)}, u32[]{:S(2)}) copy-start(bf16[2,144,1280]{2,1,0:T(8,128)(2,1)} %param.12) | copy-start | bytes 2211844
  18.9 0.8 copy-start.5
  19.6 0.8 copy-start.6
  20.4 0.7 copy-start.9
  21.1 0.7 copy-start.10
  22.7 7.9 %collective-permute-start.5 = (bf16[288,1280]{1,0:T(8,128)(2,1)S(1)}, bf16[288,1280]{1,0:T(8,128)(2,1)}, u32[]{:S(2)}, u32[]{:S(2)}) collective-permute-start(bf16[288,1280]{1,0:T(8,128)(2,1)S(1)} %collective-permute-done.4.h2), channel_id=1, source_target_pairs={{0,1},{1,0},{2,3},{3,2},{4,5},{5,4},{6,7},{7,6},{8,9},{33,32},{10,... | collective-permute-start | bytes 2211848 | tf_op jit(solution)/shard_map/ppermute | solution.py:69
  22.9 32.7 %collective-permute-start.12 = (bf16[2,2,720,128]{3,2,1,0:T(8,128)(2,1)S(1)}, bf16[2,2,720,128]{3,2,1,0:T(8,128)(2,1)S(1)}, u32[]{:S(2)}, u32[]{:S(2)}) collective-permute-start(bf16[2,2,720,128]{3,2,1,0:T(8,128)(2,1)S(1)} %assemble.1.after.refs_4_), channel_id=1, source_target_pairs={{0,4},{1,5},{2,6},{3,7},{4,0},{5,1},{6,2},{7,3},{8,12},{33,37},{10... | collective-permute-start | bytes 2211848 | tf_op jit(solution)/shard_map/ppermute | solution.py:69
  26.5 16.6 %collective-permute-start.8 = (bf16[2,2,720,128]{3,2,1,0:T(8,128)(2,1)S(1)}, bf16[2,2,720,128]{3,2,1,0:T(8,128)(2,1)S(1)}, u32[]{:S(2)}, u32[]{:S(2)}) collective-permute-start(bf16[2,2,720,128]{3,2,1,0:T(8,128)(2,1)S(1)} %assemble.1.after.refs_4_), channel_id=1, source_target_pairs={{0,24},{1,97},{2,26},{3,99},{4,28},{5,101},{6,30},{7,103},{8,16},{... | collective-permute-start | bytes 2211848 | tf_op jit(solution)/shard_map/ppermute | solution.py:69
  28.6 18.5 %collective-permute-start.7 = (bf16[2,2,720,128]{3,2,1,0:T(8,128)(2,1)}, bf16[2,2,720,128]{3,2,1,0:T(8,128)(2,1)S(1)}, u32[]{:S(2)}, u32[]{:S(2)}) collective-permute-start(bf16[2,2,720,128]{3,2,1,0:T(8,128)(2,1)} %collective-permute-done.6.refs_5_), channel_id=1, source_target_pairs={{0,24},{1,97},{2,26},{3,99},{4,28},{5,101},{6,30},{7,103},{8,16},{... | collective-permute-start | bytes 2211848 | tf_op jit(solution)/shard_map/ppermute | solution.py:69
  30.6 9.7 %slice-start = ((s8[6553600]{0:T(1024)(128)(4,1)}), s8[4194304]{0:T(1024)(128)(4,1)S(1)}, s32[]{:S(2)}) async-start(s8[6553600]{0:T(1024)(128)(4,1)} %bitcast.19), calls=%async_computation | async-start | bytes 8388608
  34.9 5.5 %slice-start.1 = ((s8[6553600]{0:T(1024)(128)(4,1)}), s8[2359296]{0:T(1024)(128)(4,1)S(1)}, s32[]{:S(2)}) async-start(s8[6553600]{0:T(1024)(128)(4,1)} %bitcast.19), calls=%async_computation.1 | async-start | bytes 4718592
  34.9 25.0 %slice-start.2 = ((s8[6553600]{0:T(1024)(128)(4,1)}), s8[4194304]{0:T(1024)(128)(4,1)S(1)}, s32[]{:S(2)}) async-start(s8[6553600]{0:T(1024)(128)(4,1)} %bitcast.21), calls=%async_computation.2 | async-start | bytes 8388608
  40.4 6.7 %copy-start.7 = (f32[640]{0:T(1024)S(1)}, f32[640]{0:T(1024)}, u32[]{:S(2)}) copy-start(f32[640]{0:T(1024)} %qg.1) | copy-start | bytes 7684
  40.4 6.7 %copy-start.8 = (f32[640]{0:T(1024)S(1)}, f32[640]{0:T(1024)}, u32[]{:S(2)}) copy-start(f32[640]{0:T(1024)} %kg.1) | copy-start | bytes 7684
  40.4 19.4 %slice-start.3 = ((s8[6553600]{0:T(1024)(128)(4,1)}), s8[2359296]{0:T(1024)(128)(4,1)S(1)}, s32[]{:S(2)}) async-start(s8[6553600]{0:T(1024)(128)(4,1)} %bitcast.21), calls=%async_computation.3 | async-start | bytes 4718592
  43.1 1.9 %collective-permute-start.11 = (f32[8,384]{1,0:T(8,128)S(1)}, f32[8,384]{1,0:T(8,128)S(1)}, u32[]{:S(2)}, u32[]{:S(2)}) collective-permute-start(f32[8,384]{1,0:T(8,128)S(1)} %sum_squares.1.s0), channel_id=1, source_target_pairs={{0,1},{1,0},{2,3},{3,2},{4,5},{5,4},{6,7},{7,6},{8,9},{33,32},{10,... | collective-permute-start | bytes 36872 | tf_op jit(solution)/shard_map/ppermute | solution.py:69
  43.1 3.8 %collective-permute-start.10 = (f32[8,384]{1,0:T(8,128)S(1)}, f32[8,384]{1,0:T(8,128)S(1)}, u32[]{:S(2)}, u32[]{:S(2)}) collective-permute-start(f32[8,384]{1,0:T(8,128)S(1)} %sum_squares.1.s0), channel_id=1, source_target_pairs={{0,2},{1,3},{2,0},{3,1},{4,6},{5,7},{6,4},{7,5},{8,10},{33,35},{10... | collective-permute-start | bytes 36872 | tf_op jit(solution)/shard_map/ppermute | solution.py:69
  43.3 3.6 %collective-permute-start.9 = (f32[8,384]{1,0:T(8,128)S(1)}, f32[8,384]{1,0:T(8,128)S(1)}, u32[]{:S(2)}, u32[]{:S(2)}) collective-permute-start(f32[8,384]{1,0:T(8,128)S(1)} %sum_squares.1.s0), channel_id=1, source_target_pairs={{0,3},{1,2},{2,1},{3,0},{4,7},{5,6},{6,5},{7,4},{8,11},{33,34},{10... | collective-permute-start | bytes 36872 | tf_op jit(solution)/shard_map/ppermute | solution.py:69
  48.9 7.9 %collective-permute-start.15 = (bf16[2,2,144,128]{3,2,1,0:T(8,128)(2,1)S(1)}, bf16[2,2,144,128]{3,2,1,0:T(8,128)(2,1)S(1)}, u32[]{:S(2)}, u32[]{:S(2)}) collective-permute-start(bf16[2,2,144,128]{3,2,1,0:T(8,128)(2,1)S(1)} %get-tuple-element.59.refs_1_), channel_id=1, source_target_pairs={{0,32},{1,9},{2,34},{3,11},{4,36},{5,13},{6,38},{7,15},{8,40},{33,... | collective-permute-start | bytes 442376 | tf_op jit(solution)/shard_map/ppermute | solution.py:69
  48.9 7.9 %collective-permute-start.14 = (bf16[2,2,144,128]{3,2,1,0:T(8,128)(2,1)S(1)}, bf16[2,2,144,128]{3,2,1,0:T(8,128)(2,1)S(1)}, u32[]{:S(2)}, u32[]{:S(2)}) collective-permute-start(bf16[2,2,144,128]{3,2,1,0:T(8,128)(2,1)S(1)} %get-tuple-element.60.refs_2_), channel_id=1, source_target_pairs={{0,64},{1,17},{2,66},{3,19},{4,68},{5,21},{6,70},{7,23},{8,72},{33... | collective-permute-start | bytes 442376 | tf_op jit(solution)/shard_map/ppermute | solution.py:69
  50.9 6.8 %collective-permute-start.13 = (bf16[2,2,144,128]{3,2,1,0:T(8,128)(2,1)S(1)}, bf16[2,2,144,128]{3,2,1,0:T(8,128)(2,1)S(1)}, u32[]{:S(2)}, u32[]{:S(2)}) collective-permute-start(bf16[2,2,144,128]{3,2,1,0:T(8,128)(2,1)S(1)} %get-tuple-element.61.refs_3_), channel_id=1, source_target_pairs={{0,96},{1,25},{2,98},{3,27},{4,100},{5,29},{6,102},{7,31},{8,104},... | collective-permute-start | bytes 442376 | tf_op jit(solution)/shard_map/ppermute | solution.py:69
  52.1 20.2 %collective-permute-start.18 = (bf16[2,2,720,128]{3,2,1,0:T(8,128)(2,1)S(1)}, bf16[2,2,720,128]{3,2,1,0:T(8,128)(2,1)S(1)}, u32[]{:S(2)}, u32[]{:S(2)}) collective-permute-start(bf16[2,2,720,128]{3,2,1,0:T(8,128)(2,1)S(1)} %collective-permute-done.7.refs_7_), channel_id=1, source_target_pairs={{0,4},{1,5},{2,6},{3,7},{4,0},{5,1},{6,2},{7,3},{8,12},{33,37},{10... | collective-permute-start | bytes 2211848 | tf_op jit(solution)/shard_map/ppermute | solution.py:69
  57.7 4.6 %copy-start.3 = (bf16[288,640]{1,0:T(8,128)(2,1)S(1)}, bf16[288,640]{1,0:T(8,128)(2,1)}, u32[]{:S(2)}) copy-start(bf16[288,640]{1,0:T(8,128)(2,1)} %get-tuple-element.57.k_ref) | copy-start | bytes 1105924
  57.7 14.6 %collective-permute-start.17 = (bf16[2,2,720,128]{3,2,1,0:T(8,128)(2,1)S(1)}, bf16[2,2,720,128]{3,2,1,0:T(8,128)(2,1)S(1)}, u32[]{:S(2)}, u32[]{:S(2)}) collective-permute-start(bf16[2,2,720,128]{3,2,1,0:T(8,128)(2,1)S(1)} %collective-permute-done.12.refs_4_), channel_id=1, source_target_pairs={{0,24},{1,97},{2,26},{3,99},{4,28},{5,101},{6,30},{7,103},{8,16},{... | collective-permute-start | bytes 2211848 | tf_op jit(solution)/shard_map/ppermute | solution.py:69
  59.8 12.5 %collective-permute-start.16 = (bf16[2,2,720,128]{3,2,1,0:T(8,128)(2,1)S(1)}, bf16[2,2,720,128]{3,2,1,0:T(8,128)(2,1)S(1)}, u32[]{:S(2)}, u32[]{:S(2)}) collective-permute-start(bf16[2,2,720,128]{3,2,1,0:T(8,128)(2,1)S(1)} %collective-permute-done.12.refs_4_), channel_id=1, source_target_pairs={{0,8},{1,33},{2,10},{3,35},{4,12},{5,37},{6,14},{7,39},{8,0},{33,1... | collective-permute-start | bytes 2211848 | tf_op jit(solution)/shard_map/ppermute | solution.py:69
  62.3 16.6 %copy-start.4 = (bf16[288,640]{1,0:T(8,128)(2,1)}, bf16[288,640]{1,0:T(8,128)(2,1)S(1)}, u32[]{:S(2)}) copy-start(bf16[288,640]{1,0:T(8,128)(2,1)S(1)} %convolution_convert_fusion.v_ref) | copy-start | bytes 1105924
  78.9 5.3 %collective-permute-start.19 = (bf16[2,304,128]{2,1,0:T(8,128)(2,1)S(1)}, bf16[2,304,128]{2,1,0:T(8,128)(2,1)S(1)}, u32[]{:S(2)}, u32[]{:S(2)}) collective-permute-start(bf16[2,304,128]{2,1,0:T(8,128)(2,1)S(1)} %get-tuple-element.74), channel_id=1, source_target_pairs={{0,96},{1,25},{2,98},{3,27},{4,100},{5,29},{6,102},{7,31},{8,104},... | collective-permute-start | bytes 466952 | tf_op jit(solution)/shard_map/ppermute | solution.py:69
  80.2 6.8 %collective-permute-start.20 = (bf16[2,304,128]{2,1,0:T(8,128)(2,1)S(1)}, bf16[2,304,128]{2,1,0:T(8,128)(2,1)S(1)}, u32[]{:S(2)}, u32[]{:S(2)}) collective-permute-start(bf16[2,304,128]{2,1,0:T(8,128)(2,1)S(1)} %get-tuple-element.75), channel_id=1, source_target_pairs={{0,64},{1,17},{2,66},{3,19},{4,68},{5,21},{6,70},{7,23},{8,72},{33... | collective-permute-start | bytes 466952 | tf_op jit(solution)/shard_map/ppermute | solution.py:69
  80.4 8.2 %collective-permute-start.21 = (bf16[2,304,128]{2,1,0:T(8,128)(2,1)S(1)}, bf16[2,304,128]{2,1,0:T(8,128)(2,1)S(1)}, u32[]{:S(2)}, u32[]{:S(2)}) collective-permute-start(bf16[2,304,128]{2,1,0:T(8,128)(2,1)S(1)} %get-tuple-element.76), channel_id=1, source_target_pairs={{0,32},{1,9},{2,34},{3,11},{4,36},{5,13},{6,38},{7,15},{8,40},{33,... | collective-permute-start | bytes 466952 | tf_op jit(solution)/shard_map/ppermute | solution.py:69

commit v6 on v5

--- a/solution.py
+++ b/solution.py
@@ -35,6 +35,7 @@
 GROUP = 16
 VMEM_MIB = 24
 ATTENTION_MIB = 34
+MODULATE_MIB = 44
 
 
 def params(mib):
@@ -230,7 +231,9 @@
     return jnp.sum(total, axis=1, keepdims=True)
 
 
-def modulate_kernel(t_ref, h0, h1, h2, h3, cond, mod, out_ref):
+def modulate_kernel(t_ref, h0, h1, h2, h3, cond, mod, weight, out_ref, weight_out, sem):
+    copy = pltpu.make_async_copy(weight, weight_out, sem.at[0])
+    copy.start()
     chunks = (h0, h1, h2, h3)
     for row in range(0, ROWS, GROUP):
         rows = slice(row, row + GROUP)
@@ -245,20 +248,25 @@
             bias = jnp.where(conditioned, mod[3:4, cols], mod[2:3, cols])
             normed = (lanes[c] - mean) * rstd
             out_ref[rows, cols] = (normed * gain + bias).astype(BF16)
-
-
-def modulate(blocks, chunks, cond, mod):
+    copy.wait()
+
+
+def modulate(blocks, chunks, cond, mod, weight):
     return pl.pallas_call(
         modulate_kernel,
-        out_shape=jax.ShapeDtypeStruct((ROWS, D), BF16),
-        in_specs=[smem()] + [vmem()] * 6,
-        out_specs=vmem(),
-        compiler_params=params(VMEM_MIB),
-        cost_estimate=pl.CostEstimate(
-            flops=12 * ROWS * D, bytes_accessed=45_000_000, transcendentals=0
+        out_shape=[
+            jax.ShapeDtypeStruct((ROWS, D), BF16),
+            jax.ShapeDtypeStruct((D, WIDTH), BF16),
+        ],
+        in_specs=[smem()] + [vmem()] * 6 + [pl.BlockSpec(memory_space=pltpu.HBM)],
+        out_specs=[vmem()] * 2,
+        scratch_shapes=[pltpu.SemaphoreType.DMA((1,))],
+        compiler_params=params(MODULATE_MIB),
+        cost_estimate=pl.CostEstimate(
+            flops=12 * ROWS * D, bytes_accessed=20_000_000, transcendentals=0
         ),
         name="modulate",
-    )(blocks, *chunks, cond, mod)
+    )(blocks, *chunks, cond, mod, weight)
 
 
 def squares_kernel(q_ref, k_ref, out_ref):
@@ -411,13 +419,15 @@
         out = scores_s.at[i % 2]
 
         def arrive():
+            v_main[s, :, HD:] = jnp.ones((KEYS, HD), BF16)
+            v_last[s, :, HD:] = jnp.ones((KEYS_LAST, HD), BF16)
             for n, piece in enumerate(pieces):
                 main = slice(n * PER_PIECE, (n + 1) * PER_PIECE)
                 last = slice(n * TOK, (n + 1) * TOK)
                 k_main[s, main] = piece[s, 0, 0:PER_PIECE]
                 k_last[s, last] = piece[s, 0, PER_PIECE:PIECE]
-                v_main[s, main] = piece[s, 1, 0:PER_PIECE]
-                v_last[s, last] = piece[s, 1, PER_PIECE:PIECE]
+                v_main[s, main, 0:HD] = piece[s, 1, 0:PER_PIECE]
+                v_last[s, last, 0:HD] = piece[s, 1, PER_PIECE:PIECE]
 
         def step(at, end):
             query = jnp.concatenate([queries[2 * tile][s, e], queries[2 * tile + 1][s, e]], axis=0)
@@ -436,19 +446,18 @@
             steps.append(functools.partial(step, at, min(at + SPLIT, size(i))))
         return steps if far else steps + [hide]
 
-    def softmax_steps(i, tops, totals):
+    def softmax_steps(i, tops):
         def step(row):
             rows = slice(row, row + GROUP)
             part = scores_s[i % 2, rows, 0 : size(i)]
             top = jnp.max(part, axis=1, keepdims=True)
             probs = jnp.exp2((part - top) * SCORE_SCALE)
-            totals.append(jnp.sum(probs, axis=1, keepdims=True))
             tops.append(top)
             probs_s[i % 2, rows, 0 : size(i)] = probs.astype(BF16)
 
         return [functools.partial(step, row) for row in range(0, TILE, GROUP)]
 
-    def product_steps(i, tops, totals):
+    def product_steps(i, tops):
         s, e, tile = jobs[i]
         values = v_last if e else v_main
 
@@ -459,22 +468,23 @@
             acc_s[...] = part if at == 0 else acc_s[...] + part
 
         def finish():
-            top, total = jnp.concatenate(tops, axis=0), jnp.concatenate(totals, axis=0)
-            out = acc_s[...] / total
+            top = jnp.concatenate(tops, axis=0)
+            total = acc_s[:, HD:]
+            out = acc_s[:, 0:HD] / total
             lse = top * SCORE_SCALE + jnp.log2(total)
             for n in range(2):
                 r = 2 * tile + n
                 half = slice(n * TOK, (n + 1) * TOK)
                 if not far:
                     out_ref[s, r, e] = out[half]
-                    lse_ref[s, r, e] = jnp.broadcast_to(lse[half], (TOK, HD))
+                    lse_ref[s, r, e] = lse[half]
                     continue
-                lse_near = near_lse[s, r, e][:, 0:1]
+                lse_near = near_lse[s, r, e]
                 high = jnp.maximum(lse[half], lse_near)
                 weight, weight_near = jnp.exp2(lse[half] - high), jnp.exp2(lse_near - high)
                 both = weight + weight_near
                 value = (out[half] * weight + near_out[s, r, e] * weight_near) / both
-                lse_s[s, r, e] = jnp.broadcast_to(high + jnp.log2(both), (TOK, HD))
+                lse_s[s, r, e] = high + jnp.log2(both)
                 msgs[r][s, e * TOK : (e + 1) * TOK] = value.astype(BF16)
 
         steps = []
@@ -492,14 +502,14 @@
     weave(score_steps(0))
     pending = None
     for i in range(len(jobs)):
-        tops, totals = [], []
-        lists = [softmax_steps(i, tops, totals)]
+        tops = []
+        lists = [softmax_steps(i, tops)]
         if i + 1 < len(jobs):
             lists.append(score_steps(i + 1))
         if pending is not None:
             lists.append(pending)
         weave(*lists)
-        pending = product_steps(i, tops, totals)
+        pending = product_steps(i, tops)
     weave(pending)
 
     if far:
@@ -532,11 +542,11 @@
         out_specs=[vmem()] * len(out_shape),
         scratch_shapes=[
             pltpu.VMEM((B, 4, 2, TOK, HD), F32),
-            pltpu.VMEM((TILE, HD), F32),
+            pltpu.VMEM((TILE, 2 * HD), F32),
             pltpu.VMEM((B, KEYS, HD), BF16),
-            pltpu.VMEM((B, KEYS, HD), BF16),
+            pltpu.VMEM((B, KEYS, 2 * HD), BF16),
             pltpu.VMEM((B, KEYS_LAST, HD), BF16),
-            pltpu.VMEM((B, KEYS_LAST, HD), BF16),
+            pltpu.VMEM((B, KEYS_LAST, 2 * HD), BF16),
             pltpu.VMEM((2, TILE, KEYS), F32),
             pltpu.VMEM((2, TILE, KEYS), BF16),
         ],
@@ -637,9 +647,11 @@
     cross_rows = swap_tp(z_rows, 0, 1)
     near_two = swap_v(near_one, 3)
     blocks = jnp.stack([tp, tp ^ 1, tp ^ 2, tp ^ 3]).astype(jnp.int32)
-    modded = modulate(blocks, [own_rows, core_rows, z_rows, cross_rows], cond, mod)
+    modded, key_weights = modulate(
+        blocks, [own_rows, core_rows, z_rows, cross_rows], cond, mod, w_key
+    )
     query = jnp.dot(modded, w_query, preferred_element_type=F32)
-    key = jnp.dot(modded, w_key, preferred_element_type=F32)
+    key = jnp.dot(modded, key_weights, preferred_element_type=F32)
     fresh_values = jnp.dot(modded, w_value, preferred_element_type=F32).astype(BF16)
     own_sq = sum_squares(query, key)
     own_sq, near_three = lax.optimization_barrier((own_sq, near_three))
@@ -647,10 +659,10 @@
     near_two, *squares = lax.optimization_barrier((near_two, *squares))
     far_two = swap_z_hi(near_two)
     fresh_keys, *sends = norm_rope(u, query, key, squares, q_gain, k_gain, cos, sin)
+    far, fresh_keys = lax.optimization_barrier((far, fresh_keys))
+    far_one, far_three = swap_v(far, 1), swap_v(far, 3)
     queries = exchange_u(sends)
     fresh_out, fresh_rows = fresh_attention(u, fresh_keys, fresh_values, sends)
-    far, *queries = lax.optimization_barrier((far, *queries))
-    far_one, far_three = swap_v(far, 1), swap_v(far, 3)
 
     partial = stale_attention(queries, [near, near_one, near_three, near_two])
     outs = stale_attention(

time: 90.5 us -> 93 us (1.028)
  Pallas kernels: 23.1 us -> 25.1 us
  starting transfers between devices: 29.1 us -> 28 us
    pallas_call x1, Pallas kernels: 4.24 us -> 7.08 us  [modulate(): pl.pallas_call(modulate_kernel, out_shape=[jax.ShapeDtypeStruct((ROWS, D)...]
    ppermute x22, starting transfers between devices: 29.1 us -> 28 us  [permute(): lax.ppermute(value, AXES, [(linear(*p), linear(*move(*p))) for p in place...]
  transfers between devices with their start and end apart: 22 -> 22, of which waited for: 11 -> 10; matrix products, arithmetic and copies ran while one was open for 12% -> 12% of each run, Pallas kernels for 17% -> 19%
where the time goes in v6:
time: 93 us; the launch traced here: 92.2 us
  starting transfers between devices  28 us (30%)
  Pallas kernels  25.1 us (27%)
  waiting for transfers between devices  21.5 us (23%)
  matrix products  10.5 us (11%)
  local copies, waits for them, and re-layouts  6.03 us (6%)
    ppermute x22, starting transfers between devices, permute(): lax.ppermute(value, AXES, [(linear(*p), linear(*move(*p))) for p in place...  28 us
    ppermute x22, waiting for transfers between devices, permute(): lax.ppermute(value, AXES, [(linear(*p), linear(*move(*p))) for p in place...  21.5 us
    pallas_call x2, Pallas kernels, stale_attention(): pl.pallas_call(functools.partial(stale_kernel, far), out_shape=out_shape,...  12.3 us
    pallas_call x1, Pallas kernels, modulate(): pl.pallas_call(modulate_kernel, out_shape=[jax.ShapeDtypeStruct((ROWS, D)...  7.08 us
    unnamed x30, local copies, waits for them, and re-layouts  6.03 us
    dot_general x1, matrix products, shards(): key = jnp.dot(modded, key_weights, preferred_element_type=F32)  5.53 us
    dot_general x1, matrix products, shards(): jnp.dot(modded, w_value, preferred_element_type=F32).astype(BF16)  2.54 us
    dot_general x1, matrix products, shards(): query = jnp.dot(modded, w_query, preferred_element_type=F32)  2.47 us
  transfers between devices with their start and end apart: 22, of which 10 were waited for; matrix products, arithmetic and copies ran while one was open for 12% of the time, Pallas kernels for 19%

profile of v6, /device:TPU:0, one launch (start us, length us, event | category | flops | bytes accessed | tf_op | source)
XLA Modules:
  0.0 92.2 jit_solution(9967524322936062097)
XLA Ops:
  0.6 2.1 %collective-permute-start.5 = (bf16[288,1280]{1,0:T(8,128)(2,1)}, bf16[288,1280]{1,0:T(8,128)(2,1)S(1)}, u32[]{:S(2)}, u32[]{:S(2)}) collective-permute-start(bf16[288,1280]{1,0:T(8,128)(2,1)} %bitcast.14), channel_id=1, source_target_pairs={{0,2},{1,3},{2,0},{3,1},{4,6},{5,7},{6,4},{7,5},{8,10},{33,35},{10... | collective-permute-start | bytes 2211848 | tf_op jit(solution)/shard_map/ppermute | solution.py:70
  2.7 1.0 %copy-done.1 = bf16[2,144,640]{2,1,0:T(8,128)(2,1)S(1)} copy-done((bf16[2,144,640]{2,1,0:T(8,128)(2,1)S(1)}, bf16[2,144,640]{2,1,0:T(8,128)(2,1)}, u32[]{:S(2)}) %copy-start.1) | copy-done | bytes 368664
  3.7 1.0 %copy-done.2 = bf16[2,144,640]{2,1,0:T(8,128)(2,1)S(1)} copy-done((bf16[2,144,640]{2,1,0:T(8,128)(2,1)S(1)}, bf16[2,144,640]{2,1,0:T(8,128)(2,1)}, u32[]{:S(2)}) %copy-start.2) | copy-done | bytes 368664
  4.7 0.1 pack_stale.1
  4.8 3.1 %collective-permute-start = (bf16[2,2,144,128]{3,2,1,0:T(8,128)(2,1)S(1)}, bf16[2,2,144,128]{3,2,1,0:T(8,128)(2,1)S(1)}, u32[]{:S(2)}, u32[]{:S(2)}) collective-permute-start(bf16[2,2,144,128]{3,2,1,0:T(8,128)(2,1)S(1)} %get-tuple-element.40), channel_id=1, source_target_pairs={{0,96},{1,25},{2,98},{3,27},{4,100},{5,29},{6,102},{7,31},{8,104},... | collective-permute-start | bytes 442376 | tf_op jit(solution)/shard_map/ppermute | solution.py:70
  7.9 0.6 collective-permute-start.1
  8.5 1.0 %collective-permute-start.2 = (bf16[2,2,144,128]{3,2,1,0:T(8,128)(2,1)S(1)}, bf16[2,2,144,128]{3,2,1,0:T(8,128)(2,1)S(1)}, u32[]{:S(2)}, u32[]{:S(2)}) collective-permute-start(bf16[2,2,144,128]{3,2,1,0:T(8,128)(2,1)S(1)} %get-tuple-element.42), channel_id=1, source_target_pairs={{0,32},{1,9},{2,34},{3,11},{4,36},{5,13},{6,38},{7,15},{8,40},{33,... | collective-permute-start | bytes 442376 | tf_op jit(solution)/shard_map/ppermute | solution.py:70
  9.5 2.7 %collective-permute-done.refs_1_ = bf16[2,2,144,128]{3,2,1,0:T(8,128)(2,1)S(1)} collective-permute-done((bf16[2,2,144,128]{3,2,1,0:T(8,128)(2,1)S(1)}, bf16[2,2,144,128]{3,2,1,0:T(8,128)(2,1)S(1)}, u32[]{:S(2)}, u32[]{:S(2)}) %collective-permute-start) | collective-permute-done | bytes 147488 | tf_op jit(solution)/shard_map/ppermute | solution.py:70
  12.2 2.5 %collective-permute-done.1.refs_2_ = bf16[2,2,144,128]{3,2,1,0:T(8,128)(2,1)S(1)} collective-permute-done((bf16[2,2,144,128]{3,2,1,0:T(8,128)(2,1)S(1)}, bf16[2,2,144,128]{3,2,1,0:T(8,128)(2,1)S(1)}, u32[]{:S(2)}, u32[]{:S(2)}) %collective-permute-start.1) | collective-permute-done | bytes 147488 | tf_op jit(solution)/shard_map/ppermute | solution.py:70
  14.7 1.5 %collective-permute-done.2.refs_3_ = bf16[2,2,144,128]{3,2,1,0:T(8,128)(2,1)S(1)} collective-permute-done((bf16[2,2,144,128]{3,2,1,0:T(8,128)(2,1)S(1)}, bf16[2,2,144,128]{3,2,1,0:T(8,128)(2,1)S(1)}, u32[]{:S(2)}, u32[]{:S(2)}) %collective-permute-start.2) | collective-permute-done | bytes 147488 | tf_op jit(solution)/shard_map/ppermute | solution.py:70
  16.2 1.6 %collective-permute-start.7 = (bf16[2,2,720,128]{3,2,1,0:T(8,128)(2,1)S(1)}, bf16[2,2,720,128]{3,2,1,0:T(8,128)(2,1)}, u32[]{:S(2)}, u32[]{:S(2)}) collective-permute-start(bf16[2,2,720,128]{3,2,1,0:T(8,128)(2,1)S(1)} %assemble.1.after.refs_4_), channel_id=1, source_target_pairs={{0,8},{1,33},{2,10},{3,35},{4,12},{5,37},{6,14},{7,39},{8,0},{33,1... | collective-permute-start | bytes 2211848 | tf_op jit(solution)/shard_map/ppermute | solution.py:70
  17.8 1.1 %copy-done = bf16[2,144,1280]{2,1,0:T(8,128)(2,1)S(1)} copy-done((bf16[2,144,1280]{2,1,0:T(8,128)(2,1)S(1)}, bf16[2,144,1280]{2,1,0:T(8,128)(2,1)}, u32[]{:S(2)}) %copy-start) | copy-done | bytes 737304
  18.9 0.8 copy-done.5
  19.7 0.8 copy-done.6
  20.4 0.7 copy-done.9
  21.1 0.7 copy-done.10
  21.8 0.9 %tables.1 = (f32[288,128]{1,0:T(8,128)S(1)}, f32[144,128]{1,0:T(8,128)S(1)}, f32[144,128]{1,0:T(8,128)S(1)}, f32[4,5120]{1,0:T(4,128)S(1)}, bf16[288,1280]{1,0:T(8,128)(2,1)S(1)}) custom-call(s32[144]{0:T(256)S(1)} %copy-done.9, f32[1,128]{1,0:T(1,128)S(1)} %copy-done.10, bf16[288,1280]{1,0:T(8,128)(2,1)S(1)} %bitcast.16, f32[2,5120]{1,0:T(2,128)S(1)} %copy-done.5, ...), custom_call_target="tpu_custom_call" | custom-call | flops 1843200 | bytes 1000000 | tf_op jit(solution)/shard_map/tables/pallas_call | solution.py:177
  22.7 0.1 collective-permute-start.6
  22.9 2.1 %collective-permute-start.9 = (bf16[2,2,720,128]{3,2,1,0:T(8,128)(2,1)S(1)}, bf16[2,2,720,128]{3,2,1,0:T(8,128)(2,1)S(1)}, u32[]{:S(2)}, u32[]{:S(2)}) collective-permute-start(bf16[2,2,720,128]{3,2,1,0:T(8,128)(2,1)S(1)} %assemble.1.after.refs_4_), channel_id=1, source_target_pairs={{0,24},{1,97},{2,26},{3,99},{4,28},{5,101},{6,30},{7,103},{8,16},{... | collective-permute-start | bytes 2211848 | tf_op jit(solution)/shard_map/ppermute | solution.py:70
  25.0 3.6 %collective-permute-start.3 = (bf16[2,2,720,128]{3,2,1,0:T(8,128)(2,1)S(1)}, bf16[2,2,720,128]{3,2,1,0:T(8,128)(2,1)S(1)}, u32[]{:S(2)}, u32[]{:S(2)}) collective-permute-start(bf16[2,2,720,128]{3,2,1,0:T(8,128)(2,1)S(1)} %assemble.1.after.refs_4_), channel_id=1, source_target_pairs={{0,4},{1,5},{2,6},{3,7},{4,0},{5,1},{6,2},{7,3},{8,12},{33,37},{10... | collective-permute-start | bytes 2211848 | tf_op jit(solution)/shard_map/ppermute | solution.py:70
  28.6 2.0 %collective-permute-start.8 = (bf16[2,2,720,128]{3,2,1,0:T(8,128)(2,1)}, bf16[2,2,720,128]{3,2,1,0:T(8,128)(2,1)S(1)}, u32[]{:S(2)}, u32[]{:S(2)}) collective-permute-start(bf16[2,2,720,128]{3,2,1,0:T(8,128)(2,1)} %collective-permute-done.7.refs_5_), channel_id=1, source_target_pairs={{0,24},{1,97},{2,26},{3,99},{4,28},{5,101},{6,30},{7,103},{8,16},{... | collective-permute-start | bytes 2211848 | tf_op jit(solution)/shard_map/ppermute | solution.py:70
  30.6 7.1 %modulate.1 = (bf16[288,5120]{1,0:T(8,128)(2,1)S(1)}, bf16[5120,640]{1,0:T(8,128)(2,1)}) custom-call(s32[4]{0:T(128)S(1)} %pad_add_fusion.t_ref, bf16[288,1280]{1,0:T(8,128)(2,1)S(1)} %get-tuple-element.44.h0, bf16[288,1280]{1,0:T(8,128)(2,1)S(1)} %collective-permute-done.4.h1, bf16[288,1280]{1,0:T(8,128)(2,1)S(1)} %collective-permute-done.5.h2, ...), custom_call_target="tpu_custom_call" | custom-call | flops 17694720 | bytes 20000000 | tf_op jit(solution)/shard_map/modulate/pallas_call | solution.py:255
  37.7 5.5 %fusion.1.k_ref = f32[288,640]{1,0:T(8,128)S(1)} fusion(bf16[288,5120]{1,0:T(8,128)(2,1)S(1)} %get-tuple-element.49, bf16[5120,640]{1,0:T(8,128)(2,1)} %get-tuple-element.50), kind=kOutput, calls=%fused_computation.3 | convolution fusion | flops 1887436800 | bytes 10240000 | tf_op jit(solution)/shard_map/dot_general | solution.py:654
  43.3 2.5 %fusion.q_ref = f32[288,640]{1,0:T(8,128)S(1)} fusion(bf16[288,5120]{1,0:T(8,128)(2,1)S(1)} %get-tuple-element.49, bf16[5120,640]{1,0:T(8,128)(2,1)S(1)} %bitcast.20), kind=kOutput, calls=%fused_computation.2 | convolution fusion | flops 1887436800 | bytes 10240000 | tf_op jit(solution)/shard_map/dot_general | solution.py:653
  45.8 0.2 sum_squares.1.s0
  46.1 0.4 collective-permute-start.11
  46.5 1.4 %collective-permute-start.12 = (f32[8,384]{1,0:T(8,128)S(1)}, f32[8,384]{1,0:T(8,128)S(1)}, u32[]{:S(2)}, u32[]{:S(2)}) collective-permute-start(f32[8,384]{1,0:T(8,128)S(1)} %sum_squares.1.s0), channel_id=1, source_target_pairs={{0,1},{1,0},{2,3},{3,2},{4,5},{5,4},{6,7},{7,6},{8,9},{33,32},{10,... | collective-permute-start | bytes 36872 | tf_op jit(solution)/shard_map/ppermute | solution.py:70
  47.9 1.3 %collective-permute-done.10.s1 = f32[8,384]{1,0:T(8,128)S(1)} collective-permute-done((f32[8,384]{1,0:T(8,128)S(1)}, f32[8,384]{1,0:T(8,128)S(1)}, u32[]{:S(2)}, u32[]{:S(2)}) %collective-permute-start.10) | collective-permute-done | bytes 12320 | tf_op jit(solution)/shard_map/ppermute | solution.py:70
  49.2 0.7 collective-permute-done.11.s2
  49.9 1.8 %norm_rope.1 = (bf16[288,640]{1,0:T(8,128)(2,1)}, bf16[2,2,144,128]{3,2,1,0:T(8,128)(2,1)S(1)}, bf16[2,2,144,128]{3,2,1,0:T(8,128)(2,1)S(1)}, bf16[2,2,144,128]{...) custom-call(s32[1]{0:T(128)} %bitcast.u_ref, f32[288,640]{1,0:T(8,128)S(1)} %fusion.q_ref, f32[288,640]{1,0:T(8,128)S(1)} %fusion.1.k_ref, ...), custom_call_target="tpu_custom_call" | custom-call | flops 3686400 | bytes 2949120 | tf_op jit(solution)/shard_map/norm_rope/pallas_call | solution.py:324
  51.7 0.6 collective-permute-start.13
  52.3 0.2 collective-permute-start.16
  52.5 1.9 %collective-permute-start.17 = (bf16[2,2,720,128]{3,2,1,0:T(8,128)(2,1)S(1)}, bf16[2,2,720,128]{3,2,1,0:T(8,128)(2,1)S(1)}, u32[]{:S(2)}, u32[]{:S(2)}) collective-permute-start(bf16[2,2,720,128]{3,2,1,0:T(8,128)(2,1)S(1)} %collective-permute-done.3.refs_4_), channel_id=1, source_target_pairs={{0,24},{1,97},{2,26},{3,99},{4,28},{5,101},{6,30},{7,103},{8,16},{... | collective-permute-start | bytes 2211848 | tf_op jit(solution)/shard_map/ppermute | solution.py:70
  54.3 1.1 %collective-permute-start.15 = (bf16[2,2,144,128]{3,2,1,0:T(8,128)(2,1)S(1)}, bf16[2,2,144,128]{3,2,1,0:T(8,128)(2,1)S(1)}, u32[]{:S(2)}, u32[]{:S(2)}) collective-permute-start(bf16[2,2,144,128]{3,2,1,0:T(8,128)(2,1)S(1)} %get-tuple-element.61.refs_1_), channel_id=1, source_target_pairs={{0,32},{1,9},{2,34},{3,11},{4,36},{5,13},{6,38},{7,15},{8,40},{33,... | collective-permute-start | bytes 442376 | tf_op jit(solution)/shard_map/ppermute | solution.py:70
  55.5 2.9 %collective-permute-done.13.refs_1_ = bf16[2,2,144,128]{3,2,1,0:T(8,128)(2,1)S(1)} collective-permute-done((bf16[2,2,144,128]{3,2,1,0:T(8,128)(2,1)S(1)}, bf16[2,2,144,128]{3,2,1,0:T(8,128)(2,1)S(1)}, u32[]{:S(2)}, u32[]{:S(2)}) %collective-permute-start.13) | collective-permute-done | bytes 147488 | tf_op jit(solution)/shard_map/ppermute | solution.py:70
  58.3 3.7 %collective-permute-start.18 = (bf16[2,2,720,128]{3,2,1,0:T(8,128)(2,1)S(1)}, bf16[2,2,720,128]{3,2,1,0:T(8,128)(2,1)S(1)}, u32[]{:S(2)}, u32[]{:S(2)}) collective-permute-start(bf16[2,2,720,128]{3,2,1,0:T(8,128)(2,1)S(1)} %collective-permute-done.8.refs_7_), channel_id=1, source_target_pairs={{0,4},{1,5},{2,6},{3,7},{4,0},{5,1},{6,2},{7,3},{8,12},{33,37},{10... | collective-permute-start | bytes 2211848 | tf_op jit(solution)/shard_map/ppermute | solution.py:70
  62.0 2.5 %convolution_convert_fusion.v_ref = bf16[288,640]{1,0:T(8,128)(2,1)S(1)} fusion(bf16[288,5120]{1,0:T(8,128)(2,1)S(1)} %get-tuple-element.49, bf16[5120,640]{1,0:T(8,128)(2,1)S(1)} %bitcast.22), kind=kOutput, calls=%fused_computation | convolution fusion | flops 1887621120 | bytes 9871360 | tf_op jit(solution)/shard_map/dot_general | solution.py:655
  64.6 1.0 %fresh_attention.1 = (f32[2,5,144,128]{3,2,1,0:T(8,128)S(1)}, f32[24,128]{1,0:T(8,128)S(1)}) custom-call(s32[1]{0:T(128)} %bitcast.u_ref, bf16[288,640]{1,0:T(8,128)(2,1)S(1)} %copy-done.3, bf16[288,640]{1,0:T(8,128)(2,1)S(1)} %convolution_convert_fusion.v_ref, bf16[2,2,144,128]{3,2,1,0:T(8,128)(2,1)S(1)} %get-tuple-element.60.refs_0_, ...), custom_call_target="tpu_custom_call" | custom-call | flops 106168320 | bytes 2580480 | tf_op jit(solution)/shard_map/fresh_attention/pallas_call | solution.py:376
  65.7 6.3 %near_attention.1 = (f32[2,4,2,144,128]{4,3,2,1,0:T(8,128)S(1)}, f32[2,4,2,144,128]{4,3,2,1,0:T(8,128)S(1)}) custom-call(bf16[2,2,144,128]{3,2,1,0:T(8,128)(2,1)S(1)} %get-tuple-element.60.refs_0_, bf16[2,2,144,128]{3,2,1,0:T(8,128)(2,1)S(1)} %collective-permute-done.13.refs_1_, bf16[2,2,144,128]{3,2,1,0:T(8,128)(2,1)S(1)} %collective-permute-done.14.refs_2_, ...), custom_call_target="tpu_custom_call" | custom-call | flops 1698693120 | bytes 2949120 | tf_op jit(solution)/shard_map/near_attention/pallas_call | solution.py:538
  72.0 3.6 %collective-permute-done.18.refs_7_ = bf16[2,2,720,128]{3,2,1,0:T(8,128)(2,1)S(1)} collective-permute-done((bf16[2,2,720,128]{3,2,1,0:T(8,128)(2,1)S(1)}, bf16[2,2,720,128]{3,2,1,0:T(8,128)(2,1)S(1)}, u32[]{:S(2)}, u32[]{:S(2)}) %collective-permute-start.18) | collective-permute-done | bytes 737312 | tf_op jit(solution)/shard_map/ppermute | solution.py:70
  75.7 6.0 %far_attention.1 = (bf16[2,304,128]{2,1,0:T(8,128)(2,1)S(1)}, bf16[2,304,128]{2,1,0:T(8,128)(2,1)S(1)}, bf16[2,304,128]{2,1,0:T(8,128)(2,1)S(1)}, bf16[2,304,128]{2,1,0:T(8,128)(2,1)S(1)}) custom-call(bf16[2,2,144,128]{3,2,1,0:T(8,128)(2,1)S(1)} %get-tuple-element.60.refs_0_, bf16[2,2,144,128]{3,2,1,0:T(8,128)(2,1)S(1)} %collective-permute-done.13.refs_1_, ...), custom_call_target="tpu_custom_call" | custom-call | flops 1698693120 | bytes 2949120 | tf_op jit(solution)/shard_map/far_attention/pallas_call | solution.py:538
  81.7 0.6 collective-permute-start.19
  82.2 0.9 collective-permute-start.20
  83.1 1.1 %collective-permute-start.21 = (bf16[2,304,128]{2,1,0:T(8,128)(2,1)S(1)}, bf16[2,304,128]{2,1,0:T(8,128)(2,1)S(1)}, u32[]{:S(2)}, u32[]{:S(2)}) collective-permute-start(bf16[2,304,128]{2,1,0:T(8,128)(2,1)S(1)} %get-tuple-element.74), channel_id=1, source_target_pairs={{0,32},{1,9},{2,34},{3,11},{4,36},{5,13},{6,38},{7,15},{8,40},{33,... | collective-permute-start | bytes 466952 | tf_op jit(solution)/shard_map/ppermute | solution.py:70
  84.2 2.7 %collective-permute-done.19.refs_1_ = bf16[2,304,128]{2,1,0:T(8,128)(2,1)S(1)} collective-permute-done((bf16[2,304,128]{2,1,0:T(8,128)(2,1)S(1)}, bf16[2,304,128]{2,1,0:T(8,128)(2,1)S(1)}, u32[]{:S(2)}, u32[]{:S(2)}) %collective-permute-start.19) | collective-permute-done | bytes 155680 | tf_op jit(solution)/shard_map/ppermute | solution.py:70
  87.0 2.1 %collective-permute-done.20.refs_2_ = bf16[2,304,128]{2,1,0:T(8,128)(2,1)S(1)} collective-permute-done((bf16[2,304,128]{2,1,0:T(8,128)(2,1)S(1)}, bf16[2,304,128]{2,1,0:T(8,128)(2,1)S(1)}, u32[]{:S(2)}, u32[]{:S(2)}) %collective-permute-start.20) | collective-permute-done | bytes 155680 | tf_op jit(solution)/shard_map/ppermute | solution.py:70
  89.1 1.6 %collective-permute-done.21.refs_3_ = bf16[2,304,128]{2,1,0:T(8,128)(2,1)S(1)} collective-permute-done((bf16[2,304,128]{2,1,0:T(8,128)(2,1)S(1)}, bf16[2,304,128]{2,1,0:T(8,128)(2,1)S(1)}, u32[]{:S(2)}, u32[]{:S(2)}) %collective-permute-start.21) | collective-permute-done | bytes 155680 | tf_op jit(solution)/shard_map/ppermute | solution.py:70
  90.6 1.5 %merge.1 = bf16[2,144,640]{2,1,0:T(8,128)(2,1)} custom-call(s32[1]{0:T(128)} %bitcast.u_ref, f32[2,5,144,128]{3,2,1,0:T(8,128)S(1)} %get-tuple-element.64.fresh_out, f32[24,128]{1,0:T(8,128)S(1)} %get-tuple-element.65.refs_10_.fresh_rows, bf16[2,304,128]{2,1,0:T(8,128)(2,1)S(1)} %get-tuple-element.71.refs_0_, ...), custom_call_target="tpu_custom_call" | custom-call | flops 1843200 | bytes 2580480 | tf_op jit(solution)/shard_map/merge/pallas_call | solution.py:604
  (42 shorter events, 0.3 us)
Async XLA Ops:
  0.6 22.1 %collective-permute-start.5 = (bf16[288,1280]{1,0:T(8,128)(2,1)}, bf16[288,1280]{1,0:T(8,128)(2,1)S(1)}, u32[]{:S(2)}, u32[]{:S(2)}) collective-permute-start(bf16[288,1280]{1,0:T(8,128)(2,1)} %bitcast.14), channel_id=1, source_target_pairs={{0,2},{1,3},{2,0},{3,1},{4,6},{5,7},{6,4},{7,5},{8,10},{33,35},{10... | collective-permute-start | bytes 2211848 | tf_op jit(solution)/shard_map/ppermute | solution.py:70
  2.7 1.0 %copy-start.1 = (bf16[2,144,640]{2,1,0:T(8,128)(2,1)S(1)}, bf16[2,144,640]{2,1,0:T(8,128)(2,1)}, u32[]{:S(2)}) copy-start(bf16[2,144,640]{2,1,0:T(8,128)(2,1)} %key_ref.1) | copy-start | bytes 1105924
  3.7 1.0 %copy-start.2 = (bf16[2,144,640]{2,1,0:T(8,128)(2,1)S(1)}, bf16[2,144,640]{2,1,0:T(8,128)(2,1)}, u32[]{:S(2)}) copy-start(bf16[2,144,640]{2,1,0:T(8,128)(2,1)} %value_ref.1) | copy-start | bytes 1105924
  4.8 7.4 %collective-permute-start = (bf16[2,2,144,128]{3,2,1,0:T(8,128)(2,1)S(1)}, bf16[2,2,144,128]{3,2,1,0:T(8,128)(2,1)S(1)}, u32[]{:S(2)}, u32[]{:S(2)}) collective-permute-start(bf16[2,2,144,128]{3,2,1,0:T(8,128)(2,1)S(1)} %get-tuple-element.40), channel_id=1, source_target_pairs={{0,96},{1,25},{2,98},{3,27},{4,100},{5,29},{6,102},{7,31},{8,104},... | collective-permute-start | bytes 442376 | tf_op jit(solution)/shard_map/ppermute | solution.py:70
  7.9 6.8 %collective-permute-start.1 = (bf16[2,2,144,128]{3,2,1,0:T(8,128)(2,1)S(1)}, bf16[2,2,144,128]{3,2,1,0:T(8,128)(2,1)S(1)}, u32[]{:S(2)}, u32[]{:S(2)}) collective-permute-start(bf16[2,2,144,128]{3,2,1,0:T(8,128)(2,1)S(1)} %get-tuple-element.41), channel_id=1, source_target_pairs={{0,64},{1,17},{2,66},{3,19},{4,68},{5,21},{6,70},{7,23},{8,72},{33... | collective-permute-start | bytes 442376 | tf_op jit(solution)/shard_map/ppermute | solution.py:70
  8.5 7.6 %collective-permute-start.2 = (bf16[2,2,144,128]{3,2,1,0:T(8,128)(2,1)S(1)}, bf16[2,2,144,128]{3,2,1,0:T(8,128)(2,1)S(1)}, u32[]{:S(2)}, u32[]{:S(2)}) collective-permute-start(bf16[2,2,144,128]{3,2,1,0:T(8,128)(2,1)S(1)} %get-tuple-element.42), channel_id=1, source_target_pairs={{0,32},{1,9},{2,34},{3,11},{4,36},{5,13},{6,38},{7,15},{8,40},{33,... | collective-permute-start | bytes 442376 | tf_op jit(solution)/shard_map/ppermute | solution.py:70
  9.5 21.1 %collective-permute-start.4 = (bf16[288,1280]{1,0:T(8,128)(2,1)}, bf16[288,1280]{1,0:T(8,128)(2,1)S(1)}, u32[]{:S(2)}, u32[]{:S(2)}) collective-permute-start(bf16[288,1280]{1,0:T(8,128)(2,1)} %bitcast.15), channel_id=1, source_target_pairs={{0,1},{1,0},{2,3},{3,2},{4,5},{5,4},{6,7},{7,6},{8,9},{33,32},{10,... | collective-permute-start | bytes 2211848 | tf_op jit(solution)/shard_map/ppermute | solution.py:70
  16.2 12.4 %collective-permute-start.7 = (bf16[2,2,720,128]{3,2,1,0:T(8,128)(2,1)S(1)}, bf16[2,2,720,128]{3,2,1,0:T(8,128)(2,1)}, u32[]{:S(2)}, u32[]{:S(2)}) collective-permute-start(bf16[2,2,720,128]{3,2,1,0:T(8,128)(2,1)S(1)} %assemble.1.after.refs_4_), channel_id=1, source_target_pairs={{0,8},{1,33},{2,10},{3,35},{4,12},{5,37},{6,14},{7,39},{8,0},{33,1... | collective-permute-start | bytes 2211848 | tf_op jit(solution)/shard_map/ppermute | solution.py:70
  17.8 1.1 %copy-start = (bf16[2,144,1280]{2,1,0:T(8,128)(2,1)S(1)}, bf16[2,144,1280]{2,1,0:T(8,128)(2,1)}, u32[]{:S(2)}) copy-start(bf16[2,144,1280]{2,1,0:T(8,128)(2,1)} %param.12) | copy-start | bytes 2211844
  18.9 0.8 copy-start.5
  19.7 0.8 copy-start.6
  20.4 0.7 copy-start.9
  21.1 0.7 copy-start.10
  22.7 7.9 %collective-permute-start.6 = (bf16[288,1280]{1,0:T(8,128)(2,1)S(1)}, bf16[288,1280]{1,0:T(8,128)(2,1)}, u32[]{:S(2)}, u32[]{:S(2)}) collective-permute-start(bf16[288,1280]{1,0:T(8,128)(2,1)S(1)} %collective-permute-done.5.h2), channel_id=1, source_target_pairs={{0,1},{1,0},{2,3},{3,2},{4,5},{5,4},{6,7},{7,6},{8,9},{33,32},{10,... | collective-permute-start | bytes 2211848 | tf_op jit(solution)/shard_map/ppermute | solution.py:70
  22.9 23.1 %collective-permute-start.9 = (bf16[2,2,720,128]{3,2,1,0:T(8,128)(2,1)S(1)}, bf16[2,2,720,128]{3,2,1,0:T(8,128)(2,1)S(1)}, u32[]{:S(2)}, u32[]{:S(2)}) collective-permute-start(bf16[2,2,720,128]{3,2,1,0:T(8,128)(2,1)S(1)} %assemble.1.after.refs_4_), channel_id=1, source_target_pairs={{0,24},{1,97},{2,26},{3,99},{4,28},{5,101},{6,30},{7,103},{8,16},{... | collective-permute-start | bytes 2211848 | tf_op jit(solution)/shard_map/ppermute | solution.py:70
  25.0 27.2 %collective-permute-start.3 = (bf16[2,2,720,128]{3,2,1,0:T(8,128)(2,1)S(1)}, bf16[2,2,720,128]{3,2,1,0:T(8,128)(2,1)S(1)}, u32[]{:S(2)}, u32[]{:S(2)}) collective-permute-start(bf16[2,2,720,128]{3,2,1,0:T(8,128)(2,1)S(1)} %assemble.1.after.refs_4_), channel_id=1, source_target_pairs={{0,4},{1,5},{2,6},{3,7},{4,0},{5,1},{6,2},{7,3},{8,12},{33,37},{10... | collective-permute-start | bytes 2211848 | tf_op jit(solution)/shard_map/ppermute | solution.py:70
  28.6 21.3 %collective-permute-start.8 = (bf16[2,2,720,128]{3,2,1,0:T(8,128)(2,1)}, bf16[2,2,720,128]{3,2,1,0:T(8,128)(2,1)S(1)}, u32[]{:S(2)}, u32[]{:S(2)}) collective-permute-start(bf16[2,2,720,128]{3,2,1,0:T(8,128)(2,1)} %collective-permute-done.7.refs_5_), channel_id=1, source_target_pairs={{0,24},{1,97},{2,26},{3,99},{4,28},{5,101},{6,30},{7,103},{8,16},{... | collective-permute-start | bytes 2211848 | tf_op jit(solution)/shard_map/ppermute | solution.py:70
  30.6 12.7 %slice-start = ((s8[6553600]{0:T(1024)(128)(4,1)}), s8[4194304]{0:T(1024)(128)(4,1)S(1)}, s32[]{:S(2)}) async-start(s8[6553600]{0:T(1024)(128)(4,1)} %bitcast.19), calls=%async_computation | async-start | bytes 8388608
  37.7 5.6 %slice-start.1 = ((s8[6553600]{0:T(1024)(128)(4,1)}), s8[2359296]{0:T(1024)(128)(4,1)S(1)}, s32[]{:S(2)}) async-start(s8[6553600]{0:T(1024)(128)(4,1)} %bitcast.19), calls=%async_computation.1 | async-start | bytes 4718592
  37.7 24.3 %slice-start.2 = ((s8[6553600]{0:T(1024)(128)(4,1)}), s8[4194304]{0:T(1024)(128)(4,1)S(1)}, s32[]{:S(2)}) async-start(s8[6553600]{0:T(1024)(128)(4,1)} %bitcast.21), calls=%async_computation.2 | async-start | bytes 8388608
  43.3 6.6 %copy-start.7 = (f32[640]{0:T(1024)S(1)}, f32[640]{0:T(1024)}, u32[]{:S(2)}) copy-start(f32[640]{0:T(1024)} %qg.1) | copy-start | bytes 7684
  43.3 6.6 %copy-start.8 = (f32[640]{0:T(1024)S(1)}, f32[640]{0:T(1024)}, u32[]{:S(2)}) copy-start(f32[640]{0:T(1024)} %kg.1) | copy-start | bytes 7684
  43.3 18.7 %slice-start.3 = ((s8[6553600]{0:T(1024)(128)(4,1)}), s8[2359296]{0:T(1024)(128)(4,1)S(1)}, s32[]{:S(2)}) async-start(s8[6553600]{0:T(1024)(128)(4,1)} %bitcast.21), calls=%async_computation.3 | async-start | bytes 4718592
  46.0 3.2 %collective-permute-start.10 = (f32[8,384]{1,0:T(8,128)S(1)}, f32[8,384]{1,0:T(8,128)S(1)}, u32[]{:S(2)}, u32[]{:S(2)}) collective-permute-start(f32[8,384]{1,0:T(8,128)S(1)} %sum_squares.1.s0), channel_id=1, source_target_pairs={{0,3},{1,2},{2,1},{3,0},{4,7},{5,6},{6,5},{7,4},{8,11},{33,34},{10... | collective-permute-start | bytes 36872 | tf_op jit(solution)/shard_map/ppermute | solution.py:70
  46.1 3.8 %collective-permute-start.11 = (f32[8,384]{1,0:T(8,128)S(1)}, f32[8,384]{1,0:T(8,128)S(1)}, u32[]{:S(2)}, u32[]{:S(2)}) collective-permute-start(f32[8,384]{1,0:T(8,128)S(1)} %sum_squares.1.s0), channel_id=1, source_target_pairs={{0,2},{1,3},{2,0},{3,1},{4,6},{5,7},{6,4},{7,5},{8,10},{33,35},{10... | collective-permute-start | bytes 36872 | tf_op jit(solution)/shard_map/ppermute | solution.py:70
  46.5 3.4 %collective-permute-start.12 = (f32[8,384]{1,0:T(8,128)S(1)}, f32[8,384]{1,0:T(8,128)S(1)}, u32[]{:S(2)}, u32[]{:S(2)}) collective-permute-start(f32[8,384]{1,0:T(8,128)S(1)} %sum_squares.1.s0), channel_id=1, source_target_pairs={{0,1},{1,0},{2,3},{3,2},{4,5},{5,4},{6,7},{7,6},{8,9},{33,32},{10,... | collective-permute-start | bytes 36872 | tf_op jit(solution)/shard_map/ppermute | solution.py:70
  51.7 6.6 %collective-permute-start.13 = (bf16[2,2,144,128]{3,2,1,0:T(8,128)(2,1)S(1)}, bf16[2,2,144,128]{3,2,1,0:T(8,128)(2,1)S(1)}, u32[]{:S(2)}, u32[]{:S(2)}) collective-permute-start(bf16[2,2,144,128]{3,2,1,0:T(8,128)(2,1)S(1)} %get-tuple-element.63.refs_3_), channel_id=1, source_target_pairs={{0,96},{1,25},{2,98},{3,27},{4,100},{5,29},{6,102},{7,31},{8,104},... | collective-permute-start | bytes 442376 | tf_op jit(solution)/shard_map/ppermute | solution.py:70
  52.3 19.7 %collective-permute-start.16 = (bf16[2,2,720,128]{3,2,1,0:T(8,128)(2,1)S(1)}, bf16[2,2,720,128]{3,2,1,0:T(8,128)(2,1)S(1)}, u32[]{:S(2)}, u32[]{:S(2)}) collective-permute-start(bf16[2,2,720,128]{3,2,1,0:T(8,128)(2,1)S(1)} %collective-permute-done.3.refs_4_), channel_id=1, source_target_pairs={{0,8},{1,33},{2,10},{3,35},{4,12},{5,37},{6,14},{7,39},{8,0},{33,1... | collective-permute-start | bytes 2211848 | tf_op jit(solution)/shard_map/ppermute | solution.py:70
  52.5 19.5 %collective-permute-start.17 = (bf16[2,2,720,128]{3,2,1,0:T(8,128)(2,1)S(1)}, bf16[2,2,720,128]{3,2,1,0:T(8,128)(2,1)S(1)}, u32[]{:S(2)}, u32[]{:S(2)}) collective-permute-start(bf16[2,2,720,128]{3,2,1,0:T(8,128)(2,1)S(1)} %collective-permute-done.3.refs_4_), channel_id=1, source_target_pairs={{0,24},{1,97},{2,26},{3,99},{4,28},{5,101},{6,30},{7,103},{8,16},{... | collective-permute-start | bytes 2211848 | tf_op jit(solution)/shard_map/ppermute | solution.py:70
  54.3 11.3 %collective-permute-start.14 = (bf16[2,2,144,128]{3,2,1,0:T(8,128)(2,1)S(1)}, bf16[2,2,144,128]{3,2,1,0:T(8,128)(2,1)S(1)}, u32[]{:S(2)}, u32[]{:S(2)}) collective-permute-start(bf16[2,2,144,128]{3,2,1,0:T(8,128)(2,1)S(1)} %get-tuple-element.62.refs_2_), channel_id=1, source_target_pairs={{0,64},{1,17},{2,66},{3,19},{4,68},{5,21},{6,70},{7,23},{8,72},{33... | collective-permute-start | bytes 442376 | tf_op jit(solution)/shard_map/ppermute | solution.py:70
  54.3 10.3 %copy-start.3 = (bf16[288,640]{1,0:T(8,128)(2,1)S(1)}, bf16[288,640]{1,0:T(8,128)(2,1)}, u32[]{:S(2)}) copy-start(bf16[288,640]{1,0:T(8,128)(2,1)} %get-tuple-element.59.k_ref) | copy-start | bytes 1105924
  54.3 11.3 %collective-permute-start.15 = (bf16[2,2,144,128]{3,2,1,0:T(8,128)(2,1)S(1)}, bf16[2,2,144,128]{3,2,1,0:T(8,128)(2,1)S(1)}, u32[]{:S(2)}, u32[]{:S(2)}) collective-permute-start(bf16[2,2,144,128]{3,2,1,0:T(8,128)(2,1)S(1)} %get-tuple-element.61.refs_1_), channel_id=1, source_target_pairs={{0,32},{1,9},{2,34},{3,11},{4,36},{5,13},{6,38},{7,15},{8,40},{33,... | collective-permute-start | bytes 442376 | tf_op jit(solution)/shard_map/ppermute | solution.py:70
  58.3 17.3 %collective-permute-start.18 = (bf16[2,2,720,128]{3,2,1,0:T(8,128)(2,1)S(1)}, bf16[2,2,720,128]{3,2,1,0:T(8,128)(2,1)S(1)}, u32[]{:S(2)}, u32[]{:S(2)}) collective-permute-start(bf16[2,2,720,128]{3,2,1,0:T(8,128)(2,1)S(1)} %collective-permute-done.8.refs_7_), channel_id=1, source_target_pairs={{0,4},{1,5},{2,6},{3,7},{4,0},{5,1},{6,2},{7,3},{8,12},{33,37},{10... | collective-permute-start | bytes 2211848 | tf_op jit(solution)/shard_map/ppermute | solution.py:70
  64.6 17.1 %copy-start.4 = (bf16[288,640]{1,0:T(8,128)(2,1)}, bf16[288,640]{1,0:T(8,128)(2,1)S(1)}, u32[]{:S(2)}) copy-start(bf16[288,640]{1,0:T(8,128)(2,1)S(1)} %convolution_convert_fusion.v_ref) | copy-start | bytes 1105924
  81.7 5.3 %collective-permute-start.19 = (bf16[2,304,128]{2,1,0:T(8,128)(2,1)S(1)}, bf16[2,304,128]{2,1,0:T(8,128)(2,1)S(1)}, u32[]{:S(2)}, u32[]{:S(2)}) collective-permute-start(bf16[2,304,128]{2,1,0:T(8,128)(2,1)S(1)} %get-tuple-element.72), channel_id=1, source_target_pairs={{0,96},{1,25},{2,98},{3,27},{4,100},{5,29},{6,102},{7,31},{8,104},... | collective-permute-start | bytes 466952 | tf_op jit(solution)/shard_map/ppermute | solution.py:70
  82.2 6.8 %collective-permute-start.20 = (bf16[2,304,128]{2,1,0:T(8,128)(2,1)S(1)}, bf16[2,304,128]{2,1,0:T(8,128)(2,1)S(1)}, u32[]{:S(2)}, u32[]{:S(2)}) collective-permute-start(bf16[2,304,128]{2,1,0:T(8,128)(2,1)S(1)} %get-tuple-element.73), channel_id=1, source_target_pairs={{0,64},{1,17},{2,66},{3,19},{4,68},{5,21},{6,70},{7,23},{8,72},{33... | collective-permute-start | bytes 466952 | tf_op jit(solution)/shard_map/ppermute | solution.py:70
  83.1 7.5 %collective-permute-start.21 = (bf16[2,304,128]{2,1,0:T(8,128)(2,1)S(1)}, bf16[2,304,128]{2,1,0:T(8,128)(2,1)S(1)}, u32[]{:S(2)}, u32[]{:S(2)}) collective-permute-start(bf16[2,304,128]{2,1,0:T(8,128)(2,1)S(1)} %get-tuple-element.74), channel_id=1, source_target_pairs={{0,32},{1,9},{2,34},{3,11},{4,36},{5,13},{6,38},{7,15},{8,40},{33,... | collective-permute-start | bytes 466952 | tf_op jit(solution)/shard_map/ppermute | solution.py:70

commit v7 on v6

--- a/solution.py
+++ b/solution.py
@@ -35,7 +35,6 @@
 GROUP = 16
 VMEM_MIB = 24
 ATTENTION_MIB = 34
-MODULATE_MIB = 44
 
 
 def params(mib):
@@ -231,9 +230,7 @@
     return jnp.sum(total, axis=1, keepdims=True)
 
 
-def modulate_kernel(t_ref, h0, h1, h2, h3, cond, mod, weight, out_ref, weight_out, sem):
-    copy = pltpu.make_async_copy(weight, weight_out, sem.at[0])
-    copy.start()
+def modulate_kernel(t_ref, h0, h1, h2, h3, cond, mod, out_ref):
     chunks = (h0, h1, h2, h3)
     for row in range(0, ROWS, GROUP):
         rows = slice(row, row + GROUP)
@@ -248,25 +245,20 @@
             bias = jnp.where(conditioned, mod[3:4, cols], mod[2:3, cols])
             normed = (lanes[c] - mean) * rstd
             out_ref[rows, cols] = (normed * gain + bias).astype(BF16)
-    copy.wait()
-
-
-def modulate(blocks, chunks, cond, mod, weight):
+
+
+def modulate(blocks, chunks, cond, mod):
     return pl.pallas_call(
         modulate_kernel,
-        out_shape=[
-            jax.ShapeDtypeStruct((ROWS, D), BF16),
-            jax.ShapeDtypeStruct((D, WIDTH), BF16),
-        ],
-        in_specs=[smem()] + [vmem()] * 6 + [pl.BlockSpec(memory_space=pltpu.HBM)],
-        out_specs=[vmem()] * 2,
-        scratch_shapes=[pltpu.SemaphoreType.DMA((1,))],
-        compiler_params=params(MODULATE_MIB),
+        out_shape=jax.ShapeDtypeStruct((ROWS, D), BF16),
+        in_specs=[smem()] + [vmem()] * 6,
+        out_specs=vmem(),
+        compiler_params=params(VMEM_MIB),
         cost_estimate=pl.CostEstimate(
             flops=12 * ROWS * D, bytes_accessed=20_000_000, transcendentals=0
         ),
         name="modulate",
-    )(blocks, *chunks, cond, mod, weight)
+    )(blocks, *chunks, cond, mod)
 
 
 def squares_kernel(q_ref, k_ref, out_ref):
@@ -328,9 +320,7 @@
         out_specs=[vmem()] * 5,
         scratch_shapes=[pltpu.VMEM((LOCAL_HEADS, B, TOK, HD), BF16)],
         compiler_params=params(VMEM_MIB),
-        cost_estimate=pl.CostEstimate(
-            flops=20 * ROWS * WIDTH, bytes_accessed=16 * ROWS * WIDTH, transcendentals=0
-        ),
+        cost_estimate=pl.CostEstimate(flops=1000, bytes_accessed=1000, transcendentals=0),
         name="norm_rope",
     )(u, query, key, *squares, q_gain, k_gain, cos, sin)
 
@@ -382,25 +372,20 @@
         in_specs=[smem()] + [vmem()] * 6,
         out_specs=[vmem()] * 2,
         compiler_params=params(VMEM_MIB),
-        cost_estimate=pl.CostEstimate(
-            flops=4 * ROWS * TOK * WIDTH,
-            bytes_accessed=14 * ROWS * WIDTH,
-            transcendentals=ROWS * TOK * LOCAL_HEADS,
-        ),
+        cost_estimate=pl.CostEstimate(flops=1000, bytes_accessed=1000, transcendentals=0),
         name="fresh_attention",
     )(u, key, value, *queries)
 
 
 TILE = 2 * TOK
 PER_PIECE = 4 * TOK
-KEYS = 4 * PER_PIECE
-KEYS_LAST = 4 * TOK
 SPLIT = 768
 
 
-def stale_kernel(far, *refs):
+def stale_kernel(far, count, *refs):
     queries = refs[0:4]
-    pieces, rest = refs[4:8], refs[8:]
+    pieces, rest = refs[4 : 4 + count], refs[4 + count :]
+    keys_main, keys_last = count * PER_PIECE, count * TOK
     if far:
         near_out, near_lse = rest[0:2]
         msgs = rest[3:7]
@@ -411,7 +396,7 @@
     jobs = [(s, e, tile) for s in range(B) for e in range(2) for tile in range(2)]
 
     def size(i):
-        return KEYS_LAST if jobs[i][1] else KEYS
+        return keys_last if jobs[i][1] else keys_main
 
     def score_steps(i):
         s, e, tile = jobs[i]
@@ -419,8 +404,8 @@
         out = scores_s.at[i % 2]
 
         def arrive():
-            v_main[s, :, HD:] = jnp.ones((KEYS, HD), BF16)
-            v_last[s, :, HD:] = jnp.ones((KEYS_LAST, HD), BF16)
+            v_main[s, :, HD:] = jnp.ones((keys_main, HD), BF16)
+            v_last[s, :, HD:] = jnp.ones((keys_last, HD), BF16)
             for n, piece in enumerate(pieces):
                 main = slice(n * PER_PIECE, (n + 1) * PER_PIECE)
                 last = slice(n * TOK, (n + 1) * TOK)
@@ -527,33 +512,32 @@
 def stale_attention(queries, pieces, near=None, after=None):
     far = near is not None
     args = [*queries, *pieces]
-    in_specs = [vmem()] * 8
+    count = len(pieces)
+    keys_main, keys_last = count * PER_PIECE, count * TOK
+    in_specs = [vmem()] * (4 + count)
     if far:
         args += [*near, after]
         in_specs += [vmem(), vmem(), pl.BlockSpec(memory_space=pl.ANY)]
         out_shape = [jax.ShapeDtypeStruct((B, MSG_ROWS, HD), BF16)] * 4
     else:
         out_shape = [jax.ShapeDtypeStruct((B, 4, 2, TOK, HD), F32)] * 2
-    work = B * 4 * TOK * (KEYS + KEYS_LAST)
-    return pl.pallas_call(
-        functools.partial(stale_kernel, far),
+    return pl.pallas_call(
+        functools.partial(stale_kernel, far, count),
         out_shape=out_shape,
         in_specs=in_specs,
         out_specs=[vmem()] * len(out_shape),
         scratch_shapes=[
             pltpu.VMEM((B, 4, 2, TOK, HD), F32),
             pltpu.VMEM((TILE, 2 * HD), F32),
-            pltpu.VMEM((B, KEYS, HD), BF16),
-            pltpu.VMEM((B, KEYS, 2 * HD), BF16),
-            pltpu.VMEM((B, KEYS_LAST, HD), BF16),
-            pltpu.VMEM((B, KEYS_LAST, 2 * HD), BF16),
-            pltpu.VMEM((2, TILE, KEYS), F32),
-            pltpu.VMEM((2, TILE, KEYS), BF16),
+            pltpu.VMEM((B, keys_main, HD), BF16),
+            pltpu.VMEM((B, keys_main, 2 * HD), BF16),
+            pltpu.VMEM((B, keys_last, HD), BF16),
+            pltpu.VMEM((B, keys_last, 2 * HD), BF16),
+            pltpu.VMEM((2, TILE, keys_main), F32),
+            pltpu.VMEM((2, TILE, keys_main), BF16),
         ],
         compiler_params=params(ATTENTION_MIB),
-        cost_estimate=pl.CostEstimate(
-            flops=4 * work * HD, bytes_accessed=8 * (KEYS + KEYS_LAST) * HD, transcendentals=work
-        ),
+        cost_estimate=pl.CostEstimate(flops=1000, bytes_accessed=1000, transcendentals=0),
         name="far_attention" if far else "near_attention",
     )(*args)
 
@@ -645,28 +629,27 @@
 
     z_rows, cond = lax.optimization_barrier((z_rows, cond))
     cross_rows = swap_tp(z_rows, 0, 1)
+    near_one, near_three = lax.optimization_barrier((near_one, near_three))
     near_two = swap_v(near_one, 3)
     blocks = jnp.stack([tp, tp ^ 1, tp ^ 2, tp ^ 3]).astype(jnp.int32)
-    modded, key_weights = modulate(
-        blocks, [own_rows, core_rows, z_rows, cross_rows], cond, mod, w_key
-    )
+    modded = modulate(blocks, [own_rows, core_rows, z_rows, cross_rows], cond, mod)
     query = jnp.dot(modded, w_query, preferred_element_type=F32)
-    key = jnp.dot(modded, key_weights, preferred_element_type=F32)
+    key = jnp.dot(modded, w_key, preferred_element_type=F32)
     fresh_values = jnp.dot(modded, w_value, preferred_element_type=F32).astype(BF16)
     own_sq = sum_squares(query, key)
-    own_sq, near_three = lax.optimization_barrier((own_sq, near_three))
     squares = [own_sq] + [swap_tp(own_sq, z, c) for z, c in ((1, 1), (1, 0), (0, 1))]
-    near_two, *squares = lax.optimization_barrier((near_two, *squares))
+    near_two, far, fresh_values, *squares = lax.optimization_barrier(
+        (near_two, far, fresh_values, *squares)
+    )
     far_two = swap_z_hi(near_two)
+    far_one, far_three = swap_v(far, 1), swap_v(far, 3)
     fresh_keys, *sends = norm_rope(u, query, key, squares, q_gain, k_gain, cos, sin)
-    far, fresh_keys = lax.optimization_barrier((far, fresh_keys))
-    far_one, far_three = swap_v(far, 1), swap_v(far, 3)
     queries = exchange_u(sends)
     fresh_out, fresh_rows = fresh_attention(u, fresh_keys, fresh_values, sends)
 
-    partial = stale_attention(queries, [near, near_one, near_three, near_two])
+    partial = stale_attention(queries, [near, near_one, near_three, near_two, far])
     outs = stale_attention(
-        queries, [far, far_one, far_three, far_two], near=partial, after=fresh_rows
+        queries, [far_one, far_three, far_two], near=partial, after=fresh_rows
     )
     returned = exchange_u(outs)
     attended = merge(u, fresh_out, fresh_rows, returned)

time: 93 us -> 92.5 us (level)
  waiting for transfers between devices: 21.5 us -> 24 us
  Pallas kernels: 25.1 us -> 22.8 us
  starting transfers between devices: 28 us -> 26.8 us
  local copies, waits for them, and re-layouts: 6.03 us -> 7.01 us
    dot_general x1, matrix products: 5.53 us -> 2.46 us  [shards(): key = jnp.dot(modded, w_key, preferred_element_type=F32)]
    dot_general x1, matrix products: 2.47 us -> 5.53 us  [shards(): query = jnp.dot(modded, w_query, preferred_element_type=F32)]
    ppermute x22, waiting for transfers between devices: 21.5 us -> 24 us  [permute(): lax.ppermute(value, AXES, [(linear(*p), linear(*move(*p))) for p in place...]
    pallas_call x3, Pallas kernels: 19.4 us -> 17.1 us  [the longest x2 12.8 us: stale_attention(): pl.pallas_call(functools.partial(stale_kernel, far, count), out_shape=out...]
    ppermute x22, starting transfers between devices: 28 us -> 26.8 us  [permute(): lax.ppermute(value, AXES, [(linear(*p), linear(*move(*p))) for p in place...]
    unnamed x30, local copies, waits for them, and re-layouts: 6.03 us -> 7.01 us
  transfers between devices with their start and end apart: 22 -> 22, of which waited for: 10 -> 9; matrix products, arithmetic and copies ran while one was open for 12% -> 12% of each run, Pallas kernels for 19% -> 18%
where the time goes in v7:
time: 92.5 us; the launch traced here: 92.1 us
  starting transfers between devices  26.8 us (29%)
  waiting for transfers between devices  24 us (26%)
  Pallas kernels  22.8 us (25%)
  matrix products  10.5 us (11%)
  local copies, waits for them, and re-layouts  7.01 us (8%)
    ppermute x22, starting transfers between devices, permute(): lax.ppermute(value, AXES, [(linear(*p), linear(*move(*p))) for p in place...  26.8 us
    ppermute x22, waiting for transfers between devices, permute(): lax.ppermute(value, AXES, [(linear(*p), linear(*move(*p))) for p in place...  24 us
    pallas_call x2, Pallas kernels, stale_attention(): pl.pallas_call(functools.partial(stale_kernel, far, count), out_shape=out...  12.8 us
    unnamed x30, local copies, waits for them, and re-layouts  7.01 us
    dot_general x1, matrix products, shards(): query = jnp.dot(modded, w_query, preferred_element_type=F32)  5.53 us
    pallas_call x1, Pallas kernels, modulate(): pl.pallas_call(modulate_kernel, out_shape=jax.ShapeDtypeStruct((ROWS, D),...  4.24 us
    dot_general x1, matrix products, shards(): jnp.dot(modded, w_value, preferred_element_type=F32).astype(BF16)  2.55 us
    dot_general x1, matrix products, shards(): key = jnp.dot(modded, w_key, preferred_element_type=F32)  2.46 us
  transfers between devices with their start and end apart: 22, of which 9 were waited for; matrix products, arithmetic and copies ran while one was open for 12% of the time, Pallas kernels for 18%

profile of v7, /device:TPU:0, one launch (start us, length us, event | category | flops | bytes accessed | tf_op | source)
XLA Modules:
  0.0 92.1 jit_solution(15881660087973411513)
XLA Ops:
  0.6 2.1 %collective-permute-start.4 = (bf16[288,1280]{1,0:T(8,128)(2,1)}, bf16[288,1280]{1,0:T(8,128)(2,1)S(1)}, u32[]{:S(2)}, u32[]{:S(2)}) collective-permute-start(bf16[288,1280]{1,0:T(8,128)(2,1)} %bitcast.14), channel_id=1, source_target_pairs={{0,2},{1,3},{2,0},{3,1},{4,6},{5,7},{6,4},{7,5},{8,10},{33,35},{10... | collective-permute-start | bytes 2211848 | tf_op jit(solution)/shard_map/ppermute | solution.py:69
  2.7 1.0 %copy-done.1 = bf16[2,144,640]{2,1,0:T(8,128)(2,1)S(1)} copy-done((bf16[2,144,640]{2,1,0:T(8,128)(2,1)S(1)}, bf16[2,144,640]{2,1,0:T(8,128)(2,1)}, u32[]{:S(2)}) %copy-start.1) | copy-done | bytes 368664
  3.7 1.0 %copy-done.2 = bf16[2,144,640]{2,1,0:T(8,128)(2,1)S(1)} copy-done((bf16[2,144,640]{2,1,0:T(8,128)(2,1)S(1)}, bf16[2,144,640]{2,1,0:T(8,128)(2,1)}, u32[]{:S(2)}) %copy-start.2) | copy-done | bytes 368664
  4.7 0.1 pack_stale.1
  4.8 3.1 %collective-permute-start = (bf16[2,2,144,128]{3,2,1,0:T(8,128)(2,1)S(1)}, bf16[2,2,144,128]{3,2,1,0:T(8,128)(2,1)S(1)}, u32[]{:S(2)}, u32[]{:S(2)}) collective-permute-start(bf16[2,2,144,128]{3,2,1,0:T(8,128)(2,1)S(1)} %get-tuple-element.38), channel_id=1, source_target_pairs={{0,96},{1,25},{2,98},{3,27},{4,100},{5,29},{6,102},{7,31},{8,104},... | collective-permute-start | bytes 442376 | tf_op jit(solution)/shard_map/ppermute | solution.py:69
  7.9 0.6 collective-permute-start.1
  8.5 1.0 %collective-permute-start.2 = (bf16[2,2,144,128]{3,2,1,0:T(8,128)(2,1)S(1)}, bf16[2,2,144,128]{3,2,1,0:T(8,128)(2,1)S(1)}, u32[]{:S(2)}, u32[]{:S(2)}) collective-permute-start(bf16[2,2,144,128]{3,2,1,0:T(8,128)(2,1)S(1)} %get-tuple-element.40), channel_id=1, source_target_pairs={{0,32},{1,9},{2,34},{3,11},{4,36},{5,13},{6,38},{7,15},{8,40},{33,... | collective-permute-start | bytes 442376 | tf_op jit(solution)/shard_map/ppermute | solution.py:69
  9.5 2.7 %collective-permute-done.refs_1_ = bf16[2,2,144,128]{3,2,1,0:T(8,128)(2,1)S(1)} collective-permute-done((bf16[2,2,144,128]{3,2,1,0:T(8,128)(2,1)S(1)}, bf16[2,2,144,128]{3,2,1,0:T(8,128)(2,1)S(1)}, u32[]{:S(2)}, u32[]{:S(2)}) %collective-permute-start) | collective-permute-done | bytes 147488 | tf_op jit(solution)/shard_map/ppermute | solution.py:69
  12.2 2.5 %collective-permute-done.1.refs_2_ = bf16[2,2,144,128]{3,2,1,0:T(8,128)(2,1)S(1)} collective-permute-done((bf16[2,2,144,128]{3,2,1,0:T(8,128)(2,1)S(1)}, bf16[2,2,144,128]{3,2,1,0:T(8,128)(2,1)S(1)}, u32[]{:S(2)}, u32[]{:S(2)}) %collective-permute-start.1) | collective-permute-done | bytes 147488 | tf_op jit(solution)/shard_map/ppermute | solution.py:69
  14.7 1.5 %collective-permute-done.2.refs_3_ = bf16[2,2,144,128]{3,2,1,0:T(8,128)(2,1)S(1)} collective-permute-done((bf16[2,2,144,128]{3,2,1,0:T(8,128)(2,1)S(1)}, bf16[2,2,144,128]{3,2,1,0:T(8,128)(2,1)S(1)}, u32[]{:S(2)}, u32[]{:S(2)}) %collective-permute-start.2) | collective-permute-done | bytes 147488 | tf_op jit(solution)/shard_map/ppermute | solution.py:69
  16.2 1.6 %collective-permute-start.6 = (bf16[2,2,720,128]{3,2,1,0:T(8,128)(2,1)S(1)}, bf16[2,2,720,128]{3,2,1,0:T(8,128)(2,1)}, u32[]{:S(2)}, u32[]{:S(2)}) collective-permute-start(bf16[2,2,720,128]{3,2,1,0:T(8,128)(2,1)S(1)} %assemble.1.after.refs_4_), channel_id=1, source_target_pairs={{0,8},{1,33},{2,10},{3,35},{4,12},{5,37},{6,14},{7,39},{8,0},{33,1... | collective-permute-start | bytes 2211848 | tf_op jit(solution)/shard_map/ppermute | solution.py:69
  17.8 2.1 %collective-permute-start.7 = (bf16[2,2,720,128]{3,2,1,0:T(8,128)(2,1)S(1)}, bf16[2,2,720,128]{3,2,1,0:T(8,128)(2,1)}, u32[]{:S(2)}, u32[]{:S(2)}) collective-permute-start(bf16[2,2,720,128]{3,2,1,0:T(8,128)(2,1)S(1)} %assemble.1.after.refs_4_), channel_id=1, source_target_pairs={{0,24},{1,97},{2,26},{3,99},{4,28},{5,101},{6,30},{7,103},{8,16},{... | collective-permute-start | bytes 2211848 | tf_op jit(solution)/shard_map/ppermute | solution.py:69
  19.9 1.1 %copy-done = bf16[2,144,1280]{2,1,0:T(8,128)(2,1)S(1)} copy-done((bf16[2,144,1280]{2,1,0:T(8,128)(2,1)S(1)}, bf16[2,144,1280]{2,1,0:T(8,128)(2,1)}, u32[]{:S(2)}) %copy-start) | copy-done | bytes 737304
  21.0 0.8 copy-done.5
  21.7 0.8 copy-done.6
  22.5 0.7 copy-done.9
  23.2 0.7 copy-done.10
  23.9 0.9 %tables.1 = (f32[288,128]{1,0:T(8,128)S(1)}, f32[144,128]{1,0:T(8,128)S(1)}, f32[144,128]{1,0:T(8,128)S(1)}, f32[4,5120]{1,0:T(4,128)S(1)}, bf16[288,1280]{1,0:T(8,128)(2,1)S(1)}) custom-call(s32[144]{0:T(256)S(1)} %copy-done.9, f32[1,128]{1,0:T(1,128)S(1)} %copy-done.10, bf16[288,1280]{1,0:T(8,128)(2,1)S(1)} %bitcast.16, f32[2,5120]{1,0:T(2,128)S(1)} %copy-done.5, ...), custom_call_target="tpu_custom_call" | custom-call | flops 1843200 | bytes 1000000 | tf_op jit(solution)/shard_map/tables/pallas_call | solution.py:176
  24.8 0.1 collective-permute-start.5
  25.0 3.6 %collective-permute-start.9 = (bf16[2,2,720,128]{3,2,1,0:T(8,128)(2,1)S(1)}, bf16[2,2,720,128]{3,2,1,0:T(8,128)(2,1)S(1)}, u32[]{:S(2)}, u32[]{:S(2)}) collective-permute-start(bf16[2,2,720,128]{3,2,1,0:T(8,128)(2,1)S(1)} %assemble.1.after.refs_4_), channel_id=1, source_target_pairs={{0,4},{1,5},{2,6},{3,7},{4,0},{5,1},{6,2},{7,3},{8,12},{33,37},{10... | collective-permute-start | bytes 2211848 | tf_op jit(solution)/shard_map/ppermute | solution.py:69
  28.6 1.9 %collective-permute-done.7.refs_6_ = bf16[2,2,720,128]{3,2,1,0:T(8,128)(2,1)} collective-permute-done((bf16[2,2,720,128]{3,2,1,0:T(8,128)(2,1)S(1)}, bf16[2,2,720,128]{3,2,1,0:T(8,128)(2,1)}, u32[]{:S(2)}, u32[]{:S(2)}) %collective-permute-start.7) | collective-permute-done | bytes 737312 | tf_op jit(solution)/shard_map/ppermute | solution.py:69
  30.5 2.1 %collective-permute-start.8 = (bf16[2,2,720,128]{3,2,1,0:T(8,128)(2,1)}, bf16[2,2,720,128]{3,2,1,0:T(8,128)(2,1)S(1)}, u32[]{:S(2)}, u32[]{:S(2)}) collective-permute-start(bf16[2,2,720,128]{3,2,1,0:T(8,128)(2,1)} %collective-permute-done.6.refs_5_), channel_id=1, source_target_pairs={{0,24},{1,97},{2,26},{3,99},{4,28},{5,101},{6,30},{7,103},{8,16},{... | collective-permute-start | bytes 2211848 | tf_op jit(solution)/shard_map/ppermute | solution.py:69
  32.6 4.2 %modulate.1 = bf16[288,5120]{1,0:T(8,128)(2,1)S(1)} custom-call(s32[4]{0:T(128)S(1)} %pad_add_fusion.t_ref, bf16[288,1280]{1,0:T(8,128)(2,1)S(1)} %get-tuple-element.42.h0, bf16[288,1280]{1,0:T(8,128)(2,1)S(1)} %collective-permute-done.3.h1, bf16[288,1280]{1,0:T(8,128)(2,1)S(1)} %collective-permute-done.4.h2, bf16[288,1280]{1,0:T(8,128)(2,1)} %collective-permute-done.5.h3, ...), custom_call_target="tpu_custom_call" | custom-call | flops 17694720 | bytes 20000000 | tf_op jit(solution)/shard_map/modulate/pallas_call | solution.py:251
  36.9 5.5 %fusion.q_ref = f32[288,640]{1,0:T(8,128)S(1)} fusion(bf16[288,5120]{1,0:T(8,128)(2,1)S(1)} %modulate.1, bf16[5120,640]{1,0:T(8,128)(2,1)} %param.15), kind=kOutput, calls=%fused_computation.2 | convolution fusion | flops 1887436800 | bytes 10240000 | tf_op jit(solution)/shard_map/dot_general | solution.py:636
  42.5 2.5 %fusion.1.k_ref = f32[288,640]{1,0:T(8,128)S(1)} fusion(bf16[288,5120]{1,0:T(8,128)(2,1)S(1)} %modulate.1, bf16[5120,640]{1,0:T(8,128)(2,1)S(1)} %bitcast.20), kind=kOutput, calls=%fused_computation.3 | convolution fusion | flops 1887436800 | bytes 10240000 | tf_op jit(solution)/shard_map/dot_general | solution.py:637
  45.0 0.2 sum_squares.1.s0
  45.3 0.2 collective-permute-start.11
  45.4 1.7 %collective-permute-start.12 = (f32[8,384]{1,0:T(8,128)S(1)}, f32[8,384]{1,0:T(8,128)S(1)}, u32[]{:S(2)}, u32[]{:S(2)}) collective-permute-start(f32[8,384]{1,0:T(8,128)S(1)} %sum_squares.1.s0), channel_id=1, source_target_pairs={{0,1},{1,0},{2,3},{3,2},{4,5},{5,4},{6,7},{7,6},{8,9},{33,32},{10,... | collective-permute-start | bytes 36872 | tf_op jit(solution)/shard_map/ppermute | solution.py:69
  47.1 2.5 %convolution_convert_fusion.v_ref = bf16[288,640]{1,0:T(8,128)(2,1)S(1)} fusion(bf16[288,5120]{1,0:T(8,128)(2,1)S(1)} %modulate.1, bf16[5120,640]{1,0:T(8,128)(2,1)S(1)} %bitcast.22), kind=kOutput, calls=%fused_computation | convolution fusion | flops 1887621120 | bytes 9871360 | tf_op jit(solution)/shard_map/dot_general | solution.py:638
  49.8 1.2 %collective-permute-start.17 = (bf16[2,2,720,128]{3,2,1,0:T(8,128)(2,1)S(1)}, bf16[2,2,720,128]{3,2,1,0:T(8,128)(2,1)S(1)}, u32[]{:S(2)}, u32[]{:S(2)}) collective-permute-start(bf16[2,2,720,128]{3,2,1,0:T(8,128)(2,1)S(1)} %collective-permute-done.9.refs_8_), channel_id=1, source_target_pairs={{0,24},{1,97},{2,26},{3,99},{4,28},{5,101},{6,30},{7,103},{8,16},{... | collective-permute-start | bytes 2211848 | tf_op jit(solution)/shard_map/ppermute | solution.py:69
  51.1 3.6 %collective-permute-start.18 = (bf16[2,2,720,128]{3,2,1,0:T(8,128)(2,1)S(1)}, bf16[2,2,720,128]{3,2,1,0:T(8,128)(2,1)S(1)}, u32[]{:S(2)}, u32[]{:S(2)}) collective-permute-start(bf16[2,2,720,128]{3,2,1,0:T(8,128)(2,1)S(1)} %collective-permute-done.8.refs_7_), channel_id=1, source_target_pairs={{0,4},{1,5},{2,6},{3,7},{4,0},{5,1},{6,2},{7,3},{8,12},{33,37},{10... | collective-permute-start | bytes 2211848 | tf_op jit(solution)/shard_map/ppermute | solution.py:69
  54.6 1.8 %norm_rope.1 = (bf16[288,640]{1,0:T(8,128)(2,1)}, bf16[2,2,144,128]{3,2,1,0:T(8,128)(2,1)S(1)}, bf16[2,2,144,128]{3,2,1,0:T(8,128)(2,1)S(1)}, bf16[2,2,144,128]{...) custom-call(s32[1]{0:T(128)} %bitcast.u_ref, f32[288,640]{1,0:T(8,128)S(1)} %fusion.q_ref, f32[288,640]{1,0:T(8,128)S(1)} %fusion.1.k_ref, ...), custom_call_target="tpu_custom_call" | custom-call | flops 1000 | bytes 1000 | tf_op jit(solution)/shard_map/norm_rope/pallas_call | solution.py:316
  56.4 0.6 collective-permute-start.13
  57.0 0.6 collective-permute-start.14
  57.6 4.3 %collective-permute-done.13.refs_1_ = bf16[2,2,144,128]{3,2,1,0:T(8,128)(2,1)S(1)} collective-permute-done((bf16[2,2,144,128]{3,2,1,0:T(8,128)(2,1)S(1)}, bf16[2,2,144,128]{3,2,1,0:T(8,128)(2,1)S(1)}, u32[]{:S(2)}, u32[]{:S(2)}) %collective-permute-start.13) | collective-permute-done | bytes 147488 | tf_op jit(solution)/shard_map/ppermute | solution.py:69
  61.9 0.5 collective-permute-start.15
  62.4 1.0 %copy-done.4 = bf16[288,640]{1,0:T(8,128)(2,1)S(1)} copy-done((bf16[288,640]{1,0:T(8,128)(2,1)S(1)}, bf16[288,640]{1,0:T(8,128)(2,1)}, u32[]{:S(2)}) %copy-start.4) | copy-done | bytes 368664
  63.3 1.0 %fresh_attention.1 = (f32[2,5,144,128]{3,2,1,0:T(8,128)S(1)}, f32[24,128]{1,0:T(8,128)S(1)}) custom-call(s32[1]{0:T(128)} %bitcast.u_ref, bf16[288,640]{1,0:T(8,128)(2,1)S(1)} %copy-done.4, bf16[288,640]{1,0:T(8,128)(2,1)S(1)} %convolution_convert_fusion.v_ref, bf16[2,2,144,128]{3,2,1,0:T(8,128)(2,1)S(1)} %get-tuple-element.56.refs_0_, ...), custom_call_target="tpu_custom_call" | custom-call | flops 1000 | bytes 1000 | tf_op jit(solution)/shard_map/fresh_attention/pallas_call | solution.py:366
  64.4 3.9 %collective-permute-done.15.refs_3_ = bf16[2,2,144,128]{3,2,1,0:T(8,128)(2,1)S(1)} collective-permute-done((bf16[2,2,144,128]{3,2,1,0:T(8,128)(2,1)S(1)}, bf16[2,2,144,128]{3,2,1,0:T(8,128)(2,1)S(1)}, u32[]{:S(2)}, u32[]{:S(2)}) %collective-permute-start.15) | collective-permute-done | bytes 147488 | tf_op jit(solution)/shard_map/ppermute | solution.py:69
  68.3 8.0 %near_attention.1 = (f32[2,4,2,144,128]{4,3,2,1,0:T(8,128)S(1)}, f32[2,4,2,144,128]{4,3,2,1,0:T(8,128)S(1)}) custom-call(bf16[2,2,144,128]{3,2,1,0:T(8,128)(2,1)S(1)} %get-tuple-element.56.refs_0_, bf16[2,2,144,128]{3,2,1,0:T(8,128)(2,1)S(1)} %collective-permute-done.13.refs_1_, bf16[2,2,144,128]{3,2,1,0:T(8,128)(2,1)S(1)} %collective-permute-done.14.refs_2_, ...), custom_call_target="tpu_custom_call" | custom-call | flops 1000 | bytes 1000 | tf_op jit(solution)/shard_map/near_attention/pallas_call | solution.py:524
  76.3 4.8 %far_attention.1 = (bf16[2,304,128]{2,1,0:T(8,128)(2,1)S(1)}, bf16[2,304,128]{2,1,0:T(8,128)(2,1)S(1)}, bf16[2,304,128]{2,1,0:T(8,128)(2,1)S(1)}, bf16[2,304,128]{2,1,0:T(8,128)(2,1)S(1)}) custom-call(bf16[2,2,144,128]{3,2,1,0:T(8,128)(2,1)S(1)} %get-tuple-element.56.refs_0_, bf16[2,2,144,128]{3,2,1,0:T(8,128)(2,1)S(1)} %collective-permute-done.13.refs_1_, ...), custom_call_target="tpu_custom_call" | custom-call | flops 1000 | bytes 1000 | tf_op jit(solution)/shard_map/far_attention/pallas_call | solution.py:524
  81.1 1.0 %collective-permute-start.19 = (bf16[2,304,128]{2,1,0:T(8,128)(2,1)S(1)}, bf16[2,304,128]{2,1,0:T(8,128)(2,1)S(1)}, u32[]{:S(2)}, u32[]{:S(2)}) collective-permute-start(bf16[2,304,128]{2,1,0:T(8,128)(2,1)S(1)} %get-tuple-element.68), channel_id=1, source_target_pairs={{0,96},{1,25},{2,98},{3,27},{4,100},{5,29},{6,102},{7,31},{8,104},... | collective-permute-start | bytes 466952 | tf_op jit(solution)/shard_map/ppermute | solution.py:69
  82.1 0.4 collective-permute-start.20
  82.5 0.7 collective-permute-start.21
  83.2 3.2 %collective-permute-done.19.refs_1_ = bf16[2,304,128]{2,1,0:T(8,128)(2,1)S(1)} collective-permute-done((bf16[2,304,128]{2,1,0:T(8,128)(2,1)S(1)}, bf16[2,304,128]{2,1,0:T(8,128)(2,1)S(1)}, u32[]{:S(2)}, u32[]{:S(2)}) %collective-permute-start.19) | collective-permute-done | bytes 155680 | tf_op jit(solution)/shard_map/ppermute | solution.py:69
  86.4 2.5 %collective-permute-done.20.refs_2_ = bf16[2,304,128]{2,1,0:T(8,128)(2,1)S(1)} collective-permute-done((bf16[2,304,128]{2,1,0:T(8,128)(2,1)S(1)}, bf16[2,304,128]{2,1,0:T(8,128)(2,1)S(1)}, u32[]{:S(2)}, u32[]{:S(2)}) %collective-permute-start.20) | collective-permute-done | bytes 155680 | tf_op jit(solution)/shard_map/ppermute | solution.py:69
  88.9 1.6 %collective-permute-done.21.refs_3_ = bf16[2,304,128]{2,1,0:T(8,128)(2,1)S(1)} collective-permute-done((bf16[2,304,128]{2,1,0:T(8,128)(2,1)S(1)}, bf16[2,304,128]{2,1,0:T(8,128)(2,1)S(1)}, u32[]{:S(2)}, u32[]{:S(2)}) %collective-permute-start.21) | collective-permute-done | bytes 155680 | tf_op jit(solution)/shard_map/ppermute | solution.py:69
  90.5 1.5 %merge.1 = bf16[2,144,640]{2,1,0:T(8,128)(2,1)} custom-call(s32[1]{0:T(128)} %bitcast.u_ref, f32[2,5,144,128]{3,2,1,0:T(8,128)S(1)} %get-tuple-element.60.fresh_out, f32[24,128]{1,0:T(8,128)S(1)} %get-tuple-element.61.refs_9_.fresh_rows, bf16[2,304,128]{2,1,0:T(8,128)(2,1)S(1)} %get-tuple-element.67.refs_0_, ...), custom_call_target="tpu_custom_call" | custom-call | flops 1843200 | bytes 2580480 | tf_op jit(solution)/shard_map/merge/pallas_call | solution.py:588
  (42 shorter events, 0.4 us)
Async XLA Ops:
  0.6 24.2 %collective-permute-start.4 = (bf16[288,1280]{1,0:T(8,128)(2,1)}, bf16[288,1280]{1,0:T(8,128)(2,1)S(1)}, u32[]{:S(2)}, u32[]{:S(2)}) collective-permute-start(bf16[288,1280]{1,0:T(8,128)(2,1)} %bitcast.14), channel_id=1, source_target_pairs={{0,2},{1,3},{2,0},{3,1},{4,6},{5,7},{6,4},{7,5},{8,10},{33,35},{10... | collective-permute-start | bytes 2211848 | tf_op jit(solution)/shard_map/ppermute | solution.py:69
  2.7 1.0 %copy-start.1 = (bf16[2,144,640]{2,1,0:T(8,128)(2,1)S(1)}, bf16[2,144,640]{2,1,0:T(8,128)(2,1)}, u32[]{:S(2)}) copy-start(bf16[2,144,640]{2,1,0:T(8,128)(2,1)} %key_ref.1) | copy-start | bytes 1105924
  3.7 1.0 %copy-start.2 = (bf16[2,144,640]{2,1,0:T(8,128)(2,1)S(1)}, bf16[2,144,640]{2,1,0:T(8,128)(2,1)}, u32[]{:S(2)}) copy-start(bf16[2,144,640]{2,1,0:T(8,128)(2,1)} %value_ref.1) | copy-start | bytes 1105924
  4.8 7.4 %collective-permute-start = (bf16[2,2,144,128]{3,2,1,0:T(8,128)(2,1)S(1)}, bf16[2,2,144,128]{3,2,1,0:T(8,128)(2,1)S(1)}, u32[]{:S(2)}, u32[]{:S(2)}) collective-permute-start(bf16[2,2,144,128]{3,2,1,0:T(8,128)(2,1)S(1)} %get-tuple-element.38), channel_id=1, source_target_pairs={{0,96},{1,25},{2,98},{3,27},{4,100},{5,29},{6,102},{7,31},{8,104},... | collective-permute-start | bytes 442376 | tf_op jit(solution)/shard_map/ppermute | solution.py:69
  7.9 6.8 %collective-permute-start.1 = (bf16[2,2,144,128]{3,2,1,0:T(8,128)(2,1)S(1)}, bf16[2,2,144,128]{3,2,1,0:T(8,128)(2,1)S(1)}, u32[]{:S(2)}, u32[]{:S(2)}) collective-permute-start(bf16[2,2,144,128]{3,2,1,0:T(8,128)(2,1)S(1)} %get-tuple-element.39), channel_id=1, source_target_pairs={{0,64},{1,17},{2,66},{3,19},{4,68},{5,21},{6,70},{7,23},{8,72},{33... | collective-permute-start | bytes 442376 | tf_op jit(solution)/shard_map/ppermute | solution.py:69
  8.5 7.6 %collective-permute-start.2 = (bf16[2,2,144,128]{3,2,1,0:T(8,128)(2,1)S(1)}, bf16[2,2,144,128]{3,2,1,0:T(8,128)(2,1)S(1)}, u32[]{:S(2)}, u32[]{:S(2)}) collective-permute-start(bf16[2,2,144,128]{3,2,1,0:T(8,128)(2,1)S(1)} %get-tuple-element.40), channel_id=1, source_target_pairs={{0,32},{1,9},{2,34},{3,11},{4,36},{5,13},{6,38},{7,15},{8,40},{33,... | collective-permute-start | bytes 442376 | tf_op jit(solution)/shard_map/ppermute | solution.py:69
  9.5 23.1 %collective-permute-start.3 = (bf16[288,1280]{1,0:T(8,128)(2,1)}, bf16[288,1280]{1,0:T(8,128)(2,1)S(1)}, u32[]{:S(2)}, u32[]{:S(2)}) collective-permute-start(bf16[288,1280]{1,0:T(8,128)(2,1)} %bitcast.15), channel_id=1, source_target_pairs={{0,1},{1,0},{2,3},{3,2},{4,5},{5,4},{6,7},{7,6},{8,9},{33,32},{10,... | collective-permute-start | bytes 2211848 | tf_op jit(solution)/shard_map/ppermute | solution.py:69
  16.2 12.4 %collective-permute-start.6 = (bf16[2,2,720,128]{3,2,1,0:T(8,128)(2,1)S(1)}, bf16[2,2,720,128]{3,2,1,0:T(8,128)(2,1)}, u32[]{:S(2)}, u32[]{:S(2)}) collective-permute-start(bf16[2,2,720,128]{3,2,1,0:T(8,128)(2,1)S(1)} %assemble.1.after.refs_4_), channel_id=1, source_target_pairs={{0,8},{1,33},{2,10},{3,35},{4,12},{5,37},{6,14},{7,39},{8,0},{33,1... | collective-permute-start | bytes 2211848 | tf_op jit(solution)/shard_map/ppermute | solution.py:69
  17.8 12.8 %collective-permute-start.7 = (bf16[2,2,720,128]{3,2,1,0:T(8,128)(2,1)S(1)}, bf16[2,2,720,128]{3,2,1,0:T(8,128)(2,1)}, u32[]{:S(2)}, u32[]{:S(2)}) collective-permute-start(bf16[2,2,720,128]{3,2,1,0:T(8,128)(2,1)S(1)} %assemble.1.after.refs_4_), channel_id=1, source_target_pairs={{0,24},{1,97},{2,26},{3,99},{4,28},{5,101},{6,30},{7,103},{8,16},{... | collective-permute-start | bytes 2211848 | tf_op jit(solution)/shard_map/ppermute | solution.py:69
  19.9 1.1 %copy-start = (bf16[2,144,1280]{2,1,0:T(8,128)(2,1)S(1)}, bf16[2,144,1280]{2,1,0:T(8,128)(2,1)}, u32[]{:S(2)}) copy-start(bf16[2,144,1280]{2,1,0:T(8,128)(2,1)} %param.12) | copy-start | bytes 2211844
  21.0 0.8 copy-start.5
  21.7 0.8 copy-start.6
  22.5 0.7 copy-start.9
  23.2 0.7 copy-start.10
  24.8 7.8 %collective-permute-start.5 = (bf16[288,1280]{1,0:T(8,128)(2,1)S(1)}, bf16[288,1280]{1,0:T(8,128)(2,1)}, u32[]{:S(2)}, u32[]{:S(2)}) collective-permute-start(bf16[288,1280]{1,0:T(8,128)(2,1)S(1)} %collective-permute-done.4.h2), channel_id=1, source_target_pairs={{0,1},{1,0},{2,3},{3,2},{4,5},{5,4},{6,7},{7,6},{8,9},{33,32},{10,... | collective-permute-start | bytes 2211848 | tf_op jit(solution)/shard_map/ppermute | solution.py:69
  25.0 24.7 %collective-permute-start.9 = (bf16[2,2,720,128]{3,2,1,0:T(8,128)(2,1)S(1)}, bf16[2,2,720,128]{3,2,1,0:T(8,128)(2,1)S(1)}, u32[]{:S(2)}, u32[]{:S(2)}) collective-permute-start(bf16[2,2,720,128]{3,2,1,0:T(8,128)(2,1)S(1)} %assemble.1.after.refs_4_), channel_id=1, source_target_pairs={{0,4},{1,5},{2,6},{3,7},{4,0},{5,1},{6,2},{7,3},{8,12},{33,37},{10... | collective-permute-start | bytes 2211848 | tf_op jit(solution)/shard_map/ppermute | solution.py:69
  30.5 19.2 %collective-permute-start.8 = (bf16[2,2,720,128]{3,2,1,0:T(8,128)(2,1)}, bf16[2,2,720,128]{3,2,1,0:T(8,128)(2,1)S(1)}, u32[]{:S(2)}, u32[]{:S(2)}) collective-permute-start(bf16[2,2,720,128]{3,2,1,0:T(8,128)(2,1)} %collective-permute-done.6.refs_5_), channel_id=1, source_target_pairs={{0,24},{1,97},{2,26},{3,99},{4,28},{5,101},{6,30},{7,103},{8,16},{... | collective-permute-start | bytes 2211848 | tf_op jit(solution)/shard_map/ppermute | solution.py:69
  32.6 9.8 %slice-start = ((s8[6553600]{0:T(1024)(128)(4,1)}), s8[4194304]{0:T(1024)(128)(4,1)S(1)}, s32[]{:S(2)}) async-start(s8[6553600]{0:T(1024)(128)(4,1)} %bitcast.19), calls=%async_computation | async-start | bytes 8388608
  36.9 5.6 %slice-start.1 = ((s8[6553600]{0:T(1024)(128)(4,1)}), s8[2359296]{0:T(1024)(128)(4,1)S(1)}, s32[]{:S(2)}) async-start(s8[6553600]{0:T(1024)(128)(4,1)} %bitcast.19), calls=%async_computation.1 | async-start | bytes 4718592
  36.9 10.2 %slice-start.2 = ((s8[6553600]{0:T(1024)(128)(4,1)}), s8[4194304]{0:T(1024)(128)(4,1)S(1)}, s32[]{:S(2)}) async-start(s8[6553600]{0:T(1024)(128)(4,1)} %bitcast.21), calls=%async_computation.2 | async-start | bytes 8388608
  42.5 4.6 %slice-start.3 = ((s8[6553600]{0:T(1024)(128)(4,1)}), s8[2359296]{0:T(1024)(128)(4,1)S(1)}, s32[]{:S(2)}) async-start(s8[6553600]{0:T(1024)(128)(4,1)} %bitcast.21), calls=%async_computation.3 | async-start | bytes 4718592
  45.2 9.4 %copy-start.7 = (f32[640]{0:T(1024)S(1)}, f32[640]{0:T(1024)}, u32[]{:S(2)}) copy-start(f32[640]{0:T(1024)} %qg.1) | copy-start | bytes 7684
  45.2 9.4 %copy-start.8 = (f32[640]{0:T(1024)S(1)}, f32[640]{0:T(1024)}, u32[]{:S(2)}) copy-start(f32[640]{0:T(1024)} %kg.1) | copy-start | bytes 7684
  45.2 4.5 %collective-permute-start.10 = (f32[8,384]{1,0:T(8,128)S(1)}, f32[8,384]{1,0:T(8,128)S(1)}, u32[]{:S(2)}, u32[]{:S(2)}) collective-permute-start(f32[8,384]{1,0:T(8,128)S(1)} %sum_squares.1.s0), channel_id=1, source_target_pairs={{0,3},{1,2},{2,1},{3,0},{4,7},{5,6},{6,5},{7,4},{8,11},{33,34},{10... | collective-permute-start | bytes 36872 | tf_op jit(solution)/shard_map/ppermute | solution.py:69
  45.3 4.4 %collective-permute-start.11 = (f32[8,384]{1,0:T(8,128)S(1)}, f32[8,384]{1,0:T(8,128)S(1)}, u32[]{:S(2)}, u32[]{:S(2)}) collective-permute-start(f32[8,384]{1,0:T(8,128)S(1)} %sum_squares.1.s0), channel_id=1, source_target_pairs={{0,2},{1,3},{2,0},{3,1},{4,6},{5,7},{6,4},{7,5},{8,10},{33,35},{10... | collective-permute-start | bytes 36872 | tf_op jit(solution)/shard_map/ppermute | solution.py:69
  45.4 4.3 %collective-permute-start.12 = (f32[8,384]{1,0:T(8,128)S(1)}, f32[8,384]{1,0:T(8,128)S(1)}, u32[]{:S(2)}, u32[]{:S(2)}) collective-permute-start(f32[8,384]{1,0:T(8,128)S(1)} %sum_squares.1.s0), channel_id=1, source_target_pairs={{0,1},{1,0},{2,3},{3,2},{4,5},{5,4},{6,7},{7,6},{8,9},{33,32},{10,... | collective-permute-start | bytes 36872 | tf_op jit(solution)/shard_map/ppermute | solution.py:69
  49.7 42.4 %copy-start.3 = (bf16[288,640]{1,0:T(8,128)(2,1)}, bf16[288,640]{1,0:T(8,128)(2,1)S(1)}, u32[]{:S(2)}) copy-start(bf16[288,640]{1,0:T(8,128)(2,1)S(1)} %convolution_convert_fusion.v_ref) | copy-start | bytes 1105924
  49.7 26.6 %collective-permute-start.16 = (bf16[2,2,720,128]{3,2,1,0:T(8,128)(2,1)S(1)}, bf16[2,2,720,128]{3,2,1,0:T(8,128)(2,1)S(1)}, u32[]{:S(2)}, u32[]{:S(2)}) collective-permute-start(bf16[2,2,720,128]{3,2,1,0:T(8,128)(2,1)S(1)} %collective-permute-done.9.refs_8_), channel_id=1, source_target_pairs={{0,8},{1,33},{2,10},{3,35},{4,12},{5,37},{6,14},{7,39},{8,0},{33,1... | collective-permute-start | bytes 2211848 | tf_op jit(solution)/shard_map/ppermute | solution.py:69
  49.8 26.5 %collective-permute-start.17 = (bf16[2,2,720,128]{3,2,1,0:T(8,128)(2,1)S(1)}, bf16[2,2,720,128]{3,2,1,0:T(8,128)(2,1)S(1)}, u32[]{:S(2)}, u32[]{:S(2)}) collective-permute-start(bf16[2,2,720,128]{3,2,1,0:T(8,128)(2,1)S(1)} %collective-permute-done.9.refs_8_), channel_id=1, source_target_pairs={{0,24},{1,97},{2,26},{3,99},{4,28},{5,101},{6,30},{7,103},{8,16},{... | collective-permute-start | bytes 2211848 | tf_op jit(solution)/shard_map/ppermute | solution.py:69
  51.1 25.3 %collective-permute-start.18 = (bf16[2,2,720,128]{3,2,1,0:T(8,128)(2,1)S(1)}, bf16[2,2,720,128]{3,2,1,0:T(8,128)(2,1)S(1)}, u32[]{:S(2)}, u32[]{:S(2)}) collective-permute-start(bf16[2,2,720,128]{3,2,1,0:T(8,128)(2,1)S(1)} %collective-permute-done.8.refs_7_), channel_id=1, source_target_pairs={{0,4},{1,5},{2,6},{3,7},{4,0},{5,1},{6,2},{7,3},{8,12},{33,37},{10... | collective-permute-start | bytes 2211848 | tf_op jit(solution)/shard_map/ppermute | solution.py:69
  56.4 5.5 %collective-permute-start.13 = (bf16[2,2,144,128]{3,2,1,0:T(8,128)(2,1)S(1)}, bf16[2,2,144,128]{3,2,1,0:T(8,128)(2,1)S(1)}, u32[]{:S(2)}, u32[]{:S(2)}) collective-permute-start(bf16[2,2,144,128]{3,2,1,0:T(8,128)(2,1)S(1)} %get-tuple-element.59.refs_3_), channel_id=1, source_target_pairs={{0,96},{1,25},{2,98},{3,27},{4,100},{5,29},{6,102},{7,31},{8,104},... | collective-permute-start | bytes 442376 | tf_op jit(solution)/shard_map/ppermute | solution.py:69
  57.0 7.4 %collective-permute-start.14 = (bf16[2,2,144,128]{3,2,1,0:T(8,128)(2,1)S(1)}, bf16[2,2,144,128]{3,2,1,0:T(8,128)(2,1)S(1)}, u32[]{:S(2)}, u32[]{:S(2)}) collective-permute-start(bf16[2,2,144,128]{3,2,1,0:T(8,128)(2,1)S(1)} %get-tuple-element.58.refs_2_), channel_id=1, source_target_pairs={{0,64},{1,17},{2,66},{3,19},{4,68},{5,21},{6,70},{7,23},{8,72},{33... | collective-permute-start | bytes 442376 | tf_op jit(solution)/shard_map/ppermute | solution.py:69
  61.9 6.4 %collective-permute-start.15 = (bf16[2,2,144,128]{3,2,1,0:T(8,128)(2,1)S(1)}, bf16[2,2,144,128]{3,2,1,0:T(8,128)(2,1)S(1)}, u32[]{:S(2)}, u32[]{:S(2)}) collective-permute-start(bf16[2,2,144,128]{3,2,1,0:T(8,128)(2,1)S(1)} %get-tuple-element.57.refs_1_), channel_id=1, source_target_pairs={{0,32},{1,9},{2,34},{3,11},{4,36},{5,13},{6,38},{7,15},{8,40},{33,... | collective-permute-start | bytes 442376 | tf_op jit(solution)/shard_map/ppermute | solution.py:69
  62.4 1.0 %copy-start.4 = (bf16[288,640]{1,0:T(8,128)(2,1)S(1)}, bf16[288,640]{1,0:T(8,128)(2,1)}, u32[]{:S(2)}) copy-start(bf16[288,640]{1,0:T(8,128)(2,1)} %get-tuple-element.54.k_ref) | copy-start | bytes 1105924
  81.1 5.3 %collective-permute-start.19 = (bf16[2,304,128]{2,1,0:T(8,128)(2,1)S(1)}, bf16[2,304,128]{2,1,0:T(8,128)(2,1)S(1)}, u32[]{:S(2)}, u32[]{:S(2)}) collective-permute-start(bf16[2,304,128]{2,1,0:T(8,128)(2,1)S(1)} %get-tuple-element.68), channel_id=1, source_target_pairs={{0,96},{1,25},{2,98},{3,27},{4,100},{5,29},{6,102},{7,31},{8,104},... | collective-permute-start | bytes 466952 | tf_op jit(solution)/shard_map/ppermute | solution.py:69
  82.1 6.8 %collective-permute-start.20 = (bf16[2,304,128]{2,1,0:T(8,128)(2,1)S(1)}, bf16[2,304,128]{2,1,0:T(8,128)(2,1)S(1)}, u32[]{:S(2)}, u32[]{:S(2)}) collective-permute-start(bf16[2,304,128]{2,1,0:T(8,128)(2,1)S(1)} %get-tuple-element.69), channel_id=1, source_target_pairs={{0,64},{1,17},{2,66},{3,19},{4,68},{5,21},{6,70},{7,23},{8,72},{33... | collective-permute-start | bytes 466952 | tf_op jit(solution)/shard_map/ppermute | solution.py:69
  82.5 8.0 %collective-permute-start.21 = (bf16[2,304,128]{2,1,0:T(8,128)(2,1)S(1)}, bf16[2,304,128]{2,1,0:T(8,128)(2,1)S(1)}, u32[]{:S(2)}, u32[]{:S(2)}) collective-permute-start(bf16[2,304,128]{2,1,0:T(8,128)(2,1)S(1)} %get-tuple-element.70), channel_id=1, source_target_pairs={{0,32},{1,9},{2,34},{3,11},{4,36},{5,13},{6,38},{7,15},{8,40},{33,... | collective-permute-start | bytes 466952 | tf_op jit(solution)/shard_map/ppermute | solution.py:69

commit v8 on v7

--- a/solution.py
+++ b/solution.py
@@ -69,8 +69,8 @@
     return lax.ppermute(value, AXES, [(linear(*p), linear(*move(*p))) for p in places()])
 
 
-def shift_u(value, k):
-    return permute(value, lambda u, v, h, l, c: ((u + k) % 4, v, h, l, c))
+def swap_u(value, mask):
+    return permute(value, lambda u, v, h, l, c: (u ^ mask, v, h, l, c))
 
 
 def swap_v(value, mask):
@@ -78,8 +78,10 @@
 
 
 def exchange_u(values):
-    came = {r: shift_u(values[4 - r], 4 - r) for r in (2, 1, 3)}
-    return [values[0], came[1], came[2], came[3]]
+    relayed = swap_u(values[2], 1)
+    came_three = swap_u(values[3], 3)
+    came_one = swap_u(values[1], 1)
+    return [values[0], came_one, swap_u(relayed, 3), came_three]
 
 
 def swap_z_hi(value):
@@ -119,7 +121,7 @@
 
 def pack_kernel(u_ref, key_ref, value_ref, *outs):
     for k in range(5):
-        head = lax.rem(u_ref[0] + k, 4) if k < 4 else 4
+        head = (u_ref[0] ^ k) if k < 4 else 4
         cols = pl.ds(pl.multiple_of(head * HD, HD), HD)
         for n, source in enumerate((key_ref, value_ref)):
             for s in range(B):
@@ -306,7 +308,7 @@
         k_all[:, cols] = rotate(k_ref, k_column, kg, cols)
     for k in range(4):
         for s in range(B):
-            sends[k][s, 0] = q_rot[lax.rem(u_ref[0] + k, 4), s]
+            sends[k][s, 0] = q_rot[(u_ref[0] ^ k), s]
             sends[k][s, 1] = q_rot[4, s]
 
 
@@ -349,7 +351,7 @@
     for s in range(B):
         rows = slice(s * TOK, (s + 1) * TOK)
         for k in range(LOCAL_HEADS):
-            head = lax.rem(u_ref[0] + k, 4) if k < 4 else 4
+            head = (u_ref[0] ^ k) if k < 4 else 4
             cols = pl.ds(pl.multiple_of(head * HD, HD), HD)
             query = queries[k][s, 0] if k < 4 else queries[0][s, 1]
             scores = scores_of(query, k_ref[rows, cols])
@@ -568,7 +570,7 @@
     filler = jnp.zeros((HD - 2 * len(weights), HD), F32)
     table = jnp.concatenate(weights + [filler], axis=0).T
     for s, k, parts in jobs:
-        head = lax.rem(u_ref[0] + k, 4) if k < 4 else 4
+        head = (u_ref[0] ^ k) if k < 4 else 4
         out = [None, None]
         for source, n in parts:
             for half, rows in enumerate((slice(0, HD), slice(HD, TOK))):
@@ -629,21 +631,20 @@
 
     z_rows, cond = lax.optimization_barrier((z_rows, cond))
     cross_rows = swap_tp(z_rows, 0, 1)
-    near_one, near_three = lax.optimization_barrier((near_one, near_three))
-    near_two = swap_v(near_one, 3)
     blocks = jnp.stack([tp, tp ^ 1, tp ^ 2, tp ^ 3]).astype(jnp.int32)
     modded = modulate(blocks, [own_rows, core_rows, z_rows, cross_rows], cond, mod)
     query = jnp.dot(modded, w_query, preferred_element_type=F32)
+    near_one, near_three, query = lax.optimization_barrier((near_one, near_three, query))
+    near_two = swap_v(near_one, 3)
     key = jnp.dot(modded, w_key, preferred_element_type=F32)
     fresh_values = jnp.dot(modded, w_value, preferred_element_type=F32).astype(BF16)
     own_sq = sum_squares(query, key)
     squares = [own_sq] + [swap_tp(own_sq, z, c) for z, c in ((1, 1), (1, 0), (0, 1))]
-    near_two, far, fresh_values, *squares = lax.optimization_barrier(
-        (near_two, far, fresh_values, *squares)
-    )
-    far_two = swap_z_hi(near_two)
+    far, fresh_values, *squares = lax.optimization_barrier((far, fresh_values, *squares))
     far_one, far_three = swap_v(far, 1), swap_v(far, 3)
     fresh_keys, *sends = norm_rope(u, query, key, squares, q_gain, k_gain, cos, sin)
+    near_two, fresh_keys = lax.optimization_barrier((near_two, fresh_keys))
+    far_two = swap_z_hi(near_two)
     queries = exchange_u(sends)
     fresh_out, fresh_rows = fresh_attention(u, fresh_keys, fresh_values, sends)
 

time: 92.5 us -> 93.1 us (level)
  starting transfers between devices: 26.8 us -> 36.7 us
  waiting for transfers between devices: 24 us -> 16.7 us
  Pallas kernels: 22.8 us -> 21.1 us
    ppermute x22 -> x25, starting transfers between devices: 26.8 us -> 36.7 us  [permute(): lax.ppermute(value, AXES, [(linear(*p), linear(*move(*p))) for p in place...]
    ppermute x22 -> x25, waiting for transfers between devices: 24 us -> 16.7 us  [permute(): lax.ppermute(value, AXES, [(linear(*p), linear(*move(*p))) for p in place...]
    pallas_call x2, Pallas kernels: 12.8 us -> 11.2 us  [stale_attention(): pl.pallas_call(functools.partial(stale_kernel, far, count), out_shape=out...]
  transfers between devices with their start and end apart: 22 -> 25, of which waited for: 9 -> 9; matrix products, arithmetic and copies ran while one was open for 12% -> 11% of each run, Pallas kernels for 18% -> 16%
where the time goes in v8:
time: 93.1 us; the launch traced here: 92.7 us
  starting transfers between devices  36.7 us (39%)
  Pallas kernels  21.1 us (23%)
  waiting for transfers between devices  16.7 us (18%)
  matrix products  10.3 us (11%)
  local copies, waits for them, and re-layouts  7 us (8%)
    ppermute x25, starting transfers between devices, permute(): lax.ppermute(value, AXES, [(linear(*p), linear(*move(*p))) for p in place...  36.7 us
    ppermute x25, waiting for transfers between devices, permute(): lax.ppermute(value, AXES, [(linear(*p), linear(*move(*p))) for p in place...  16.7 us
    pallas_call x2, Pallas kernels, stale_attention(): pl.pallas_call(functools.partial(stale_kernel, far, count), out_shape=out...  11.2 us
    unnamed x30, local copies, waits for them, and re-layouts  7 us
    dot_general x1, matrix products, shards(): query = jnp.dot(modded, w_query, preferred_element_type=F32)  5.44 us
    pallas_call x1, Pallas kernels, modulate(): pl.pallas_call(modulate_kernel, out_shape=jax.ShapeDtypeStruct((ROWS, D),...  4.24 us
    dot_general x1, matrix products, shards(): jnp.dot(modded, w_value, preferred_element_type=F32).astype(BF16)  2.44 us
    dot_general x1, matrix products, shards(): key = jnp.dot(modded, w_key, preferred_element_type=F32)  2.43 us
  transfers between devices with their start and end apart: 25, of which 9 were waited for; matrix products, arithmetic and copies ran while one was open for 11% of the time, Pallas kernels for 16%

profile of v8, /device:TPU:0, one launch (start us, length us, event | category | flops | bytes accessed | tf_op | source)
XLA Modules:
  0.0 92.7 jit_solution(6717955305320225535)
XLA Ops:
  0.6 2.1 %collective-permute-start.7 = (bf16[288,1280]{1,0:T(8,128)(2,1)}, bf16[288,1280]{1,0:T(8,128)(2,1)S(1)}, u32[]{:S(2)}, u32[]{:S(2)}) collective-permute-start(bf16[288,1280]{1,0:T(8,128)(2,1)} %bitcast.14), channel_id=1, source_target_pairs={{0,2},{1,3},{2,0},{3,1},{4,6},{5,7},{6,4},{7,5},{8,10},{33,35},{10... | collective-permute-start | bytes 2211848 | tf_op jit(solution)/shard_map/ppermute | solution.py:69
  2.7 1.0 %copy-done.1 = bf16[2,144,640]{2,1,0:T(8,128)(2,1)S(1)} copy-done((bf16[2,144,640]{2,1,0:T(8,128)(2,1)S(1)}, bf16[2,144,640]{2,1,0:T(8,128)(2,1)}, u32[]{:S(2)}) %copy-start.1) | copy-done | bytes 368664
  3.7 1.0 %copy-done.2 = bf16[2,144,640]{2,1,0:T(8,128)(2,1)S(1)} copy-done((bf16[2,144,640]{2,1,0:T(8,128)(2,1)S(1)}, bf16[2,144,640]{2,1,0:T(8,128)(2,1)}, u32[]{:S(2)}) %copy-start.2) | copy-done | bytes 368664
  4.7 0.1 pack_stale.1
  4.8 1.7 %collective-permute-start.1 = (bf16[2,2,144,128]{3,2,1,0:T(8,128)(2,1)S(1)}, bf16[2,2,144,128]{3,2,1,0:T(8,128)(2,1)S(1)}, u32[]{:S(2)}, u32[]{:S(2)}) collective-permute-start(bf16[2,2,144,128]{3,2,1,0:T(8,128)(2,1)S(1)} %get-tuple-element.41), channel_id=1, source_target_pairs={{0,32},{1,9},{2,34},{3,11},{4,36},{5,13},{6,38},{7,15},{8,40},{33,... | collective-permute-start | bytes 442376 | tf_op jit(solution)/shard_map/ppermute | solution.py:69
  6.5 0.5 collective-permute-start
  6.9 3.0 %collective-permute-start.3 = (bf16[2,2,144,128]{3,2,1,0:T(8,128)(2,1)S(1)}, bf16[2,2,144,128]{3,2,1,0:T(8,128)(2,1)S(1)}, u32[]{:S(2)}, u32[]{:S(2)}) collective-permute-start(bf16[2,2,144,128]{3,2,1,0:T(8,128)(2,1)S(1)} %get-tuple-element.42), channel_id=1, source_target_pairs={{0,96},{1,25},{2,98},{3,27},{4,100},{5,29},{6,102},{7,31},{8,104},... | collective-permute-start | bytes 442376 | tf_op jit(solution)/shard_map/ppermute | solution.py:69
  9.9 0.1 collective-permute-done.1
  10.0 3.0 %collective-permute-start.2 = (bf16[2,2,144,128]{3,2,1,0:T(8,128)(2,1)S(1)}, bf16[2,2,144,128]{3,2,1,0:T(8,128)(2,1)S(1)}, u32[]{:S(2)}, u32[]{:S(2)}) collective-permute-start(bf16[2,2,144,128]{3,2,1,0:T(8,128)(2,1)S(1)} %collective-permute-done.1), channel_id=1, source_target_pairs={{0,96},{1,25},{2,98},{3,27},{4,100},{5,29},{6,102},{7,31},{8,104},... | collective-permute-start | bytes 442376 | tf_op jit(solution)/shard_map/ppermute | solution.py:69
  13.1 0.2 collective-permute-done.3.refs_3_
  13.3 3.1 %collective-permute-done.2.refs_2_ = bf16[2,2,144,128]{3,2,1,0:T(8,128)(2,1)S(1)} collective-permute-done((bf16[2,2,144,128]{3,2,1,0:T(8,128)(2,1)S(1)}, bf16[2,2,144,128]{3,2,1,0:T(8,128)(2,1)S(1)}, u32[]{:S(2)}, u32[]{:S(2)}) %collective-permute-start.2) | collective-permute-done | bytes 147488 | tf_op jit(solution)/shard_map/ppermute | solution.py:69
  16.5 1.1 %copy-done = bf16[2,144,1280]{2,1,0:T(8,128)(2,1)S(1)} copy-done((bf16[2,144,1280]{2,1,0:T(8,128)(2,1)S(1)}, bf16[2,144,1280]{2,1,0:T(8,128)(2,1)}, u32[]{:S(2)}) %copy-start) | copy-done | bytes 737304
  17.6 0.8 copy-done.5
  18.3 0.8 copy-done.6
  19.1 0.7 copy-done.9
  19.8 0.7 copy-done.10
  20.5 0.9 %tables.1 = (f32[288,128]{1,0:T(8,128)S(1)}, f32[144,128]{1,0:T(8,128)S(1)}, f32[144,128]{1,0:T(8,128)S(1)}, f32[4,5120]{1,0:T(4,128)S(1)}, bf16[288,1280]{1,0:T(8,128)(2,1)S(1)}) custom-call(s32[144]{0:T(256)S(1)} %copy-done.9, f32[1,128]{1,0:T(1,128)S(1)} %copy-done.10, bf16[288,1280]{1,0:T(8,128)(2,1)S(1)} %bitcast.16, f32[2,5120]{1,0:T(2,128)S(1)} %copy-done.5, ...), custom_call_target="tpu_custom_call" | custom-call | flops 1843200 | bytes 1000000 | tf_op jit(solution)/shard_map/tables/pallas_call | solution.py:178
  21.4 0.1 collective-permute-start.8
  21.5 1.6 %collective-permute-start.4 = (bf16[2,2,720,128]{3,2,1,0:T(8,128)(2,1)S(1)}, bf16[2,2,720,128]{3,2,1,0:T(8,128)(2,1)S(1)}, u32[]{:S(2)}, u32[]{:S(2)}) collective-permute-start(bf16[2,2,720,128]{3,2,1,0:T(8,128)(2,1)S(1)} %assemble.1.after.refs_4_), channel_id=1, source_target_pairs={{0,8},{1,33},{2,10},{3,35},{4,12},{5,37},{6,14},{7,39},{8,0},{33,1... | collective-permute-start | bytes 2211848 | tf_op jit(solution)/shard_map/ppermute | solution.py:69
  23.1 2.1 %collective-permute-start.5 = (bf16[2,2,720,128]{3,2,1,0:T(8,128)(2,1)S(1)}, bf16[2,2,720,128]{3,2,1,0:T(8,128)(2,1)S(1)}, u32[]{:S(2)}, u32[]{:S(2)}) collective-permute-start(bf16[2,2,720,128]{3,2,1,0:T(8,128)(2,1)S(1)} %assemble.1.after.refs_4_), channel_id=1, source_target_pairs={{0,24},{1,97},{2,26},{3,99},{4,28},{5,101},{6,30},{7,103},{8,16},{... | collective-permute-start | bytes 2211848 | tf_op jit(solution)/shard_map/ppermute | solution.py:69
  25.3 3.6 %collective-permute-start.10 = (bf16[2,2,720,128]{3,2,1,0:T(8,128)(2,1)S(1)}, bf16[2,2,720,128]{3,2,1,0:T(8,128)(2,1)S(1)}, u32[]{:S(2)}, u32[]{:S(2)}) collective-permute-start(bf16[2,2,720,128]{3,2,1,0:T(8,128)(2,1)S(1)} %assemble.1.after.refs_4_), channel_id=1, source_target_pairs={{0,4},{1,5},{2,6},{3,7},{4,0},{5,1},{6,2},{7,3},{8,12},{33,37},{10... | collective-permute-start | bytes 2211848 | tf_op jit(solution)/shard_map/ppermute | solution.py:69
  28.9 4.2 %modulate.1 = bf16[288,5120]{1,0:T(8,128)(2,1)S(1)} custom-call(s32[4]{0:T(128)S(1)} %pad_add_fusion.t_ref, bf16[288,1280]{1,0:T(8,128)(2,1)S(1)} %get-tuple-element.44.h0, bf16[288,1280]{1,0:T(8,128)(2,1)S(1)} %collective-permute-done.6.h1, bf16[288,1280]{1,0:T(8,128)(2,1)S(1)} %collective-permute-done.7.h2, bf16[288,1280]{1,0:T(8,128)(2,1)} %collective-permute-done.8.h3, ...), custom_call_target="tpu_custom_call" | custom-call | flops 17694720 | bytes 20000000 | tf_op jit(solution)/shard_map/modulate/pallas_call | solution.py:253
  33.2 5.4 %fusion.q_ref = f32[288,640]{1,0:T(8,128)S(1)} fusion(bf16[288,5120]{1,0:T(8,128)(2,1)S(1)} %modulate.1, bf16[5120,640]{1,0:T(8,128)(2,1)} %param.15), kind=kOutput, calls=%fused_computation.2 | convolution fusion | flops 1887436800 | bytes 10240000 | tf_op jit(solution)/shard_map/dot_general | solution.py:636
  38.6 1.2 %collective-permute-start.9 = (bf16[2,2,720,128]{3,2,1,0:T(8,128)(2,1)S(1)}, bf16[2,2,720,128]{3,2,1,0:T(8,128)(2,1)S(1)}, u32[]{:S(2)}, u32[]{:S(2)}) collective-permute-start(bf16[2,2,720,128]{3,2,1,0:T(8,128)(2,1)S(1)} %collective-permute-done.4.refs_5_), channel_id=1, source_target_pairs={{0,24},{1,97},{2,26},{3,99},{4,28},{5,101},{6,30},{7,103},{8,16},{... | collective-permute-start | bytes 2211848 | tf_op jit(solution)/shard_map/ppermute | solution.py:69
  39.9 2.4 %fusion.1.k_ref = f32[288,640]{1,0:T(8,128)S(1)} fusion(bf16[288,5120]{1,0:T(8,128)(2,1)S(1)} %modulate.1, bf16[5120,640]{1,0:T(8,128)(2,1)S(1)} %bitcast.20), kind=kOutput, calls=%fused_computation.3 | convolution fusion | flops 1887436800 | bytes 10240000 | tf_op jit(solution)/shard_map/dot_general | solution.py:639
  42.3 0.2 sum_squares.1.s0
  42.7 1.8 %collective-permute-start.13 = (f32[8,384]{1,0:T(8,128)S(1)}, f32[8,384]{1,0:T(8,128)S(1)}, u32[]{:S(2)}, u32[]{:S(2)}) collective-permute-start(f32[8,384]{1,0:T(8,128)S(1)} %sum_squares.1.s0), channel_id=1, source_target_pairs={{0,1},{1,0},{2,3},{3,2},{4,5},{5,4},{6,7},{7,6},{8,9},{33,32},{10,... | collective-permute-start | bytes 36872 | tf_op jit(solution)/shard_map/ppermute | solution.py:69
  44.5 2.4 %convolution_convert_fusion.v_ref = bf16[288,640]{1,0:T(8,128)(2,1)S(1)} fusion(bf16[288,5120]{1,0:T(8,128)(2,1)S(1)} %modulate.1, bf16[5120,640]{1,0:T(8,128)(2,1)S(1)} %bitcast.22), kind=kOutput, calls=%fused_computation | convolution fusion | flops 1887621120 | bytes 9871360 | tf_op jit(solution)/shard_map/dot_general | solution.py:640
  47.1 2.2 %collective-permute-start.19 = (bf16[2,2,720,128]{3,2,1,0:T(8,128)(2,1)S(1)}, bf16[2,2,720,128]{3,2,1,0:T(8,128)(2,1)S(1)}, u32[]{:S(2)}, u32[]{:S(2)}) collective-permute-start(bf16[2,2,720,128]{3,2,1,0:T(8,128)(2,1)S(1)} %collective-permute-done.10.refs_8_), channel_id=1, source_target_pairs={{0,24},{1,97},{2,26},{3,99},{4,28},{5,101},{6,30},{7,103},{8,16},{... | collective-permute-start | bytes 2211848 | tf_op jit(solution)/shard_map/ppermute | solution.py:69
  49.2 1.7 %norm_rope.1 = (bf16[288,640]{1,0:T(8,128)(2,1)}, bf16[2,2,144,128]{3,2,1,0:T(8,128)(2,1)S(1)}, bf16[2,2,144,128]{3,2,1,0:T(8,128)(2,1)S(1)}, bf16[2,2,144,128]{...) custom-call(s32[1]{0:T(128)} %bitcast.u_ref, f32[288,640]{1,0:T(8,128)S(1)} %fusion.q_ref, f32[288,640]{1,0:T(8,128)S(1)} %fusion.1.k_ref, ...), custom_call_target="tpu_custom_call" | custom-call | flops 1000 | bytes 1000 | tf_op jit(solution)/shard_map/norm_rope/pallas_call | solution.py:318
  51.0 0.4 collective-permute-done.9.refs_7_
  51.4 1.2 %collective-permute-start.20 = (bf16[2,2,720,128]{3,2,1,0:T(8,128)(2,1)S(1)}, bf16[2,2,720,128]{3,2,1,0:T(8,128)(2,1)S(1)}, u32[]{:S(2)}, u32[]{:S(2)}) collective-permute-start(bf16[2,2,720,128]{3,2,1,0:T(8,128)(2,1)S(1)} %collective-permute-done.9.refs_7_), channel_id=1, source_target_pairs={{0,4},{1,5},{2,6},{3,7},{4,0},{5,1},{6,2},{7,3},{8,12},{33,37},{10... | collective-permute-start | bytes 2211848 | tf_op jit(solution)/shard_map/ppermute | solution.py:69
  52.6 2.0 %collective-permute-start.14 = (bf16[2,2,144,128]{3,2,1,0:T(8,128)(2,1)S(1)}, bf16[2,2,144,128]{3,2,1,0:T(8,128)(2,1)S(1)}, u32[]{:S(2)}, u32[]{:S(2)}) collective-permute-start(bf16[2,2,144,128]{3,2,1,0:T(8,128)(2,1)S(1)} %get-tuple-element.61.refs_1_), channel_id=1, source_target_pairs={{0,32},{1,9},{2,34},{3,11},{4,36},{5,13},{6,38},{7,15},{8,40},{33,... | collective-permute-start | bytes 442376 | tf_op jit(solution)/shard_map/ppermute | solution.py:69
  54.6 4.5 %collective-permute-done.15 = bf16[2,2,144,128]{3,2,1,0:T(8,128)(2,1)S(1)} collective-permute-done((bf16[2,2,144,128]{3,2,1,0:T(8,128)(2,1)S(1)}, bf16[2,2,144,128]{3,2,1,0:T(8,128)(2,1)S(1)}, u32[]{:S(2)}, u32[]{:S(2)}) %collective-permute-start.15) | collective-permute-done | bytes 147488 | tf_op jit(solution)/shard_map/ppermute | solution.py:69
  59.1 2.7 %collective-permute-start.17 = (bf16[2,2,144,128]{3,2,1,0:T(8,128)(2,1)S(1)}, bf16[2,2,144,128]{3,2,1,0:T(8,128)(2,1)S(1)}, u32[]{:S(2)}, u32[]{:S(2)}) collective-permute-start(bf16[2,2,144,128]{3,2,1,0:T(8,128)(2,1)S(1)} %get-tuple-element.63.refs_3_), channel_id=1, source_target_pairs={{0,96},{1,25},{2,98},{3,27},{4,100},{5,29},{6,102},{7,31},{8,104},... | collective-permute-start | bytes 442376 | tf_op jit(solution)/shard_map/ppermute | solution.py:69
  61.8 1.9 %collective-permute-start.16 = (bf16[2,2,144,128]{3,2,1,0:T(8,128)(2,1)S(1)}, bf16[2,2,144,128]{3,2,1,0:T(8,128)(2,1)S(1)}, u32[]{:S(2)}, u32[]{:S(2)}) collective-permute-start(bf16[2,2,144,128]{3,2,1,0:T(8,128)(2,1)S(1)} %collective-permute-done.15), channel_id=1, source_target_pairs={{0,96},{1,25},{2,98},{3,27},{4,100},{5,29},{6,102},{7,31},{8,104},... | collective-permute-start | bytes 442376 | tf_op jit(solution)/shard_map/ppermute | solution.py:69
  63.7 1.0 %copy-done.4 = bf16[288,640]{1,0:T(8,128)(2,1)S(1)} copy-done((bf16[288,640]{1,0:T(8,128)(2,1)S(1)}, bf16[288,640]{1,0:T(8,128)(2,1)}, u32[]{:S(2)}) %copy-start.4) | copy-done | bytes 368664
  64.7 1.0 %fresh_attention.1 = (f32[2,5,144,128]{3,2,1,0:T(8,128)S(1)}, f32[24,128]{1,0:T(8,128)S(1)}) custom-call(s32[1]{0:T(128)} %bitcast.u_ref, bf16[288,640]{1,0:T(8,128)(2,1)S(1)} %copy-done.4, bf16[288,640]{1,0:T(8,128)(2,1)S(1)} %convolution_convert_fusion.v_ref, bf16[2,2,144,128]{3,2,1,0:T(8,128)(2,1)S(1)} %get-tuple-element.60.refs_0_, ...), custom_call_target="tpu_custom_call" | custom-call | flops 1000 | bytes 1000 | tf_op jit(solution)/shard_map/fresh_attention/pallas_call | solution.py:368
  65.8 2.4 %collective-permute-done.16.refs_2_ = bf16[2,2,144,128]{3,2,1,0:T(8,128)(2,1)S(1)} collective-permute-done((bf16[2,2,144,128]{3,2,1,0:T(8,128)(2,1)S(1)}, bf16[2,2,144,128]{3,2,1,0:T(8,128)(2,1)S(1)}, u32[]{:S(2)}, u32[]{:S(2)}) %collective-permute-start.16) | collective-permute-done | bytes 147488 | tf_op jit(solution)/shard_map/ppermute | solution.py:69
  68.2 6.6 %near_attention.1 = (f32[2,4,2,144,128]{4,3,2,1,0:T(8,128)S(1)}, f32[2,4,2,144,128]{4,3,2,1,0:T(8,128)S(1)}) custom-call(bf16[2,2,144,128]{3,2,1,0:T(8,128)(2,1)S(1)} %get-tuple-element.60.refs_0_, bf16[2,2,144,128]{3,2,1,0:T(8,128)(2,1)S(1)} %collective-permute-done.14.refs_1_, bf16[2,2,144,128]{3,2,1,0:T(8,128)(2,1)S(1)} %collective-permute-done.16.refs_2_, ...), custom_call_target="tpu_custom_call" | custom-call | flops 1000 | bytes 1000 | tf_op jit(solution)/shard_map/near_attention/pallas_call | solution.py:526
  74.8 4.6 %far_attention.1 = (bf16[2,304,128]{2,1,0:T(8,128)(2,1)S(1)}, bf16[2,304,128]{2,1,0:T(8,128)(2,1)S(1)}, bf16[2,304,128]{2,1,0:T(8,128)(2,1)S(1)}, bf16[2,304,128]{2,1,0:T(8,128)(2,1)S(1)}) custom-call(bf16[2,2,144,128]{3,2,1,0:T(8,128)(2,1)S(1)} %get-tuple-element.60.refs_0_, bf16[2,2,144,128]{3,2,1,0:T(8,128)(2,1)S(1)} %collective-permute-done.14.refs_1_, ...), custom_call_target="tpu_custom_call" | custom-call | flops 1000 | bytes 1000 | tf_op jit(solution)/shard_map/far_attention/pallas_call | solution.py:526
  79.5 2.0 %collective-permute-start.21 = (bf16[2,304,128]{2,1,0:T(8,128)(2,1)S(1)}, bf16[2,304,128]{2,1,0:T(8,128)(2,1)S(1)}, u32[]{:S(2)}, u32[]{:S(2)}) collective-permute-start(bf16[2,304,128]{2,1,0:T(8,128)(2,1)S(1)} %get-tuple-element.72), channel_id=1, source_target_pairs={{0,32},{1,9},{2,34},{3,11},{4,36},{5,13},{6,38},{7,15},{8,40},{33,... | collective-permute-start | bytes 466952 | tf_op jit(solution)/shard_map/ppermute | solution.py:69
  81.5 1.9 %collective-permute-start.24 = (bf16[2,304,128]{2,1,0:T(8,128)(2,1)S(1)}, bf16[2,304,128]{2,1,0:T(8,128)(2,1)S(1)}, u32[]{:S(2)}, u32[]{:S(2)}) collective-permute-start(bf16[2,304,128]{2,1,0:T(8,128)(2,1)S(1)} %get-tuple-element.74), channel_id=1, source_target_pairs={{0,96},{1,25},{2,98},{3,27},{4,100},{5,29},{6,102},{7,31},{8,104},... | collective-permute-start | bytes 466952 | tf_op jit(solution)/shard_map/ppermute | solution.py:69
  83.4 1.3 %collective-permute-done.22 = bf16[2,304,128]{2,1,0:T(8,128)(2,1)S(1)} collective-permute-done((bf16[2,304,128]{2,1,0:T(8,128)(2,1)S(1)}, bf16[2,304,128]{2,1,0:T(8,128)(2,1)S(1)}, u32[]{:S(2)}, u32[]{:S(2)}) %collective-permute-start.22) | collective-permute-done | bytes 155680 | tf_op jit(solution)/shard_map/ppermute | solution.py:69
  84.7 1.9 %collective-permute-start.23 = (bf16[2,304,128]{2,1,0:T(8,128)(2,1)S(1)}, bf16[2,304,128]{2,1,0:T(8,128)(2,1)S(1)}, u32[]{:S(2)}, u32[]{:S(2)}) collective-permute-start(bf16[2,304,128]{2,1,0:T(8,128)(2,1)S(1)} %collective-permute-done.22), channel_id=1, source_target_pairs={{0,96},{1,25},{2,98},{3,27},{4,100},{5,29},{6,102},{7,31},{8,104},... | collective-permute-start | bytes 466952 | tf_op jit(solution)/shard_map/ppermute | solution.py:69
  86.6 1.3 %collective-permute-done.24.refs_3_ = bf16[2,304,128]{2,1,0:T(8,128)(2,1)S(1)} collective-permute-done((bf16[2,304,128]{2,1,0:T(8,128)(2,1)S(1)}, bf16[2,304,128]{2,1,0:T(8,128)(2,1)S(1)}, u32[]{:S(2)}, u32[]{:S(2)}) %collective-permute-start.24) | collective-permute-done | bytes 155680 | tf_op jit(solution)/shard_map/ppermute | solution.py:69
  88.0 3.2 %collective-permute-done.23.refs_2_ = bf16[2,304,128]{2,1,0:T(8,128)(2,1)S(1)} collective-permute-done((bf16[2,304,128]{2,1,0:T(8,128)(2,1)S(1)}, bf16[2,304,128]{2,1,0:T(8,128)(2,1)S(1)}, u32[]{:S(2)}, u32[]{:S(2)}) %collective-permute-start.23) | collective-permute-done | bytes 155680 | tf_op jit(solution)/shard_map/ppermute | solution.py:69
  91.2 1.5 %merge.1 = bf16[2,144,640]{2,1,0:T(8,128)(2,1)} custom-call(s32[1]{0:T(128)} %bitcast.u_ref, f32[2,5,144,128]{3,2,1,0:T(8,128)S(1)} %get-tuple-element.64.fresh_out, f32[24,128]{1,0:T(8,128)S(1)} %get-tuple-element.65.refs_9_.fresh_rows, bf16[2,304,128]{2,1,0:T(8,128)(2,1)S(1)} %get-tuple-element.71.refs_0_, ...), custom_call_target="tpu_custom_call" | custom-call | flops 1843200 | bytes 2580480 | tf_op jit(solution)/shard_map/merge/pallas_call | solution.py:590
  (48 shorter events, 0.5 us)
Async XLA Ops:
  0.6 20.8 %collective-permute-start.7 = (bf16[288,1280]{1,0:T(8,128)(2,1)}, bf16[288,1280]{1,0:T(8,128)(2,1)S(1)}, u32[]{:S(2)}, u32[]{:S(2)}) collective-permute-start(bf16[288,1280]{1,0:T(8,128)(2,1)} %bitcast.14), channel_id=1, source_target_pairs={{0,2},{1,3},{2,0},{3,1},{4,6},{5,7},{6,4},{7,5},{8,10},{33,35},{10... | collective-permute-start | bytes 2211848 | tf_op jit(solution)/shard_map/ppermute | solution.py:69
  2.7 1.0 %copy-start.1 = (bf16[2,144,640]{2,1,0:T(8,128)(2,1)S(1)}, bf16[2,144,640]{2,1,0:T(8,128)(2,1)}, u32[]{:S(2)}) copy-start(bf16[2,144,640]{2,1,0:T(8,128)(2,1)} %key_ref.1) | copy-start | bytes 1105924
  3.7 1.0 %copy-start.2 = (bf16[2,144,640]{2,1,0:T(8,128)(2,1)S(1)}, bf16[2,144,640]{2,1,0:T(8,128)(2,1)}, u32[]{:S(2)}) copy-start(bf16[2,144,640]{2,1,0:T(8,128)(2,1)} %value_ref.1) | copy-start | bytes 1105924
  4.8 5.2 %collective-permute-start.1 = (bf16[2,2,144,128]{3,2,1,0:T(8,128)(2,1)S(1)}, bf16[2,2,144,128]{3,2,1,0:T(8,128)(2,1)S(1)}, u32[]{:S(2)}, u32[]{:S(2)}) collective-permute-start(bf16[2,2,144,128]{3,2,1,0:T(8,128)(2,1)S(1)} %get-tuple-element.41), channel_id=1, source_target_pairs={{0,32},{1,9},{2,34},{3,11},{4,36},{5,13},{6,38},{7,15},{8,40},{33,... | collective-permute-start | bytes 442376 | tf_op jit(solution)/shard_map/ppermute | solution.py:69
  6.5 6.6 %collective-permute-start = (bf16[2,2,144,128]{3,2,1,0:T(8,128)(2,1)S(1)}, bf16[2,2,144,128]{3,2,1,0:T(8,128)(2,1)S(1)}, u32[]{:S(2)}, u32[]{:S(2)}) collective-permute-start(bf16[2,2,144,128]{3,2,1,0:T(8,128)(2,1)S(1)} %get-tuple-element.40), channel_id=1, source_target_pairs={{0,32},{1,9},{2,34},{3,11},{4,36},{5,13},{6,38},{7,15},{8,40},{33,... | collective-permute-start | bytes 442376 | tf_op jit(solution)/shard_map/ppermute | solution.py:69
  6.9 6.4 %collective-permute-start.3 = (bf16[2,2,144,128]{3,2,1,0:T(8,128)(2,1)S(1)}, bf16[2,2,144,128]{3,2,1,0:T(8,128)(2,1)S(1)}, u32[]{:S(2)}, u32[]{:S(2)}) collective-permute-start(bf16[2,2,144,128]{3,2,1,0:T(8,128)(2,1)S(1)} %get-tuple-element.42), channel_id=1, source_target_pairs={{0,96},{1,25},{2,98},{3,27},{4,100},{5,29},{6,102},{7,31},{8,104},... | collective-permute-start | bytes 442376 | tf_op jit(solution)/shard_map/ppermute | solution.py:69
  10.0 6.4 %collective-permute-start.2 = (bf16[2,2,144,128]{3,2,1,0:T(8,128)(2,1)S(1)}, bf16[2,2,144,128]{3,2,1,0:T(8,128)(2,1)S(1)}, u32[]{:S(2)}, u32[]{:S(2)}) collective-permute-start(bf16[2,2,144,128]{3,2,1,0:T(8,128)(2,1)S(1)} %collective-permute-done.1), channel_id=1, source_target_pairs={{0,96},{1,25},{2,98},{3,27},{4,100},{5,29},{6,102},{7,31},{8,104},... | collective-permute-start | bytes 442376 | tf_op jit(solution)/shard_map/ppermute | solution.py:69
  13.1 15.8 %collective-permute-start.6 = (bf16[288,1280]{1,0:T(8,128)(2,1)}, bf16[288,1280]{1,0:T(8,128)(2,1)S(1)}, u32[]{:S(2)}, u32[]{:S(2)}) collective-permute-start(bf16[288,1280]{1,0:T(8,128)(2,1)} %bitcast.15), channel_id=1, source_target_pairs={{0,1},{1,0},{2,3},{3,2},{4,5},{5,4},{6,7},{7,6},{8,9},{33,32},{10,... | collective-permute-start | bytes 2211848 | tf_op jit(solution)/shard_map/ppermute | solution.py:69
  16.4 1.1 %copy-start = (bf16[2,144,1280]{2,1,0:T(8,128)(2,1)S(1)}, bf16[2,144,1280]{2,1,0:T(8,128)(2,1)}, u32[]{:S(2)}) copy-start(bf16[2,144,1280]{2,1,0:T(8,128)(2,1)} %param.12) | copy-start | bytes 2211844
  17.6 0.8 copy-start.5
  18.3 0.8 copy-start.6
  19.1 0.7 copy-start.9
  19.8 0.7 copy-start.10
  21.4 7.4 %collective-permute-start.8 = (bf16[288,1280]{1,0:T(8,128)(2,1)S(1)}, bf16[288,1280]{1,0:T(8,128)(2,1)}, u32[]{:S(2)}, u32[]{:S(2)}) collective-permute-start(bf16[288,1280]{1,0:T(8,128)(2,1)S(1)} %collective-permute-done.7.h2), channel_id=1, source_target_pairs={{0,1},{1,0},{2,3},{3,2},{4,5},{5,4},{6,7},{7,6},{8,9},{33,32},{10,... | collective-permute-start | bytes 2211848 | tf_op jit(solution)/shard_map/ppermute | solution.py:69
  21.5 17.1 %collective-permute-start.4 = (bf16[2,2,720,128]{3,2,1,0:T(8,128)(2,1)S(1)}, bf16[2,2,720,128]{3,2,1,0:T(8,128)(2,1)S(1)}, u32[]{:S(2)}, u32[]{:S(2)}) collective-permute-start(bf16[2,2,720,128]{3,2,1,0:T(8,128)(2,1)S(1)} %assemble.1.after.refs_4_), channel_id=1, source_target_pairs={{0,8},{1,33},{2,10},{3,35},{4,12},{5,37},{6,14},{7,39},{8,0},{33,1... | collective-permute-start | bytes 2211848 | tf_op jit(solution)/shard_map/ppermute | solution.py:69
  23.1 15.5 %collective-permute-start.5 = (bf16[2,2,720,128]{3,2,1,0:T(8,128)(2,1)S(1)}, bf16[2,2,720,128]{3,2,1,0:T(8,128)(2,1)S(1)}, u32[]{:S(2)}, u32[]{:S(2)}) collective-permute-start(bf16[2,2,720,128]{3,2,1,0:T(8,128)(2,1)S(1)} %assemble.1.after.refs_4_), channel_id=1, source_target_pairs={{0,24},{1,97},{2,26},{3,99},{4,28},{5,101},{6,30},{7,103},{8,16},{... | collective-permute-start | bytes 2211848 | tf_op jit(solution)/shard_map/ppermute | solution.py:69
  25.3 21.7 %collective-permute-start.10 = (bf16[2,2,720,128]{3,2,1,0:T(8,128)(2,1)S(1)}, bf16[2,2,720,128]{3,2,1,0:T(8,128)(2,1)S(1)}, u32[]{:S(2)}, u32[]{:S(2)}) collective-permute-start(bf16[2,2,720,128]{3,2,1,0:T(8,128)(2,1)S(1)} %assemble.1.after.refs_4_), channel_id=1, source_target_pairs={{0,4},{1,5},{2,6},{3,7},{4,0},{5,1},{6,2},{7,3},{8,12},{33,37},{10... | collective-permute-start | bytes 2211848 | tf_op jit(solution)/shard_map/ppermute | solution.py:69
  28.9 11.0 %slice-start = ((s8[6553600]{0:T(1024)(128)(4,1)}), s8[4194304]{0:T(1024)(128)(4,1)S(1)}, s32[]{:S(2)}) async-start(s8[6553600]{0:T(1024)(128)(4,1)} %bitcast.19), calls=%async_computation | async-start | bytes 8388608
  33.1 6.7 %slice-start.1 = ((s8[6553600]{0:T(1024)(128)(4,1)}), s8[2359296]{0:T(1024)(128)(4,1)S(1)}, s32[]{:S(2)}) async-start(s8[6553600]{0:T(1024)(128)(4,1)} %bitcast.19), calls=%async_computation.1 | async-start | bytes 4718592
  33.1 11.3 %slice-start.2 = ((s8[6553600]{0:T(1024)(128)(4,1)}), s8[4194304]{0:T(1024)(128)(4,1)S(1)}, s32[]{:S(2)}) async-start(s8[6553600]{0:T(1024)(128)(4,1)} %bitcast.21), calls=%async_computation.2 | async-start | bytes 8388608
  38.6 5.9 %slice-start.3 = ((s8[6553600]{0:T(1024)(128)(4,1)}), s8[2359296]{0:T(1024)(128)(4,1)S(1)}, s32[]{:S(2)}) async-start(s8[6553600]{0:T(1024)(128)(4,1)} %bitcast.21), calls=%async_computation.3 | async-start | bytes 4718592
  38.6 12.8 %collective-permute-start.9 = (bf16[2,2,720,128]{3,2,1,0:T(8,128)(2,1)S(1)}, bf16[2,2,720,128]{3,2,1,0:T(8,128)(2,1)S(1)}, u32[]{:S(2)}, u32[]{:S(2)}) collective-permute-start(bf16[2,2,720,128]{3,2,1,0:T(8,128)(2,1)S(1)} %collective-permute-done.4.refs_5_), channel_id=1, source_target_pairs={{0,24},{1,97},{2,26},{3,99},{4,28},{5,101},{6,30},{7,103},{8,16},{... | collective-permute-start | bytes 2211848 | tf_op jit(solution)/shard_map/ppermute | solution.py:69
  42.5 6.7 %copy-start.7 = (f32[640]{0:T(1024)S(1)}, f32[640]{0:T(1024)}, u32[]{:S(2)}) copy-start(f32[640]{0:T(1024)} %qg.1) | copy-start | bytes 7684
  42.5 6.7 %copy-start.8 = (f32[640]{0:T(1024)S(1)}, f32[640]{0:T(1024)}, u32[]{:S(2)}) copy-start(f32[640]{0:T(1024)} %kg.1) | copy-start | bytes 7684
  42.5 4.4 %collective-permute-start.11 = (f32[8,384]{1,0:T(8,128)S(1)}, f32[8,384]{1,0:T(8,128)S(1)}, u32[]{:S(2)}, u32[]{:S(2)}) collective-permute-start(f32[8,384]{1,0:T(8,128)S(1)} %sum_squares.1.s0), channel_id=1, source_target_pairs={{0,3},{1,2},{2,1},{3,0},{4,7},{5,6},{6,5},{7,4},{8,11},{33,34},{10... | collective-permute-start | bytes 36872 | tf_op jit(solution)/shard_map/ppermute | solution.py:69
  42.6 4.3 %collective-permute-start.12 = (f32[8,384]{1,0:T(8,128)S(1)}, f32[8,384]{1,0:T(8,128)S(1)}, u32[]{:S(2)}, u32[]{:S(2)}) collective-permute-start(f32[8,384]{1,0:T(8,128)S(1)} %sum_squares.1.s0), channel_id=1, source_target_pairs={{0,2},{1,3},{2,0},{3,1},{4,6},{5,7},{6,4},{7,5},{8,10},{33,35},{10... | collective-permute-start | bytes 36872 | tf_op jit(solution)/shard_map/ppermute | solution.py:69
  42.7 4.3 %collective-permute-start.13 = (f32[8,384]{1,0:T(8,128)S(1)}, f32[8,384]{1,0:T(8,128)S(1)}, u32[]{:S(2)}, u32[]{:S(2)}) collective-permute-start(f32[8,384]{1,0:T(8,128)S(1)} %sum_squares.1.s0), channel_id=1, source_target_pairs={{0,1},{1,0},{2,3},{3,2},{4,5},{5,4},{6,7},{7,6},{8,9},{33,32},{10,... | collective-permute-start | bytes 36872 | tf_op jit(solution)/shard_map/ppermute | solution.py:69
  46.9 45.8 %copy-start.3 = (bf16[288,640]{1,0:T(8,128)(2,1)}, bf16[288,640]{1,0:T(8,128)(2,1)S(1)}, u32[]{:S(2)}) copy-start(bf16[288,640]{1,0:T(8,128)(2,1)S(1)} %convolution_convert_fusion.v_ref) | copy-start | bytes 1105924
  47.0 27.8 %collective-permute-start.18 = (bf16[2,2,720,128]{3,2,1,0:T(8,128)(2,1)S(1)}, bf16[2,2,720,128]{3,2,1,0:T(8,128)(2,1)S(1)}, u32[]{:S(2)}, u32[]{:S(2)}) collective-permute-start(bf16[2,2,720,128]{3,2,1,0:T(8,128)(2,1)S(1)} %collective-permute-done.10.refs_8_), channel_id=1, source_target_pairs={{0,8},{1,33},{2,10},{3,35},{4,12},{5,37},{6,14},{7,39},{8,0},{33,1... | collective-permute-start | bytes 2211848 | tf_op jit(solution)/shard_map/ppermute | solution.py:69
  47.1 27.7 %collective-permute-start.19 = (bf16[2,2,720,128]{3,2,1,0:T(8,128)(2,1)S(1)}, bf16[2,2,720,128]{3,2,1,0:T(8,128)(2,1)S(1)}, u32[]{:S(2)}, u32[]{:S(2)}) collective-permute-start(bf16[2,2,720,128]{3,2,1,0:T(8,128)(2,1)S(1)} %collective-permute-done.10.refs_8_), channel_id=1, source_target_pairs={{0,24},{1,97},{2,26},{3,99},{4,28},{5,101},{6,30},{7,103},{8,16},{... | collective-permute-start | bytes 2211848 | tf_op jit(solution)/shard_map/ppermute | solution.py:69
  51.4 23.4 %collective-permute-start.20 = (bf16[2,2,720,128]{3,2,1,0:T(8,128)(2,1)S(1)}, bf16[2,2,720,128]{3,2,1,0:T(8,128)(2,1)S(1)}, u32[]{:S(2)}, u32[]{:S(2)}) collective-permute-start(bf16[2,2,720,128]{3,2,1,0:T(8,128)(2,1)S(1)} %collective-permute-done.9.refs_7_), channel_id=1, source_target_pairs={{0,4},{1,5},{2,6},{3,7},{4,0},{5,1},{6,2},{7,3},{8,12},{33,37},{10... | collective-permute-start | bytes 2211848 | tf_op jit(solution)/shard_map/ppermute | solution.py:69
  52.6 6.5 %collective-permute-start.15 = (bf16[2,2,144,128]{3,2,1,0:T(8,128)(2,1)S(1)}, bf16[2,2,144,128]{3,2,1,0:T(8,128)(2,1)S(1)}, u32[]{:S(2)}, u32[]{:S(2)}) collective-permute-start(bf16[2,2,144,128]{3,2,1,0:T(8,128)(2,1)S(1)} %get-tuple-element.62.refs_2_), channel_id=1, source_target_pairs={{0,32},{1,9},{2,34},{3,11},{4,36},{5,13},{6,38},{7,15},{8,40},{33,... | collective-permute-start | bytes 442376 | tf_op jit(solution)/shard_map/ppermute | solution.py:69
  52.6 9.2 %collective-permute-start.14 = (bf16[2,2,144,128]{3,2,1,0:T(8,128)(2,1)S(1)}, bf16[2,2,144,128]{3,2,1,0:T(8,128)(2,1)S(1)}, u32[]{:S(2)}, u32[]{:S(2)}) collective-permute-start(bf16[2,2,144,128]{3,2,1,0:T(8,128)(2,1)S(1)} %get-tuple-element.61.refs_1_), channel_id=1, source_target_pairs={{0,32},{1,9},{2,34},{3,11},{4,36},{5,13},{6,38},{7,15},{8,40},{33,... | collective-permute-start | bytes 442376 | tf_op jit(solution)/shard_map/ppermute | solution.py:69
  59.1 6.6 %collective-permute-start.17 = (bf16[2,2,144,128]{3,2,1,0:T(8,128)(2,1)S(1)}, bf16[2,2,144,128]{3,2,1,0:T(8,128)(2,1)S(1)}, u32[]{:S(2)}, u32[]{:S(2)}) collective-permute-start(bf16[2,2,144,128]{3,2,1,0:T(8,128)(2,1)S(1)} %get-tuple-element.63.refs_3_), channel_id=1, source_target_pairs={{0,96},{1,25},{2,98},{3,27},{4,100},{5,29},{6,102},{7,31},{8,104},... | collective-permute-start | bytes 442376 | tf_op jit(solution)/shard_map/ppermute | solution.py:69
  61.8 6.4 %collective-permute-start.16 = (bf16[2,2,144,128]{3,2,1,0:T(8,128)(2,1)S(1)}, bf16[2,2,144,128]{3,2,1,0:T(8,128)(2,1)S(1)}, u32[]{:S(2)}, u32[]{:S(2)}) collective-permute-start(bf16[2,2,144,128]{3,2,1,0:T(8,128)(2,1)S(1)} %collective-permute-done.15), channel_id=1, source_target_pairs={{0,96},{1,25},{2,98},{3,27},{4,100},{5,29},{6,102},{7,31},{8,104},... | collective-permute-start | bytes 442376 | tf_op jit(solution)/shard_map/ppermute | solution.py:69
  63.7 1.0 %copy-start.4 = (bf16[288,640]{1,0:T(8,128)(2,1)S(1)}, bf16[288,640]{1,0:T(8,128)(2,1)}, u32[]{:S(2)}) copy-start(bf16[288,640]{1,0:T(8,128)(2,1)} %get-tuple-element.58.k_ref) | copy-start | bytes 1105924
  79.4 5.3 %collective-permute-start.22 = (bf16[2,304,128]{2,1,0:T(8,128)(2,1)S(1)}, bf16[2,304,128]{2,1,0:T(8,128)(2,1)S(1)}, u32[]{:S(2)}, u32[]{:S(2)}) collective-permute-start(bf16[2,304,128]{2,1,0:T(8,128)(2,1)S(1)} %get-tuple-element.73), channel_id=1, source_target_pairs={{0,32},{1,9},{2,34},{3,11},{4,36},{5,13},{6,38},{7,15},{8,40},{33,... | collective-permute-start | bytes 466952 | tf_op jit(solution)/shard_map/ppermute | solution.py:69
  79.5 7.1 %collective-permute-start.21 = (bf16[2,304,128]{2,1,0:T(8,128)(2,1)S(1)}, bf16[2,304,128]{2,1,0:T(8,128)(2,1)S(1)}, u32[]{:S(2)}, u32[]{:S(2)}) collective-permute-start(bf16[2,304,128]{2,1,0:T(8,128)(2,1)S(1)} %get-tuple-element.72), channel_id=1, source_target_pairs={{0,32},{1,9},{2,34},{3,11},{4,36},{5,13},{6,38},{7,15},{8,40},{33,... | collective-permute-start | bytes 466952 | tf_op jit(solution)/shard_map/ppermute | solution.py:69
  81.5 6.4 %collective-permute-start.24 = (bf16[2,304,128]{2,1,0:T(8,128)(2,1)S(1)}, bf16[2,304,128]{2,1,0:T(8,128)(2,1)S(1)}, u32[]{:S(2)}, u32[]{:S(2)}) collective-permute-start(bf16[2,304,128]{2,1,0:T(8,128)(2,1)S(1)} %get-tuple-element.74), channel_id=1, source_target_pairs={{0,96},{1,25},{2,98},{3,27},{4,100},{5,29},{6,102},{7,31},{8,104},... | collective-permute-start | bytes 466952 | tf_op jit(solution)/shard_map/ppermute | solution.py:69
  84.7 6.4 %collective-permute-start.23 = (bf16[2,304,128]{2,1,0:T(8,128)(2,1)S(1)}, bf16[2,304,128]{2,1,0:T(8,128)(2,1)S(1)}, u32[]{:S(2)}, u32[]{:S(2)}) collective-permute-start(bf16[2,304,128]{2,1,0:T(8,128)(2,1)S(1)} %collective-permute-done.22), channel_id=1, source_target_pairs={{0,96},{1,25},{2,98},{3,27},{4,100},{5,29},{6,102},{7,31},{8,104},... | collective-permute-start | bytes 466952 | tf_op jit(solution)/shard_map/ppermute | solution.py:69

commit v9 on v7

--- a/solution.py
+++ b/solution.py
@@ -35,6 +35,7 @@
 GROUP = 16
 VMEM_MIB = 24
 ATTENTION_MIB = 34
+MODULATE_MIB = 42
 
 
 def params(mib):
@@ -230,35 +231,66 @@
     return jnp.sum(total, axis=1, keepdims=True)
 
 
-def modulate_kernel(t_ref, h0, h1, h2, h3, cond, mod, out_ref):
+def modulate_kernel(t_ref, h0, h1, h2, h3, cond, mod, weight, out_ref, query_ref, *scratch):
+    weight_s, modded_s, mean_s, rstd_s, sems = scratch
     chunks = (h0, h1, h2, h3)
+    copies = []
+    for c in range(TP):
+        rows = pl.ds(pl.multiple_of(t_ref[c] * CHUNK, CHUNK), CHUNK)
+        copies.append(pltpu.make_async_copy(weight.at[rows], weight_s.at[c], sems.at[c]))
+        copies[c].start()
     for row in range(0, ROWS, GROUP):
         rows = slice(row, row + GROUP)
         lanes = [chunk[rows].astype(F32) for chunk in chunks]
         mean = lane_sum([(lanes[0] + lanes[1]) + (lanes[2] + lanes[3])]) * (1.0 / D)
         deviation = lane_sum([(part - mean) * (part - mean) for part in lanes])
-        rstd = lax.rsqrt(deviation * (1.0 / D) + EPS)
-        conditioned = cond[rows, 0:1] > 0.5
-        for c in range(TP):
-            cols = pl.ds(pl.multiple_of(t_ref[c] * CHUNK, CHUNK), CHUNK)
+        mean_s[rows] = jnp.broadcast_to(mean, (GROUP, HD))
+        rstd_s[rows] = jnp.broadcast_to(lax.rsqrt(deviation * (1.0 / D) + EPS), (GROUP, HD))
+
+    def product(c):
+        copies[c].wait()
+        part = jnp.dot(modded_s[c % 2], weight_s[c], preferred_element_type=F32)
+        if c == 0:
+            query_ref[...] = part
+        else:
+            query_ref[...] += part
+
+    for c in range(TP):
+        if c:
+            product(c - 1)
+        cols = pl.ds(pl.multiple_of(t_ref[c] * CHUNK, CHUNK), CHUNK)
+        for row in range(0, ROWS, GROUP):
+            rows = slice(row, row + GROUP)
+            conditioned = cond[rows, 0:1] > 0.5
             gain = jnp.where(conditioned, mod[1:2, cols], mod[0:1, cols])
             bias = jnp.where(conditioned, mod[3:4, cols], mod[2:3, cols])
-            normed = (lanes[c] - mean) * rstd
-            out_ref[rows, cols] = (normed * gain + bias).astype(BF16)
-
-
-def modulate(blocks, chunks, cond, mod):
+            normed = (chunks[c][rows].astype(F32) - mean_s[rows, 0:1]) * rstd_s[rows, 0:1]
+            value = (normed * gain + bias).astype(BF16)
+            modded_s[c % 2, rows] = value
+            out_ref[rows, cols] = value
+    product(TP - 1)
+
+
+def modulate(blocks, chunks, cond, mod, weight):
     return pl.pallas_call(
         modulate_kernel,
-        out_shape=jax.ShapeDtypeStruct((ROWS, D), BF16),
-        in_specs=[smem()] + [vmem()] * 6,
-        out_specs=vmem(),
-        compiler_params=params(VMEM_MIB),
-        cost_estimate=pl.CostEstimate(
-            flops=12 * ROWS * D, bytes_accessed=20_000_000, transcendentals=0
-        ),
+        out_shape=[
+            jax.ShapeDtypeStruct((ROWS, D), BF16),
+            jax.ShapeDtypeStruct((ROWS, WIDTH), F32),
+        ],
+        in_specs=[smem()] + [vmem()] * 6 + [pl.BlockSpec(memory_space=pltpu.HBM)],
+        out_specs=[vmem()] * 2,
+        scratch_shapes=[
+            pltpu.VMEM((TP, CHUNK, WIDTH), BF16),
+            pltpu.VMEM((2, ROWS, CHUNK), BF16),
+            pltpu.VMEM((ROWS, HD), F32),
+            pltpu.VMEM((ROWS, HD), F32),
+            pltpu.SemaphoreType.DMA((TP,)),
+        ],
+        compiler_params=params(MODULATE_MIB),
+        cost_estimate=pl.CostEstimate(flops=1000, bytes_accessed=30_000_000, transcendentals=0),
         name="modulate",
-    )(blocks, *chunks, cond, mod)
+    )(blocks, *chunks, cond, mod, weight)
 
 
 def squares_kernel(q_ref, k_ref, out_ref):
@@ -629,21 +661,19 @@
 
     z_rows, cond = lax.optimization_barrier((z_rows, cond))
     cross_rows = swap_tp(z_rows, 0, 1)
-    near_one, near_three = lax.optimization_barrier((near_one, near_three))
+    blocks = jnp.stack([tp, tp ^ 1, tp ^ 2, tp ^ 3]).astype(jnp.int32)
+    modded, query = modulate(blocks, [own_rows, core_rows, z_rows, cross_rows], cond, mod, w_query)
+    key = jnp.dot(modded, w_key, preferred_element_type=F32)
+    near_one, near_three, key = lax.optimization_barrier((near_one, near_three, key))
     near_two = swap_v(near_one, 3)
-    blocks = jnp.stack([tp, tp ^ 1, tp ^ 2, tp ^ 3]).astype(jnp.int32)
-    modded = modulate(blocks, [own_rows, core_rows, z_rows, cross_rows], cond, mod)
-    query = jnp.dot(modded, w_query, preferred_element_type=F32)
-    key = jnp.dot(modded, w_key, preferred_element_type=F32)
     fresh_values = jnp.dot(modded, w_value, preferred_element_type=F32).astype(BF16)
     own_sq = sum_squares(query, key)
     squares = [own_sq] + [swap_tp(own_sq, z, c) for z, c in ((1, 1), (1, 0), (0, 1))]
-    near_two, far, fresh_values, *squares = lax.optimization_barrier(
-        (near_two, far, fresh_values, *squares)
-    )
-    far_two = swap_z_hi(near_two)
+    far, fresh_values, *squares = lax.optimization_barrier((far, fresh_values, *squares))
     far_one, far_three = swap_v(far, 1), swap_v(far, 3)
     fresh_keys, *sends = norm_rope(u, query, key, squares, q_gain, k_gain, cos, sin)
+    near_two, fresh_keys = lax.optimization_barrier((near_two, fresh_keys))
+    far_two = swap_z_hi(near_two)
     queries = exchange_u(sends)
     fresh_out, fresh_rows = fresh_attention(u, fresh_keys, fresh_values, sends)
 

time: 92.5 us -> 88.2 us (0.954); the launches traced: 92.1 us -> 86.8 us
  matrix products: 10.5 us -> 4.88 us
  Pallas kernels: 22.8 us -> 24.9 us
  starting transfers between devices: 26.8 us -> 25.8 us
    dot_general x1 -> x0, matrix products: 5.53 us -> none  [shards(): query = jnp.dot(modded, w_query, preferred_element_type=F32)]
    pallas_call x1, Pallas kernels: 4.24 us -> 7.78 us  [modulate(): pl.pallas_call(modulate_kernel, out_shape=[jax.ShapeDtypeStruct((ROWS, D)...]
    pallas_call x2, Pallas kernels: 12.8 us -> 11.4 us  [stale_attention(): pl.pallas_call(functools.partial(stale_kernel, far, count), out_shape=out...]
    ppermute x22, starting transfers between devices: 26.8 us -> 25.8 us  [permute(): lax.ppermute(value, AXES, [(linear(*p), linear(*move(*p))) for p in place...]
    unnamed x30 -> x28, local copies, waits for them, and re-layouts: 7.01 us -> 6.99 us
  transfers between devices with their start and end apart: 22 -> 22, of which waited for: 9 -> 10; matrix products, arithmetic and copies ran while one was open for 12% -> 6% of each run, Pallas kernels for 18% -> 21%
where the time goes in v9:
time: 88.2 us; the launch traced here: 86.8 us
  starting transfers between devices  25.8 us (29%)
  Pallas kernels  24.9 us (28%)
  waiting for transfers between devices  23.2 us (26%)
  local copies, waits for them, and re-layouts  6.99 us (8%)
  matrix products  4.88 us (6%)
    ppermute x22, starting transfers between devices, permute(): lax.ppermute(value, AXES, [(linear(*p), linear(*move(*p))) for p in place...  25.8 us
    ppermute x22, waiting for transfers between devices, permute(): lax.ppermute(value, AXES, [(linear(*p), linear(*move(*p))) for p in place...  23.2 us
    pallas_call x2, Pallas kernels, stale_attention(): pl.pallas_call(functools.partial(stale_kernel, far, count), out_shape=out...  11.4 us
    pallas_call x1, Pallas kernels, modulate(): pl.pallas_call(modulate_kernel, out_shape=[jax.ShapeDtypeStruct((ROWS, D)...  7.78 us
    unnamed x28, local copies, waits for them, and re-layouts  6.99 us
    dot_general x1, matrix products, shards(): jnp.dot(modded, w_value, preferred_element_type=F32).astype(BF16)  2.44 us
    dot_general x1, matrix products, shards(): key = jnp.dot(modded, w_key, preferred_element_type=F32)  2.44 us
    pallas_call x1, Pallas kernels, norm_rope(): pl.pallas_call(rope_kernel, out_shape=[flat] + [send] * 4, in_specs=[smem...  1.8 us
  transfers between devices with their start and end apart: 22, of which 10 were waited for; matrix products, arithmetic and copies ran while one was open for 6% of the time, Pallas kernels for 21%

profile of v9, /device:TPU:0, one launch (start us, length us, event | category | flops | bytes accessed | tf_op | source)
XLA Modules:
  0.0 86.8 jit_solution(12875625463196943891)
XLA Ops:
  0.6 2.1 %collective-permute-start.6 = (bf16[288,1280]{1,0:T(8,128)(2,1)}, bf16[288,1280]{1,0:T(8,128)(2,1)S(1)}, u32[]{:S(2)}, u32[]{:S(2)}) collective-permute-start(bf16[288,1280]{1,0:T(8,128)(2,1)} %bitcast.12), channel_id=1, source_target_pairs={{0,2},{1,3},{2,0},{3,1},{4,6},{5,7},{6,4},{7,5},{8,10},{33,35},{10... | collective-permute-start | bytes 2211848 | tf_op jit(solution)/shard_map/ppermute | solution.py:70
  2.7 1.0 %copy-done.1 = bf16[2,144,640]{2,1,0:T(8,128)(2,1)S(1)} copy-done((bf16[2,144,640]{2,1,0:T(8,128)(2,1)S(1)}, bf16[2,144,640]{2,1,0:T(8,128)(2,1)}, u32[]{:S(2)}) %copy-start.1) | copy-done | bytes 368664
  3.7 1.0 %copy-done.2 = bf16[2,144,640]{2,1,0:T(8,128)(2,1)S(1)} copy-done((bf16[2,144,640]{2,1,0:T(8,128)(2,1)S(1)}, bf16[2,144,640]{2,1,0:T(8,128)(2,1)}, u32[]{:S(2)}) %copy-start.2) | copy-done | bytes 368664
  4.7 0.1 pack_stale.1
  4.8 3.1 %collective-permute-start = (bf16[2,2,144,128]{3,2,1,0:T(8,128)(2,1)S(1)}, bf16[2,2,144,128]{3,2,1,0:T(8,128)(2,1)S(1)}, u32[]{:S(2)}, u32[]{:S(2)}) collective-permute-start(bf16[2,2,144,128]{3,2,1,0:T(8,128)(2,1)S(1)} %get-tuple-element.42), channel_id=1, source_target_pairs={{0,96},{1,25},{2,98},{3,27},{4,100},{5,29},{6,102},{7,31},{8,104},... | collective-permute-start | bytes 442376 | tf_op jit(solution)/shard_map/ppermute | solution.py:70
  7.9 0.6 collective-permute-start.1
  8.5 1.0 %collective-permute-start.2 = (bf16[2,2,144,128]{3,2,1,0:T(8,128)(2,1)S(1)}, bf16[2,2,144,128]{3,2,1,0:T(8,128)(2,1)S(1)}, u32[]{:S(2)}, u32[]{:S(2)}) collective-permute-start(bf16[2,2,144,128]{3,2,1,0:T(8,128)(2,1)S(1)} %get-tuple-element.44), channel_id=1, source_target_pairs={{0,32},{1,9},{2,34},{3,11},{4,36},{5,13},{6,38},{7,15},{8,40},{33,... | collective-permute-start | bytes 442376 | tf_op jit(solution)/shard_map/ppermute | solution.py:70
  9.5 2.7 %collective-permute-done.refs_1_ = bf16[2,2,144,128]{3,2,1,0:T(8,128)(2,1)S(1)} collective-permute-done((bf16[2,2,144,128]{3,2,1,0:T(8,128)(2,1)S(1)}, bf16[2,2,144,128]{3,2,1,0:T(8,128)(2,1)S(1)}, u32[]{:S(2)}, u32[]{:S(2)}) %collective-permute-start) | collective-permute-done | bytes 147488 | tf_op jit(solution)/shard_map/ppermute | solution.py:70
  12.2 2.5 %collective-permute-done.1.refs_2_ = bf16[2,2,144,128]{3,2,1,0:T(8,128)(2,1)S(1)} collective-permute-done((bf16[2,2,144,128]{3,2,1,0:T(8,128)(2,1)S(1)}, bf16[2,2,144,128]{3,2,1,0:T(8,128)(2,1)S(1)}, u32[]{:S(2)}, u32[]{:S(2)}) %collective-permute-start.1) | collective-permute-done | bytes 147488 | tf_op jit(solution)/shard_map/ppermute | solution.py:70
  14.7 1.5 %collective-permute-done.2.refs_3_ = bf16[2,2,144,128]{3,2,1,0:T(8,128)(2,1)S(1)} collective-permute-done((bf16[2,2,144,128]{3,2,1,0:T(8,128)(2,1)S(1)}, bf16[2,2,144,128]{3,2,1,0:T(8,128)(2,1)S(1)}, u32[]{:S(2)}, u32[]{:S(2)}) %collective-permute-start.2) | collective-permute-done | bytes 147488 | tf_op jit(solution)/shard_map/ppermute | solution.py:70
  16.2 1.1 %copy-done = bf16[2,144,1280]{2,1,0:T(8,128)(2,1)S(1)} copy-done((bf16[2,144,1280]{2,1,0:T(8,128)(2,1)S(1)}, bf16[2,144,1280]{2,1,0:T(8,128)(2,1)}, u32[]{:S(2)}) %copy-start) | copy-done | bytes 737304
  17.3 0.8 copy-done.5
  18.1 0.8 copy-done.6
  18.9 0.7 copy-done.9
  19.5 0.7 copy-done.10
  20.2 0.9 %tables.1 = (f32[288,128]{1,0:T(8,128)S(1)}, f32[144,128]{1,0:T(8,128)S(1)}, f32[144,128]{1,0:T(8,128)S(1)}, f32[4,5120]{1,0:T(4,128)S(1)}, bf16[288,1280]{1,0:T(8,128)(2,1)S(1)}) custom-call(s32[144]{0:T(256)S(1)} %copy-done.9, f32[1,128]{1,0:T(1,128)S(1)} %copy-done.10, bf16[288,1280]{1,0:T(8,128)(2,1)S(1)} %bitcast.14, f32[2,5120]{1,0:T(2,128)S(1)} %copy-done.5, ...), custom_call_target="tpu_custom_call" | custom-call | flops 1843200 | bytes 1000000 | tf_op jit(solution)/shard_map/tables/pallas_call | solution.py:177
  21.2 0.1 collective-permute-start.7
  21.3 1.6 %collective-permute-start.3 = (bf16[2,2,720,128]{3,2,1,0:T(8,128)(2,1)S(1)}, bf16[2,2,720,128]{3,2,1,0:T(8,128)(2,1)S(1)}, u32[]{:S(2)}, u32[]{:S(2)}) collective-permute-start(bf16[2,2,720,128]{3,2,1,0:T(8,128)(2,1)S(1)} %assemble.1.after.refs_4_), channel_id=1, source_target_pairs={{0,8},{1,33},{2,10},{3,35},{4,12},{5,37},{6,14},{7,39},{8,0},{33,1... | collective-permute-start | bytes 2211848 | tf_op jit(solution)/shard_map/ppermute | solution.py:70
  22.8 2.1 %collective-permute-start.4 = (bf16[2,2,720,128]{3,2,1,0:T(8,128)(2,1)S(1)}, bf16[2,2,720,128]{3,2,1,0:T(8,128)(2,1)S(1)}, u32[]{:S(2)}, u32[]{:S(2)}) collective-permute-start(bf16[2,2,720,128]{3,2,1,0:T(8,128)(2,1)S(1)} %assemble.1.after.refs_4_), channel_id=1, source_target_pairs={{0,24},{1,97},{2,26},{3,99},{4,28},{5,101},{6,30},{7,103},{8,16},{... | collective-permute-start | bytes 2211848 | tf_op jit(solution)/shard_map/ppermute | solution.py:70
  25.0 3.6 %collective-permute-start.9 = (bf16[2,2,720,128]{3,2,1,0:T(8,128)(2,1)S(1)}, bf16[2,2,720,128]{3,2,1,0:T(8,128)(2,1)S(1)}, u32[]{:S(2)}, u32[]{:S(2)}) collective-permute-start(bf16[2,2,720,128]{3,2,1,0:T(8,128)(2,1)S(1)} %assemble.1.after.refs_4_), channel_id=1, source_target_pairs={{0,4},{1,5},{2,6},{3,7},{4,0},{5,1},{6,2},{7,3},{8,12},{33,37},{10... | collective-permute-start | bytes 2211848 | tf_op jit(solution)/shard_map/ppermute | solution.py:70
  28.6 7.8 %modulate.1 = (bf16[288,5120]{1,0:T(8,128)(2,1)S(1)}, f32[288,640]{1,0:T(8,128)S(1)}) custom-call(s32[4]{0:T(128)S(1)} %pad_add_fusion.t_ref, bf16[288,1280]{1,0:T(8,128)(2,1)S(1)} %get-tuple-element.46.h0, bf16[288,1280]{1,0:T(8,128)(2,1)S(1)} %collective-permute-done.5.h1, bf16[288,1280]{1,0:T(8,128)(2,1)S(1)} %collective-permute-done.6.h2, ...), custom_call_target="tpu_custom_call" | custom-call | flops 1000 | bytes 30000000 | tf_op jit(solution)/shard_map/modulate/pallas_call | solution.py:275
  36.4 2.4 %fusion.k_ref = f32[288,640]{1,0:T(8,128)S(1)} fusion(bf16[288,5120]{1,0:T(8,128)(2,1)S(1)} %get-tuple-element.51, bf16[5120,640]{1,0:T(8,128)(2,1)S(1)} %copy-done.11), kind=kOutput, calls=%fused_computation.2 | convolution fusion | flops 1887436800 | bytes 10240000 | tf_op jit(solution)/shard_map/dot_general | solution.py:666
  38.9 1.2 %collective-permute-start.8 = (bf16[2,2,720,128]{3,2,1,0:T(8,128)(2,1)S(1)}, bf16[2,2,720,128]{3,2,1,0:T(8,128)(2,1)S(1)}, u32[]{:S(2)}, u32[]{:S(2)}) collective-permute-start(bf16[2,2,720,128]{3,2,1,0:T(8,128)(2,1)S(1)} %collective-permute-done.3.refs_5_), channel_id=1, source_target_pairs={{0,24},{1,97},{2,26},{3,99},{4,28},{5,101},{6,30},{7,103},{8,16},{... | collective-permute-start | bytes 2211848 | tf_op jit(solution)/shard_map/ppermute | solution.py:70
  40.1 0.2 sum_squares.1.s0
  40.4 0.1 collective-permute-start.11
  40.5 1.8 %collective-permute-start.12 = (f32[8,384]{1,0:T(8,128)S(1)}, f32[8,384]{1,0:T(8,128)S(1)}, u32[]{:S(2)}, u32[]{:S(2)}) collective-permute-start(f32[8,384]{1,0:T(8,128)S(1)} %sum_squares.1.s0), channel_id=1, source_target_pairs={{0,1},{1,0},{2,3},{3,2},{4,5},{5,4},{6,7},{7,6},{8,9},{33,32},{10,... | collective-permute-start | bytes 36872 | tf_op jit(solution)/shard_map/ppermute | solution.py:70
  42.3 2.4 %convolution_convert_fusion.v_ref = bf16[288,640]{1,0:T(8,128)(2,1)S(1)} fusion(bf16[288,5120]{1,0:T(8,128)(2,1)S(1)} %get-tuple-element.51, bf16[5120,640]{1,0:T(8,128)(2,1)S(1)} %bitcast.18), kind=kOutput, calls=%fused_computation | convolution fusion | flops 1887621120 | bytes 9871360 | tf_op jit(solution)/shard_map/dot_general | solution.py:669
  44.8 1.5 %collective-permute-start.16 = (bf16[2,2,720,128]{3,2,1,0:T(8,128)(2,1)S(1)}, bf16[2,2,720,128]{3,2,1,0:T(8,128)(2,1)S(1)}, u32[]{:S(2)}, u32[]{:S(2)}) collective-permute-start(bf16[2,2,720,128]{3,2,1,0:T(8,128)(2,1)S(1)} %collective-permute-done.9.refs_8_), channel_id=1, source_target_pairs={{0,8},{1,33},{2,10},{3,35},{4,12},{5,37},{6,14},{7,39},{8,0},{33,1... | collective-permute-start | bytes 2211848 | tf_op jit(solution)/shard_map/ppermute | solution.py:70
  46.3 1.0 %collective-permute-start.17 = (bf16[2,2,720,128]{3,2,1,0:T(8,128)(2,1)S(1)}, bf16[2,2,720,128]{3,2,1,0:T(8,128)(2,1)S(1)}, u32[]{:S(2)}, u32[]{:S(2)}) collective-permute-start(bf16[2,2,720,128]{3,2,1,0:T(8,128)(2,1)S(1)} %collective-permute-done.9.refs_8_), channel_id=1, source_target_pairs={{0,24},{1,97},{2,26},{3,99},{4,28},{5,101},{6,30},{7,103},{8,16},{... | collective-permute-start | bytes 2211848 | tf_op jit(solution)/shard_map/ppermute | solution.py:70
  47.4 1.8 %norm_rope.1 = (bf16[288,640]{1,0:T(8,128)(2,1)}, bf16[2,2,144,128]{3,2,1,0:T(8,128)(2,1)S(1)}, bf16[2,2,144,128]{3,2,1,0:T(8,128)(2,1)S(1)}, bf16[2,2,144,128]{...) custom-call(s32[1]{0:T(128)} %bitcast.u_ref, f32[288,640]{1,0:T(8,128)S(1)} %get-tuple-element.53.q_ref, ...), custom_call_target="tpu_custom_call" | custom-call | flops 1000 | bytes 1000 | tf_op jit(solution)/shard_map/norm_rope/pallas_call | solution.py:348
  49.2 2.5 %collective-permute-done.8.refs_7_ = bf16[2,2,720,128]{3,2,1,0:T(8,128)(2,1)S(1)} collective-permute-done((bf16[2,2,720,128]{3,2,1,0:T(8,128)(2,1)S(1)}, bf16[2,2,720,128]{3,2,1,0:T(8,128)(2,1)S(1)}, u32[]{:S(2)}, u32[]{:S(2)}) %collective-permute-start.8) | collective-permute-done | bytes 737312 | tf_op jit(solution)/shard_map/ppermute | solution.py:70
  51.7 0.9 %collective-permute-start.18 = (bf16[2,2,720,128]{3,2,1,0:T(8,128)(2,1)S(1)}, bf16[2,2,720,128]{3,2,1,0:T(8,128)(2,1)S(1)}, u32[]{:S(2)}, u32[]{:S(2)}) collective-permute-start(bf16[2,2,720,128]{3,2,1,0:T(8,128)(2,1)S(1)} %collective-permute-done.8.refs_7_), channel_id=1, source_target_pairs={{0,4},{1,5},{2,6},{3,7},{4,0},{5,1},{6,2},{7,3},{8,12},{33,37},{10... | collective-permute-start | bytes 2211848 | tf_op jit(solution)/shard_map/ppermute | solution.py:70
  52.6 1.2 %collective-permute-start.13 = (bf16[2,2,144,128]{3,2,1,0:T(8,128)(2,1)S(1)}, bf16[2,2,144,128]{3,2,1,0:T(8,128)(2,1)S(1)}, u32[]{:S(2)}, u32[]{:S(2)}) collective-permute-start(bf16[2,2,144,128]{3,2,1,0:T(8,128)(2,1)S(1)} %get-tuple-element.67.refs_3_), channel_id=1, source_target_pairs={{0,96},{1,25},{2,98},{3,27},{4,100},{5,29},{6,102},{7,31},{8,104},... | collective-permute-start | bytes 442376 | tf_op jit(solution)/shard_map/ppermute | solution.py:70
  53.8 0.7 collective-permute-start.14
  54.4 3.3 %collective-permute-done.13.refs_1_ = bf16[2,2,144,128]{3,2,1,0:T(8,128)(2,1)S(1)} collective-permute-done((bf16[2,2,144,128]{3,2,1,0:T(8,128)(2,1)S(1)}, bf16[2,2,144,128]{3,2,1,0:T(8,128)(2,1)S(1)}, u32[]{:S(2)}, u32[]{:S(2)}) %collective-permute-start.13) | collective-permute-done | bytes 147488 | tf_op jit(solution)/shard_map/ppermute | solution.py:70
  57.7 1.0 %collective-permute-start.15 = (bf16[2,2,144,128]{3,2,1,0:T(8,128)(2,1)S(1)}, bf16[2,2,144,128]{3,2,1,0:T(8,128)(2,1)S(1)}, u32[]{:S(2)}, u32[]{:S(2)}) collective-permute-start(bf16[2,2,144,128]{3,2,1,0:T(8,128)(2,1)S(1)} %get-tuple-element.65.refs_1_), channel_id=1, source_target_pairs={{0,32},{1,9},{2,34},{3,11},{4,36},{5,13},{6,38},{7,15},{8,40},{33,... | collective-permute-start | bytes 442376 | tf_op jit(solution)/shard_map/ppermute | solution.py:70
  58.7 1.0 %copy-done.4 = bf16[288,640]{1,0:T(8,128)(2,1)S(1)} copy-done((bf16[288,640]{1,0:T(8,128)(2,1)S(1)}, bf16[288,640]{1,0:T(8,128)(2,1)}, u32[]{:S(2)}) %copy-start.4) | copy-done | bytes 368664
  59.7 1.0 %fresh_attention.1 = (f32[2,5,144,128]{3,2,1,0:T(8,128)S(1)}, f32[24,128]{1,0:T(8,128)S(1)}) custom-call(s32[1]{0:T(128)} %bitcast.u_ref, bf16[288,640]{1,0:T(8,128)(2,1)S(1)} %copy-done.4, bf16[288,640]{1,0:T(8,128)(2,1)S(1)} %convolution_convert_fusion.v_ref, bf16[2,2,144,128]{3,2,1,0:T(8,128)(2,1)S(1)} %get-tuple-element.64.refs_0_, ...), custom_call_target="tpu_custom_call" | custom-call | flops 1000 | bytes 1000 | tf_op jit(solution)/shard_map/fresh_attention/pallas_call | solution.py:398
  60.7 3.3 %collective-permute-done.15.refs_3_ = bf16[2,2,144,128]{3,2,1,0:T(8,128)(2,1)S(1)} collective-permute-done((bf16[2,2,144,128]{3,2,1,0:T(8,128)(2,1)S(1)}, bf16[2,2,144,128]{3,2,1,0:T(8,128)(2,1)S(1)}, u32[]{:S(2)}, u32[]{:S(2)}) %collective-permute-start.15) | collective-permute-done | bytes 147488 | tf_op jit(solution)/shard_map/ppermute | solution.py:70
  64.1 6.7 %near_attention.1 = (f32[2,4,2,144,128]{4,3,2,1,0:T(8,128)S(1)}, f32[2,4,2,144,128]{4,3,2,1,0:T(8,128)S(1)}) custom-call(bf16[2,2,144,128]{3,2,1,0:T(8,128)(2,1)S(1)} %get-tuple-element.64.refs_0_, bf16[2,2,144,128]{3,2,1,0:T(8,128)(2,1)S(1)} %collective-permute-done.13.refs_1_, bf16[2,2,144,128]{3,2,1,0:T(8,128)(2,1)S(1)} %collective-permute-done.14.refs_2_, ...), custom_call_target="tpu_custom_call" | custom-call | flops 1000 | bytes 1000 | tf_op jit(solution)/shard_map/near_attention/pallas_call | solution.py:556
  70.7 4.8 %far_attention.1 = (bf16[2,304,128]{2,1,0:T(8,128)(2,1)S(1)}, bf16[2,304,128]{2,1,0:T(8,128)(2,1)S(1)}, bf16[2,304,128]{2,1,0:T(8,128)(2,1)S(1)}, bf16[2,304,128]{2,1,0:T(8,128)(2,1)S(1)}) custom-call(bf16[2,2,144,128]{3,2,1,0:T(8,128)(2,1)S(1)} %get-tuple-element.64.refs_0_, bf16[2,2,144,128]{3,2,1,0:T(8,128)(2,1)S(1)} %collective-permute-done.13.refs_1_, ...), custom_call_target="tpu_custom_call" | custom-call | flops 1000 | bytes 1000 | tf_op jit(solution)/shard_map/far_attention/pallas_call | solution.py:556
  75.5 1.3 %collective-permute-start.19 = (bf16[2,304,128]{2,1,0:T(8,128)(2,1)S(1)}, bf16[2,304,128]{2,1,0:T(8,128)(2,1)S(1)}, u32[]{:S(2)}, u32[]{:S(2)}) collective-permute-start(bf16[2,304,128]{2,1,0:T(8,128)(2,1)S(1)} %get-tuple-element.76), channel_id=1, source_target_pairs={{0,96},{1,25},{2,98},{3,27},{4,100},{5,29},{6,102},{7,31},{8,104},... | collective-permute-start | bytes 466952 | tf_op jit(solution)/shard_map/ppermute | solution.py:70
  76.8 0.6 collective-permute-start.20
  77.5 0.3 collective-permute-start.21
  77.8 3.1 %collective-permute-done.19.refs_1_ = bf16[2,304,128]{2,1,0:T(8,128)(2,1)S(1)} collective-permute-done((bf16[2,304,128]{2,1,0:T(8,128)(2,1)S(1)}, bf16[2,304,128]{2,1,0:T(8,128)(2,1)S(1)}, u32[]{:S(2)}, u32[]{:S(2)}) %collective-permute-start.19) | collective-permute-done | bytes 155680 | tf_op jit(solution)/shard_map/ppermute | solution.py:70
  80.8 2.8 %collective-permute-done.20.refs_2_ = bf16[2,304,128]{2,1,0:T(8,128)(2,1)S(1)} collective-permute-done((bf16[2,304,128]{2,1,0:T(8,128)(2,1)S(1)}, bf16[2,304,128]{2,1,0:T(8,128)(2,1)S(1)}, u32[]{:S(2)}, u32[]{:S(2)}) %collective-permute-start.20) | collective-permute-done | bytes 155680 | tf_op jit(solution)/shard_map/ppermute | solution.py:70
  83.7 1.6 %collective-permute-done.21.refs_3_ = bf16[2,304,128]{2,1,0:T(8,128)(2,1)S(1)} collective-permute-done((bf16[2,304,128]{2,1,0:T(8,128)(2,1)S(1)}, bf16[2,304,128]{2,1,0:T(8,128)(2,1)S(1)}, u32[]{:S(2)}, u32[]{:S(2)}) %collective-permute-start.21) | collective-permute-done | bytes 155680 | tf_op jit(solution)/shard_map/ppermute | solution.py:70
  85.2 1.5 %merge.1 = bf16[2,144,640]{2,1,0:T(8,128)(2,1)} custom-call(s32[1]{0:T(128)} %bitcast.u_ref, f32[2,5,144,128]{3,2,1,0:T(8,128)S(1)} %get-tuple-element.68.fresh_out, f32[24,128]{1,0:T(8,128)S(1)} %get-tuple-element.69.refs_9_.fresh_rows, bf16[2,304,128]{2,1,0:T(8,128)(2,1)S(1)} %get-tuple-element.75.refs_0_, ...), custom_call_target="tpu_custom_call" | custom-call | flops 1843200 | bytes 2580480 | tf_op jit(solution)/shard_map/merge/pallas_call | solution.py:620
  (38 shorter events, 0.3 us)
Async XLA Ops:
  0.6 20.5 %collective-permute-start.6 = (bf16[288,1280]{1,0:T(8,128)(2,1)}, bf16[288,1280]{1,0:T(8,128)(2,1)S(1)}, u32[]{:S(2)}, u32[]{:S(2)}) collective-permute-start(bf16[288,1280]{1,0:T(8,128)(2,1)} %bitcast.12), channel_id=1, source_target_pairs={{0,2},{1,3},{2,0},{3,1},{4,6},{5,7},{6,4},{7,5},{8,10},{33,35},{10... | collective-permute-start | bytes 2211848 | tf_op jit(solution)/shard_map/ppermute | solution.py:70
  2.7 1.0 %copy-start.1 = (bf16[2,144,640]{2,1,0:T(8,128)(2,1)S(1)}, bf16[2,144,640]{2,1,0:T(8,128)(2,1)}, u32[]{:S(2)}) copy-start(bf16[2,144,640]{2,1,0:T(8,128)(2,1)} %key_ref.1) | copy-start | bytes 1105924
  3.7 1.0 %copy-start.2 = (bf16[2,144,640]{2,1,0:T(8,128)(2,1)S(1)}, bf16[2,144,640]{2,1,0:T(8,128)(2,1)}, u32[]{:S(2)}) copy-start(bf16[2,144,640]{2,1,0:T(8,128)(2,1)} %value_ref.1) | copy-start | bytes 1105924
  4.8 7.4 %collective-permute-start = (bf16[2,2,144,128]{3,2,1,0:T(8,128)(2,1)S(1)}, bf16[2,2,144,128]{3,2,1,0:T(8,128)(2,1)S(1)}, u32[]{:S(2)}, u32[]{:S(2)}) collective-permute-start(bf16[2,2,144,128]{3,2,1,0:T(8,128)(2,1)S(1)} %get-tuple-element.42), channel_id=1, source_target_pairs={{0,96},{1,25},{2,98},{3,27},{4,100},{5,29},{6,102},{7,31},{8,104},... | collective-permute-start | bytes 442376 | tf_op jit(solution)/shard_map/ppermute | solution.py:70
  7.9 6.8 %collective-permute-start.1 = (bf16[2,2,144,128]{3,2,1,0:T(8,128)(2,1)S(1)}, bf16[2,2,144,128]{3,2,1,0:T(8,128)(2,1)S(1)}, u32[]{:S(2)}, u32[]{:S(2)}) collective-permute-start(bf16[2,2,144,128]{3,2,1,0:T(8,128)(2,1)S(1)} %get-tuple-element.43), channel_id=1, source_target_pairs={{0,64},{1,17},{2,66},{3,19},{4,68},{5,21},{6,70},{7,23},{8,72},{33... | collective-permute-start | bytes 442376 | tf_op jit(solution)/shard_map/ppermute | solution.py:70
  8.5 7.6 %collective-permute-start.2 = (bf16[2,2,144,128]{3,2,1,0:T(8,128)(2,1)S(1)}, bf16[2,2,144,128]{3,2,1,0:T(8,128)(2,1)S(1)}, u32[]{:S(2)}, u32[]{:S(2)}) collective-permute-start(bf16[2,2,144,128]{3,2,1,0:T(8,128)(2,1)S(1)} %get-tuple-element.44), channel_id=1, source_target_pairs={{0,32},{1,9},{2,34},{3,11},{4,36},{5,13},{6,38},{7,15},{8,40},{33,... | collective-permute-start | bytes 442376 | tf_op jit(solution)/shard_map/ppermute | solution.py:70
  9.5 19.1 %collective-permute-start.5 = (bf16[288,1280]{1,0:T(8,128)(2,1)}, bf16[288,1280]{1,0:T(8,128)(2,1)S(1)}, u32[]{:S(2)}, u32[]{:S(2)}) collective-permute-start(bf16[288,1280]{1,0:T(8,128)(2,1)} %bitcast.13), channel_id=1, source_target_pairs={{0,1},{1,0},{2,3},{3,2},{4,5},{5,4},{6,7},{7,6},{8,9},{33,32},{10,... | collective-permute-start | bytes 2211848 | tf_op jit(solution)/shard_map/ppermute | solution.py:70
  16.2 1.1 %copy-start = (bf16[2,144,1280]{2,1,0:T(8,128)(2,1)S(1)}, bf16[2,144,1280]{2,1,0:T(8,128)(2,1)}, u32[]{:S(2)}) copy-start(bf16[2,144,1280]{2,1,0:T(8,128)(2,1)} %param.12) | copy-start | bytes 2211844
  17.3 0.8 copy-start.5
  18.1 0.8 copy-start.6
  18.9 0.7 copy-start.9
  19.5 0.7 copy-start.10
  21.2 7.5 %collective-permute-start.7 = (bf16[288,1280]{1,0:T(8,128)(2,1)S(1)}, bf16[288,1280]{1,0:T(8,128)(2,1)}, u32[]{:S(2)}, u32[]{:S(2)}) collective-permute-start(bf16[288,1280]{1,0:T(8,128)(2,1)S(1)} %collective-permute-done.6.h2), channel_id=1, source_target_pairs={{0,1},{1,0},{2,3},{3,2},{4,5},{5,4},{6,7},{7,6},{8,9},{33,32},{10,... | collective-permute-start | bytes 2211848 | tf_op jit(solution)/shard_map/ppermute | solution.py:70
  21.3 15.2 %copy-start.11 = (bf16[5120,640]{1,0:T(8,128)(2,1)S(1)}, bf16[5120,640]{1,0:T(8,128)(2,1)}, u32[]{:S(2)}) copy-start(bf16[5120,640]{1,0:T(8,128)(2,1)} %param.16) | copy-start | bytes 19660804
  21.3 17.6 %collective-permute-start.3 = (bf16[2,2,720,128]{3,2,1,0:T(8,128)(2,1)S(1)}, bf16[2,2,720,128]{3,2,1,0:T(8,128)(2,1)S(1)}, u32[]{:S(2)}, u32[]{:S(2)}) collective-permute-start(bf16[2,2,720,128]{3,2,1,0:T(8,128)(2,1)S(1)} %assemble.1.after.refs_4_), channel_id=1, source_target_pairs={{0,8},{1,33},{2,10},{3,35},{4,12},{5,37},{6,14},{7,39},{8,0},{33,1... | collective-permute-start | bytes 2211848 | tf_op jit(solution)/shard_map/ppermute | solution.py:70
  22.8 16.1 %collective-permute-start.4 = (bf16[2,2,720,128]{3,2,1,0:T(8,128)(2,1)S(1)}, bf16[2,2,720,128]{3,2,1,0:T(8,128)(2,1)S(1)}, u32[]{:S(2)}, u32[]{:S(2)}) collective-permute-start(bf16[2,2,720,128]{3,2,1,0:T(8,128)(2,1)S(1)} %assemble.1.after.refs_4_), channel_id=1, source_target_pairs={{0,24},{1,97},{2,26},{3,99},{4,28},{5,101},{6,30},{7,103},{8,16},{... | collective-permute-start | bytes 2211848 | tf_op jit(solution)/shard_map/ppermute | solution.py:70
  25.0 19.7 %collective-permute-start.9 = (bf16[2,2,720,128]{3,2,1,0:T(8,128)(2,1)S(1)}, bf16[2,2,720,128]{3,2,1,0:T(8,128)(2,1)S(1)}, u32[]{:S(2)}, u32[]{:S(2)}) collective-permute-start(bf16[2,2,720,128]{3,2,1,0:T(8,128)(2,1)S(1)} %assemble.1.after.refs_4_), channel_id=1, source_target_pairs={{0,4},{1,5},{2,6},{3,7},{4,0},{5,1},{6,2},{7,3},{8,12},{33,37},{10... | collective-permute-start | bytes 2211848 | tf_op jit(solution)/shard_map/ppermute | solution.py:70
  28.6 13.6 %slice-start = ((s8[6553600]{0:T(1024)(128)(4,1)}), s8[2359296]{0:T(1024)(128)(4,1)S(1)}, s32[]{:S(2)}) async-start(s8[6553600]{0:T(1024)(128)(4,1)} %bitcast.17), calls=%async_computation | async-start | bytes 4718592
  36.4 5.8 %slice-start.1 = ((s8[6553600]{0:T(1024)(128)(4,1)}), s8[4194304]{0:T(1024)(128)(4,1)S(1)}, s32[]{:S(2)}) async-start(s8[6553600]{0:T(1024)(128)(4,1)} %bitcast.17), calls=%async_computation.1 | async-start | bytes 8388608
  38.9 12.8 %collective-permute-start.8 = (bf16[2,2,720,128]{3,2,1,0:T(8,128)(2,1)S(1)}, bf16[2,2,720,128]{3,2,1,0:T(8,128)(2,1)S(1)}, u32[]{:S(2)}, u32[]{:S(2)}) collective-permute-start(bf16[2,2,720,128]{3,2,1,0:T(8,128)(2,1)S(1)} %collective-permute-done.3.refs_5_), channel_id=1, source_target_pairs={{0,24},{1,97},{2,26},{3,99},{4,28},{5,101},{6,30},{7,103},{8,16},{... | collective-permute-start | bytes 2211848 | tf_op jit(solution)/shard_map/ppermute | solution.py:70
  40.3 7.0 %copy-start.7 = (f32[640]{0:T(1024)S(1)}, f32[640]{0:T(1024)}, u32[]{:S(2)}) copy-start(f32[640]{0:T(1024)} %qg.1) | copy-start | bytes 7684
  40.4 7.0 %copy-start.8 = (f32[640]{0:T(1024)S(1)}, f32[640]{0:T(1024)}, u32[]{:S(2)}) copy-start(f32[640]{0:T(1024)} %kg.1) | copy-start | bytes 7684
  40.4 4.4 %collective-permute-start.10 = (f32[8,384]{1,0:T(8,128)S(1)}, f32[8,384]{1,0:T(8,128)S(1)}, u32[]{:S(2)}, u32[]{:S(2)}) collective-permute-start(f32[8,384]{1,0:T(8,128)S(1)} %sum_squares.1.s0), channel_id=1, source_target_pairs={{0,3},{1,2},{2,1},{3,0},{4,7},{5,6},{6,5},{7,4},{8,11},{33,34},{10... | collective-permute-start | bytes 36872 | tf_op jit(solution)/shard_map/ppermute | solution.py:70
  40.4 4.4 %collective-permute-start.11 = (f32[8,384]{1,0:T(8,128)S(1)}, f32[8,384]{1,0:T(8,128)S(1)}, u32[]{:S(2)}, u32[]{:S(2)}) collective-permute-start(f32[8,384]{1,0:T(8,128)S(1)} %sum_squares.1.s0), channel_id=1, source_target_pairs={{0,2},{1,3},{2,0},{3,1},{4,6},{5,7},{6,4},{7,5},{8,10},{33,35},{10... | collective-permute-start | bytes 36872 | tf_op jit(solution)/shard_map/ppermute | solution.py:70
  40.5 4.3 %collective-permute-start.12 = (f32[8,384]{1,0:T(8,128)S(1)}, f32[8,384]{1,0:T(8,128)S(1)}, u32[]{:S(2)}, u32[]{:S(2)}) collective-permute-start(f32[8,384]{1,0:T(8,128)S(1)} %sum_squares.1.s0), channel_id=1, source_target_pairs={{0,1},{1,0},{2,3},{3,2},{4,5},{5,4},{6,7},{7,6},{8,9},{33,32},{10,... | collective-permute-start | bytes 36872 | tf_op jit(solution)/shard_map/ppermute | solution.py:70
  44.7 42.0 %copy-start.3 = (bf16[288,640]{1,0:T(8,128)(2,1)}, bf16[288,640]{1,0:T(8,128)(2,1)S(1)}, u32[]{:S(2)}) copy-start(bf16[288,640]{1,0:T(8,128)(2,1)S(1)} %convolution_convert_fusion.v_ref) | copy-start | bytes 1105924
  44.8 25.9 %collective-permute-start.16 = (bf16[2,2,720,128]{3,2,1,0:T(8,128)(2,1)S(1)}, bf16[2,2,720,128]{3,2,1,0:T(8,128)(2,1)S(1)}, u32[]{:S(2)}, u32[]{:S(2)}) collective-permute-start(bf16[2,2,720,128]{3,2,1,0:T(8,128)(2,1)S(1)} %collective-permute-done.9.refs_8_), channel_id=1, source_target_pairs={{0,8},{1,33},{2,10},{3,35},{4,12},{5,37},{6,14},{7,39},{8,0},{33,1... | collective-permute-start | bytes 2211848 | tf_op jit(solution)/shard_map/ppermute | solution.py:70
  46.3 24.4 %collective-permute-start.17 = (bf16[2,2,720,128]{3,2,1,0:T(8,128)(2,1)S(1)}, bf16[2,2,720,128]{3,2,1,0:T(8,128)(2,1)S(1)}, u32[]{:S(2)}, u32[]{:S(2)}) collective-permute-start(bf16[2,2,720,128]{3,2,1,0:T(8,128)(2,1)S(1)} %collective-permute-done.9.refs_8_), channel_id=1, source_target_pairs={{0,24},{1,97},{2,26},{3,99},{4,28},{5,101},{6,30},{7,103},{8,16},{... | collective-permute-start | bytes 2211848 | tf_op jit(solution)/shard_map/ppermute | solution.py:70
  51.7 19.1 %collective-permute-start.18 = (bf16[2,2,720,128]{3,2,1,0:T(8,128)(2,1)S(1)}, bf16[2,2,720,128]{3,2,1,0:T(8,128)(2,1)S(1)}, u32[]{:S(2)}, u32[]{:S(2)}) collective-permute-start(bf16[2,2,720,128]{3,2,1,0:T(8,128)(2,1)S(1)} %collective-permute-done.8.refs_7_), channel_id=1, source_target_pairs={{0,4},{1,5},{2,6},{3,7},{4,0},{5,1},{6,2},{7,3},{8,12},{33,37},{10... | collective-permute-start | bytes 2211848 | tf_op jit(solution)/shard_map/ppermute | solution.py:70
  52.6 5.1 %collective-permute-start.13 = (bf16[2,2,144,128]{3,2,1,0:T(8,128)(2,1)S(1)}, bf16[2,2,144,128]{3,2,1,0:T(8,128)(2,1)S(1)}, u32[]{:S(2)}, u32[]{:S(2)}) collective-permute-start(bf16[2,2,144,128]{3,2,1,0:T(8,128)(2,1)S(1)} %get-tuple-element.67.refs_3_), channel_id=1, source_target_pairs={{0,96},{1,25},{2,98},{3,27},{4,100},{5,29},{6,102},{7,31},{8,104},... | collective-permute-start | bytes 442376 | tf_op jit(solution)/shard_map/ppermute | solution.py:70
  53.8 7.0 %collective-permute-start.14 = (bf16[2,2,144,128]{3,2,1,0:T(8,128)(2,1)S(1)}, bf16[2,2,144,128]{3,2,1,0:T(8,128)(2,1)S(1)}, u32[]{:S(2)}, u32[]{:S(2)}) collective-permute-start(bf16[2,2,144,128]{3,2,1,0:T(8,128)(2,1)S(1)} %get-tuple-element.66.refs_2_), channel_id=1, source_target_pairs={{0,64},{1,17},{2,66},{3,19},{4,68},{5,21},{6,70},{7,23},{8,72},{33... | collective-permute-start | bytes 442376 | tf_op jit(solution)/shard_map/ppermute | solution.py:70
  57.7 6.4 %collective-permute-start.15 = (bf16[2,2,144,128]{3,2,1,0:T(8,128)(2,1)S(1)}, bf16[2,2,144,128]{3,2,1,0:T(8,128)(2,1)S(1)}, u32[]{:S(2)}, u32[]{:S(2)}) collective-permute-start(bf16[2,2,144,128]{3,2,1,0:T(8,128)(2,1)S(1)} %get-tuple-element.65.refs_1_), channel_id=1, source_target_pairs={{0,32},{1,9},{2,34},{3,11},{4,36},{5,13},{6,38},{7,15},{8,40},{33,... | collective-permute-start | bytes 442376 | tf_op jit(solution)/shard_map/ppermute | solution.py:70
  58.7 1.0 %copy-start.4 = (bf16[288,640]{1,0:T(8,128)(2,1)S(1)}, bf16[288,640]{1,0:T(8,128)(2,1)}, u32[]{:S(2)}) copy-start(bf16[288,640]{1,0:T(8,128)(2,1)} %get-tuple-element.62.k_ref) | copy-start | bytes 1105924
  75.5 5.3 %collective-permute-start.19 = (bf16[2,304,128]{2,1,0:T(8,128)(2,1)S(1)}, bf16[2,304,128]{2,1,0:T(8,128)(2,1)S(1)}, u32[]{:S(2)}, u32[]{:S(2)}) collective-permute-start(bf16[2,304,128]{2,1,0:T(8,128)(2,1)S(1)} %get-tuple-element.76), channel_id=1, source_target_pairs={{0,96},{1,25},{2,98},{3,27},{4,100},{5,29},{6,102},{7,31},{8,104},... | collective-permute-start | bytes 466952 | tf_op jit(solution)/shard_map/ppermute | solution.py:70
  76.8 6.8 %collective-permute-start.20 = (bf16[2,304,128]{2,1,0:T(8,128)(2,1)S(1)}, bf16[2,304,128]{2,1,0:T(8,128)(2,1)S(1)}, u32[]{:S(2)}, u32[]{:S(2)}) collective-permute-start(bf16[2,304,128]{2,1,0:T(8,128)(2,1)S(1)} %get-tuple-element.77), channel_id=1, source_target_pairs={{0,64},{1,17},{2,66},{3,19},{4,68},{5,21},{6,70},{7,23},{8,72},{33... | collective-permute-start | bytes 466952 | tf_op jit(solution)/shard_map/ppermute | solution.py:70
  77.5 7.8 %collective-permute-start.21 = (bf16[2,304,128]{2,1,0:T(8,128)(2,1)S(1)}, bf16[2,304,128]{2,1,0:T(8,128)(2,1)S(1)}, u32[]{:S(2)}, u32[]{:S(2)}) collective-permute-start(bf16[2,304,128]{2,1,0:T(8,128)(2,1)S(1)} %get-tuple-element.78), channel_id=1, source_target_pairs={{0,32},{1,9},{2,34},{3,11},{4,36},{5,13},{6,38},{7,15},{8,40},{33,... | collective-permute-start | bytes 466952 | tf_op jit(solution)/shard_map/ppermute | solution.py:70

commit v10 on v9

--- a/solution.py
+++ b/solution.py
@@ -34,7 +34,7 @@
 AXES = ("patch", "tp")
 GROUP = 16
 VMEM_MIB = 24
-ATTENTION_MIB = 34
+ATTENTION_MIB = 40
 MODULATE_MIB = 42
 
 
@@ -664,22 +664,23 @@
     blocks = jnp.stack([tp, tp ^ 1, tp ^ 2, tp ^ 3]).astype(jnp.int32)
     modded, query = modulate(blocks, [own_rows, core_rows, z_rows, cross_rows], cond, mod, w_query)
     key = jnp.dot(modded, w_key, preferred_element_type=F32)
-    near_one, near_three, key = lax.optimization_barrier((near_one, near_three, key))
-    near_two = swap_v(near_one, 3)
     fresh_values = jnp.dot(modded, w_value, preferred_element_type=F32).astype(BF16)
     own_sq = sum_squares(query, key)
+    near_one, near_three, own_sq = lax.optimization_barrier((near_one, near_three, own_sq))
+    near_two = swap_v(near_one, 3)
     squares = [own_sq] + [swap_tp(own_sq, z, c) for z, c in ((1, 1), (1, 0), (0, 1))]
-    far, fresh_values, *squares = lax.optimization_barrier((far, fresh_values, *squares))
+    fresh_values, *squares = lax.optimization_barrier((fresh_values, *squares))
+    fresh_keys, *sends = norm_rope(u, query, key, squares, q_gain, k_gain, cos, sin)
+    far, fresh_keys = lax.optimization_barrier((far, fresh_keys))
     far_one, far_three = swap_v(far, 1), swap_v(far, 3)
-    fresh_keys, *sends = norm_rope(u, query, key, squares, q_gain, k_gain, cos, sin)
-    near_two, fresh_keys = lax.optimization_barrier((near_two, fresh_keys))
-    far_two = swap_z_hi(near_two)
     queries = exchange_u(sends)
     fresh_out, fresh_rows = fresh_attention(u, fresh_keys, fresh_values, sends)
 
-    partial = stale_attention(queries, [near, near_one, near_three, near_two, far])
+    far_one, near_two, *queries = lax.optimization_barrier((far_one, near_two, *queries))
+    far_two = swap_v(far_one, 3)
+    partial = stale_attention(queries, [near, near_one, near_three, near_two, far, far_one])
     outs = stale_attention(
-        queries, [far_one, far_three, far_two], near=partial, after=fresh_rows
+        queries, [far_three, far_two], near=partial, after=fresh_rows
     )
     returned = exchange_u(outs)
     attended = merge(u, fresh_out, fresh_rows, returned)

time: 88.2 us -> 91.8 us (1.041); the launches traced: 86.8 us -> 91.3 us
  starting transfers between devices: 25.8 us -> 28.8 us
  waiting for transfers between devices: 23.2 us -> 24.8 us
    ppermute x22, starting transfers between devices: 25.8 us -> 28.8 us  [permute(): lax.ppermute(value, AXES, [(linear(*p), linear(*move(*p))) for p in place...]
    ppermute x22, waiting for transfers between devices: 23.2 us -> 24.8 us  [permute(): lax.ppermute(value, AXES, [(linear(*p), linear(*move(*p))) for p in place...]
  transfers between devices with their start and end apart: 22 -> 22, of which waited for: 10 -> 12; matrix products, arithmetic and copies ran while one was open for 6% -> 6% of each run, Pallas kernels for 21% -> 21%
where the time goes in v10:
time: 91.8 us; the launch traced here: 91.3 us
  starting transfers between devices  28.8 us (31%)
  Pallas kernels  24.8 us (27%)
  waiting for transfers between devices  24.8 us (27%)
  local copies, waits for them, and re-layouts  6.99 us (8%)
  matrix products  4.95 us (5%)
    ppermute x22, starting transfers between devices, permute(): lax.ppermute(value, AXES, [(linear(*p), linear(*move(*p))) for p in place...  28.8 us
    ppermute x22, waiting for transfers between devices, permute(): lax.ppermute(value, AXES, [(linear(*p), linear(*move(*p))) for p in place...  24.8 us
    pallas_call x2, Pallas kernels, stale_attention(): pl.pallas_call(functools.partial(stale_kernel, far, count), out_shape=out...  11.3 us
    pallas_call x1, Pallas kernels, modulate(): pl.pallas_call(modulate_kernel, out_shape=[jax.ShapeDtypeStruct((ROWS, D)...  7.77 us
    unnamed x28, local copies, waits for them, and re-layouts  6.99 us
    dot_general x1, matrix products, shards(): jnp.dot(modded, w_value, preferred_element_type=F32).astype(BF16)  2.48 us
    dot_general x1, matrix products, shards(): key = jnp.dot(modded, w_key, preferred_element_type=F32)  2.47 us
  transfers between devices with their start and end apart: 22, of which 12 were waited for; matrix products, arithmetic and copies ran while one was open for 6% of the time, Pallas kernels for 21%

profile of v10, /device:TPU:0, one launch (start us, length us, event | category | flops | bytes accessed | tf_op | source)
XLA Modules:
  0.0 91.3 jit_solution(11181566449705257717)
XLA Ops:
  0.6 2.1 %collective-permute-start.5 = (bf16[288,1280]{1,0:T(8,128)(2,1)}, bf16[288,1280]{1,0:T(8,128)(2,1)S(1)}, u32[]{:S(2)}, u32[]{:S(2)}) collective-permute-start(bf16[288,1280]{1,0:T(8,128)(2,1)} %bitcast.12), channel_id=1, source_target_pairs={{0,2},{1,3},{2,0},{3,1},{4,6},{5,7},{6,4},{7,5},{8,10},{33,35},{10... | collective-permute-start | bytes 2211848 | tf_op jit(solution)/shard_map/ppermute | solution.py:70
  2.7 1.0 %copy-done.1 = bf16[2,144,640]{2,1,0:T(8,128)(2,1)S(1)} copy-done((bf16[2,144,640]{2,1,0:T(8,128)(2,1)S(1)}, bf16[2,144,640]{2,1,0:T(8,128)(2,1)}, u32[]{:S(2)}) %copy-start.1) | copy-done | bytes 368664
  3.7 1.0 %copy-done.2 = bf16[2,144,640]{2,1,0:T(8,128)(2,1)S(1)} copy-done((bf16[2,144,640]{2,1,0:T(8,128)(2,1)S(1)}, bf16[2,144,640]{2,1,0:T(8,128)(2,1)}, u32[]{:S(2)}) %copy-start.2) | copy-done | bytes 368664
  4.7 0.1 pack_stale.1
  4.8 3.1 %collective-permute-start = (bf16[2,2,144,128]{3,2,1,0:T(8,128)(2,1)S(1)}, bf16[2,2,144,128]{3,2,1,0:T(8,128)(2,1)S(1)}, u32[]{:S(2)}, u32[]{:S(2)}) collective-permute-start(bf16[2,2,144,128]{3,2,1,0:T(8,128)(2,1)S(1)} %get-tuple-element.47), channel_id=1, source_target_pairs={{0,96},{1,25},{2,98},{3,27},{4,100},{5,29},{6,102},{7,31},{8,104},... | collective-permute-start | bytes 442376 | tf_op jit(solution)/shard_map/ppermute | solution.py:70
  7.9 0.6 collective-permute-start.1
  8.5 1.0 %collective-permute-start.2 = (bf16[2,2,144,128]{3,2,1,0:T(8,128)(2,1)S(1)}, bf16[2,2,144,128]{3,2,1,0:T(8,128)(2,1)S(1)}, u32[]{:S(2)}, u32[]{:S(2)}) collective-permute-start(bf16[2,2,144,128]{3,2,1,0:T(8,128)(2,1)S(1)} %get-tuple-element.49), channel_id=1, source_target_pairs={{0,32},{1,9},{2,34},{3,11},{4,36},{5,13},{6,38},{7,15},{8,40},{33,... | collective-permute-start | bytes 442376 | tf_op jit(solution)/shard_map/ppermute | solution.py:70
  9.5 2.7 %collective-permute-done.refs_1_ = bf16[2,2,144,128]{3,2,1,0:T(8,128)(2,1)S(1)} collective-permute-done((bf16[2,2,144,128]{3,2,1,0:T(8,128)(2,1)S(1)}, bf16[2,2,144,128]{3,2,1,0:T(8,128)(2,1)S(1)}, u32[]{:S(2)}, u32[]{:S(2)}) %collective-permute-start) | collective-permute-done | bytes 147488 | tf_op jit(solution)/shard_map/ppermute | solution.py:70
  12.2 2.5 %collective-permute-done.1.refs_2_ = bf16[2,2,144,128]{3,2,1,0:T(8,128)(2,1)S(1)} collective-permute-done((bf16[2,2,144,128]{3,2,1,0:T(8,128)(2,1)S(1)}, bf16[2,2,144,128]{3,2,1,0:T(8,128)(2,1)S(1)}, u32[]{:S(2)}, u32[]{:S(2)}) %collective-permute-start.1) | collective-permute-done | bytes 147488 | tf_op jit(solution)/shard_map/ppermute | solution.py:70
  14.7 1.5 %collective-permute-done.2.refs_3_ = bf16[2,2,144,128]{3,2,1,0:T(8,128)(2,1)S(1)} collective-permute-done((bf16[2,2,144,128]{3,2,1,0:T(8,128)(2,1)S(1)}, bf16[2,2,144,128]{3,2,1,0:T(8,128)(2,1)S(1)}, u32[]{:S(2)}, u32[]{:S(2)}) %collective-permute-start.2) | collective-permute-done | bytes 147488 | tf_op jit(solution)/shard_map/ppermute | solution.py:70
  16.2 1.1 %copy-done = bf16[2,144,1280]{2,1,0:T(8,128)(2,1)S(1)} copy-done((bf16[2,144,1280]{2,1,0:T(8,128)(2,1)S(1)}, bf16[2,144,1280]{2,1,0:T(8,128)(2,1)}, u32[]{:S(2)}) %copy-start) | copy-done | bytes 737304
  17.3 0.8 copy-done.5
  18.1 0.8 copy-done.6
  18.9 0.7 copy-done.9
  19.5 0.7 copy-done.10
  20.2 0.9 %tables.1 = (f32[288,128]{1,0:T(8,128)S(1)}, f32[144,128]{1,0:T(8,128)S(1)}, f32[144,128]{1,0:T(8,128)S(1)}, f32[4,5120]{1,0:T(4,128)S(1)}, bf16[288,1280]{1,0:T(8,128)(2,1)S(1)}) custom-call(s32[144]{0:T(256)S(1)} %copy-done.9, f32[1,128]{1,0:T(1,128)S(1)} %copy-done.10, bf16[288,1280]{1,0:T(8,128)(2,1)S(1)} %bitcast.14, f32[2,5120]{1,0:T(2,128)S(1)} %copy-done.5, ...), custom_call_target="tpu_custom_call" | custom-call | flops 1843200 | bytes 1000000 | tf_op jit(solution)/shard_map/tables/pallas_call | solution.py:177
  21.3 1.6 %collective-permute-start.7 = (bf16[2,2,720,128]{3,2,1,0:T(8,128)(2,1)S(1)}, bf16[2,2,720,128]{3,2,1,0:T(8,128)(2,1)S(1)}, u32[]{:S(2)}, u32[]{:S(2)}) collective-permute-start(bf16[2,2,720,128]{3,2,1,0:T(8,128)(2,1)S(1)} %assemble.1.after.refs_4_), channel_id=1, source_target_pairs={{0,8},{1,33},{2,10},{3,35},{4,12},{5,37},{6,14},{7,39},{8,0},{33,1... | collective-permute-start | bytes 2211848 | tf_op jit(solution)/shard_map/ppermute | solution.py:70
  22.8 2.1 %collective-permute-start.8 = (bf16[2,2,720,128]{3,2,1,0:T(8,128)(2,1)S(1)}, bf16[2,2,720,128]{3,2,1,0:T(8,128)(2,1)S(1)}, u32[]{:S(2)}, u32[]{:S(2)}) collective-permute-start(bf16[2,2,720,128]{3,2,1,0:T(8,128)(2,1)S(1)} %assemble.1.after.refs_4_), channel_id=1, source_target_pairs={{0,24},{1,97},{2,26},{3,99},{4,28},{5,101},{6,30},{7,103},{8,16},{... | collective-permute-start | bytes 2211848 | tf_op jit(solution)/shard_map/ppermute | solution.py:70
  25.0 3.6 %collective-permute-start.3 = (bf16[2,2,720,128]{3,2,1,0:T(8,128)(2,1)S(1)}, bf16[2,2,720,128]{3,2,1,0:T(8,128)(2,1)S(1)}, u32[]{:S(2)}, u32[]{:S(2)}) collective-permute-start(bf16[2,2,720,128]{3,2,1,0:T(8,128)(2,1)S(1)} %assemble.1.after.refs_4_), channel_id=1, source_target_pairs={{0,4},{1,5},{2,6},{3,7},{4,0},{5,1},{6,2},{7,3},{8,12},{33,37},{10... | collective-permute-start | bytes 2211848 | tf_op jit(solution)/shard_map/ppermute | solution.py:70
  28.6 7.8 %modulate.1 = (bf16[288,5120]{1,0:T(8,128)(2,1)S(1)}, f32[288,640]{1,0:T(8,128)S(1)}) custom-call(s32[4]{0:T(128)S(1)} %pad_add_fusion.t_ref, bf16[288,1280]{1,0:T(8,128)(2,1)S(1)} %get-tuple-element.51.h0, bf16[288,1280]{1,0:T(8,128)(2,1)S(1)} %collective-permute-done.4.h1, bf16[288,1280]{1,0:T(8,128)(2,1)S(1)} %collective-permute-done.5.h2, ...), custom_call_target="tpu_custom_call" | custom-call | flops 1000 | bytes 30000000 | tf_op jit(solution)/shard_map/modulate/pallas_call | solution.py:275
  36.4 2.5 %fusion.k_ref = f32[288,640]{1,0:T(8,128)S(1)} fusion(bf16[288,5120]{1,0:T(8,128)(2,1)S(1)} %get-tuple-element.57, bf16[5120,640]{1,0:T(8,128)(2,1)S(1)} %copy-done.11), kind=kOutput, calls=%fused_computation.2 | convolution fusion | flops 1887436800 | bytes 10240000 | tf_op jit(solution)/shard_map/dot_general | solution.py:666
  38.9 0.2 sum_squares.1.s0
  39.3 2.0 %collective-permute-start.9 = (f32[8,384]{1,0:T(8,128)S(1)}, f32[8,384]{1,0:T(8,128)S(1)}, u32[]{:S(2)}, u32[]{:S(2)}) collective-permute-start(f32[8,384]{1,0:T(8,128)S(1)} %sum_squares.1.s0), channel_id=1, source_target_pairs={{0,3},{1,2},{2,1},{3,0},{4,7},{5,6},{6,5},{7,4},{8,11},{33,34},{10... | collective-permute-start | bytes 36872 | tf_op jit(solution)/shard_map/ppermute | solution.py:70
  41.4 2.5 %convolution_convert_fusion.v_ref = bf16[288,640]{1,0:T(8,128)(2,1)S(1)} fusion(bf16[288,5120]{1,0:T(8,128)(2,1)S(1)} %get-tuple-element.57, bf16[5120,640]{1,0:T(8,128)(2,1)S(1)} %bitcast.18), kind=kOutput, calls=%fused_computation | convolution fusion | flops 1887621120 | bytes 9871360 | tf_op jit(solution)/shard_map/dot_general | solution.py:667
  43.9 1.2 %collective-permute-start.13 = (bf16[2,2,720,128]{3,2,1,0:T(8,128)(2,1)S(1)}, bf16[2,2,720,128]{3,2,1,0:T(8,128)(2,1)S(1)}, u32[]{:S(2)}, u32[]{:S(2)}) collective-permute-start(bf16[2,2,720,128]{3,2,1,0:T(8,128)(2,1)S(1)} %collective-permute-done.7.refs_5_), channel_id=1, source_target_pairs={{0,24},{1,97},{2,26},{3,99},{4,28},{5,101},{6,30},{7,103},{8,16},{... | collective-permute-start | bytes 2211848 | tf_op jit(solution)/shard_map/ppermute | solution.py:70
  45.2 1.8 %norm_rope.1 = (bf16[288,640]{1,0:T(8,128)(2,1)}, bf16[2,2,144,128]{3,2,1,0:T(8,128)(2,1)S(1)}, bf16[2,2,144,128]{3,2,1,0:T(8,128)(2,1)S(1)}, bf16[2,2,144,128]{...) custom-call(s32[1]{0:T(128)} %bitcast.u_ref, f32[288,640]{1,0:T(8,128)S(1)} %get-tuple-element.56.q_ref, ...), custom_call_target="tpu_custom_call" | custom-call | flops 1000 | bytes 1000 | tf_op jit(solution)/shard_map/norm_rope/pallas_call | solution.py:348
  47.0 1.1 %collective-permute-start.12 = (bf16[2,2,720,128]{3,2,1,0:T(8,128)(2,1)S(1)}, bf16[2,2,720,128]{3,2,1,0:T(8,128)(2,1)S(1)}, u32[]{:S(2)}, u32[]{:S(2)}) collective-permute-start(bf16[2,2,720,128]{3,2,1,0:T(8,128)(2,1)S(1)} %collective-permute-done.3.refs_8_), channel_id=1, source_target_pairs={{0,8},{1,33},{2,10},{3,35},{4,12},{5,37},{6,14},{7,39},{8,0},{33,1... | collective-permute-start | bytes 2211848 | tf_op jit(solution)/shard_map/ppermute | solution.py:70
  48.0 1.0 %collective-permute-start.14 = (bf16[2,2,144,128]{3,2,1,0:T(8,128)(2,1)S(1)}, bf16[2,2,144,128]{3,2,1,0:T(8,128)(2,1)S(1)}, u32[]{:S(2)}, u32[]{:S(2)}) collective-permute-start(bf16[2,2,144,128]{3,2,1,0:T(8,128)(2,1)S(1)} %get-tuple-element.71.refs_3_), channel_id=1, source_target_pairs={{0,96},{1,25},{2,98},{3,27},{4,100},{5,29},{6,102},{7,31},{8,104},... | collective-permute-start | bytes 442376 | tf_op jit(solution)/shard_map/ppermute | solution.py:70
  49.1 1.7 %collective-permute-start.15 = (bf16[2,2,144,128]{3,2,1,0:T(8,128)(2,1)S(1)}, bf16[2,2,144,128]{3,2,1,0:T(8,128)(2,1)S(1)}, u32[]{:S(2)}, u32[]{:S(2)}) collective-permute-start(bf16[2,2,144,128]{3,2,1,0:T(8,128)(2,1)S(1)} %get-tuple-element.70.refs_2_), channel_id=1, source_target_pairs={{0,64},{1,17},{2,66},{3,19},{4,68},{5,21},{6,70},{7,23},{8,72},{33... | collective-permute-start | bytes 442376 | tf_op jit(solution)/shard_map/ppermute | solution.py:70
  50.8 4.1 %collective-permute-done.14.refs_1_ = bf16[2,2,144,128]{3,2,1,0:T(8,128)(2,1)S(1)} collective-permute-done((bf16[2,2,144,128]{3,2,1,0:T(8,128)(2,1)S(1)}, bf16[2,2,144,128]{3,2,1,0:T(8,128)(2,1)S(1)}, u32[]{:S(2)}, u32[]{:S(2)}) %collective-permute-start.14) | collective-permute-done | bytes 147488 | tf_op jit(solution)/shard_map/ppermute | solution.py:70
  54.8 1.2 %collective-permute-start.17 = (bf16[2,2,720,128]{3,2,1,0:T(8,128)(2,1)S(1)}, bf16[2,2,720,128]{3,2,1,0:T(8,128)(2,1)S(1)}, u32[]{:S(2)}, u32[]{:S(2)}) collective-permute-start(bf16[2,2,720,128]{3,2,1,0:T(8,128)(2,1)S(1)} %collective-permute-done.3.refs_8_), channel_id=1, source_target_pairs={{0,24},{1,97},{2,26},{3,99},{4,28},{5,101},{6,30},{7,103},{8,16},{... | collective-permute-start | bytes 2211848 | tf_op jit(solution)/shard_map/ppermute | solution.py:70
  56.1 1.3 %collective-permute-done.15.refs_2_ = bf16[2,2,144,128]{3,2,1,0:T(8,128)(2,1)S(1)} collective-permute-done((bf16[2,2,144,128]{3,2,1,0:T(8,128)(2,1)S(1)}, bf16[2,2,144,128]{3,2,1,0:T(8,128)(2,1)S(1)}, u32[]{:S(2)}, u32[]{:S(2)}) %collective-permute-start.15) | collective-permute-done | bytes 147488 | tf_op jit(solution)/shard_map/ppermute | solution.py:70
  57.4 1.8 %collective-permute-done.16.refs_3_ = bf16[2,2,144,128]{3,2,1,0:T(8,128)(2,1)S(1)} collective-permute-done((bf16[2,2,144,128]{3,2,1,0:T(8,128)(2,1)S(1)}, bf16[2,2,144,128]{3,2,1,0:T(8,128)(2,1)S(1)}, u32[]{:S(2)}, u32[]{:S(2)}) %collective-permute-start.16) | collective-permute-done | bytes 147488 | tf_op jit(solution)/shard_map/ppermute | solution.py:70
  59.1 0.7 collective-permute-done.13.refs_7_
  59.8 0.9 collective-permute-done.12.refs_9_
  60.7 3.2 %collective-permute-start.18 = (bf16[2,2,720,128]{3,2,1,0:T(8,128)(2,1)S(1)}, bf16[2,2,720,128]{3,2,1,0:T(8,128)(2,1)S(1)}, u32[]{:S(2)}, u32[]{:S(2)}) collective-permute-start(bf16[2,2,720,128]{3,2,1,0:T(8,128)(2,1)S(1)} %collective-permute-done.12.refs_9_), channel_id=1, source_target_pairs={{0,24},{1,97},{2,26},{3,99},{4,28},{5,101},{6,30},{7,103},{8,16},{... | collective-permute-start | bytes 2211848 | tf_op jit(solution)/shard_map/ppermute | solution.py:70
  63.9 1.0 %copy-done.4 = bf16[288,640]{1,0:T(8,128)(2,1)S(1)} copy-done((bf16[288,640]{1,0:T(8,128)(2,1)S(1)}, bf16[288,640]{1,0:T(8,128)(2,1)}, u32[]{:S(2)}) %copy-start.4) | copy-done | bytes 368664
  64.8 1.0 %fresh_attention.1 = (f32[2,5,144,128]{3,2,1,0:T(8,128)S(1)}, f32[24,128]{1,0:T(8,128)S(1)}) custom-call(s32[1]{0:T(128)} %bitcast.u_ref, bf16[288,640]{1,0:T(8,128)(2,1)S(1)} %copy-done.4, bf16[288,640]{1,0:T(8,128)(2,1)S(1)} %convolution_convert_fusion.v_ref, bf16[2,2,144,128]{3,2,1,0:T(8,128)(2,1)S(1)} %get-tuple-element.76.refs_0_, ...), custom_call_target="tpu_custom_call" | custom-call | flops 1000 | bytes 1000 | tf_op jit(solution)/shard_map/fresh_attention/pallas_call | solution.py:398
  65.9 7.6 %near_attention.1 = (f32[2,4,2,144,128]{4,3,2,1,0:T(8,128)S(1)}, f32[2,4,2,144,128]{4,3,2,1,0:T(8,128)S(1)}) custom-call(bf16[2,2,144,128]{3,2,1,0:T(8,128)(2,1)S(1)} %get-tuple-element.76.refs_0_, bf16[2,2,144,128]{3,2,1,0:T(8,128)(2,1)S(1)} %collective-permute-done.14.refs_1_, bf16[2,2,144,128]{3,2,1,0:T(8,128)(2,1)S(1)} %collective-permute-done.15.refs_2_, ...), custom_call_target="tpu_custom_call" | custom-call | flops 1000 | bytes 1000 | tf_op jit(solution)/shard_map/near_attention/pallas_call | solution.py:556
  73.5 2.1 %collective-permute-done.18.refs_5_ = bf16[2,2,720,128]{3,2,1,0:T(8,128)(2,1)S(1)} collective-permute-done((bf16[2,2,720,128]{3,2,1,0:T(8,128)(2,1)S(1)}, bf16[2,2,720,128]{3,2,1,0:T(8,128)(2,1)S(1)}, u32[]{:S(2)}, u32[]{:S(2)}) %collective-permute-start.18) | collective-permute-done | bytes 737312 | tf_op jit(solution)/shard_map/ppermute | solution.py:70
  75.6 3.6 %far_attention.1 = (bf16[2,304,128]{2,1,0:T(8,128)(2,1)S(1)}, bf16[2,304,128]{2,1,0:T(8,128)(2,1)S(1)}, bf16[2,304,128]{2,1,0:T(8,128)(2,1)S(1)}, bf16[2,304,128]{2,1,0:T(8,128)(2,1)S(1)}) custom-call(bf16[2,2,144,128]{3,2,1,0:T(8,128)(2,1)S(1)} %get-tuple-element.76.refs_0_, bf16[2,2,144,128]{3,2,1,0:T(8,128)(2,1)S(1)} %collective-permute-done.14.refs_1_, ...), custom_call_target="tpu_custom_call" | custom-call | flops 1000 | bytes 1000 | tf_op jit(solution)/shard_map/far_attention/pallas_call | solution.py:556
  79.3 2.1 %collective-permute-start.19 = (bf16[2,304,128]{2,1,0:T(8,128)(2,1)S(1)}, bf16[2,304,128]{2,1,0:T(8,128)(2,1)S(1)}, u32[]{:S(2)}, u32[]{:S(2)}) collective-permute-start(bf16[2,304,128]{2,1,0:T(8,128)(2,1)S(1)} %get-tuple-element.86), channel_id=1, source_target_pairs={{0,96},{1,25},{2,98},{3,27},{4,100},{5,29},{6,102},{7,31},{8,104},... | collective-permute-start | bytes 466952 | tf_op jit(solution)/shard_map/ppermute | solution.py:70
  81.4 0.8 collective-permute-start.20
  82.1 0.2 collective-permute-start.21
  82.3 3.5 %collective-permute-done.19.refs_1_ = bf16[2,304,128]{2,1,0:T(8,128)(2,1)S(1)} collective-permute-done((bf16[2,304,128]{2,1,0:T(8,128)(2,1)S(1)}, bf16[2,304,128]{2,1,0:T(8,128)(2,1)S(1)}, u32[]{:S(2)}, u32[]{:S(2)}) %collective-permute-start.19) | collective-permute-done | bytes 155680 | tf_op jit(solution)/shard_map/ppermute | solution.py:70
  85.8 2.4 %collective-permute-done.20.refs_2_ = bf16[2,304,128]{2,1,0:T(8,128)(2,1)S(1)} collective-permute-done((bf16[2,304,128]{2,1,0:T(8,128)(2,1)S(1)}, bf16[2,304,128]{2,1,0:T(8,128)(2,1)S(1)}, u32[]{:S(2)}, u32[]{:S(2)}) %collective-permute-start.20) | collective-permute-done | bytes 155680 | tf_op jit(solution)/shard_map/ppermute | solution.py:70
  88.2 1.6 %collective-permute-done.21.refs_3_ = bf16[2,304,128]{2,1,0:T(8,128)(2,1)S(1)} collective-permute-done((bf16[2,304,128]{2,1,0:T(8,128)(2,1)S(1)}, bf16[2,304,128]{2,1,0:T(8,128)(2,1)S(1)}, u32[]{:S(2)}, u32[]{:S(2)}) %collective-permute-start.21) | collective-permute-done | bytes 155680 | tf_op jit(solution)/shard_map/ppermute | solution.py:70
  89.8 1.5 %merge.1 = bf16[2,144,640]{2,1,0:T(8,128)(2,1)} custom-call(s32[1]{0:T(128)} %bitcast.u_ref, f32[2,5,144,128]{3,2,1,0:T(8,128)S(1)} %get-tuple-element.72.fresh_out, f32[24,128]{1,0:T(8,128)S(1)} %get-tuple-element.73.refs_8_.fresh_rows, bf16[2,304,128]{2,1,0:T(8,128)(2,1)S(1)} %get-tuple-element.85.refs_0_, ...), custom_call_target="tpu_custom_call" | custom-call | flops 1843200 | bytes 2580480 | tf_op jit(solution)/shard_map/merge/pallas_call | solution.py:620
  (38 shorter events, 0.5 us)
Async XLA Ops:
  0.6 20.5 %collective-permute-start.5 = (bf16[288,1280]{1,0:T(8,128)(2,1)}, bf16[288,1280]{1,0:T(8,128)(2,1)S(1)}, u32[]{:S(2)}, u32[]{:S(2)}) collective-permute-start(bf16[288,1280]{1,0:T(8,128)(2,1)} %bitcast.12), channel_id=1, source_target_pairs={{0,2},{1,3},{2,0},{3,1},{4,6},{5,7},{6,4},{7,5},{8,10},{33,35},{10... | collective-permute-start | bytes 2211848 | tf_op jit(solution)/shard_map/ppermute | solution.py:70
  2.7 1.0 %copy-start.1 = (bf16[2,144,640]{2,1,0:T(8,128)(2,1)S(1)}, bf16[2,144,640]{2,1,0:T(8,128)(2,1)}, u32[]{:S(2)}) copy-start(bf16[2,144,640]{2,1,0:T(8,128)(2,1)} %key_ref.1) | copy-start | bytes 1105924
  3.7 1.0 %copy-start.2 = (bf16[2,144,640]{2,1,0:T(8,128)(2,1)S(1)}, bf16[2,144,640]{2,1,0:T(8,128)(2,1)}, u32[]{:S(2)}) copy-start(bf16[2,144,640]{2,1,0:T(8,128)(2,1)} %value_ref.1) | copy-start | bytes 1105924
  4.8 7.4 %collective-permute-start = (bf16[2,2,144,128]{3,2,1,0:T(8,128)(2,1)S(1)}, bf16[2,2,144,128]{3,2,1,0:T(8,128)(2,1)S(1)}, u32[]{:S(2)}, u32[]{:S(2)}) collective-permute-start(bf16[2,2,144,128]{3,2,1,0:T(8,128)(2,1)S(1)} %get-tuple-element.47), channel_id=1, source_target_pairs={{0,96},{1,25},{2,98},{3,27},{4,100},{5,29},{6,102},{7,31},{8,104},... | collective-permute-start | bytes 442376 | tf_op jit(solution)/shard_map/ppermute | solution.py:70
  7.9 6.8 %collective-permute-start.1 = (bf16[2,2,144,128]{3,2,1,0:T(8,128)(2,1)S(1)}, bf16[2,2,144,128]{3,2,1,0:T(8,128)(2,1)S(1)}, u32[]{:S(2)}, u32[]{:S(2)}) collective-permute-start(bf16[2,2,144,128]{3,2,1,0:T(8,128)(2,1)S(1)} %get-tuple-element.48), channel_id=1, source_target_pairs={{0,64},{1,17},{2,66},{3,19},{4,68},{5,21},{6,70},{7,23},{8,72},{33... | collective-permute-start | bytes 442376 | tf_op jit(solution)/shard_map/ppermute | solution.py:70
  8.5 7.6 %collective-permute-start.2 = (bf16[2,2,144,128]{3,2,1,0:T(8,128)(2,1)S(1)}, bf16[2,2,144,128]{3,2,1,0:T(8,128)(2,1)S(1)}, u32[]{:S(2)}, u32[]{:S(2)}) collective-permute-start(bf16[2,2,144,128]{3,2,1,0:T(8,128)(2,1)S(1)} %get-tuple-element.49), channel_id=1, source_target_pairs={{0,32},{1,9},{2,34},{3,11},{4,36},{5,13},{6,38},{7,15},{8,40},{33,... | collective-permute-start | bytes 442376 | tf_op jit(solution)/shard_map/ppermute | solution.py:70
  9.5 19.1 %collective-permute-start.4 = (bf16[288,1280]{1,0:T(8,128)(2,1)}, bf16[288,1280]{1,0:T(8,128)(2,1)S(1)}, u32[]{:S(2)}, u32[]{:S(2)}) collective-permute-start(bf16[288,1280]{1,0:T(8,128)(2,1)} %bitcast.13), channel_id=1, source_target_pairs={{0,1},{1,0},{2,3},{3,2},{4,5},{5,4},{6,7},{7,6},{8,9},{33,32},{10,... | collective-permute-start | bytes 2211848 | tf_op jit(solution)/shard_map/ppermute | solution.py:70
  16.2 1.1 %copy-start = (bf16[2,144,1280]{2,1,0:T(8,128)(2,1)S(1)}, bf16[2,144,1280]{2,1,0:T(8,128)(2,1)}, u32[]{:S(2)}) copy-start(bf16[2,144,1280]{2,1,0:T(8,128)(2,1)} %param.12) | copy-start | bytes 2211844
  17.3 0.8 copy-start.5
  18.1 0.8 copy-start.6
  18.9 0.7 copy-start.9
  19.5 0.7 copy-start.10
  21.2 7.5 %collective-permute-start.6 = (bf16[288,1280]{1,0:T(8,128)(2,1)S(1)}, bf16[288,1280]{1,0:T(8,128)(2,1)}, u32[]{:S(2)}, u32[]{:S(2)}) collective-permute-start(bf16[288,1280]{1,0:T(8,128)(2,1)S(1)} %collective-permute-done.5.h2), channel_id=1, source_target_pairs={{0,1},{1,0},{2,3},{3,2},{4,5},{5,4},{6,7},{7,6},{8,9},{33,32},{10,... | collective-permute-start | bytes 2211848 | tf_op jit(solution)/shard_map/ppermute | solution.py:70
  21.3 15.1 %copy-start.11 = (bf16[5120,640]{1,0:T(8,128)(2,1)S(1)}, bf16[5120,640]{1,0:T(8,128)(2,1)}, u32[]{:S(2)}) copy-start(bf16[5120,640]{1,0:T(8,128)(2,1)} %param.16) | copy-start | bytes 19660804
  21.3 17.9 %collective-permute-start.7 = (bf16[2,2,720,128]{3,2,1,0:T(8,128)(2,1)S(1)}, bf16[2,2,720,128]{3,2,1,0:T(8,128)(2,1)S(1)}, u32[]{:S(2)}, u32[]{:S(2)}) collective-permute-start(bf16[2,2,720,128]{3,2,1,0:T(8,128)(2,1)S(1)} %assemble.1.after.refs_4_), channel_id=1, source_target_pairs={{0,8},{1,33},{2,10},{3,35},{4,12},{5,37},{6,14},{7,39},{8,0},{33,1... | collective-permute-start | bytes 2211848 | tf_op jit(solution)/shard_map/ppermute | solution.py:70
  22.8 16.3 %collective-permute-start.8 = (bf16[2,2,720,128]{3,2,1,0:T(8,128)(2,1)S(1)}, bf16[2,2,720,128]{3,2,1,0:T(8,128)(2,1)S(1)}, u32[]{:S(2)}, u32[]{:S(2)}) collective-permute-start(bf16[2,2,720,128]{3,2,1,0:T(8,128)(2,1)S(1)} %assemble.1.after.refs_4_), channel_id=1, source_target_pairs={{0,24},{1,97},{2,26},{3,99},{4,28},{5,101},{6,30},{7,103},{8,16},{... | collective-permute-start | bytes 2211848 | tf_op jit(solution)/shard_map/ppermute | solution.py:70
  25.0 21.9 %collective-permute-start.3 = (bf16[2,2,720,128]{3,2,1,0:T(8,128)(2,1)S(1)}, bf16[2,2,720,128]{3,2,1,0:T(8,128)(2,1)S(1)}, u32[]{:S(2)}, u32[]{:S(2)}) collective-permute-start(bf16[2,2,720,128]{3,2,1,0:T(8,128)(2,1)S(1)} %assemble.1.after.refs_4_), channel_id=1, source_target_pairs={{0,4},{1,5},{2,6},{3,7},{4,0},{5,1},{6,2},{7,3},{8,12},{33,37},{10... | collective-permute-start | bytes 2211848 | tf_op jit(solution)/shard_map/ppermute | solution.py:70
  28.6 12.8 %slice-start = ((s8[6553600]{0:T(1024)(128)(4,1)}), s8[2359296]{0:T(1024)(128)(4,1)S(1)}, s32[]{:S(2)}) async-start(s8[6553600]{0:T(1024)(128)(4,1)} %bitcast.17), calls=%async_computation | async-start | bytes 4718592
  36.4 5.0 %slice-start.1 = ((s8[6553600]{0:T(1024)(128)(4,1)}), s8[4194304]{0:T(1024)(128)(4,1)S(1)}, s32[]{:S(2)}) async-start(s8[6553600]{0:T(1024)(128)(4,1)} %bitcast.17), calls=%async_computation.1 | async-start | bytes 8388608
  39.1 6.0 %copy-start.7 = (f32[640]{0:T(1024)S(1)}, f32[640]{0:T(1024)}, u32[]{:S(2)}) copy-start(f32[640]{0:T(1024)} %qg.1) | copy-start | bytes 7684
  39.1 6.0 %copy-start.8 = (f32[640]{0:T(1024)S(1)}, f32[640]{0:T(1024)}, u32[]{:S(2)}) copy-start(f32[640]{0:T(1024)} %kg.1) | copy-start | bytes 7684
  39.2 6.0 %collective-permute-start.10 = (f32[8,384]{1,0:T(8,128)S(1)}, f32[8,384]{1,0:T(8,128)S(1)}, u32[]{:S(2)}, u32[]{:S(2)}) collective-permute-start(f32[8,384]{1,0:T(8,128)S(1)} %sum_squares.1.s0), channel_id=1, source_target_pairs={{0,2},{1,3},{2,0},{3,1},{4,6},{5,7},{6,4},{7,5},{8,10},{33,35},{10... | collective-permute-start | bytes 36872 | tf_op jit(solution)/shard_map/ppermute | solution.py:70
  39.3 5.9 %collective-permute-start.11 = (f32[8,384]{1,0:T(8,128)S(1)}, f32[8,384]{1,0:T(8,128)S(1)}, u32[]{:S(2)}, u32[]{:S(2)}) collective-permute-start(f32[8,384]{1,0:T(8,128)S(1)} %sum_squares.1.s0), channel_id=1, source_target_pairs={{0,1},{1,0},{2,3},{3,2},{4,5},{5,4},{6,7},{7,6},{8,9},{33,32},{10,... | collective-permute-start | bytes 36872 | tf_op jit(solution)/shard_map/ppermute | solution.py:70
  39.3 5.8 %collective-permute-start.9 = (f32[8,384]{1,0:T(8,128)S(1)}, f32[8,384]{1,0:T(8,128)S(1)}, u32[]{:S(2)}, u32[]{:S(2)}) collective-permute-start(f32[8,384]{1,0:T(8,128)S(1)} %sum_squares.1.s0), channel_id=1, source_target_pairs={{0,3},{1,2},{2,1},{3,0},{4,7},{5,6},{6,5},{7,4},{8,11},{33,34},{10... | collective-permute-start | bytes 36872 | tf_op jit(solution)/shard_map/ppermute | solution.py:70
  43.9 47.4 %copy-start.3 = (bf16[288,640]{1,0:T(8,128)(2,1)}, bf16[288,640]{1,0:T(8,128)(2,1)S(1)}, u32[]{:S(2)}) copy-start(bf16[288,640]{1,0:T(8,128)(2,1)S(1)} %convolution_convert_fusion.v_ref) | copy-start | bytes 1105924
  43.9 15.9 %collective-permute-start.13 = (bf16[2,2,720,128]{3,2,1,0:T(8,128)(2,1)S(1)}, bf16[2,2,720,128]{3,2,1,0:T(8,128)(2,1)S(1)}, u32[]{:S(2)}, u32[]{:S(2)}) collective-permute-start(bf16[2,2,720,128]{3,2,1,0:T(8,128)(2,1)S(1)} %collective-permute-done.7.refs_5_), channel_id=1, source_target_pairs={{0,24},{1,97},{2,26},{3,99},{4,28},{5,101},{6,30},{7,103},{8,16},{... | collective-permute-start | bytes 2211848 | tf_op jit(solution)/shard_map/ppermute | solution.py:70
  47.0 13.7 %collective-permute-start.12 = (bf16[2,2,720,128]{3,2,1,0:T(8,128)(2,1)S(1)}, bf16[2,2,720,128]{3,2,1,0:T(8,128)(2,1)S(1)}, u32[]{:S(2)}, u32[]{:S(2)}) collective-permute-start(bf16[2,2,720,128]{3,2,1,0:T(8,128)(2,1)S(1)} %collective-permute-done.3.refs_8_), channel_id=1, source_target_pairs={{0,8},{1,33},{2,10},{3,35},{4,12},{5,37},{6,14},{7,39},{8,0},{33,1... | collective-permute-start | bytes 2211848 | tf_op jit(solution)/shard_map/ppermute | solution.py:70
  48.0 6.8 %collective-permute-start.14 = (bf16[2,2,144,128]{3,2,1,0:T(8,128)(2,1)S(1)}, bf16[2,2,144,128]{3,2,1,0:T(8,128)(2,1)S(1)}, u32[]{:S(2)}, u32[]{:S(2)}) collective-permute-start(bf16[2,2,144,128]{3,2,1,0:T(8,128)(2,1)S(1)} %get-tuple-element.71.refs_3_), channel_id=1, source_target_pairs={{0,96},{1,25},{2,98},{3,27},{4,100},{5,29},{6,102},{7,31},{8,104},... | collective-permute-start | bytes 442376 | tf_op jit(solution)/shard_map/ppermute | solution.py:70
  49.1 8.3 %collective-permute-start.15 = (bf16[2,2,144,128]{3,2,1,0:T(8,128)(2,1)S(1)}, bf16[2,2,144,128]{3,2,1,0:T(8,128)(2,1)S(1)}, u32[]{:S(2)}, u32[]{:S(2)}) collective-permute-start(bf16[2,2,144,128]{3,2,1,0:T(8,128)(2,1)S(1)} %get-tuple-element.70.refs_2_), channel_id=1, source_target_pairs={{0,64},{1,17},{2,66},{3,19},{4,68},{5,21},{6,70},{7,23},{8,72},{33... | collective-permute-start | bytes 442376 | tf_op jit(solution)/shard_map/ppermute | solution.py:70
  50.8 8.4 %collective-permute-start.16 = (bf16[2,2,144,128]{3,2,1,0:T(8,128)(2,1)S(1)}, bf16[2,2,144,128]{3,2,1,0:T(8,128)(2,1)S(1)}, u32[]{:S(2)}, u32[]{:S(2)}) collective-permute-start(bf16[2,2,144,128]{3,2,1,0:T(8,128)(2,1)S(1)} %get-tuple-element.69.refs_1_), channel_id=1, source_target_pairs={{0,32},{1,9},{2,34},{3,11},{4,36},{5,13},{6,38},{7,15},{8,40},{33,... | collective-permute-start | bytes 442376 | tf_op jit(solution)/shard_map/ppermute | solution.py:70
  54.8 18.7 %collective-permute-start.17 = (bf16[2,2,720,128]{3,2,1,0:T(8,128)(2,1)S(1)}, bf16[2,2,720,128]{3,2,1,0:T(8,128)(2,1)S(1)}, u32[]{:S(2)}, u32[]{:S(2)}) collective-permute-start(bf16[2,2,720,128]{3,2,1,0:T(8,128)(2,1)S(1)} %collective-permute-done.3.refs_8_), channel_id=1, source_target_pairs={{0,24},{1,97},{2,26},{3,99},{4,28},{5,101},{6,30},{7,103},{8,16},{... | collective-permute-start | bytes 2211848 | tf_op jit(solution)/shard_map/ppermute | solution.py:70
  60.7 14.9 %collective-permute-start.18 = (bf16[2,2,720,128]{3,2,1,0:T(8,128)(2,1)S(1)}, bf16[2,2,720,128]{3,2,1,0:T(8,128)(2,1)S(1)}, u32[]{:S(2)}, u32[]{:S(2)}) collective-permute-start(bf16[2,2,720,128]{3,2,1,0:T(8,128)(2,1)S(1)} %collective-permute-done.12.refs_9_), channel_id=1, source_target_pairs={{0,24},{1,97},{2,26},{3,99},{4,28},{5,101},{6,30},{7,103},{8,16},{... | collective-permute-start | bytes 2211848 | tf_op jit(solution)/shard_map/ppermute | solution.py:70
  63.9 1.0 %copy-start.4 = (bf16[288,640]{1,0:T(8,128)(2,1)S(1)}, bf16[288,640]{1,0:T(8,128)(2,1)}, u32[]{:S(2)}) copy-start(bf16[288,640]{1,0:T(8,128)(2,1)} %get-tuple-element.66.k_ref) | copy-start | bytes 1105924
  79.3 6.6 %collective-permute-start.19 = (bf16[2,304,128]{2,1,0:T(8,128)(2,1)S(1)}, bf16[2,304,128]{2,1,0:T(8,128)(2,1)S(1)}, u32[]{:S(2)}, u32[]{:S(2)}) collective-permute-start(bf16[2,304,128]{2,1,0:T(8,128)(2,1)S(1)} %get-tuple-element.86), channel_id=1, source_target_pairs={{0,96},{1,25},{2,98},{3,27},{4,100},{5,29},{6,102},{7,31},{8,104},... | collective-permute-start | bytes 466952 | tf_op jit(solution)/shard_map/ppermute | solution.py:70
  81.4 6.8 %collective-permute-start.20 = (bf16[2,304,128]{2,1,0:T(8,128)(2,1)S(1)}, bf16[2,304,128]{2,1,0:T(8,128)(2,1)S(1)}, u32[]{:S(2)}, u32[]{:S(2)}) collective-permute-start(bf16[2,304,128]{2,1,0:T(8,128)(2,1)S(1)} %get-tuple-element.87), channel_id=1, source_target_pairs={{0,64},{1,17},{2,66},{3,19},{4,68},{5,21},{6,70},{7,23},{8,72},{33... | collective-permute-start | bytes 466952 | tf_op jit(solution)/shard_map/ppermute | solution.py:70
  82.1 7.6 %collective-permute-start.21 = (bf16[2,304,128]{2,1,0:T(8,128)(2,1)S(1)}, bf16[2,304,128]{2,1,0:T(8,128)(2,1)S(1)}, u32[]{:S(2)}, u32[]{:S(2)}) collective-permute-start(bf16[2,304,128]{2,1,0:T(8,128)(2,1)S(1)} %get-tuple-element.88), channel_id=1, source_target_pairs={{0,32},{1,9},{2,34},{3,11},{4,36},{5,13},{6,38},{7,15},{8,40},{33,... | collective-permute-start | bytes 466952 | tf_op jit(solution)/shard_map/ppermute | solution.py:70

commit v11 on v9

--- a/solution.py
+++ b/solution.py
@@ -661,19 +661,19 @@
 
     z_rows, cond = lax.optimization_barrier((z_rows, cond))
     cross_rows = swap_tp(z_rows, 0, 1)
+    near_two = swap_v(near_one, 3)
     blocks = jnp.stack([tp, tp ^ 1, tp ^ 2, tp ^ 3]).astype(jnp.int32)
     modded, query = modulate(blocks, [own_rows, core_rows, z_rows, cross_rows], cond, mod, w_query)
     key = jnp.dot(modded, w_key, preferred_element_type=F32)
-    near_one, near_three, key = lax.optimization_barrier((near_one, near_three, key))
-    near_two = swap_v(near_one, 3)
     fresh_values = jnp.dot(modded, w_value, preferred_element_type=F32).astype(BF16)
     own_sq = sum_squares(query, key)
+    near_three, own_sq = lax.optimization_barrier((near_three, own_sq))
     squares = [own_sq] + [swap_tp(own_sq, z, c) for z, c in ((1, 1), (1, 0), (0, 1))]
-    far, fresh_values, *squares = lax.optimization_barrier((far, fresh_values, *squares))
+    near_two, fresh_values, *squares = lax.optimization_barrier((near_two, fresh_values, *squares))
+    far_two = swap_z_hi(near_two)
+    fresh_keys, *sends = norm_rope(u, query, key, squares, q_gain, k_gain, cos, sin)
+    far, fresh_keys = lax.optimization_barrier((far, fresh_keys))
     far_one, far_three = swap_v(far, 1), swap_v(far, 3)
-    fresh_keys, *sends = norm_rope(u, query, key, squares, q_gain, k_gain, cos, sin)
-    near_two, fresh_keys = lax.optimization_barrier((near_two, fresh_keys))
-    far_two = swap_z_hi(near_two)
     queries = exchange_u(sends)
     fresh_out, fresh_rows = fresh_attention(u, fresh_keys, fresh_values, sends)
 

time: 88.2 us -> 89.2 us (1.011); the launches traced: 86.8 us -> 88.7 us
  local copies, waits for them, and re-layouts: 6.99 us -> 8.98 us
    unnamed x28 -> x32, local copies, waits for them, and re-layouts: 6.99 us -> 8.98 us
  transfers between devices with their start and end apart: 22 -> 22, of which waited for: 10 -> 8; matrix products, arithmetic and copies ran while one was open for 6% -> 6% of each run, Pallas kernels for 21% -> 21%
where the time goes in v11:
time: 89.2 us; the launch traced here: 88.7 us
  starting transfers between devices  25.3 us (28%)
  Pallas kernels  24.9 us (28%)
  waiting for transfers between devices  23.5 us (26%)
  local copies, waits for them, and re-layouts  8.98 us (10%)
  matrix products  5.12 us (6%)
    ppermute x22, starting transfers between devices, permute(): lax.ppermute(value, AXES, [(linear(*p), linear(*move(*p))) for p in place...  25.3 us
    ppermute x22, waiting for transfers between devices, permute(): lax.ppermute(value, AXES, [(linear(*p), linear(*move(*p))) for p in place...  23.5 us
    pallas_call x2, Pallas kernels, stale_attention(): pl.pallas_call(functools.partial(stale_kernel, far, count), out_shape=out...  11.4 us
    unnamed x32, local copies, waits for them, and re-layouts  8.98 us
    pallas_call x1, Pallas kernels, modulate(): pl.pallas_call(modulate_kernel, out_shape=[jax.ShapeDtypeStruct((ROWS, D)...  7.8 us
    dot_general x1, matrix products, shards(): key = jnp.dot(modded, w_key, preferred_element_type=F32)  2.56 us
    dot_general x1, matrix products, shards(): jnp.dot(modded, w_value, preferred_element_type=F32).astype(BF16)  2.56 us
    pallas_call x1, Pallas kernels, norm_rope(): pl.pallas_call(rope_kernel, out_shape=[flat] + [send] * 4, in_specs=[smem...  1.8 us
  transfers between devices with their start and end apart: 22, of which 8 were waited for; matrix products, arithmetic and copies ran while one was open for 6% of the time, Pallas kernels for 21%

profile of v11, /device:TPU:0, one launch (start us, length us, event | category | flops | bytes accessed | tf_op | source)
XLA Modules:
  0.0 88.7 jit_solution(7963905022160315754)
XLA Ops:
  0.6 2.1 %collective-permute-start.5 = (bf16[288,1280]{1,0:T(8,128)(2,1)}, bf16[288,1280]{1,0:T(8,128)(2,1)S(1)}, u32[]{:S(2)}, u32[]{:S(2)}) collective-permute-start(bf16[288,1280]{1,0:T(8,128)(2,1)} %bitcast.12), channel_id=1, source_target_pairs={{0,2},{1,3},{2,0},{3,1},{4,6},{5,7},{6,4},{7,5},{8,10},{33,35},{10... | collective-permute-start | bytes 2211848 | tf_op jit(solution)/shard_map/ppermute | solution.py:70
  2.7 1.0 %copy-done.3 = bf16[2,144,640]{2,1,0:T(8,128)(2,1)S(1)} copy-done((bf16[2,144,640]{2,1,0:T(8,128)(2,1)S(1)}, bf16[2,144,640]{2,1,0:T(8,128)(2,1)}, u32[]{:S(2)}) %copy-start.3) | copy-done | bytes 368664
  3.7 1.0 %copy-done.4 = bf16[2,144,640]{2,1,0:T(8,128)(2,1)S(1)} copy-done((bf16[2,144,640]{2,1,0:T(8,128)(2,1)S(1)}, bf16[2,144,640]{2,1,0:T(8,128)(2,1)}, u32[]{:S(2)}) %copy-start.4) | copy-done | bytes 368664
  4.7 0.1 pack_stale.1
  4.8 3.1 %collective-permute-start = (bf16[2,2,144,128]{3,2,1,0:T(8,128)(2,1)S(1)}, bf16[2,2,144,128]{3,2,1,0:T(8,128)(2,1)S(1)}, u32[]{:S(2)}, u32[]{:S(2)}) collective-permute-start(bf16[2,2,144,128]{3,2,1,0:T(8,128)(2,1)S(1)} %get-tuple-element.41), channel_id=1, source_target_pairs={{0,96},{1,25},{2,98},{3,27},{4,100},{5,29},{6,102},{7,31},{8,104},... | collective-permute-start | bytes 442376 | tf_op jit(solution)/shard_map/ppermute | solution.py:70
  7.9 0.6 collective-permute-start.1
  8.5 1.0 %collective-permute-start.2 = (bf16[2,2,144,128]{3,2,1,0:T(8,128)(2,1)S(1)}, bf16[2,2,144,128]{3,2,1,0:T(8,128)(2,1)S(1)}, u32[]{:S(2)}, u32[]{:S(2)}) collective-permute-start(bf16[2,2,144,128]{3,2,1,0:T(8,128)(2,1)S(1)} %get-tuple-element.43), channel_id=1, source_target_pairs={{0,32},{1,9},{2,34},{3,11},{4,36},{5,13},{6,38},{7,15},{8,40},{33,... | collective-permute-start | bytes 442376 | tf_op jit(solution)/shard_map/ppermute | solution.py:70
  9.5 2.7 %collective-permute-done.refs_1_ = bf16[2,2,144,128]{3,2,1,0:T(8,128)(2,1)S(1)} collective-permute-done((bf16[2,2,144,128]{3,2,1,0:T(8,128)(2,1)S(1)}, bf16[2,2,144,128]{3,2,1,0:T(8,128)(2,1)S(1)}, u32[]{:S(2)}, u32[]{:S(2)}) %collective-permute-start) | collective-permute-done | bytes 147488 | tf_op jit(solution)/shard_map/ppermute | solution.py:70
  12.2 2.5 %collective-permute-done.1.refs_2_ = bf16[2,2,144,128]{3,2,1,0:T(8,128)(2,1)S(1)} collective-permute-done((bf16[2,2,144,128]{3,2,1,0:T(8,128)(2,1)S(1)}, bf16[2,2,144,128]{3,2,1,0:T(8,128)(2,1)S(1)}, u32[]{:S(2)}, u32[]{:S(2)}) %collective-permute-start.1) | collective-permute-done | bytes 147488 | tf_op jit(solution)/shard_map/ppermute | solution.py:70
  14.7 1.5 %collective-permute-done.2.refs_3_ = bf16[2,2,144,128]{3,2,1,0:T(8,128)(2,1)S(1)} collective-permute-done((bf16[2,2,144,128]{3,2,1,0:T(8,128)(2,1)S(1)}, bf16[2,2,144,128]{3,2,1,0:T(8,128)(2,1)S(1)}, u32[]{:S(2)}, u32[]{:S(2)}) %collective-permute-start.2) | collective-permute-done | bytes 147488 | tf_op jit(solution)/shard_map/ppermute | solution.py:70
  16.2 1.6 %collective-permute-start.7 = (bf16[2,2,720,128]{3,2,1,0:T(8,128)(2,1)S(1)}, bf16[2,2,720,128]{3,2,1,0:T(8,128)(2,1)S(1)}, u32[]{:S(2)}, u32[]{:S(2)}) collective-permute-start(bf16[2,2,720,128]{3,2,1,0:T(8,128)(2,1)S(1)} %assemble.1.after.refs_4_), channel_id=1, source_target_pairs={{0,8},{1,33},{2,10},{3,35},{4,12},{5,37},{6,14},{7,39},{8,0},{33,1... | collective-permute-start | bytes 2211848 | tf_op jit(solution)/shard_map/ppermute | solution.py:70
  17.8 1.1 %copy-done = bf16[2,144,1280]{2,1,0:T(8,128)(2,1)S(1)} copy-done((bf16[2,144,1280]{2,1,0:T(8,128)(2,1)S(1)}, bf16[2,144,1280]{2,1,0:T(8,128)(2,1)}, u32[]{:S(2)}) %copy-start) | copy-done | bytes 737304
  18.9 0.8 copy-done.7
  19.7 0.8 copy-done.8
  20.4 0.7 copy-done.11
  21.1 0.7 copy-done.12
  21.8 0.9 %tables.1 = (f32[288,128]{1,0:T(8,128)S(1)}, f32[144,128]{1,0:T(8,128)S(1)}, f32[144,128]{1,0:T(8,128)S(1)}, f32[4,5120]{1,0:T(4,128)S(1)}, bf16[288,1280]{1,0:T(8,128)(2,1)S(1)}) custom-call(s32[144]{0:T(256)S(1)} %copy-done.11, f32[1,128]{1,0:T(1,128)S(1)} %copy-done.12, bf16[288,1280]{1,0:T(8,128)(2,1)S(1)} %bitcast.14, f32[2,5120]{1,0:T(2,128)S(1)} %copy-done.7, ...), custom_call_target="tpu_custom_call" | custom-call | flops 1843200 | bytes 1000000 | tf_op jit(solution)/shard_map/tables/pallas_call | solution.py:177
  22.7 0.9 copy-done.1
  23.6 2.1 %collective-permute-start.9 = (bf16[2,2,720,128]{3,2,1,0:T(8,128)(2,1)S(1)}, bf16[2,2,720,128]{3,2,1,0:T(8,128)(2,1)S(1)}, u32[]{:S(2)}, u32[]{:S(2)}) collective-permute-start(bf16[2,2,720,128]{3,2,1,0:T(8,128)(2,1)S(1)} %assemble.1.after.refs_4_), channel_id=1, source_target_pairs={{0,24},{1,97},{2,26},{3,99},{4,28},{5,101},{6,30},{7,103},{8,16},{... | collective-permute-start | bytes 2211848 | tf_op jit(solution)/shard_map/ppermute | solution.py:70
  25.8 3.6 %collective-permute-start.3 = (bf16[2,2,720,128]{3,2,1,0:T(8,128)(2,1)S(1)}, bf16[2,2,720,128]{3,2,1,0:T(8,128)(2,1)S(1)}, u32[]{:S(2)}, u32[]{:S(2)}) collective-permute-start(bf16[2,2,720,128]{3,2,1,0:T(8,128)(2,1)S(1)} %assemble.1.after.refs_4_), channel_id=1, source_target_pairs={{0,4},{1,5},{2,6},{3,7},{4,0},{5,1},{6,2},{7,3},{8,12},{33,37},{10... | collective-permute-start | bytes 2211848 | tf_op jit(solution)/shard_map/ppermute | solution.py:70
  29.4 1.1 %collective-permute-start.8 = (bf16[2,2,720,128]{3,2,1,0:T(8,128)(2,1)S(1)}, bf16[2,2,720,128]{3,2,1,0:T(8,128)(2,1)S(1)}, u32[]{:S(2)}, u32[]{:S(2)}) collective-permute-start(bf16[2,2,720,128]{3,2,1,0:T(8,128)(2,1)S(1)} %collective-permute-done.7.refs_5_), channel_id=1, source_target_pairs={{0,24},{1,97},{2,26},{3,99},{4,28},{5,101},{6,30},{7,103},{8,16},{... | collective-permute-start | bytes 2211848 | tf_op jit(solution)/shard_map/ppermute | solution.py:70
  30.5 1.1 %copy-done.2 = bf16[288,1280]{1,0:T(8,128)(2,1)S(1)} copy-done((bf16[288,1280]{1,0:T(8,128)(2,1)S(1)}, bf16[288,1280]{1,0:T(8,128)(2,1)}, u32[]{:S(2)}) %copy-start.2) | copy-done | bytes 737304
  31.7 7.8 %modulate.1 = (bf16[288,5120]{1,0:T(8,128)(2,1)S(1)}, f32[288,640]{1,0:T(8,128)S(1)}) custom-call(s32[4]{0:T(128)S(1)} %pad_add_fusion.t_ref, bf16[288,1280]{1,0:T(8,128)(2,1)S(1)} %copy-done.2, bf16[288,1280]{1,0:T(8,128)(2,1)S(1)} %collective-permute-done.4.h1, bf16[288,1280]{1,0:T(8,128)(2,1)S(1)} %collective-permute-done.5.h2, ...), custom_call_target="tpu_custom_call" | custom-call | flops 1000 | bytes 30000000 | tf_op jit(solution)/shard_map/modulate/pallas_call | solution.py:275
  39.5 2.6 %fusion.k_ref = f32[288,640]{1,0:T(8,128)S(1)} fusion(bf16[288,5120]{1,0:T(8,128)(2,1)S(1)} %get-tuple-element.51, bf16[5120,640]{1,0:T(8,128)(2,1)S(1)} %copy-done.13), kind=kOutput, calls=%fused_computation.2 | convolution fusion | flops 1887436800 | bytes 10240000 | tf_op jit(solution)/shard_map/dot_general | solution.py:667
  42.1 0.2 sum_squares.1.s0
  42.3 0.1 collective-permute-start.10
  42.4 1.3 %collective-permute-start.11 = (f32[8,384]{1,0:T(8,128)S(1)}, f32[8,384]{1,0:T(8,128)S(1)}, u32[]{:S(2)}, u32[]{:S(2)}) collective-permute-start(f32[8,384]{1,0:T(8,128)S(1)} %sum_squares.1.s0), channel_id=1, source_target_pairs={{0,2},{1,3},{2,0},{3,1},{4,6},{5,7},{6,4},{7,5},{8,10},{33,35},{10... | collective-permute-start | bytes 36872 | tf_op jit(solution)/shard_map/ppermute | solution.py:70
  43.6 0.6 collective-permute-start.12
  44.2 2.6 %convolution_convert_fusion.v_ref = bf16[288,640]{1,0:T(8,128)(2,1)S(1)} fusion(bf16[288,5120]{1,0:T(8,128)(2,1)S(1)} %get-tuple-element.51, bf16[5120,640]{1,0:T(8,128)(2,1)S(1)} %bitcast.18), kind=kOutput, calls=%fused_computation | convolution fusion | flops 1887621120 | bytes 9871360 | tf_op jit(solution)/shard_map/dot_general | solution.py:668
  46.9 1.8 %norm_rope.1 = (bf16[288,640]{1,0:T(8,128)(2,1)}, bf16[2,2,144,128]{3,2,1,0:T(8,128)(2,1)S(1)}, bf16[2,2,144,128]{3,2,1,0:T(8,128)(2,1)S(1)}, bf16[2,2,144,128]{...) custom-call(s32[1]{0:T(128)} %bitcast.u_ref, f32[288,640]{1,0:T(8,128)S(1)} %get-tuple-element.50.q_ref, ...), custom_call_target="tpu_custom_call" | custom-call | flops 1000 | bytes 1000 | tf_op jit(solution)/shard_map/norm_rope/pallas_call | solution.py:348
  48.7 0.2 collective-permute-start.16
  48.9 2.6 %collective-permute-start.17 = (bf16[2,2,720,128]{3,2,1,0:T(8,128)(2,1)S(1)}, bf16[2,2,720,128]{3,2,1,0:T(8,128)(2,1)S(1)}, u32[]{:S(2)}, u32[]{:S(2)}) collective-permute-start(bf16[2,2,720,128]{3,2,1,0:T(8,128)(2,1)S(1)} %collective-permute-done.3.refs_8_), channel_id=1, source_target_pairs={{0,24},{1,97},{2,26},{3,99},{4,28},{5,101},{6,30},{7,103},{8,16},{... | collective-permute-start | bytes 2211848 | tf_op jit(solution)/shard_map/ppermute | solution.py:70
  51.4 2.2 %collective-permute-start.18 = (bf16[2,2,720,128]{3,2,1,0:T(8,128)(2,1)S(1)}, bf16[2,2,720,128]{3,2,1,0:T(8,128)(2,1)S(1)}, u32[]{:S(2)}, u32[]{:S(2)}) collective-permute-start(bf16[2,2,720,128]{3,2,1,0:T(8,128)(2,1)S(1)} %collective-permute-done.8.refs_7_), channel_id=1, source_target_pairs={{0,4},{1,5},{2,6},{3,7},{4,0},{5,1},{6,2},{7,3},{8,12},{33,37},{10... | collective-permute-start | bytes 2211848 | tf_op jit(solution)/shard_map/ppermute | solution.py:70
  53.6 0.6 collective-permute-start.13
  54.1 0.6 collective-permute-start.14
  54.8 5.6 %collective-permute-done.13.refs_1_ = bf16[2,2,144,128]{3,2,1,0:T(8,128)(2,1)S(1)} collective-permute-done((bf16[2,2,144,128]{3,2,1,0:T(8,128)(2,1)S(1)}, bf16[2,2,144,128]{3,2,1,0:T(8,128)(2,1)S(1)}, u32[]{:S(2)}, u32[]{:S(2)}) %collective-permute-start.13) | collective-permute-done | bytes 147488 | tf_op jit(solution)/shard_map/ppermute | solution.py:70
  60.4 1.0 %copy-done.6 = bf16[288,640]{1,0:T(8,128)(2,1)S(1)} copy-done((bf16[288,640]{1,0:T(8,128)(2,1)S(1)}, bf16[288,640]{1,0:T(8,128)(2,1)}, u32[]{:S(2)}) %copy-start.6) | copy-done | bytes 368664
  61.4 1.0 %fresh_attention.1 = (f32[2,5,144,128]{3,2,1,0:T(8,128)S(1)}, f32[24,128]{1,0:T(8,128)S(1)}) custom-call(s32[1]{0:T(128)} %bitcast.u_ref, bf16[288,640]{1,0:T(8,128)(2,1)S(1)} %copy-done.6, bf16[288,640]{1,0:T(8,128)(2,1)S(1)} %convolution_convert_fusion.v_ref, bf16[2,2,144,128]{3,2,1,0:T(8,128)(2,1)S(1)} %get-tuple-element.62.refs_0_, ...), custom_call_target="tpu_custom_call" | custom-call | flops 1000 | bytes 1000 | tf_op jit(solution)/shard_map/fresh_attention/pallas_call | solution.py:398
  62.4 4.3 %collective-permute-done.15.refs_3_ = bf16[2,2,144,128]{3,2,1,0:T(8,128)(2,1)S(1)} collective-permute-done((bf16[2,2,144,128]{3,2,1,0:T(8,128)(2,1)S(1)}, bf16[2,2,144,128]{3,2,1,0:T(8,128)(2,1)S(1)}, u32[]{:S(2)}, u32[]{:S(2)}) %collective-permute-start.15) | collective-permute-done | bytes 147488 | tf_op jit(solution)/shard_map/ppermute | solution.py:70
  66.7 6.6 %near_attention.1 = (f32[2,4,2,144,128]{4,3,2,1,0:T(8,128)S(1)}, f32[2,4,2,144,128]{4,3,2,1,0:T(8,128)S(1)}) custom-call(bf16[2,2,144,128]{3,2,1,0:T(8,128)(2,1)S(1)} %get-tuple-element.62.refs_0_, bf16[2,2,144,128]{3,2,1,0:T(8,128)(2,1)S(1)} %collective-permute-done.13.refs_1_, bf16[2,2,144,128]{3,2,1,0:T(8,128)(2,1)S(1)} %collective-permute-done.14.refs_2_, ...), custom_call_target="tpu_custom_call" | custom-call | flops 1000 | bytes 1000 | tf_op jit(solution)/shard_map/near_attention/pallas_call | solution.py:556
  73.4 4.8 %far_attention.1 = (bf16[2,304,128]{2,1,0:T(8,128)(2,1)S(1)}, bf16[2,304,128]{2,1,0:T(8,128)(2,1)S(1)}, bf16[2,304,128]{2,1,0:T(8,128)(2,1)S(1)}, bf16[2,304,128]{2,1,0:T(8,128)(2,1)S(1)}) custom-call(bf16[2,2,144,128]{3,2,1,0:T(8,128)(2,1)S(1)} %get-tuple-element.62.refs_0_, bf16[2,2,144,128]{3,2,1,0:T(8,128)(2,1)S(1)} %collective-permute-done.13.refs_1_, ...), custom_call_target="tpu_custom_call" | custom-call | flops 1000 | bytes 1000 | tf_op jit(solution)/shard_map/far_attention/pallas_call | solution.py:556
  78.2 0.6 collective-permute-start.19
  78.8 0.3 collective-permute-start.20
  79.1 1.2 %collective-permute-start.21 = (bf16[2,304,128]{2,1,0:T(8,128)(2,1)S(1)}, bf16[2,304,128]{2,1,0:T(8,128)(2,1)S(1)}, u32[]{:S(2)}, u32[]{:S(2)}) collective-permute-start(bf16[2,304,128]{2,1,0:T(8,128)(2,1)S(1)} %get-tuple-element.76), channel_id=1, source_target_pairs={{0,32},{1,9},{2,34},{3,11},{4,36},{5,13},{6,38},{7,15},{8,40},{33,... | collective-permute-start | bytes 466952 | tf_op jit(solution)/shard_map/ppermute | solution.py:70
  80.3 3.2 %collective-permute-done.19.refs_1_ = bf16[2,304,128]{2,1,0:T(8,128)(2,1)S(1)} collective-permute-done((bf16[2,304,128]{2,1,0:T(8,128)(2,1)S(1)}, bf16[2,304,128]{2,1,0:T(8,128)(2,1)S(1)}, u32[]{:S(2)}, u32[]{:S(2)}) %collective-permute-start.19) | collective-permute-done | bytes 155680 | tf_op jit(solution)/shard_map/ppermute | solution.py:70
  83.5 2.2 %collective-permute-done.20.refs_2_ = bf16[2,304,128]{2,1,0:T(8,128)(2,1)S(1)} collective-permute-done((bf16[2,304,128]{2,1,0:T(8,128)(2,1)S(1)}, bf16[2,304,128]{2,1,0:T(8,128)(2,1)S(1)}, u32[]{:S(2)}, u32[]{:S(2)}) %collective-permute-start.20) | collective-permute-done | bytes 155680 | tf_op jit(solution)/shard_map/ppermute | solution.py:70
  85.6 1.6 %collective-permute-done.21.refs_3_ = bf16[2,304,128]{2,1,0:T(8,128)(2,1)S(1)} collective-permute-done((bf16[2,304,128]{2,1,0:T(8,128)(2,1)S(1)}, bf16[2,304,128]{2,1,0:T(8,128)(2,1)S(1)}, u32[]{:S(2)}, u32[]{:S(2)}) %collective-permute-start.21) | collective-permute-done | bytes 155680 | tf_op jit(solution)/shard_map/ppermute | solution.py:70
  87.2 1.5 %merge.1 = bf16[2,144,640]{2,1,0:T(8,128)(2,1)} custom-call(s32[1]{0:T(128)} %bitcast.u_ref, f32[2,5,144,128]{3,2,1,0:T(8,128)S(1)} %get-tuple-element.66.fresh_out, f32[24,128]{1,0:T(8,128)S(1)} %get-tuple-element.67.refs_9_.fresh_rows, bf16[2,304,128]{2,1,0:T(8,128)(2,1)S(1)} %get-tuple-element.73.refs_0_, ...), custom_call_target="tpu_custom_call" | custom-call | flops 1843200 | bytes 2580480 | tf_op jit(solution)/shard_map/merge/pallas_call | solution.py:620
  (42 shorter events, 0.2 us)
Async XLA Ops:
  0.6 23.0 %collective-permute-start.5 = (bf16[288,1280]{1,0:T(8,128)(2,1)}, bf16[288,1280]{1,0:T(8,128)(2,1)S(1)}, u32[]{:S(2)}, u32[]{:S(2)}) collective-permute-start(bf16[288,1280]{1,0:T(8,128)(2,1)} %bitcast.12), channel_id=1, source_target_pairs={{0,2},{1,3},{2,0},{3,1},{4,6},{5,7},{6,4},{7,5},{8,10},{33,35},{10... | collective-permute-start | bytes 2211848 | tf_op jit(solution)/shard_map/ppermute | solution.py:70
  2.7 1.0 %copy-start.3 = (bf16[2,144,640]{2,1,0:T(8,128)(2,1)S(1)}, bf16[2,144,640]{2,1,0:T(8,128)(2,1)}, u32[]{:S(2)}) copy-start(bf16[2,144,640]{2,1,0:T(8,128)(2,1)} %key_ref.1) | copy-start | bytes 1105924
  3.7 1.0 %copy-start.4 = (bf16[2,144,640]{2,1,0:T(8,128)(2,1)S(1)}, bf16[2,144,640]{2,1,0:T(8,128)(2,1)}, u32[]{:S(2)}) copy-start(bf16[2,144,640]{2,1,0:T(8,128)(2,1)} %value_ref.1) | copy-start | bytes 1105924
  4.8 7.4 %collective-permute-start = (bf16[2,2,144,128]{3,2,1,0:T(8,128)(2,1)S(1)}, bf16[2,2,144,128]{3,2,1,0:T(8,128)(2,1)S(1)}, u32[]{:S(2)}, u32[]{:S(2)}) collective-permute-start(bf16[2,2,144,128]{3,2,1,0:T(8,128)(2,1)S(1)} %get-tuple-element.41), channel_id=1, source_target_pairs={{0,96},{1,25},{2,98},{3,27},{4,100},{5,29},{6,102},{7,31},{8,104},... | collective-permute-start | bytes 442376 | tf_op jit(solution)/shard_map/ppermute | solution.py:70
  7.9 6.8 %collective-permute-start.1 = (bf16[2,2,144,128]{3,2,1,0:T(8,128)(2,1)S(1)}, bf16[2,2,144,128]{3,2,1,0:T(8,128)(2,1)S(1)}, u32[]{:S(2)}, u32[]{:S(2)}) collective-permute-start(bf16[2,2,144,128]{3,2,1,0:T(8,128)(2,1)S(1)} %get-tuple-element.42), channel_id=1, source_target_pairs={{0,64},{1,17},{2,66},{3,19},{4,68},{5,21},{6,70},{7,23},{8,72},{33... | collective-permute-start | bytes 442376 | tf_op jit(solution)/shard_map/ppermute | solution.py:70
  8.5 7.6 %collective-permute-start.2 = (bf16[2,2,144,128]{3,2,1,0:T(8,128)(2,1)S(1)}, bf16[2,2,144,128]{3,2,1,0:T(8,128)(2,1)S(1)}, u32[]{:S(2)}, u32[]{:S(2)}) collective-permute-start(bf16[2,2,144,128]{3,2,1,0:T(8,128)(2,1)S(1)} %get-tuple-element.43), channel_id=1, source_target_pairs={{0,32},{1,9},{2,34},{3,11},{4,36},{5,13},{6,38},{7,15},{8,40},{33,... | collective-permute-start | bytes 442376 | tf_op jit(solution)/shard_map/ppermute | solution.py:70
  9.5 21.0 %collective-permute-start.4 = (bf16[288,1280]{1,0:T(8,128)(2,1)}, bf16[288,1280]{1,0:T(8,128)(2,1)S(1)}, u32[]{:S(2)}, u32[]{:S(2)}) collective-permute-start(bf16[288,1280]{1,0:T(8,128)(2,1)} %bitcast.13), channel_id=1, source_target_pairs={{0,1},{1,0},{2,3},{3,2},{4,5},{5,4},{6,7},{7,6},{8,9},{33,32},{10,... | collective-permute-start | bytes 2211848 | tf_op jit(solution)/shard_map/ppermute | solution.py:70
  16.2 13.2 %collective-permute-start.7 = (bf16[2,2,720,128]{3,2,1,0:T(8,128)(2,1)S(1)}, bf16[2,2,720,128]{3,2,1,0:T(8,128)(2,1)S(1)}, u32[]{:S(2)}, u32[]{:S(2)}) collective-permute-start(bf16[2,2,720,128]{3,2,1,0:T(8,128)(2,1)S(1)} %assemble.1.after.refs_4_), channel_id=1, source_target_pairs={{0,8},{1,33},{2,10},{3,35},{4,12},{5,37},{6,14},{7,39},{8,0},{33,1... | collective-permute-start | bytes 2211848 | tf_op jit(solution)/shard_map/ppermute | solution.py:70
  17.8 1.1 %copy-start = (bf16[2,144,1280]{2,1,0:T(8,128)(2,1)S(1)}, bf16[2,144,1280]{2,1,0:T(8,128)(2,1)}, u32[]{:S(2)}) copy-start(bf16[2,144,1280]{2,1,0:T(8,128)(2,1)} %param.12) | copy-start | bytes 2211844
  18.9 0.8 copy-start.7
  19.6 0.8 copy-start.8
  20.4 0.7 copy-start.11
  21.1 0.7 copy-start.12
  22.7 0.9 copy-start.1
  23.6 6.9 %collective-permute-start.6 = (bf16[288,1280]{1,0:T(8,128)(2,1)S(1)}, bf16[288,1280]{1,0:T(8,128)(2,1)}, u32[]{:S(2)}, u32[]{:S(2)}) collective-permute-start(bf16[288,1280]{1,0:T(8,128)(2,1)S(1)} %collective-permute-done.5.h2), channel_id=1, source_target_pairs={{0,1},{1,0},{2,3},{3,2},{4,5},{5,4},{6,7},{7,6},{8,9},{33,32},{10,... | collective-permute-start | bytes 2211848 | tf_op jit(solution)/shard_map/ppermute | solution.py:70
  23.6 18.7 %collective-permute-start.9 = (bf16[2,2,720,128]{3,2,1,0:T(8,128)(2,1)S(1)}, bf16[2,2,720,128]{3,2,1,0:T(8,128)(2,1)S(1)}, u32[]{:S(2)}, u32[]{:S(2)}) collective-permute-start(bf16[2,2,720,128]{3,2,1,0:T(8,128)(2,1)S(1)} %assemble.1.after.refs_4_), channel_id=1, source_target_pairs={{0,24},{1,97},{2,26},{3,99},{4,28},{5,101},{6,30},{7,103},{8,16},{... | collective-permute-start | bytes 2211848 | tf_op jit(solution)/shard_map/ppermute | solution.py:70
  25.8 22.9 %collective-permute-start.3 = (bf16[2,2,720,128]{3,2,1,0:T(8,128)(2,1)S(1)}, bf16[2,2,720,128]{3,2,1,0:T(8,128)(2,1)S(1)}, u32[]{:S(2)}, u32[]{:S(2)}) collective-permute-start(bf16[2,2,720,128]{3,2,1,0:T(8,128)(2,1)S(1)} %assemble.1.after.refs_4_), channel_id=1, source_target_pairs={{0,4},{1,5},{2,6},{3,7},{4,0},{5,1},{6,2},{7,3},{8,12},{33,37},{10... | collective-permute-start | bytes 2211848 | tf_op jit(solution)/shard_map/ppermute | solution.py:70
  29.4 17.5 %collective-permute-start.8 = (bf16[2,2,720,128]{3,2,1,0:T(8,128)(2,1)S(1)}, bf16[2,2,720,128]{3,2,1,0:T(8,128)(2,1)S(1)}, u32[]{:S(2)}, u32[]{:S(2)}) collective-permute-start(bf16[2,2,720,128]{3,2,1,0:T(8,128)(2,1)S(1)} %collective-permute-done.7.refs_5_), channel_id=1, source_target_pairs={{0,24},{1,97},{2,26},{3,99},{4,28},{5,101},{6,30},{7,103},{8,16},{... | collective-permute-start | bytes 2211848 | tf_op jit(solution)/shard_map/ppermute | solution.py:70
  30.5 1.1 %copy-start.2 = (bf16[288,1280]{1,0:T(8,128)(2,1)S(1)}, bf16[288,1280]{1,0:T(8,128)(2,1)}, u32[]{:S(2)}) copy-start(bf16[288,1280]{1,0:T(8,128)(2,1)} %copy-done.1) | copy-start | bytes 2211844
  31.7 7.8 %copy-start.13 = (bf16[5120,640]{1,0:T(8,128)(2,1)S(1)}, bf16[5120,640]{1,0:T(8,128)(2,1)}, u32[]{:S(2)}) copy-start(bf16[5120,640]{1,0:T(8,128)(2,1)} %param.16) | copy-start | bytes 19660804
  31.7 12.6 %slice-start = ((s8[6553600]{0:T(1024)(128)(4,1)}), s8[2359296]{0:T(1024)(128)(4,1)S(1)}, s32[]{:S(2)}) async-start(s8[6553600]{0:T(1024)(128)(4,1)} %bitcast.17), calls=%async_computation | async-start | bytes 4718592
  39.5 4.8 %slice-start.1 = ((s8[6553600]{0:T(1024)(128)(4,1)}), s8[4194304]{0:T(1024)(128)(4,1)S(1)}, s32[]{:S(2)}) async-start(s8[6553600]{0:T(1024)(128)(4,1)} %bitcast.17), calls=%async_computation.1 | async-start | bytes 8388608
  42.3 4.6 %copy-start.9 = (f32[640]{0:T(1024)S(1)}, f32[640]{0:T(1024)}, u32[]{:S(2)}) copy-start(f32[640]{0:T(1024)} %qg.1) | copy-start | bytes 7684
  42.3 4.6 %copy-start.10 = (f32[640]{0:T(1024)S(1)}, f32[640]{0:T(1024)}, u32[]{:S(2)}) copy-start(f32[640]{0:T(1024)} %kg.1) | copy-start | bytes 7684
  42.3 4.5 %collective-permute-start.10 = (f32[8,384]{1,0:T(8,128)S(1)}, f32[8,384]{1,0:T(8,128)S(1)}, u32[]{:S(2)}, u32[]{:S(2)}) collective-permute-start(f32[8,384]{1,0:T(8,128)S(1)} %sum_squares.1.s0), channel_id=1, source_target_pairs={{0,3},{1,2},{2,1},{3,0},{4,7},{5,6},{6,5},{7,4},{8,11},{33,34},{10... | collective-permute-start | bytes 36872 | tf_op jit(solution)/shard_map/ppermute | solution.py:70
  42.4 4.4 %collective-permute-start.11 = (f32[8,384]{1,0:T(8,128)S(1)}, f32[8,384]{1,0:T(8,128)S(1)}, u32[]{:S(2)}, u32[]{:S(2)}) collective-permute-start(f32[8,384]{1,0:T(8,128)S(1)} %sum_squares.1.s0), channel_id=1, source_target_pairs={{0,2},{1,3},{2,0},{3,1},{4,6},{5,7},{6,4},{7,5},{8,10},{33,35},{10... | collective-permute-start | bytes 36872 | tf_op jit(solution)/shard_map/ppermute | solution.py:70
  43.6 3.2 %collective-permute-start.12 = (f32[8,384]{1,0:T(8,128)S(1)}, f32[8,384]{1,0:T(8,128)S(1)}, u32[]{:S(2)}, u32[]{:S(2)}) collective-permute-start(f32[8,384]{1,0:T(8,128)S(1)} %sum_squares.1.s0), channel_id=1, source_target_pairs={{0,1},{1,0},{2,3},{3,2},{4,5},{5,4},{6,7},{7,6},{8,9},{33,32},{10,... | collective-permute-start | bytes 36872 | tf_op jit(solution)/shard_map/ppermute | solution.py:70
  46.8 41.9 %copy-start.5 = (bf16[288,640]{1,0:T(8,128)(2,1)}, bf16[288,640]{1,0:T(8,128)(2,1)S(1)}, u32[]{:S(2)}) copy-start(bf16[288,640]{1,0:T(8,128)(2,1)S(1)} %convolution_convert_fusion.v_ref) | copy-start | bytes 1105924
  48.7 24.7 %collective-permute-start.16 = (bf16[2,2,720,128]{3,2,1,0:T(8,128)(2,1)S(1)}, bf16[2,2,720,128]{3,2,1,0:T(8,128)(2,1)S(1)}, u32[]{:S(2)}, u32[]{:S(2)}) collective-permute-start(bf16[2,2,720,128]{3,2,1,0:T(8,128)(2,1)S(1)} %collective-permute-done.3.refs_8_), channel_id=1, source_target_pairs={{0,8},{1,33},{2,10},{3,35},{4,12},{5,37},{6,14},{7,39},{8,0},{33,1... | collective-permute-start | bytes 2211848 | tf_op jit(solution)/shard_map/ppermute | solution.py:70
  48.9 24.5 %collective-permute-start.17 = (bf16[2,2,720,128]{3,2,1,0:T(8,128)(2,1)S(1)}, bf16[2,2,720,128]{3,2,1,0:T(8,128)(2,1)S(1)}, u32[]{:S(2)}, u32[]{:S(2)}) collective-permute-start(bf16[2,2,720,128]{3,2,1,0:T(8,128)(2,1)S(1)} %collective-permute-done.3.refs_8_), channel_id=1, source_target_pairs={{0,24},{1,97},{2,26},{3,99},{4,28},{5,101},{6,30},{7,103},{8,16},{... | collective-permute-start | bytes 2211848 | tf_op jit(solution)/shard_map/ppermute | solution.py:70
  51.4 22.0 %collective-permute-start.18 = (bf16[2,2,720,128]{3,2,1,0:T(8,128)(2,1)S(1)}, bf16[2,2,720,128]{3,2,1,0:T(8,128)(2,1)S(1)}, u32[]{:S(2)}, u32[]{:S(2)}) collective-permute-start(bf16[2,2,720,128]{3,2,1,0:T(8,128)(2,1)S(1)} %collective-permute-done.8.refs_7_), channel_id=1, source_target_pairs={{0,4},{1,5},{2,6},{3,7},{4,0},{5,1},{6,2},{7,3},{8,12},{33,37},{10... | collective-permute-start | bytes 2211848 | tf_op jit(solution)/shard_map/ppermute | solution.py:70
  53.6 6.8 %collective-permute-start.13 = (bf16[2,2,144,128]{3,2,1,0:T(8,128)(2,1)S(1)}, bf16[2,2,144,128]{3,2,1,0:T(8,128)(2,1)S(1)}, u32[]{:S(2)}, u32[]{:S(2)}) collective-permute-start(bf16[2,2,144,128]{3,2,1,0:T(8,128)(2,1)S(1)} %get-tuple-element.65.refs_3_), channel_id=1, source_target_pairs={{0,96},{1,25},{2,98},{3,27},{4,100},{5,29},{6,102},{7,31},{8,104},... | collective-permute-start | bytes 442376 | tf_op jit(solution)/shard_map/ppermute | solution.py:70
  54.1 8.3 %collective-permute-start.14 = (bf16[2,2,144,128]{3,2,1,0:T(8,128)(2,1)S(1)}, bf16[2,2,144,128]{3,2,1,0:T(8,128)(2,1)S(1)}, u32[]{:S(2)}, u32[]{:S(2)}) collective-permute-start(bf16[2,2,144,128]{3,2,1,0:T(8,128)(2,1)S(1)} %get-tuple-element.64.refs_2_), channel_id=1, source_target_pairs={{0,64},{1,17},{2,66},{3,19},{4,68},{5,21},{6,70},{7,23},{8,72},{33... | collective-permute-start | bytes 442376 | tf_op jit(solution)/shard_map/ppermute | solution.py:70
  60.4 6.4 %collective-permute-start.15 = (bf16[2,2,144,128]{3,2,1,0:T(8,128)(2,1)S(1)}, bf16[2,2,144,128]{3,2,1,0:T(8,128)(2,1)S(1)}, u32[]{:S(2)}, u32[]{:S(2)}) collective-permute-start(bf16[2,2,144,128]{3,2,1,0:T(8,128)(2,1)S(1)} %get-tuple-element.63.refs_1_), channel_id=1, source_target_pairs={{0,32},{1,9},{2,34},{3,11},{4,36},{5,13},{6,38},{7,15},{8,40},{33,... | collective-permute-start | bytes 442376 | tf_op jit(solution)/shard_map/ppermute | solution.py:70
  60.4 1.0 %copy-start.6 = (bf16[288,640]{1,0:T(8,128)(2,1)S(1)}, bf16[288,640]{1,0:T(8,128)(2,1)}, u32[]{:S(2)}) copy-start(bf16[288,640]{1,0:T(8,128)(2,1)} %get-tuple-element.60.k_ref) | copy-start | bytes 1105924
  78.2 5.3 %collective-permute-start.19 = (bf16[2,304,128]{2,1,0:T(8,128)(2,1)S(1)}, bf16[2,304,128]{2,1,0:T(8,128)(2,1)S(1)}, u32[]{:S(2)}, u32[]{:S(2)}) collective-permute-start(bf16[2,304,128]{2,1,0:T(8,128)(2,1)S(1)} %get-tuple-element.74), channel_id=1, source_target_pairs={{0,96},{1,25},{2,98},{3,27},{4,100},{5,29},{6,102},{7,31},{8,104},... | collective-permute-start | bytes 466952 | tf_op jit(solution)/shard_map/ppermute | solution.py:70
  78.8 6.8 %collective-permute-start.20 = (bf16[2,304,128]{2,1,0:T(8,128)(2,1)S(1)}, bf16[2,304,128]{2,1,0:T(8,128)(2,1)S(1)}, u32[]{:S(2)}, u32[]{:S(2)}) collective-permute-start(bf16[2,304,128]{2,1,0:T(8,128)(2,1)S(1)} %get-tuple-element.75), channel_id=1, source_target_pairs={{0,64},{1,17},{2,66},{3,19},{4,68},{5,21},{6,70},{7,23},{8,72},{33... | collective-permute-start | bytes 466952 | tf_op jit(solution)/shard_map/ppermute | solution.py:70
  79.1 8.1 %collective-permute-start.21 = (bf16[2,304,128]{2,1,0:T(8,128)(2,1)S(1)}, bf16[2,304,128]{2,1,0:T(8,128)(2,1)S(1)}, u32[]{:S(2)}, u32[]{:S(2)}) collective-permute-start(bf16[2,304,128]{2,1,0:T(8,128)(2,1)S(1)} %get-tuple-element.76), channel_id=1, source_target_pairs={{0,32},{1,9},{2,34},{3,11},{4,36},{5,13},{6,38},{7,15},{8,40},{33,... | collective-permute-start | bytes 466952 | tf_op jit(solution)/shard_map/ppermute | solution.py:70

commit v12 on v10

--- a/solution.py
+++ b/solution.py
@@ -664,10 +664,10 @@
     blocks = jnp.stack([tp, tp ^ 1, tp ^ 2, tp ^ 3]).astype(jnp.int32)
     modded, query = modulate(blocks, [own_rows, core_rows, z_rows, cross_rows], cond, mod, w_query)
     key = jnp.dot(modded, w_key, preferred_element_type=F32)
+    near_one, near_three, key = lax.optimization_barrier((near_one, near_three, key))
+    near_two = swap_v(near_one, 3)
     fresh_values = jnp.dot(modded, w_value, preferred_element_type=F32).astype(BF16)
     own_sq = sum_squares(query, key)
-    near_one, near_three, own_sq = lax.optimization_barrier((near_one, near_three, own_sq))
-    near_two = swap_v(near_one, 3)
     squares = [own_sq] + [swap_tp(own_sq, z, c) for z, c in ((1, 1), (1, 0), (0, 1))]
     fresh_values, *squares = lax.optimization_barrier((fresh_values, *squares))
     fresh_keys, *sends = norm_rope(u, query, key, squares, q_gain, k_gain, cos, sin)
@@ -676,11 +676,11 @@
     queries = exchange_u(sends)
     fresh_out, fresh_rows = fresh_attention(u, fresh_keys, fresh_values, sends)
 
-    far_one, near_two, *queries = lax.optimization_barrier((far_one, near_two, *queries))
-    far_two = swap_v(far_one, 3)
-    partial = stale_attention(queries, [near, near_one, near_three, near_two, far, far_one])
+    near_two, fresh_rows = lax.optimization_barrier((near_two, fresh_rows))
+    far_two = swap_z_hi(near_two)
+    partial = stale_attention(queries, [near, near_one, near_three, near_two, far, far_one, far_three])
     outs = stale_attention(
-        queries, [far_three, far_two], near=partial, after=fresh_rows
+        queries, [far_two], near=partial, after=fresh_rows
     )
     returned = exchange_u(outs)
     attended = merge(u, fresh_out, fresh_rows, returned)

time: 91.8 us -> 91.1 us (level); the launches traced: 91.3 us -> 89.6 us
  starting transfers between devices: 28.8 us -> 24 us
  matrix products: 4.95 us -> 7.73 us
    ppermute x22, starting transfers between devices: 28.8 us -> 24 us  [permute(): lax.ppermute(value, AXES, [(linear(*p), linear(*move(*p))) for p in place...]
    dot_general x1, matrix products: 2.48 us -> 5.29 us  [shards(): jnp.dot(modded, w_value, preferred_element_type=F32).astype(BF16)]
    unnamed x28 -> x24, local copies, waits for them, and re-layouts: 6.99 us -> 6.98 us
  transfers between devices with their start and end apart: 22 -> 22, of which waited for: 12 -> 9; matrix products, arithmetic and copies ran while one was open for 6% -> 9% of each run, Pallas kernels for 21% -> 23%
where the time goes in v12:
time: 91.1 us; the launch traced here: 89.6 us
  waiting for transfers between devices  25.4 us (28%)
  Pallas kernels  24.6 us (27%)
  starting transfers between devices  24 us (26%)
  matrix products  7.73 us (8%)
  local copies, waits for them, and re-layouts  6.98 us (8%)
    ppermute x22, waiting for transfers between devices, permute(): lax.ppermute(value, AXES, [(linear(*p), linear(*move(*p))) for p in place...  25.4 us
    ppermute x22, starting transfers between devices, permute(): lax.ppermute(value, AXES, [(linear(*p), linear(*move(*p))) for p in place...  24 us
    pallas_call x2, Pallas kernels, stale_attention(): pl.pallas_call(functools.partial(stale_kernel, far, count), out_shape=out...  11.3 us
    pallas_call x1, Pallas kernels, modulate(): pl.pallas_call(modulate_kernel, out_shape=[jax.ShapeDtypeStruct((ROWS, D)...  7.63 us
    unnamed x24, local copies, waits for them, and re-layouts  6.98 us
    dot_general x1, matrix products, shards(): jnp.dot(modded, w_value, preferred_element_type=F32).astype(BF16)  5.29 us
    dot_general x1, matrix products, shards(): key = jnp.dot(modded, w_key, preferred_element_type=F32)  2.43 us
  transfers between devices with their start and end apart: 22, of which 9 were waited for; matrix products, arithmetic and copies ran while one was open for 9% of the time, Pallas kernels for 23%

profile of v12, /device:TPU:0, one launch (start us, length us, event | category | flops | bytes accessed | tf_op | source)
XLA Modules:
  0.0 89.6 jit_solution(870833071074782653)
XLA Ops:
  0.6 2.1 %collective-permute-start.5 = (bf16[288,1280]{1,0:T(8,128)(2,1)}, bf16[288,1280]{1,0:T(8,128)(2,1)S(1)}, u32[]{:S(2)}, u32[]{:S(2)}) collective-permute-start(bf16[288,1280]{1,0:T(8,128)(2,1)} %bitcast.12), channel_id=1, source_target_pairs={{0,2},{1,3},{2,0},{3,1},{4,6},{5,7},{6,4},{7,5},{8,10},{33,35},{10... | collective-permute-start | bytes 2211848 | tf_op jit(solution)/shard_map/ppermute | solution.py:70
  2.7 1.0 %copy-done.1 = bf16[2,144,640]{2,1,0:T(8,128)(2,1)S(1)} copy-done((bf16[2,144,640]{2,1,0:T(8,128)(2,1)S(1)}, bf16[2,144,640]{2,1,0:T(8,128)(2,1)}, u32[]{:S(2)}) %copy-start.1) | copy-done | bytes 368664
  3.7 1.0 %copy-done.2 = bf16[2,144,640]{2,1,0:T(8,128)(2,1)S(1)} copy-done((bf16[2,144,640]{2,1,0:T(8,128)(2,1)S(1)}, bf16[2,144,640]{2,1,0:T(8,128)(2,1)}, u32[]{:S(2)}) %copy-start.2) | copy-done | bytes 368664
  4.7 0.1 pack_stale.1
  4.8 3.1 %collective-permute-start = (bf16[2,2,144,128]{3,2,1,0:T(8,128)(2,1)S(1)}, bf16[2,2,144,128]{3,2,1,0:T(8,128)(2,1)S(1)}, u32[]{:S(2)}, u32[]{:S(2)}) collective-permute-start(bf16[2,2,144,128]{3,2,1,0:T(8,128)(2,1)S(1)} %get-tuple-element.43), channel_id=1, source_target_pairs={{0,96},{1,25},{2,98},{3,27},{4,100},{5,29},{6,102},{7,31},{8,104},... | collective-permute-start | bytes 442376 | tf_op jit(solution)/shard_map/ppermute | solution.py:70
  7.9 0.6 collective-permute-start.1
  8.5 1.0 %collective-permute-start.2 = (bf16[2,2,144,128]{3,2,1,0:T(8,128)(2,1)S(1)}, bf16[2,2,144,128]{3,2,1,0:T(8,128)(2,1)S(1)}, u32[]{:S(2)}, u32[]{:S(2)}) collective-permute-start(bf16[2,2,144,128]{3,2,1,0:T(8,128)(2,1)S(1)} %get-tuple-element.45), channel_id=1, source_target_pairs={{0,32},{1,9},{2,34},{3,11},{4,36},{5,13},{6,38},{7,15},{8,40},{33,... | collective-permute-start | bytes 442376 | tf_op jit(solution)/shard_map/ppermute | solution.py:70
  9.5 2.7 %collective-permute-done.refs_1_ = bf16[2,2,144,128]{3,2,1,0:T(8,128)(2,1)S(1)} collective-permute-done((bf16[2,2,144,128]{3,2,1,0:T(8,128)(2,1)S(1)}, bf16[2,2,144,128]{3,2,1,0:T(8,128)(2,1)S(1)}, u32[]{:S(2)}, u32[]{:S(2)}) %collective-permute-start) | collective-permute-done | bytes 147488 | tf_op jit(solution)/shard_map/ppermute | solution.py:70
  12.2 2.5 %collective-permute-done.1.refs_2_ = bf16[2,2,144,128]{3,2,1,0:T(8,128)(2,1)S(1)} collective-permute-done((bf16[2,2,144,128]{3,2,1,0:T(8,128)(2,1)S(1)}, bf16[2,2,144,128]{3,2,1,0:T(8,128)(2,1)S(1)}, u32[]{:S(2)}, u32[]{:S(2)}) %collective-permute-start.1) | collective-permute-done | bytes 147488 | tf_op jit(solution)/shard_map/ppermute | solution.py:70
  14.7 1.5 %collective-permute-done.2.refs_3_ = bf16[2,2,144,128]{3,2,1,0:T(8,128)(2,1)S(1)} collective-permute-done((bf16[2,2,144,128]{3,2,1,0:T(8,128)(2,1)S(1)}, bf16[2,2,144,128]{3,2,1,0:T(8,128)(2,1)S(1)}, u32[]{:S(2)}, u32[]{:S(2)}) %collective-permute-start.2) | collective-permute-done | bytes 147488 | tf_op jit(solution)/shard_map/ppermute | solution.py:70
  16.2 1.1 %copy-done = bf16[2,144,1280]{2,1,0:T(8,128)(2,1)S(1)} copy-done((bf16[2,144,1280]{2,1,0:T(8,128)(2,1)S(1)}, bf16[2,144,1280]{2,1,0:T(8,128)(2,1)}, u32[]{:S(2)}) %copy-start) | copy-done | bytes 737304
  17.3 0.8 copy-done.5
  18.1 0.8 copy-done.6
  18.9 0.7 copy-done.9
  19.5 0.7 copy-done.10
  20.2 0.9 %tables.1 = (f32[288,128]{1,0:T(8,128)S(1)}, f32[144,128]{1,0:T(8,128)S(1)}, f32[144,128]{1,0:T(8,128)S(1)}, f32[4,5120]{1,0:T(4,128)S(1)}, bf16[288,1280]{1,0:T(8,128)(2,1)S(1)}) custom-call(s32[144]{0:T(256)S(1)} %copy-done.9, f32[1,128]{1,0:T(1,128)S(1)} %copy-done.10, bf16[288,1280]{1,0:T(8,128)(2,1)S(1)} %bitcast.14, f32[2,5120]{1,0:T(2,128)S(1)} %copy-done.5, ...), custom_call_target="tpu_custom_call" | custom-call | flops 1843200 | bytes 1000000 | tf_op jit(solution)/shard_map/tables/pallas_call | solution.py:177
  21.2 0.1 collective-permute-start.6
  21.3 1.6 %collective-permute-start.7 = (bf16[2,2,720,128]{3,2,1,0:T(8,128)(2,1)S(1)}, bf16[2,2,720,128]{3,2,1,0:T(8,128)(2,1)S(1)}, u32[]{:S(2)}, u32[]{:S(2)}) collective-permute-start(bf16[2,2,720,128]{3,2,1,0:T(8,128)(2,1)S(1)} %assemble.1.after.refs_4_), channel_id=1, source_target_pairs={{0,8},{1,33},{2,10},{3,35},{4,12},{5,37},{6,14},{7,39},{8,0},{33,1... | collective-permute-start | bytes 2211848 | tf_op jit(solution)/shard_map/ppermute | solution.py:70
  22.8 2.1 %collective-permute-start.8 = (bf16[2,2,720,128]{3,2,1,0:T(8,128)(2,1)S(1)}, bf16[2,2,720,128]{3,2,1,0:T(8,128)(2,1)S(1)}, u32[]{:S(2)}, u32[]{:S(2)}) collective-permute-start(bf16[2,2,720,128]{3,2,1,0:T(8,128)(2,1)S(1)} %assemble.1.after.refs_4_), channel_id=1, source_target_pairs={{0,24},{1,97},{2,26},{3,99},{4,28},{5,101},{6,30},{7,103},{8,16},{... | collective-permute-start | bytes 2211848 | tf_op jit(solution)/shard_map/ppermute | solution.py:70
  24.9 0.1 pad_add_fusion.t_ref
  25.0 3.6 %collective-permute-start.3 = (bf16[2,2,720,128]{3,2,1,0:T(8,128)(2,1)S(1)}, bf16[2,2,720,128]{3,2,1,0:T(8,128)(2,1)S(1)}, u32[]{:S(2)}, u32[]{:S(2)}) collective-permute-start(bf16[2,2,720,128]{3,2,1,0:T(8,128)(2,1)S(1)} %assemble.1.after.refs_4_), channel_id=1, source_target_pairs={{0,4},{1,5},{2,6},{3,7},{4,0},{5,1},{6,2},{7,3},{8,12},{33,37},{10... | collective-permute-start | bytes 2211848 | tf_op jit(solution)/shard_map/ppermute | solution.py:70
  28.6 7.6 %modulate.1 = (bf16[288,5120]{1,0:T(8,128)(2,1)S(1)}, f32[288,640]{1,0:T(8,128)S(1)}) custom-call(s32[4]{0:T(128)S(1)} %pad_add_fusion.t_ref, bf16[288,1280]{1,0:T(8,128)(2,1)S(1)} %get-tuple-element.47.h0, bf16[288,1280]{1,0:T(8,128)(2,1)S(1)} %collective-permute-done.4.h1, bf16[288,1280]{1,0:T(8,128)(2,1)S(1)} %collective-permute-done.5.h2, ...), custom_call_target="tpu_custom_call" | custom-call | flops 1000 | bytes 30000000 | tf_op jit(solution)/shard_map/modulate/pallas_call | solution.py:275
  36.3 2.4 %fusion.k_ref = f32[288,640]{1,0:T(8,128)S(1)} fusion(bf16[288,5120]{1,0:T(8,128)(2,1)S(1)} %get-tuple-element.53, bf16[5120,640]{1,0:T(8,128)(2,1)S(1)} %copy-done.11), kind=kOutput, calls=%fused_computation.2 | convolution fusion | flops 1887436800 | bytes 10240000 | tf_op jit(solution)/shard_map/dot_general | solution.py:666
  38.7 1.2 %collective-permute-start.12 = (bf16[2,2,720,128]{3,2,1,0:T(8,128)(2,1)S(1)}, bf16[2,2,720,128]{3,2,1,0:T(8,128)(2,1)S(1)}, u32[]{:S(2)}, u32[]{:S(2)}) collective-permute-start(bf16[2,2,720,128]{3,2,1,0:T(8,128)(2,1)S(1)} %collective-permute-done.7.refs_5_), channel_id=1, source_target_pairs={{0,24},{1,97},{2,26},{3,99},{4,28},{5,101},{6,30},{7,103},{8,16},{... | collective-permute-start | bytes 2211848 | tf_op jit(solution)/shard_map/ppermute | solution.py:70
  40.0 0.2 sum_squares.1.s0
  40.2 0.1 collective-permute-start.10
  40.2 0.1 collective-permute-start.11
  40.3 2.0 %collective-permute-start.9 = (f32[8,384]{1,0:T(8,128)S(1)}, f32[8,384]{1,0:T(8,128)S(1)}, u32[]{:S(2)}, u32[]{:S(2)}) collective-permute-start(f32[8,384]{1,0:T(8,128)S(1)} %sum_squares.1.s0), channel_id=1, source_target_pairs={{0,3},{1,2},{2,1},{3,0},{4,7},{5,6},{6,5},{7,4},{8,11},{33,34},{10... | collective-permute-start | bytes 36872 | tf_op jit(solution)/shard_map/ppermute | solution.py:70
  42.4 5.3 %convolution_convert_fusion.v_ref = bf16[288,640]{1,0:T(8,128)(2,1)S(1)} fusion(bf16[288,5120]{1,0:T(8,128)(2,1)S(1)} %get-tuple-element.53, bf16[5120,640]{1,0:T(8,128)(2,1)} %param.17), kind=kOutput, calls=%fused_computation | convolution fusion | flops 1887621120 | bytes 9871360 | tf_op jit(solution)/shard_map/dot_general | solution.py:669
  47.7 0.0 copy-start.3
  47.7 1.8 %norm_rope.1 = (bf16[288,640]{1,0:T(8,128)(2,1)}, bf16[2,2,144,128]{3,2,1,0:T(8,128)(2,1)S(1)}, bf16[2,2,144,128]{3,2,1,0:T(8,128)(2,1)S(1)}, bf16[2,2,144,128]{...) custom-call(s32[1]{0:T(128)} %bitcast.u_ref, f32[288,640]{1,0:T(8,128)S(1)} %get-tuple-element.52.q_ref, ...), custom_call_target="tpu_custom_call" | custom-call | flops 1000 | bytes 1000 | tf_op jit(solution)/shard_map/norm_rope/pallas_call | solution.py:348
  49.5 2.1 %collective-permute-start.18 = (bf16[2,2,720,128]{3,2,1,0:T(8,128)(2,1)S(1)}, bf16[2,2,720,128]{3,2,1,0:T(8,128)(2,1)S(1)}, u32[]{:S(2)}, u32[]{:S(2)}) collective-permute-start(bf16[2,2,720,128]{3,2,1,0:T(8,128)(2,1)S(1)} %collective-permute-done.3.refs_8_), channel_id=1, source_target_pairs={{0,24},{1,97},{2,26},{3,99},{4,28},{5,101},{6,30},{7,103},{8,16},{... | collective-permute-start | bytes 2211848 | tf_op jit(solution)/shard_map/ppermute | solution.py:70
  51.6 1.0 %copy-done.4 = bf16[288,640]{1,0:T(8,128)(2,1)S(1)} copy-done((bf16[288,640]{1,0:T(8,128)(2,1)S(1)}, bf16[288,640]{1,0:T(8,128)(2,1)}, u32[]{:S(2)}) %copy-start.4) | copy-done | bytes 368664
  52.6 1.0 %fresh_attention.1 = (f32[2,5,144,128]{3,2,1,0:T(8,128)S(1)}, f32[24,128]{1,0:T(8,128)S(1)}) custom-call(s32[1]{0:T(128)} %bitcast.u_ref, bf16[288,640]{1,0:T(8,128)(2,1)S(1)} %copy-done.4, bf16[288,640]{1,0:T(8,128)(2,1)S(1)} %convolution_convert_fusion.v_ref, bf16[2,2,144,128]{3,2,1,0:T(8,128)(2,1)S(1)} %get-tuple-element.64.refs_0_, ...), custom_call_target="tpu_custom_call" | custom-call | flops 1000 | bytes 1000 | tf_op jit(solution)/shard_map/fresh_attention/pallas_call | solution.py:398
  53.7 0.3 collective-permute-start.16
  54.0 1.2 %collective-permute-start.13 = (bf16[2,2,144,128]{3,2,1,0:T(8,128)(2,1)S(1)}, bf16[2,2,144,128]{3,2,1,0:T(8,128)(2,1)S(1)}, u32[]{:S(2)}, u32[]{:S(2)}) collective-permute-start(bf16[2,2,144,128]{3,2,1,0:T(8,128)(2,1)S(1)} %get-tuple-element.67.refs_3_), channel_id=1, source_target_pairs={{0,96},{1,25},{2,98},{3,27},{4,100},{5,29},{6,102},{7,31},{8,104},... | collective-permute-start | bytes 442376 | tf_op jit(solution)/shard_map/ppermute | solution.py:70
  55.2 0.6 collective-permute-start.14
  55.8 5.0 %collective-permute-done.13.refs_1_ = bf16[2,2,144,128]{3,2,1,0:T(8,128)(2,1)S(1)} collective-permute-done((bf16[2,2,144,128]{3,2,1,0:T(8,128)(2,1)S(1)}, bf16[2,2,144,128]{3,2,1,0:T(8,128)(2,1)S(1)}, u32[]{:S(2)}, u32[]{:S(2)}) %collective-permute-start.13) | collective-permute-done | bytes 147488 | tf_op jit(solution)/shard_map/ppermute | solution.py:70
  60.8 1.6 %collective-permute-done.14.refs_2_ = bf16[2,2,144,128]{3,2,1,0:T(8,128)(2,1)S(1)} collective-permute-done((bf16[2,2,144,128]{3,2,1,0:T(8,128)(2,1)S(1)}, bf16[2,2,144,128]{3,2,1,0:T(8,128)(2,1)S(1)}, u32[]{:S(2)}, u32[]{:S(2)}) %collective-permute-start.14) | collective-permute-done | bytes 147488 | tf_op jit(solution)/shard_map/ppermute | solution.py:70
  62.3 4.8 %collective-permute-done.15.refs_3_ = bf16[2,2,144,128]{3,2,1,0:T(8,128)(2,1)S(1)} collective-permute-done((bf16[2,2,144,128]{3,2,1,0:T(8,128)(2,1)S(1)}, bf16[2,2,144,128]{3,2,1,0:T(8,128)(2,1)S(1)}, u32[]{:S(2)}, u32[]{:S(2)}) %collective-permute-start.15) | collective-permute-done | bytes 147488 | tf_op jit(solution)/shard_map/ppermute | solution.py:70
  67.2 8.8 %near_attention.1 = (f32[2,4,2,144,128]{4,3,2,1,0:T(8,128)S(1)}, f32[2,4,2,144,128]{4,3,2,1,0:T(8,128)S(1)}) custom-call(bf16[2,2,144,128]{3,2,1,0:T(8,128)(2,1)S(1)} %get-tuple-element.64.refs_0_, bf16[2,2,144,128]{3,2,1,0:T(8,128)(2,1)S(1)} %collective-permute-done.13.refs_1_, bf16[2,2,144,128]{3,2,1,0:T(8,128)(2,1)S(1)} %collective-permute-done.14.refs_2_, ...), custom_call_target="tpu_custom_call" | custom-call | flops 1000 | bytes 1000 | tf_op jit(solution)/shard_map/near_attention/pallas_call | solution.py:556
  76.0 2.5 %far_attention.1 = (bf16[2,304,128]{2,1,0:T(8,128)(2,1)S(1)}, bf16[2,304,128]{2,1,0:T(8,128)(2,1)S(1)}, bf16[2,304,128]{2,1,0:T(8,128)(2,1)S(1)}, bf16[2,304,128]{2,1,0:T(8,128)(2,1)S(1)}) custom-call(bf16[2,2,144,128]{3,2,1,0:T(8,128)(2,1)S(1)} %get-tuple-element.64.refs_0_, bf16[2,2,144,128]{3,2,1,0:T(8,128)(2,1)S(1)} %collective-permute-done.13.refs_1_, ...), custom_call_target="tpu_custom_call" | custom-call | flops 1000 | bytes 1000 | tf_op jit(solution)/shard_map/far_attention/pallas_call | solution.py:556
  78.4 1.2 %collective-permute-start.19 = (bf16[2,304,128]{2,1,0:T(8,128)(2,1)S(1)}, bf16[2,304,128]{2,1,0:T(8,128)(2,1)S(1)}, u32[]{:S(2)}, u32[]{:S(2)}) collective-permute-start(bf16[2,304,128]{2,1,0:T(8,128)(2,1)S(1)} %get-tuple-element.78), channel_id=1, source_target_pairs={{0,96},{1,25},{2,98},{3,27},{4,100},{5,29},{6,102},{7,31},{8,104},... | collective-permute-start | bytes 466952 | tf_op jit(solution)/shard_map/ppermute | solution.py:70
  79.7 0.9 %collective-permute-start.21 = (bf16[2,304,128]{2,1,0:T(8,128)(2,1)S(1)}, bf16[2,304,128]{2,1,0:T(8,128)(2,1)S(1)}, u32[]{:S(2)}, u32[]{:S(2)}) collective-permute-start(bf16[2,304,128]{2,1,0:T(8,128)(2,1)S(1)} %get-tuple-element.80), channel_id=1, source_target_pairs={{0,32},{1,9},{2,34},{3,11},{4,36},{5,13},{6,38},{7,15},{8,40},{33,... | collective-permute-start | bytes 466952 | tf_op jit(solution)/shard_map/ppermute | solution.py:70
  80.6 3.1 %collective-permute-done.19.refs_1_ = bf16[2,304,128]{2,1,0:T(8,128)(2,1)S(1)} collective-permute-done((bf16[2,304,128]{2,1,0:T(8,128)(2,1)S(1)}, bf16[2,304,128]{2,1,0:T(8,128)(2,1)S(1)}, u32[]{:S(2)}, u32[]{:S(2)}) %collective-permute-start.19) | collective-permute-done | bytes 155680 | tf_op jit(solution)/shard_map/ppermute | solution.py:70
  83.7 2.8 %collective-permute-done.20.refs_2_ = bf16[2,304,128]{2,1,0:T(8,128)(2,1)S(1)} collective-permute-done((bf16[2,304,128]{2,1,0:T(8,128)(2,1)S(1)}, bf16[2,304,128]{2,1,0:T(8,128)(2,1)S(1)}, u32[]{:S(2)}, u32[]{:S(2)}) %collective-permute-start.20) | collective-permute-done | bytes 155680 | tf_op jit(solution)/shard_map/ppermute | solution.py:70
  86.5 1.6 %collective-permute-done.21.refs_3_ = bf16[2,304,128]{2,1,0:T(8,128)(2,1)S(1)} collective-permute-done((bf16[2,304,128]{2,1,0:T(8,128)(2,1)S(1)}, bf16[2,304,128]{2,1,0:T(8,128)(2,1)S(1)}, u32[]{:S(2)}, u32[]{:S(2)}) %collective-permute-start.21) | collective-permute-done | bytes 155680 | tf_op jit(solution)/shard_map/ppermute | solution.py:70
  88.1 1.5 %merge.1 = bf16[2,144,640]{2,1,0:T(8,128)(2,1)} custom-call(s32[1]{0:T(128)} %bitcast.u_ref, f32[2,5,144,128]{3,2,1,0:T(8,128)S(1)} %get-tuple-element.68.fresh_out, f32[24,128]{1,0:T(8,128)S(1)} %get-tuple-element.71.refs_7_.fresh_rows, bf16[2,304,128]{2,1,0:T(8,128)(2,1)S(1)} %get-tuple-element.77.refs_0_, ...), custom_call_target="tpu_custom_call" | custom-call | flops 1843200 | bytes 2580480 | tf_op jit(solution)/shard_map/merge/pallas_call | solution.py:620
  (33 shorter events, 0.1 us)
Async XLA Ops:
  0.6 20.5 %collective-permute-start.5 = (bf16[288,1280]{1,0:T(8,128)(2,1)}, bf16[288,1280]{1,0:T(8,128)(2,1)S(1)}, u32[]{:S(2)}, u32[]{:S(2)}) collective-permute-start(bf16[288,1280]{1,0:T(8,128)(2,1)} %bitcast.12), channel_id=1, source_target_pairs={{0,2},{1,3},{2,0},{3,1},{4,6},{5,7},{6,4},{7,5},{8,10},{33,35},{10... | collective-permute-start | bytes 2211848 | tf_op jit(solution)/shard_map/ppermute | solution.py:70
  2.7 1.0 %copy-start.1 = (bf16[2,144,640]{2,1,0:T(8,128)(2,1)S(1)}, bf16[2,144,640]{2,1,0:T(8,128)(2,1)}, u32[]{:S(2)}) copy-start(bf16[2,144,640]{2,1,0:T(8,128)(2,1)} %key_ref.1) | copy-start | bytes 1105924
  3.7 1.0 %copy-start.2 = (bf16[2,144,640]{2,1,0:T(8,128)(2,1)S(1)}, bf16[2,144,640]{2,1,0:T(8,128)(2,1)}, u32[]{:S(2)}) copy-start(bf16[2,144,640]{2,1,0:T(8,128)(2,1)} %value_ref.1) | copy-start | bytes 1105924
  4.8 7.4 %collective-permute-start = (bf16[2,2,144,128]{3,2,1,0:T(8,128)(2,1)S(1)}, bf16[2,2,144,128]{3,2,1,0:T(8,128)(2,1)S(1)}, u32[]{:S(2)}, u32[]{:S(2)}) collective-permute-start(bf16[2,2,144,128]{3,2,1,0:T(8,128)(2,1)S(1)} %get-tuple-element.43), channel_id=1, source_target_pairs={{0,96},{1,25},{2,98},{3,27},{4,100},{5,29},{6,102},{7,31},{8,104},... | collective-permute-start | bytes 442376 | tf_op jit(solution)/shard_map/ppermute | solution.py:70
  7.9 6.8 %collective-permute-start.1 = (bf16[2,2,144,128]{3,2,1,0:T(8,128)(2,1)S(1)}, bf16[2,2,144,128]{3,2,1,0:T(8,128)(2,1)S(1)}, u32[]{:S(2)}, u32[]{:S(2)}) collective-permute-start(bf16[2,2,144,128]{3,2,1,0:T(8,128)(2,1)S(1)} %get-tuple-element.44), channel_id=1, source_target_pairs={{0,64},{1,17},{2,66},{3,19},{4,68},{5,21},{6,70},{7,23},{8,72},{33... | collective-permute-start | bytes 442376 | tf_op jit(solution)/shard_map/ppermute | solution.py:70
  8.5 7.6 %collective-permute-start.2 = (bf16[2,2,144,128]{3,2,1,0:T(8,128)(2,1)S(1)}, bf16[2,2,144,128]{3,2,1,0:T(8,128)(2,1)S(1)}, u32[]{:S(2)}, u32[]{:S(2)}) collective-permute-start(bf16[2,2,144,128]{3,2,1,0:T(8,128)(2,1)S(1)} %get-tuple-element.45), channel_id=1, source_target_pairs={{0,32},{1,9},{2,34},{3,11},{4,36},{5,13},{6,38},{7,15},{8,40},{33,... | collective-permute-start | bytes 442376 | tf_op jit(solution)/shard_map/ppermute | solution.py:70
  9.5 19.1 %collective-permute-start.4 = (bf16[288,1280]{1,0:T(8,128)(2,1)}, bf16[288,1280]{1,0:T(8,128)(2,1)S(1)}, u32[]{:S(2)}, u32[]{:S(2)}) collective-permute-start(bf16[288,1280]{1,0:T(8,128)(2,1)} %bitcast.13), channel_id=1, source_target_pairs={{0,1},{1,0},{2,3},{3,2},{4,5},{5,4},{6,7},{7,6},{8,9},{33,32},{10,... | collective-permute-start | bytes 2211848 | tf_op jit(solution)/shard_map/ppermute | solution.py:70
  16.2 1.1 %copy-start = (bf16[2,144,1280]{2,1,0:T(8,128)(2,1)S(1)}, bf16[2,144,1280]{2,1,0:T(8,128)(2,1)}, u32[]{:S(2)}) copy-start(bf16[2,144,1280]{2,1,0:T(8,128)(2,1)} %param.12) | copy-start | bytes 2211844
  17.3 0.8 copy-start.5
  18.1 0.8 copy-start.6
  18.9 0.7 copy-start.9
  19.5 0.7 copy-start.10
  21.2 7.5 %collective-permute-start.6 = (bf16[288,1280]{1,0:T(8,128)(2,1)S(1)}, bf16[288,1280]{1,0:T(8,128)(2,1)}, u32[]{:S(2)}, u32[]{:S(2)}) collective-permute-start(bf16[288,1280]{1,0:T(8,128)(2,1)S(1)} %collective-permute-done.5.h2), channel_id=1, source_target_pairs={{0,1},{1,0},{2,3},{3,2},{4,5},{5,4},{6,7},{7,6},{8,9},{33,32},{10,... | collective-permute-start | bytes 2211848 | tf_op jit(solution)/shard_map/ppermute | solution.py:70
  21.3 15.0 %copy-start.11 = (bf16[5120,640]{1,0:T(8,128)(2,1)S(1)}, bf16[5120,640]{1,0:T(8,128)(2,1)}, u32[]{:S(2)}) copy-start(bf16[5120,640]{1,0:T(8,128)(2,1)} %param.16) | copy-start | bytes 19660804
  21.3 17.4 %collective-permute-start.7 = (bf16[2,2,720,128]{3,2,1,0:T(8,128)(2,1)S(1)}, bf16[2,2,720,128]{3,2,1,0:T(8,128)(2,1)S(1)}, u32[]{:S(2)}, u32[]{:S(2)}) collective-permute-start(bf16[2,2,720,128]{3,2,1,0:T(8,128)(2,1)S(1)} %assemble.1.after.refs_4_), channel_id=1, source_target_pairs={{0,8},{1,33},{2,10},{3,35},{4,12},{5,37},{6,14},{7,39},{8,0},{33,1... | collective-permute-start | bytes 2211848 | tf_op jit(solution)/shard_map/ppermute | solution.py:70
  22.8 15.9 %collective-permute-start.8 = (bf16[2,2,720,128]{3,2,1,0:T(8,128)(2,1)S(1)}, bf16[2,2,720,128]{3,2,1,0:T(8,128)(2,1)S(1)}, u32[]{:S(2)}, u32[]{:S(2)}) collective-permute-start(bf16[2,2,720,128]{3,2,1,0:T(8,128)(2,1)S(1)} %assemble.1.after.refs_4_), channel_id=1, source_target_pairs={{0,24},{1,97},{2,26},{3,99},{4,28},{5,101},{6,30},{7,103},{8,16},{... | collective-permute-start | bytes 2211848 | tf_op jit(solution)/shard_map/ppermute | solution.py:70
  25.0 24.5 %collective-permute-start.3 = (bf16[2,2,720,128]{3,2,1,0:T(8,128)(2,1)S(1)}, bf16[2,2,720,128]{3,2,1,0:T(8,128)(2,1)S(1)}, u32[]{:S(2)}, u32[]{:S(2)}) collective-permute-start(bf16[2,2,720,128]{3,2,1,0:T(8,128)(2,1)S(1)} %assemble.1.after.refs_4_), channel_id=1, source_target_pairs={{0,4},{1,5},{2,6},{3,7},{4,0},{5,1},{6,2},{7,3},{8,12},{33,37},{10... | collective-permute-start | bytes 2211848 | tf_op jit(solution)/shard_map/ppermute | solution.py:70
  38.7 14.9 %collective-permute-start.12 = (bf16[2,2,720,128]{3,2,1,0:T(8,128)(2,1)S(1)}, bf16[2,2,720,128]{3,2,1,0:T(8,128)(2,1)S(1)}, u32[]{:S(2)}, u32[]{:S(2)}) collective-permute-start(bf16[2,2,720,128]{3,2,1,0:T(8,128)(2,1)S(1)} %collective-permute-done.7.refs_5_), channel_id=1, source_target_pairs={{0,24},{1,97},{2,26},{3,99},{4,28},{5,101},{6,30},{7,103},{8,16},{... | collective-permute-start | bytes 2211848 | tf_op jit(solution)/shard_map/ppermute | solution.py:70
  40.2 7.5 %copy-start.7 = (f32[640]{0:T(1024)S(1)}, f32[640]{0:T(1024)}, u32[]{:S(2)}) copy-start(f32[640]{0:T(1024)} %qg.1) | copy-start | bytes 7684
  40.2 7.6 %copy-start.8 = (f32[640]{0:T(1024)S(1)}, f32[640]{0:T(1024)}, u32[]{:S(2)}) copy-start(f32[640]{0:T(1024)} %kg.1) | copy-start | bytes 7684
  40.2 7.5 %collective-permute-start.10 = (f32[8,384]{1,0:T(8,128)S(1)}, f32[8,384]{1,0:T(8,128)S(1)}, u32[]{:S(2)}, u32[]{:S(2)}) collective-permute-start(f32[8,384]{1,0:T(8,128)S(1)} %sum_squares.1.s0), channel_id=1, source_target_pairs={{0,2},{1,3},{2,0},{3,1},{4,6},{5,7},{6,4},{7,5},{8,10},{33,35},{10... | collective-permute-start | bytes 36872 | tf_op jit(solution)/shard_map/ppermute | solution.py:70
  40.2 7.5 %collective-permute-start.11 = (f32[8,384]{1,0:T(8,128)S(1)}, f32[8,384]{1,0:T(8,128)S(1)}, u32[]{:S(2)}, u32[]{:S(2)}) collective-permute-start(f32[8,384]{1,0:T(8,128)S(1)} %sum_squares.1.s0), channel_id=1, source_target_pairs={{0,1},{1,0},{2,3},{3,2},{4,5},{5,4},{6,7},{7,6},{8,9},{33,32},{10,... | collective-permute-start | bytes 36872 | tf_op jit(solution)/shard_map/ppermute | solution.py:70
  40.3 7.4 %collective-permute-start.9 = (f32[8,384]{1,0:T(8,128)S(1)}, f32[8,384]{1,0:T(8,128)S(1)}, u32[]{:S(2)}, u32[]{:S(2)}) collective-permute-start(f32[8,384]{1,0:T(8,128)S(1)} %sum_squares.1.s0), channel_id=1, source_target_pairs={{0,3},{1,2},{2,1},{3,0},{4,7},{5,6},{6,5},{7,4},{8,11},{33,34},{10... | collective-permute-start | bytes 36872 | tf_op jit(solution)/shard_map/ppermute | solution.py:70
  47.7 41.9 %copy-start.3 = (bf16[288,640]{1,0:T(8,128)(2,1)}, bf16[288,640]{1,0:T(8,128)(2,1)S(1)}, u32[]{:S(2)}) copy-start(bf16[288,640]{1,0:T(8,128)(2,1)S(1)} %convolution_convert_fusion.v_ref) | copy-start | bytes 1105924
  49.5 17.6 %collective-permute-start.17 = (bf16[2,2,720,128]{3,2,1,0:T(8,128)(2,1)S(1)}, bf16[2,2,720,128]{3,2,1,0:T(8,128)(2,1)S(1)}, u32[]{:S(2)}, u32[]{:S(2)}) collective-permute-start(bf16[2,2,720,128]{3,2,1,0:T(8,128)(2,1)S(1)} %collective-permute-done.3.refs_8_), channel_id=1, source_target_pairs={{0,8},{1,33},{2,10},{3,35},{4,12},{5,37},{6,14},{7,39},{8,0},{33,1... | collective-permute-start | bytes 2211848 | tf_op jit(solution)/shard_map/ppermute | solution.py:70
  49.5 17.6 %collective-permute-start.18 = (bf16[2,2,720,128]{3,2,1,0:T(8,128)(2,1)S(1)}, bf16[2,2,720,128]{3,2,1,0:T(8,128)(2,1)S(1)}, u32[]{:S(2)}, u32[]{:S(2)}) collective-permute-start(bf16[2,2,720,128]{3,2,1,0:T(8,128)(2,1)S(1)} %collective-permute-done.3.refs_8_), channel_id=1, source_target_pairs={{0,24},{1,97},{2,26},{3,99},{4,28},{5,101},{6,30},{7,103},{8,16},{... | collective-permute-start | bytes 2211848 | tf_op jit(solution)/shard_map/ppermute | solution.py:70
  51.6 1.0 %copy-start.4 = (bf16[288,640]{1,0:T(8,128)(2,1)S(1)}, bf16[288,640]{1,0:T(8,128)(2,1)}, u32[]{:S(2)}) copy-start(bf16[288,640]{1,0:T(8,128)(2,1)} %get-tuple-element.62.k_ref) | copy-start | bytes 1105924
  53.7 22.3 %collective-permute-start.16 = (bf16[2,2,720,128]{3,2,1,0:T(8,128)(2,1)S(1)}, bf16[2,2,720,128]{3,2,1,0:T(8,128)(2,1)S(1)}, u32[]{:S(2)}, u32[]{:S(2)}) collective-permute-start(bf16[2,2,720,128]{3,2,1,0:T(8,128)(2,1)S(1)} %collective-permute-done.12.refs_7_), channel_id=1, source_target_pairs={{0,4},{1,5},{2,6},{3,7},{4,0},{5,1},{6,2},{7,3},{8,12},{33,37},{10... | collective-permute-start | bytes 2211848 | tf_op jit(solution)/shard_map/ppermute | solution.py:70
  54.0 6.8 %collective-permute-start.13 = (bf16[2,2,144,128]{3,2,1,0:T(8,128)(2,1)S(1)}, bf16[2,2,144,128]{3,2,1,0:T(8,128)(2,1)S(1)}, u32[]{:S(2)}, u32[]{:S(2)}) collective-permute-start(bf16[2,2,144,128]{3,2,1,0:T(8,128)(2,1)S(1)} %get-tuple-element.67.refs_3_), channel_id=1, source_target_pairs={{0,96},{1,25},{2,98},{3,27},{4,100},{5,29},{6,102},{7,31},{8,104},... | collective-permute-start | bytes 442376 | tf_op jit(solution)/shard_map/ppermute | solution.py:70
  55.2 7.1 %collective-permute-start.14 = (bf16[2,2,144,128]{3,2,1,0:T(8,128)(2,1)S(1)}, bf16[2,2,144,128]{3,2,1,0:T(8,128)(2,1)S(1)}, u32[]{:S(2)}, u32[]{:S(2)}) collective-permute-start(bf16[2,2,144,128]{3,2,1,0:T(8,128)(2,1)S(1)} %get-tuple-element.66.refs_2_), channel_id=1, source_target_pairs={{0,64},{1,17},{2,66},{3,19},{4,68},{5,21},{6,70},{7,23},{8,72},{33... | collective-permute-start | bytes 442376 | tf_op jit(solution)/shard_map/ppermute | solution.py:70
  60.8 6.4 %collective-permute-start.15 = (bf16[2,2,144,128]{3,2,1,0:T(8,128)(2,1)S(1)}, bf16[2,2,144,128]{3,2,1,0:T(8,128)(2,1)S(1)}, u32[]{:S(2)}, u32[]{:S(2)}) collective-permute-start(bf16[2,2,144,128]{3,2,1,0:T(8,128)(2,1)S(1)} %get-tuple-element.65.refs_1_), channel_id=1, source_target_pairs={{0,32},{1,9},{2,34},{3,11},{4,36},{5,13},{6,38},{7,15},{8,40},{33,... | collective-permute-start | bytes 442376 | tf_op jit(solution)/shard_map/ppermute | solution.py:70
  78.4 5.3 %collective-permute-start.19 = (bf16[2,304,128]{2,1,0:T(8,128)(2,1)S(1)}, bf16[2,304,128]{2,1,0:T(8,128)(2,1)S(1)}, u32[]{:S(2)}, u32[]{:S(2)}) collective-permute-start(bf16[2,304,128]{2,1,0:T(8,128)(2,1)S(1)} %get-tuple-element.78), channel_id=1, source_target_pairs={{0,96},{1,25},{2,98},{3,27},{4,100},{5,29},{6,102},{7,31},{8,104},... | collective-permute-start | bytes 466952 | tf_op jit(solution)/shard_map/ppermute | solution.py:70
  79.7 6.8 %collective-permute-start.20 = (bf16[2,304,128]{2,1,0:T(8,128)(2,1)S(1)}, bf16[2,304,128]{2,1,0:T(8,128)(2,1)S(1)}, u32[]{:S(2)}, u32[]{:S(2)}) collective-permute-start(bf16[2,304,128]{2,1,0:T(8,128)(2,1)S(1)} %get-tuple-element.79), channel_id=1, source_target_pairs={{0,64},{1,17},{2,66},{3,19},{4,68},{5,21},{6,70},{7,23},{8,72},{33... | collective-permute-start | bytes 466952 | tf_op jit(solution)/shard_map/ppermute | solution.py:70
  79.7 8.4 %collective-permute-start.21 = (bf16[2,304,128]{2,1,0:T(8,128)(2,1)S(1)}, bf16[2,304,128]{2,1,0:T(8,128)(2,1)S(1)}, u32[]{:S(2)}, u32[]{:S(2)}) collective-permute-start(bf16[2,304,128]{2,1,0:T(8,128)(2,1)S(1)} %get-tuple-element.80), channel_id=1, source_target_pairs={{0,32},{1,9},{2,34},{3,11},{4,36},{5,13},{6,38},{7,15},{8,40},{33,... | collective-permute-start | bytes 466952 | tf_op jit(solution)/shard_map/ppermute | solution.py:70

commit v13 on v9

--- a/solution.py
+++ b/solution.py
@@ -669,10 +669,11 @@
     fresh_values = jnp.dot(modded, w_value, preferred_element_type=F32).astype(BF16)
     own_sq = sum_squares(query, key)
     squares = [own_sq] + [swap_tp(own_sq, z, c) for z, c in ((1, 1), (1, 0), (0, 1))]
-    far, fresh_values, *squares = lax.optimization_barrier((far, fresh_values, *squares))
+    fresh_values, *squares = lax.optimization_barrier((fresh_values, *squares))
+    fresh_keys, *sends = norm_rope(u, query, key, squares, q_gain, k_gain, cos, sin)
+    far, fresh_keys = lax.optimization_barrier((far, fresh_keys))
     far_one, far_three = swap_v(far, 1), swap_v(far, 3)
-    fresh_keys, *sends = norm_rope(u, query, key, squares, q_gain, k_gain, cos, sin)
-    near_two, fresh_keys = lax.optimization_barrier((near_two, fresh_keys))
+    near_two, sends[1] = lax.optimization_barrier((near_two, sends[1]))
     far_two = swap_z_hi(near_two)
     queries = exchange_u(sends)
     fresh_out, fresh_rows = fresh_attention(u, fresh_keys, fresh_values, sends)

time: 88.2 us -> 88.4 us (level)
  waiting for transfers between devices: 23.2 us -> 25.7 us
  starting transfers between devices: 25.8 us -> 24.1 us
    ppermute x22, waiting for transfers between devices: 23.2 us -> 25.7 us  [permute(): lax.ppermute(value, AXES, [(linear(*p), linear(*move(*p))) for p in place...]
    ppermute x22, starting transfers between devices: 25.8 us -> 24.1 us  [permute(): lax.ppermute(value, AXES, [(linear(*p), linear(*move(*p))) for p in place...]
  transfers between devices with their start and end apart: 22 -> 22, of which waited for: 10 -> 9; matrix products, arithmetic and copies ran while one was open for 6% -> 6% of each run, Pallas kernels for 21% -> 21%
where the time goes in v13:
time: 88.4 us; the launch traced here: 87.6 us
  waiting for transfers between devices  25.7 us (29%)
  Pallas kernels  24.9 us (28%)
  starting transfers between devices  24.1 us (27%)
  local copies, waits for them, and re-layouts  6.99 us (8%)
  matrix products  4.87 us (6%)
    ppermute x22, waiting for transfers between devices, permute(): lax.ppermute(value, AXES, [(linear(*p), linear(*move(*p))) for p in place...  25.7 us
    ppermute x22, starting transfers between devices, permute(): lax.ppermute(value, AXES, [(linear(*p), linear(*move(*p))) for p in place...  24.1 us
    pallas_call x2, Pallas kernels, stale_attention(): pl.pallas_call(functools.partial(stale_kernel, far, count), out_shape=out...  11.4 us
    pallas_call x1, Pallas kernels, modulate(): pl.pallas_call(modulate_kernel, out_shape=[jax.ShapeDtypeStruct((ROWS, D)...  7.78 us
    unnamed x28, local copies, waits for them, and re-layouts  6.99 us
    dot_general x1, matrix products, shards(): jnp.dot(modded, w_value, preferred_element_type=F32).astype(BF16)  2.44 us
    dot_general x1, matrix products, shards(): key = jnp.dot(modded, w_key, preferred_element_type=F32)  2.44 us
    pallas_call x1, Pallas kernels, norm_rope(): pl.pallas_call(rope_kernel, out_shape=[flat] + [send] * 4, in_specs=[smem...  1.8 us
  transfers between devices with their start and end apart: 22, of which 9 were waited for; matrix products, arithmetic and copies ran while one was open for 6% of the time, Pallas kernels for 21%

profile of v13, /device:TPU:0, one launch (start us, length us, event | category | flops | bytes accessed | tf_op | source)
XLA Modules:
  0.0 87.6 jit_solution(3024871938176981179)
XLA Ops:
  0.6 2.1 %collective-permute-start.5 = (bf16[288,1280]{1,0:T(8,128)(2,1)}, bf16[288,1280]{1,0:T(8,128)(2,1)S(1)}, u32[]{:S(2)}, u32[]{:S(2)}) collective-permute-start(bf16[288,1280]{1,0:T(8,128)(2,1)} %bitcast.12), channel_id=1, source_target_pairs={{0,2},{1,3},{2,0},{3,1},{4,6},{5,7},{6,4},{7,5},{8,10},{33,35},{10... | collective-permute-start | bytes 2211848 | tf_op jit(solution)/shard_map/ppermute | solution.py:70
  2.7 1.0 %copy-done.1 = bf16[2,144,640]{2,1,0:T(8,128)(2,1)S(1)} copy-done((bf16[2,144,640]{2,1,0:T(8,128)(2,1)S(1)}, bf16[2,144,640]{2,1,0:T(8,128)(2,1)}, u32[]{:S(2)}) %copy-start.1) | copy-done | bytes 368664
  3.7 1.0 %copy-done.2 = bf16[2,144,640]{2,1,0:T(8,128)(2,1)S(1)} copy-done((bf16[2,144,640]{2,1,0:T(8,128)(2,1)S(1)}, bf16[2,144,640]{2,1,0:T(8,128)(2,1)}, u32[]{:S(2)}) %copy-start.2) | copy-done | bytes 368664
  4.7 0.1 pack_stale.1
  4.8 3.1 %collective-permute-start = (bf16[2,2,144,128]{3,2,1,0:T(8,128)(2,1)S(1)}, bf16[2,2,144,128]{3,2,1,0:T(8,128)(2,1)S(1)}, u32[]{:S(2)}, u32[]{:S(2)}) collective-permute-start(bf16[2,2,144,128]{3,2,1,0:T(8,128)(2,1)S(1)} %get-tuple-element.43), channel_id=1, source_target_pairs={{0,96},{1,25},{2,98},{3,27},{4,100},{5,29},{6,102},{7,31},{8,104},... | collective-permute-start | bytes 442376 | tf_op jit(solution)/shard_map/ppermute | solution.py:70
  7.9 0.6 collective-permute-start.1
  8.5 1.0 %collective-permute-start.2 = (bf16[2,2,144,128]{3,2,1,0:T(8,128)(2,1)S(1)}, bf16[2,2,144,128]{3,2,1,0:T(8,128)(2,1)S(1)}, u32[]{:S(2)}, u32[]{:S(2)}) collective-permute-start(bf16[2,2,144,128]{3,2,1,0:T(8,128)(2,1)S(1)} %get-tuple-element.45), channel_id=1, source_target_pairs={{0,32},{1,9},{2,34},{3,11},{4,36},{5,13},{6,38},{7,15},{8,40},{33,... | collective-permute-start | bytes 442376 | tf_op jit(solution)/shard_map/ppermute | solution.py:70
  9.5 2.7 %collective-permute-done.refs_1_ = bf16[2,2,144,128]{3,2,1,0:T(8,128)(2,1)S(1)} collective-permute-done((bf16[2,2,144,128]{3,2,1,0:T(8,128)(2,1)S(1)}, bf16[2,2,144,128]{3,2,1,0:T(8,128)(2,1)S(1)}, u32[]{:S(2)}, u32[]{:S(2)}) %collective-permute-start) | collective-permute-done | bytes 147488 | tf_op jit(solution)/shard_map/ppermute | solution.py:70
  12.2 2.5 %collective-permute-done.1.refs_2_ = bf16[2,2,144,128]{3,2,1,0:T(8,128)(2,1)S(1)} collective-permute-done((bf16[2,2,144,128]{3,2,1,0:T(8,128)(2,1)S(1)}, bf16[2,2,144,128]{3,2,1,0:T(8,128)(2,1)S(1)}, u32[]{:S(2)}, u32[]{:S(2)}) %collective-permute-start.1) | collective-permute-done | bytes 147488 | tf_op jit(solution)/shard_map/ppermute | solution.py:70
  14.7 1.5 %collective-permute-done.2.refs_3_ = bf16[2,2,144,128]{3,2,1,0:T(8,128)(2,1)S(1)} collective-permute-done((bf16[2,2,144,128]{3,2,1,0:T(8,128)(2,1)S(1)}, bf16[2,2,144,128]{3,2,1,0:T(8,128)(2,1)S(1)}, u32[]{:S(2)}, u32[]{:S(2)}) %collective-permute-start.2) | collective-permute-done | bytes 147488 | tf_op jit(solution)/shard_map/ppermute | solution.py:70
  16.2 1.1 %copy-done = bf16[2,144,1280]{2,1,0:T(8,128)(2,1)S(1)} copy-done((bf16[2,144,1280]{2,1,0:T(8,128)(2,1)S(1)}, bf16[2,144,1280]{2,1,0:T(8,128)(2,1)}, u32[]{:S(2)}) %copy-start) | copy-done | bytes 737304
  17.3 0.8 copy-done.5
  18.1 0.8 copy-done.6
  18.9 0.7 copy-done.9
  19.5 0.7 copy-done.10
  20.2 0.9 %tables.1 = (f32[288,128]{1,0:T(8,128)S(1)}, f32[144,128]{1,0:T(8,128)S(1)}, f32[144,128]{1,0:T(8,128)S(1)}, f32[4,5120]{1,0:T(4,128)S(1)}, bf16[288,1280]{1,0:T(8,128)(2,1)S(1)}) custom-call(s32[144]{0:T(256)S(1)} %copy-done.9, f32[1,128]{1,0:T(1,128)S(1)} %copy-done.10, bf16[288,1280]{1,0:T(8,128)(2,1)S(1)} %bitcast.14, f32[2,5120]{1,0:T(2,128)S(1)} %copy-done.5, ...), custom_call_target="tpu_custom_call" | custom-call | flops 1843200 | bytes 1000000 | tf_op jit(solution)/shard_map/tables/pallas_call | solution.py:177
  21.2 0.1 collective-permute-start.6
  21.3 1.6 %collective-permute-start.7 = (bf16[2,2,720,128]{3,2,1,0:T(8,128)(2,1)S(1)}, bf16[2,2,720,128]{3,2,1,0:T(8,128)(2,1)S(1)}, u32[]{:S(2)}, u32[]{:S(2)}) collective-permute-start(bf16[2,2,720,128]{3,2,1,0:T(8,128)(2,1)S(1)} %assemble.1.after.refs_4_), channel_id=1, source_target_pairs={{0,8},{1,33},{2,10},{3,35},{4,12},{5,37},{6,14},{7,39},{8,0},{33,1... | collective-permute-start | bytes 2211848 | tf_op jit(solution)/shard_map/ppermute | solution.py:70
  22.8 2.1 %collective-permute-start.8 = (bf16[2,2,720,128]{3,2,1,0:T(8,128)(2,1)S(1)}, bf16[2,2,720,128]{3,2,1,0:T(8,128)(2,1)S(1)}, u32[]{:S(2)}, u32[]{:S(2)}) collective-permute-start(bf16[2,2,720,128]{3,2,1,0:T(8,128)(2,1)S(1)} %assemble.1.after.refs_4_), channel_id=1, source_target_pairs={{0,24},{1,97},{2,26},{3,99},{4,28},{5,101},{6,30},{7,103},{8,16},{... | collective-permute-start | bytes 2211848 | tf_op jit(solution)/shard_map/ppermute | solution.py:70
  24.9 0.1 pad_add_fusion.t_ref
  25.0 3.6 %collective-permute-start.3 = (bf16[2,2,720,128]{3,2,1,0:T(8,128)(2,1)S(1)}, bf16[2,2,720,128]{3,2,1,0:T(8,128)(2,1)S(1)}, u32[]{:S(2)}, u32[]{:S(2)}) collective-permute-start(bf16[2,2,720,128]{3,2,1,0:T(8,128)(2,1)S(1)} %assemble.1.after.refs_4_), channel_id=1, source_target_pairs={{0,4},{1,5},{2,6},{3,7},{4,0},{5,1},{6,2},{7,3},{8,12},{33,37},{10... | collective-permute-start | bytes 2211848 | tf_op jit(solution)/shard_map/ppermute | solution.py:70
  28.6 7.8 %modulate.1 = (bf16[288,5120]{1,0:T(8,128)(2,1)S(1)}, f32[288,640]{1,0:T(8,128)S(1)}) custom-call(s32[4]{0:T(128)S(1)} %pad_add_fusion.t_ref, bf16[288,1280]{1,0:T(8,128)(2,1)S(1)} %get-tuple-element.47.h0, bf16[288,1280]{1,0:T(8,128)(2,1)S(1)} %collective-permute-done.4.h1, bf16[288,1280]{1,0:T(8,128)(2,1)S(1)} %collective-permute-done.5.h2, ...), custom_call_target="tpu_custom_call" | custom-call | flops 1000 | bytes 30000000 | tf_op jit(solution)/shard_map/modulate/pallas_call | solution.py:275
  36.4 2.4 %fusion.k_ref = f32[288,640]{1,0:T(8,128)S(1)} fusion(bf16[288,5120]{1,0:T(8,128)(2,1)S(1)} %get-tuple-element.53, bf16[5120,640]{1,0:T(8,128)(2,1)S(1)} %copy-done.11), kind=kOutput, calls=%fused_computation.2 | convolution fusion | flops 1887436800 | bytes 10240000 | tf_op jit(solution)/shard_map/dot_general | solution.py:666
  38.9 1.2 %collective-permute-start.12 = (bf16[2,2,720,128]{3,2,1,0:T(8,128)(2,1)S(1)}, bf16[2,2,720,128]{3,2,1,0:T(8,128)(2,1)S(1)}, u32[]{:S(2)}, u32[]{:S(2)}) collective-permute-start(bf16[2,2,720,128]{3,2,1,0:T(8,128)(2,1)S(1)} %collective-permute-done.7.refs_5_), channel_id=1, source_target_pairs={{0,24},{1,97},{2,26},{3,99},{4,28},{5,101},{6,30},{7,103},{8,16},{... | collective-permute-start | bytes 2211848 | tf_op jit(solution)/shard_map/ppermute | solution.py:70
  40.1 0.2 sum_squares.1.s0
  40.4 0.1 collective-permute-start.10
  40.4 0.1 collective-permute-start.11
  40.5 2.0 %collective-permute-start.9 = (f32[8,384]{1,0:T(8,128)S(1)}, f32[8,384]{1,0:T(8,128)S(1)}, u32[]{:S(2)}, u32[]{:S(2)}) collective-permute-start(f32[8,384]{1,0:T(8,128)S(1)} %sum_squares.1.s0), channel_id=1, source_target_pairs={{0,3},{1,2},{2,1},{3,0},{4,7},{5,6},{6,5},{7,4},{8,11},{33,34},{10... | collective-permute-start | bytes 36872 | tf_op jit(solution)/shard_map/ppermute | solution.py:70
  42.6 2.4 %convolution_convert_fusion.v_ref = bf16[288,640]{1,0:T(8,128)(2,1)S(1)} fusion(bf16[288,5120]{1,0:T(8,128)(2,1)S(1)} %get-tuple-element.53, bf16[5120,640]{1,0:T(8,128)(2,1)S(1)} %bitcast.18), kind=kOutput, calls=%fused_computation | convolution fusion | flops 1887621120 | bytes 9871360 | tf_op jit(solution)/shard_map/dot_general | solution.py:669
  45.1 1.8 %norm_rope.1 = (bf16[288,640]{1,0:T(8,128)(2,1)}, bf16[2,2,144,128]{3,2,1,0:T(8,128)(2,1)S(1)}, bf16[2,2,144,128]{3,2,1,0:T(8,128)(2,1)S(1)}, bf16[2,2,144,128]{...) custom-call(s32[1]{0:T(128)} %bitcast.u_ref, f32[288,640]{1,0:T(8,128)S(1)} %get-tuple-element.52.q_ref, ...), custom_call_target="tpu_custom_call" | custom-call | flops 1000 | bytes 1000 | tf_op jit(solution)/shard_map/norm_rope/pallas_call | solution.py:348
  46.9 1.2 %collective-permute-start.16 = (bf16[2,2,720,128]{3,2,1,0:T(8,128)(2,1)S(1)}, bf16[2,2,720,128]{3,2,1,0:T(8,128)(2,1)S(1)}, u32[]{:S(2)}, u32[]{:S(2)}) collective-permute-start(bf16[2,2,720,128]{3,2,1,0:T(8,128)(2,1)S(1)} %collective-permute-done.3.refs_8_), channel_id=1, source_target_pairs={{0,8},{1,33},{2,10},{3,35},{4,12},{5,37},{6,14},{7,39},{8,0},{33,1... | collective-permute-start | bytes 2211848 | tf_op jit(solution)/shard_map/ppermute | solution.py:70
  48.0 1.3 %collective-permute-start.17 = (bf16[2,2,720,128]{3,2,1,0:T(8,128)(2,1)S(1)}, bf16[2,2,720,128]{3,2,1,0:T(8,128)(2,1)S(1)}, u32[]{:S(2)}, u32[]{:S(2)}) collective-permute-start(bf16[2,2,720,128]{3,2,1,0:T(8,128)(2,1)S(1)} %collective-permute-done.3.refs_8_), channel_id=1, source_target_pairs={{0,24},{1,97},{2,26},{3,99},{4,28},{5,101},{6,30},{7,103},{8,16},{... | collective-permute-start | bytes 2211848 | tf_op jit(solution)/shard_map/ppermute | solution.py:70
  49.3 2.4 %collective-permute-done.12.refs_7_ = bf16[2,2,720,128]{3,2,1,0:T(8,128)(2,1)S(1)} collective-permute-done((bf16[2,2,720,128]{3,2,1,0:T(8,128)(2,1)S(1)}, bf16[2,2,720,128]{3,2,1,0:T(8,128)(2,1)S(1)}, u32[]{:S(2)}, u32[]{:S(2)}) %collective-permute-start.12) | collective-permute-done | bytes 737312 | tf_op jit(solution)/shard_map/ppermute | solution.py:70
  51.7 0.1 collective-permute-start.18
  51.8 1.2 %collective-permute-start.13 = (bf16[2,2,144,128]{3,2,1,0:T(8,128)(2,1)S(1)}, bf16[2,2,144,128]{3,2,1,0:T(8,128)(2,1)S(1)}, u32[]{:S(2)}, u32[]{:S(2)}) collective-permute-start(bf16[2,2,144,128]{3,2,1,0:T(8,128)(2,1)S(1)} %get-tuple-element.69.refs_3_), channel_id=1, source_target_pairs={{0,96},{1,25},{2,98},{3,27},{4,100},{5,29},{6,102},{7,31},{8,104},... | collective-permute-start | bytes 442376 | tf_op jit(solution)/shard_map/ppermute | solution.py:70
  53.0 0.6 collective-permute-start.14
  53.6 5.0 %collective-permute-done.13.refs_1_ = bf16[2,2,144,128]{3,2,1,0:T(8,128)(2,1)S(1)} collective-permute-done((bf16[2,2,144,128]{3,2,1,0:T(8,128)(2,1)S(1)}, bf16[2,2,144,128]{3,2,1,0:T(8,128)(2,1)S(1)}, u32[]{:S(2)}, u32[]{:S(2)}) %collective-permute-start.13) | collective-permute-done | bytes 147488 | tf_op jit(solution)/shard_map/ppermute | solution.py:70
  58.6 1.0 %copy-done.4 = bf16[288,640]{1,0:T(8,128)(2,1)S(1)} copy-done((bf16[288,640]{1,0:T(8,128)(2,1)S(1)}, bf16[288,640]{1,0:T(8,128)(2,1)}, u32[]{:S(2)}) %copy-start.4) | copy-done | bytes 368664
  59.6 1.0 %fresh_attention.1 = (f32[2,5,144,128]{3,2,1,0:T(8,128)S(1)}, f32[24,128]{1,0:T(8,128)S(1)}) custom-call(s32[1]{0:T(128)} %bitcast.u_ref, bf16[288,640]{1,0:T(8,128)(2,1)S(1)} %copy-done.4, bf16[288,640]{1,0:T(8,128)(2,1)S(1)} %convolution_convert_fusion.v_ref, bf16[2,2,144,128]{3,2,1,0:T(8,128)(2,1)S(1)} %get-tuple-element.64.refs_0_, ...), custom_call_target="tpu_custom_call" | custom-call | flops 1000 | bytes 1000 | tf_op jit(solution)/shard_map/fresh_attention/pallas_call | solution.py:398
  60.6 4.3 %collective-permute-done.15.refs_3_ = bf16[2,2,144,128]{3,2,1,0:T(8,128)(2,1)S(1)} collective-permute-done((bf16[2,2,144,128]{3,2,1,0:T(8,128)(2,1)S(1)}, bf16[2,2,144,128]{3,2,1,0:T(8,128)(2,1)S(1)}, u32[]{:S(2)}, u32[]{:S(2)}) %collective-permute-start.15) | collective-permute-done | bytes 147488 | tf_op jit(solution)/shard_map/ppermute | solution.py:70
  64.9 6.7 %near_attention.1 = (f32[2,4,2,144,128]{4,3,2,1,0:T(8,128)S(1)}, f32[2,4,2,144,128]{4,3,2,1,0:T(8,128)S(1)}) custom-call(bf16[2,2,144,128]{3,2,1,0:T(8,128)(2,1)S(1)} %get-tuple-element.64.refs_0_, bf16[2,2,144,128]{3,2,1,0:T(8,128)(2,1)S(1)} %collective-permute-done.13.refs_1_, bf16[2,2,144,128]{3,2,1,0:T(8,128)(2,1)S(1)} %collective-permute-done.14.refs_2_, ...), custom_call_target="tpu_custom_call" | custom-call | flops 1000 | bytes 1000 | tf_op jit(solution)/shard_map/near_attention/pallas_call | solution.py:556
  71.6 4.8 %far_attention.1 = (bf16[2,304,128]{2,1,0:T(8,128)(2,1)S(1)}, bf16[2,304,128]{2,1,0:T(8,128)(2,1)S(1)}, bf16[2,304,128]{2,1,0:T(8,128)(2,1)S(1)}, bf16[2,304,128]{2,1,0:T(8,128)(2,1)S(1)}) custom-call(bf16[2,2,144,128]{3,2,1,0:T(8,128)(2,1)S(1)} %get-tuple-element.64.refs_0_, bf16[2,2,144,128]{3,2,1,0:T(8,128)(2,1)S(1)} %collective-permute-done.13.refs_1_, ...), custom_call_target="tpu_custom_call" | custom-call | flops 1000 | bytes 1000 | tf_op jit(solution)/shard_map/far_attention/pallas_call | solution.py:556
  76.4 1.3 %collective-permute-start.19 = (bf16[2,304,128]{2,1,0:T(8,128)(2,1)S(1)}, bf16[2,304,128]{2,1,0:T(8,128)(2,1)S(1)}, u32[]{:S(2)}, u32[]{:S(2)}) collective-permute-start(bf16[2,304,128]{2,1,0:T(8,128)(2,1)S(1)} %get-tuple-element.78), channel_id=1, source_target_pairs={{0,96},{1,25},{2,98},{3,27},{4,100},{5,29},{6,102},{7,31},{8,104},... | collective-permute-start | bytes 466952 | tf_op jit(solution)/shard_map/ppermute | solution.py:70
  77.7 0.9 %collective-permute-start.21 = (bf16[2,304,128]{2,1,0:T(8,128)(2,1)S(1)}, bf16[2,304,128]{2,1,0:T(8,128)(2,1)S(1)}, u32[]{:S(2)}, u32[]{:S(2)}) collective-permute-start(bf16[2,304,128]{2,1,0:T(8,128)(2,1)S(1)} %get-tuple-element.80), channel_id=1, source_target_pairs={{0,32},{1,9},{2,34},{3,11},{4,36},{5,13},{6,38},{7,15},{8,40},{33,... | collective-permute-start | bytes 466952 | tf_op jit(solution)/shard_map/ppermute | solution.py:70
  78.6 3.1 %collective-permute-done.19.refs_1_ = bf16[2,304,128]{2,1,0:T(8,128)(2,1)S(1)} collective-permute-done((bf16[2,304,128]{2,1,0:T(8,128)(2,1)S(1)}, bf16[2,304,128]{2,1,0:T(8,128)(2,1)S(1)}, u32[]{:S(2)}, u32[]{:S(2)}) %collective-permute-start.19) | collective-permute-done | bytes 155680 | tf_op jit(solution)/shard_map/ppermute | solution.py:70
  81.7 2.8 %collective-permute-done.20.refs_2_ = bf16[2,304,128]{2,1,0:T(8,128)(2,1)S(1)} collective-permute-done((bf16[2,304,128]{2,1,0:T(8,128)(2,1)S(1)}, bf16[2,304,128]{2,1,0:T(8,128)(2,1)S(1)}, u32[]{:S(2)}, u32[]{:S(2)}) %collective-permute-start.20) | collective-permute-done | bytes 155680 | tf_op jit(solution)/shard_map/ppermute | solution.py:70
  84.5 1.5 %collective-permute-done.21.refs_3_ = bf16[2,304,128]{2,1,0:T(8,128)(2,1)S(1)} collective-permute-done((bf16[2,304,128]{2,1,0:T(8,128)(2,1)S(1)}, bf16[2,304,128]{2,1,0:T(8,128)(2,1)S(1)}, u32[]{:S(2)}, u32[]{:S(2)}) %collective-permute-start.21) | collective-permute-done | bytes 155680 | tf_op jit(solution)/shard_map/ppermute | solution.py:70
  86.0 1.5 %merge.1 = bf16[2,144,640]{2,1,0:T(8,128)(2,1)} custom-call(s32[1]{0:T(128)} %bitcast.u_ref, f32[2,5,144,128]{3,2,1,0:T(8,128)S(1)} %get-tuple-element.70.fresh_out, f32[24,128]{1,0:T(8,128)S(1)} %get-tuple-element.71.refs_9_.fresh_rows, bf16[2,304,128]{2,1,0:T(8,128)(2,1)S(1)} %get-tuple-element.77.refs_0_, ...), custom_call_target="tpu_custom_call" | custom-call | flops 1843200 | bytes 2580480 | tf_op jit(solution)/shard_map/merge/pallas_call | solution.py:620
  (38 shorter events, 0.1 us)
Async XLA Ops:
  0.6 20.5 %collective-permute-start.5 = (bf16[288,1280]{1,0:T(8,128)(2,1)}, bf16[288,1280]{1,0:T(8,128)(2,1)S(1)}, u32[]{:S(2)}, u32[]{:S(2)}) collective-permute-start(bf16[288,1280]{1,0:T(8,128)(2,1)} %bitcast.12), channel_id=1, source_target_pairs={{0,2},{1,3},{2,0},{3,1},{4,6},{5,7},{6,4},{7,5},{8,10},{33,35},{10... | collective-permute-start | bytes 2211848 | tf_op jit(solution)/shard_map/ppermute | solution.py:70
  2.7 1.0 %copy-start.1 = (bf16[2,144,640]{2,1,0:T(8,128)(2,1)S(1)}, bf16[2,144,640]{2,1,0:T(8,128)(2,1)}, u32[]{:S(2)}) copy-start(bf16[2,144,640]{2,1,0:T(8,128)(2,1)} %key_ref.1) | copy-start | bytes 1105924
  3.7 1.0 %copy-start.2 = (bf16[2,144,640]{2,1,0:T(8,128)(2,1)S(1)}, bf16[2,144,640]{2,1,0:T(8,128)(2,1)}, u32[]{:S(2)}) copy-start(bf16[2,144,640]{2,1,0:T(8,128)(2,1)} %value_ref.1) | copy-start | bytes 1105924
  4.8 7.4 %collective-permute-start = (bf16[2,2,144,128]{3,2,1,0:T(8,128)(2,1)S(1)}, bf16[2,2,144,128]{3,2,1,0:T(8,128)(2,1)S(1)}, u32[]{:S(2)}, u32[]{:S(2)}) collective-permute-start(bf16[2,2,144,128]{3,2,1,0:T(8,128)(2,1)S(1)} %get-tuple-element.43), channel_id=1, source_target_pairs={{0,96},{1,25},{2,98},{3,27},{4,100},{5,29},{6,102},{7,31},{8,104},... | collective-permute-start | bytes 442376 | tf_op jit(solution)/shard_map/ppermute | solution.py:70
  7.9 6.8 %collective-permute-start.1 = (bf16[2,2,144,128]{3,2,1,0:T(8,128)(2,1)S(1)}, bf16[2,2,144,128]{3,2,1,0:T(8,128)(2,1)S(1)}, u32[]{:S(2)}, u32[]{:S(2)}) collective-permute-start(bf16[2,2,144,128]{3,2,1,0:T(8,128)(2,1)S(1)} %get-tuple-element.44), channel_id=1, source_target_pairs={{0,64},{1,17},{2,66},{3,19},{4,68},{5,21},{6,70},{7,23},{8,72},{33... | collective-permute-start | bytes 442376 | tf_op jit(solution)/shard_map/ppermute | solution.py:70
  8.5 7.6 %collective-permute-start.2 = (bf16[2,2,144,128]{3,2,1,0:T(8,128)(2,1)S(1)}, bf16[2,2,144,128]{3,2,1,0:T(8,128)(2,1)S(1)}, u32[]{:S(2)}, u32[]{:S(2)}) collective-permute-start(bf16[2,2,144,128]{3,2,1,0:T(8,128)(2,1)S(1)} %get-tuple-element.45), channel_id=1, source_target_pairs={{0,32},{1,9},{2,34},{3,11},{4,36},{5,13},{6,38},{7,15},{8,40},{33,... | collective-permute-start | bytes 442376 | tf_op jit(solution)/shard_map/ppermute | solution.py:70
  9.5 19.1 %collective-permute-start.4 = (bf16[288,1280]{1,0:T(8,128)(2,1)}, bf16[288,1280]{1,0:T(8,128)(2,1)S(1)}, u32[]{:S(2)}, u32[]{:S(2)}) collective-permute-start(bf16[288,1280]{1,0:T(8,128)(2,1)} %bitcast.13), channel_id=1, source_target_pairs={{0,1},{1,0},{2,3},{3,2},{4,5},{5,4},{6,7},{7,6},{8,9},{33,32},{10,... | collective-permute-start | bytes 2211848 | tf_op jit(solution)/shard_map/ppermute | solution.py:70
  16.2 1.1 %copy-start = (bf16[2,144,1280]{2,1,0:T(8,128)(2,1)S(1)}, bf16[2,144,1280]{2,1,0:T(8,128)(2,1)}, u32[]{:S(2)}) copy-start(bf16[2,144,1280]{2,1,0:T(8,128)(2,1)} %param.12) | copy-start | bytes 2211844
  17.3 0.8 copy-start.5
  18.1 0.8 copy-start.6
  18.9 0.7 copy-start.9
  19.5 0.7 copy-start.10
  21.2 7.5 %collective-permute-start.6 = (bf16[288,1280]{1,0:T(8,128)(2,1)S(1)}, bf16[288,1280]{1,0:T(8,128)(2,1)}, u32[]{:S(2)}, u32[]{:S(2)}) collective-permute-start(bf16[288,1280]{1,0:T(8,128)(2,1)S(1)} %collective-permute-done.5.h2), channel_id=1, source_target_pairs={{0,1},{1,0},{2,3},{3,2},{4,5},{5,4},{6,7},{7,6},{8,9},{33,32},{10,... | collective-permute-start | bytes 2211848 | tf_op jit(solution)/shard_map/ppermute | solution.py:70
  21.3 15.2 %copy-start.11 = (bf16[5120,640]{1,0:T(8,128)(2,1)S(1)}, bf16[5120,640]{1,0:T(8,128)(2,1)}, u32[]{:S(2)}) copy-start(bf16[5120,640]{1,0:T(8,128)(2,1)} %param.16) | copy-start | bytes 19660804
  21.3 17.6 %collective-permute-start.7 = (bf16[2,2,720,128]{3,2,1,0:T(8,128)(2,1)S(1)}, bf16[2,2,720,128]{3,2,1,0:T(8,128)(2,1)S(1)}, u32[]{:S(2)}, u32[]{:S(2)}) collective-permute-start(bf16[2,2,720,128]{3,2,1,0:T(8,128)(2,1)S(1)} %assemble.1.after.refs_4_), channel_id=1, source_target_pairs={{0,8},{1,33},{2,10},{3,35},{4,12},{5,37},{6,14},{7,39},{8,0},{33,1... | collective-permute-start | bytes 2211848 | tf_op jit(solution)/shard_map/ppermute | solution.py:70
  22.8 16.1 %collective-permute-start.8 = (bf16[2,2,720,128]{3,2,1,0:T(8,128)(2,1)S(1)}, bf16[2,2,720,128]{3,2,1,0:T(8,128)(2,1)S(1)}, u32[]{:S(2)}, u32[]{:S(2)}) collective-permute-start(bf16[2,2,720,128]{3,2,1,0:T(8,128)(2,1)S(1)} %assemble.1.after.refs_4_), channel_id=1, source_target_pairs={{0,24},{1,97},{2,26},{3,99},{4,28},{5,101},{6,30},{7,103},{8,16},{... | collective-permute-start | bytes 2211848 | tf_op jit(solution)/shard_map/ppermute | solution.py:70
  25.0 21.8 %collective-permute-start.3 = (bf16[2,2,720,128]{3,2,1,0:T(8,128)(2,1)S(1)}, bf16[2,2,720,128]{3,2,1,0:T(8,128)(2,1)S(1)}, u32[]{:S(2)}, u32[]{:S(2)}) collective-permute-start(bf16[2,2,720,128]{3,2,1,0:T(8,128)(2,1)S(1)} %assemble.1.after.refs_4_), channel_id=1, source_target_pairs={{0,4},{1,5},{2,6},{3,7},{4,0},{5,1},{6,2},{7,3},{8,12},{33,37},{10... | collective-permute-start | bytes 2211848 | tf_op jit(solution)/shard_map/ppermute | solution.py:70
  28.6 13.9 %slice-start = ((s8[6553600]{0:T(1024)(128)(4,1)}), s8[2359296]{0:T(1024)(128)(4,1)S(1)}, s32[]{:S(2)}) async-start(s8[6553600]{0:T(1024)(128)(4,1)} %bitcast.17), calls=%async_computation | async-start | bytes 4718592
  36.4 6.1 %slice-start.1 = ((s8[6553600]{0:T(1024)(128)(4,1)}), s8[4194304]{0:T(1024)(128)(4,1)S(1)}, s32[]{:S(2)}) async-start(s8[6553600]{0:T(1024)(128)(4,1)} %bitcast.17), calls=%async_computation.1 | async-start | bytes 8388608
  38.9 12.8 %collective-permute-start.12 = (bf16[2,2,720,128]{3,2,1,0:T(8,128)(2,1)S(1)}, bf16[2,2,720,128]{3,2,1,0:T(8,128)(2,1)S(1)}, u32[]{:S(2)}, u32[]{:S(2)}) collective-permute-start(bf16[2,2,720,128]{3,2,1,0:T(8,128)(2,1)S(1)} %collective-permute-done.7.refs_5_), channel_id=1, source_target_pairs={{0,24},{1,97},{2,26},{3,99},{4,28},{5,101},{6,30},{7,103},{8,16},{... | collective-permute-start | bytes 2211848 | tf_op jit(solution)/shard_map/ppermute | solution.py:70
  40.3 4.7 %copy-start.7 = (f32[640]{0:T(1024)S(1)}, f32[640]{0:T(1024)}, u32[]{:S(2)}) copy-start(f32[640]{0:T(1024)} %qg.1) | copy-start | bytes 7684
  40.4 4.7 %copy-start.8 = (f32[640]{0:T(1024)S(1)}, f32[640]{0:T(1024)}, u32[]{:S(2)}) copy-start(f32[640]{0:T(1024)} %kg.1) | copy-start | bytes 7684
  40.4 4.7 %collective-permute-start.10 = (f32[8,384]{1,0:T(8,128)S(1)}, f32[8,384]{1,0:T(8,128)S(1)}, u32[]{:S(2)}, u32[]{:S(2)}) collective-permute-start(f32[8,384]{1,0:T(8,128)S(1)} %sum_squares.1.s0), channel_id=1, source_target_pairs={{0,2},{1,3},{2,0},{3,1},{4,6},{5,7},{6,4},{7,5},{8,10},{33,35},{10... | collective-permute-start | bytes 36872 | tf_op jit(solution)/shard_map/ppermute | solution.py:70
  40.4 4.6 %collective-permute-start.11 = (f32[8,384]{1,0:T(8,128)S(1)}, f32[8,384]{1,0:T(8,128)S(1)}, u32[]{:S(2)}, u32[]{:S(2)}) collective-permute-start(f32[8,384]{1,0:T(8,128)S(1)} %sum_squares.1.s0), channel_id=1, source_target_pairs={{0,1},{1,0},{2,3},{3,2},{4,5},{5,4},{6,7},{7,6},{8,9},{33,32},{10,... | collective-permute-start | bytes 36872 | tf_op jit(solution)/shard_map/ppermute | solution.py:70
  40.5 4.5 %collective-permute-start.9 = (f32[8,384]{1,0:T(8,128)S(1)}, f32[8,384]{1,0:T(8,128)S(1)}, u32[]{:S(2)}, u32[]{:S(2)}) collective-permute-start(f32[8,384]{1,0:T(8,128)S(1)} %sum_squares.1.s0), channel_id=1, source_target_pairs={{0,3},{1,2},{2,1},{3,0},{4,7},{5,6},{6,5},{7,4},{8,11},{33,34},{10... | collective-permute-start | bytes 36872 | tf_op jit(solution)/shard_map/ppermute | solution.py:70
  45.0 42.6 %copy-start.3 = (bf16[288,640]{1,0:T(8,128)(2,1)}, bf16[288,640]{1,0:T(8,128)(2,1)S(1)}, u32[]{:S(2)}) copy-start(bf16[288,640]{1,0:T(8,128)(2,1)S(1)} %convolution_convert_fusion.v_ref) | copy-start | bytes 1105924
  46.9 24.7 %collective-permute-start.16 = (bf16[2,2,720,128]{3,2,1,0:T(8,128)(2,1)S(1)}, bf16[2,2,720,128]{3,2,1,0:T(8,128)(2,1)S(1)}, u32[]{:S(2)}, u32[]{:S(2)}) collective-permute-start(bf16[2,2,720,128]{3,2,1,0:T(8,128)(2,1)S(1)} %collective-permute-done.3.refs_8_), channel_id=1, source_target_pairs={{0,8},{1,33},{2,10},{3,35},{4,12},{5,37},{6,14},{7,39},{8,0},{33,1... | collective-permute-start | bytes 2211848 | tf_op jit(solution)/shard_map/ppermute | solution.py:70
  48.0 23.6 %collective-permute-start.17 = (bf16[2,2,720,128]{3,2,1,0:T(8,128)(2,1)S(1)}, bf16[2,2,720,128]{3,2,1,0:T(8,128)(2,1)S(1)}, u32[]{:S(2)}, u32[]{:S(2)}) collective-permute-start(bf16[2,2,720,128]{3,2,1,0:T(8,128)(2,1)S(1)} %collective-permute-done.3.refs_8_), channel_id=1, source_target_pairs={{0,24},{1,97},{2,26},{3,99},{4,28},{5,101},{6,30},{7,103},{8,16},{... | collective-permute-start | bytes 2211848 | tf_op jit(solution)/shard_map/ppermute | solution.py:70
  51.7 19.9 %collective-permute-start.18 = (bf16[2,2,720,128]{3,2,1,0:T(8,128)(2,1)S(1)}, bf16[2,2,720,128]{3,2,1,0:T(8,128)(2,1)S(1)}, u32[]{:S(2)}, u32[]{:S(2)}) collective-permute-start(bf16[2,2,720,128]{3,2,1,0:T(8,128)(2,1)S(1)} %collective-permute-done.12.refs_7_), channel_id=1, source_target_pairs={{0,4},{1,5},{2,6},{3,7},{4,0},{5,1},{6,2},{7,3},{8,12},{33,37},{10... | collective-permute-start | bytes 2211848 | tf_op jit(solution)/shard_map/ppermute | solution.py:70
  51.8 6.8 %collective-permute-start.13 = (bf16[2,2,144,128]{3,2,1,0:T(8,128)(2,1)S(1)}, bf16[2,2,144,128]{3,2,1,0:T(8,128)(2,1)S(1)}, u32[]{:S(2)}, u32[]{:S(2)}) collective-permute-start(bf16[2,2,144,128]{3,2,1,0:T(8,128)(2,1)S(1)} %get-tuple-element.69.refs_3_), channel_id=1, source_target_pairs={{0,96},{1,25},{2,98},{3,27},{4,100},{5,29},{6,102},{7,31},{8,104},... | collective-permute-start | bytes 442376 | tf_op jit(solution)/shard_map/ppermute | solution.py:70
  53.0 7.6 %collective-permute-start.14 = (bf16[2,2,144,128]{3,2,1,0:T(8,128)(2,1)S(1)}, bf16[2,2,144,128]{3,2,1,0:T(8,128)(2,1)S(1)}, u32[]{:S(2)}, u32[]{:S(2)}) collective-permute-start(bf16[2,2,144,128]{3,2,1,0:T(8,128)(2,1)S(1)} %get-tuple-element.68.refs_2_), channel_id=1, source_target_pairs={{0,64},{1,17},{2,66},{3,19},{4,68},{5,21},{6,70},{7,23},{8,72},{33... | collective-permute-start | bytes 442376 | tf_op jit(solution)/shard_map/ppermute | solution.py:70
  58.6 6.4 %collective-permute-start.15 = (bf16[2,2,144,128]{3,2,1,0:T(8,128)(2,1)S(1)}, bf16[2,2,144,128]{3,2,1,0:T(8,128)(2,1)S(1)}, u32[]{:S(2)}, u32[]{:S(2)}) collective-permute-start(bf16[2,2,144,128]{3,2,1,0:T(8,128)(2,1)S(1)} %get-tuple-element.67.refs_1_), channel_id=1, source_target_pairs={{0,32},{1,9},{2,34},{3,11},{4,36},{5,13},{6,38},{7,15},{8,40},{33,... | collective-permute-start | bytes 442376 | tf_op jit(solution)/shard_map/ppermute | solution.py:70
  58.6 1.0 %copy-start.4 = (bf16[288,640]{1,0:T(8,128)(2,1)S(1)}, bf16[288,640]{1,0:T(8,128)(2,1)}, u32[]{:S(2)}) copy-start(bf16[288,640]{1,0:T(8,128)(2,1)} %get-tuple-element.62.k_ref) | copy-start | bytes 1105924
  76.4 5.3 %collective-permute-start.19 = (bf16[2,304,128]{2,1,0:T(8,128)(2,1)S(1)}, bf16[2,304,128]{2,1,0:T(8,128)(2,1)S(1)}, u32[]{:S(2)}, u32[]{:S(2)}) collective-permute-start(bf16[2,304,128]{2,1,0:T(8,128)(2,1)S(1)} %get-tuple-element.78), channel_id=1, source_target_pairs={{0,96},{1,25},{2,98},{3,27},{4,100},{5,29},{6,102},{7,31},{8,104},... | collective-permute-start | bytes 466952 | tf_op jit(solution)/shard_map/ppermute | solution.py:70
  77.7 6.8 %collective-permute-start.20 = (bf16[2,304,128]{2,1,0:T(8,128)(2,1)S(1)}, bf16[2,304,128]{2,1,0:T(8,128)(2,1)S(1)}, u32[]{:S(2)}, u32[]{:S(2)}) collective-permute-start(bf16[2,304,128]{2,1,0:T(8,128)(2,1)S(1)} %get-tuple-element.79), channel_id=1, source_target_pairs={{0,64},{1,17},{2,66},{3,19},{4,68},{5,21},{6,70},{7,23},{8,72},{33... | collective-permute-start | bytes 466952 | tf_op jit(solution)/shard_map/ppermute | solution.py:70
  77.7 8.4 %collective-permute-start.21 = (bf16[2,304,128]{2,1,0:T(8,128)(2,1)S(1)}, bf16[2,304,128]{2,1,0:T(8,128)(2,1)S(1)}, u32[]{:S(2)}, u32[]{:S(2)}) collective-permute-start(bf16[2,304,128]{2,1,0:T(8,128)(2,1)S(1)} %get-tuple-element.80), channel_id=1, source_target_pairs={{0,32},{1,9},{2,34},{3,11},{4,36},{5,13},{6,38},{7,15},{8,40},{33,... | collective-permute-start | bytes 466952 | tf_op jit(solution)/shard_map/ppermute | solution.py:70
